TPU v7x, 32 devices: a whole 2x2x4 slice. The times are simulated.
32 devices in a mesh: seq: 2 (over core), vocab: 4 (over y, x), section: 4 (over z).
Axes of the slice: x: 2, y: 2, z: 4, core: 2. Of those that a mesh axis runs over, the one named last changes fastest.
Arguments:
- hidden: bfloat16 [4096, 5120], P(('seq', 'vocab', 'section')), parts along dimension 0, may hold values from -8 to 8
- head_weight: bfloat16 [1024, 5120], P(('seq', 'vocab')), parts along dimension 0, may hold values from -1 to 1
- tokens: int32 [4096], P(('seq', 'vocab', 'section')), parts along dimension 0, may hold values from 0 to 511
- rewards: float32 [4096], P(('seq', 'vocab', 'section')), parts along dimension 0, may hold values from -48 to 48
- group_ids: int32 [4096], P(('seq', 'vocab', 'section')), parts along dimension 0, may hold values from 0 to 255, never falling along the last dimension, each value on 1 to 16 neighbouring positions
Outputs:
- logits: bfloat16 [4096, 512], P(('seq', 'vocab', 'section')), parts along dimension 0
- logprob: float32 [4096], P(('seq', 'vocab', 'section')), parts along dimension 0
- entropy: float32 [4096], P(('seq', 'vocab', 'section')), parts along dimension 0
- previous_grad: bfloat16 [4096, 5120], P(('seq', 'vocab', 'section')), parts along dimension 0
There are 2 independent parts, one for each index of `seq`. A program takes and returns all parts, laid end to end along the dimension named above; each array names one. Nothing has to cross between parts.
Inputs may be any that keep to these rules, and one draw needn't show every extreme that they name: `group_ids`: ids never fall along the rows, every id is used, a group holds 1 to 16 rows and some group exactly 16; row counts of groups, and any partial count of one device, are whole numbers of at most 16 that a program may pack several to a word before they are summed.
All inputs are finite; a program needn't handle non-finite values.
Results may differ from a plain program's by a relative error of at most 0.0049.
Values may be sent and summed in bfloat16 or wider, within the bound.
No kernel may reach another device: no remote copies, remote signals or barrier semaphores. Data moves between devices by JAX's collectives and lax.ppermute only.
A program may use at most 64 MiB of HBM per device.

v0:
```python
import jax
import jax.numpy as jnp
from jax import lax
from jax.sharding import PartitionSpec as P


def swapped(value, axis, distance):
    mask = 2**distance
    pairs = [(source, source ^ mask) for source in range(lax.axis_size(axis))]
    return lax.ppermute(value, axis, pairs)


def body(hidden, head_weight, tokens, rewards, group_ids):
    members = lax.axis_size(("vocab", "section"))
    shards = lax.axis_size("vocab")
    row_count, model_width = hidden.shape
    shard_rows = head_weight.shape[0]
    vocab_all = shard_rows * shards
    incoming = lax.all_gather(head_weight, "vocab", axis=0, tiled=True)
    stored_scores = lax.dot_general(
        hidden, incoming, (((1,), (1,)), ((), ())), preferred_element_type=jnp.float32
    )
    logits = stored_scores.astype(jnp.bfloat16)
    row_max = jnp.max(stored_scores, axis=1, keepdims=True)
    unnormed = jnp.exp(stored_scores - row_max)
    denominator = jnp.sum(unnormed, axis=1, keepdims=True)
    probabilities = unnormed / denominator
    log_total = (row_max + jnp.log(denominator))[:, 0]
    chosen = jnp.arange(vocab_all, dtype=jnp.int32)[None, :] == tokens[:, None]
    picked = jnp.sum(jnp.where(chosen, stored_scores, jnp.zeros_like(stored_scores)), axis=1)
    logprob = picked - log_total
    entropy = log_total - jnp.sum(probabilities * stored_scores, axis=1)
    group_total = row_count * members // 8
    member = (group_ids[:, None] == jnp.arange(group_total, dtype=jnp.int32)[None, :]).astype(
        jnp.float32
    )
    local_sums = jnp.dot(rewards, member, precision=lax.Precision.HIGHEST)
    local_counts = jnp.sum(member, axis=0)
    group_sums, group_counts = lax.psum((local_sums, local_counts), ("vocab", "section"))
    row_means = jnp.dot(member, group_sums / group_counts, precision=lax.Precision.HIGHEST)
    advantage = rewards - row_means
    dlogits = (advantage[:, None] * (probabilities - chosen.astype(jnp.float32))).astype(
        jnp.bfloat16
    )
    gradient = jnp.dot(dlogits, incoming, preferred_element_type=jnp.float32)
    previous_grad = swapped(gradient.astype(jnp.bfloat16), "section", 0)
    return (logits, logprob, entropy, previous_grad)


def solution(mesh):
    placed = (
        P(("seq", "vocab", "section"), None),
        P(("seq", "vocab"), None),
        P(("seq", "vocab", "section")),
        P(("seq", "vocab", "section")),
        P(("seq", "vocab", "section")),
    )
    return jax.shard_map(
        body,
        mesh=mesh,
        in_specs=placed,
        out_specs=(
            P(("seq", "vocab", "section"), None),
            P(("seq", "vocab", "section")),
            P(("seq", "vocab", "section")),
            P(("seq", "vocab", "section"), None),
        ),
        check_vma=False,
    )
```

profile of v0, /device:TPU:0, one launch (start us, length us, event | category | flops | bytes accessed | tf_op | source)
XLA Modules:
  0.0 118.6 jit_solution(5243568740213153953)
XLA Ops:
  7.2 0.0 copy-start
  7.2 0.0 copy-start.4
  7.2 0.0 copy-start.3
  7.2 0.0 all-gather.2.cloned.1.call-start
  7.2 0.7 all-gather.2.cloned.1.call-update
  7.9 0.0 copy-done.4
  7.9 0.1 convert_reduce_fusion
  8.0 0.0 copy-done.3
  8.1 0.2 fusion.4
  8.2 44.3 %all-reduce = (f32[256]{0:T(256)S(1)}, f32[256]{0:T(256)S(1)}) all-reduce(f32[256]{0:T(256)S(1)} %bitcast.14, f32[256]{0:T(256)S(1)} %convert_reduce_fusion), channel_id=1, replica_groups=mesh['seq'=2,'vocab'=4,'section'=4] {'vocab','section'}, use_global_device_ids=true, to_apply=%region_4.5 | all-reduce | flops 512 | bytes 4096 | tf_op jit(solution)/shard_map/psum | solution.py:39
  52.5 0.2 fusion
  52.7 0.0 copy-start.2
  52.7 21.7 %all-gather.2.cloned.1.call-done = bf16[512,5120]{1,0:T(8,128)(2,1)} async-done(((bf16[128,5120]{1,0:T(8,128)(2,1)}), bf16[512,5120]{1,0:T(8,128)(2,1)}) %all-gather.2.cloned.1.call-update) | async-done | bytes 5242896 | tf_op jit(solution)/shard_map/all_gather | solution.py:19
  74.4 0.0 copy-done
  74.4 4.6 %fusion.13 = (f32[128]{0:T(128)S(1)}, f32[128,512]{1,0:T(8,128)S(1)}) fusion(bf16[128,5120]{1,0:T(8,128)(2,1)S(1)} %copy-done, bf16[512,5120]{1,0:T(8,128)(2,1)} %all-gather.2.cloned.1.call-done), kind=kOutput, calls=%fused_computation.23 | convolution fusion | flops 671154048 | bytes 6816256 | tf_op jit(solution)/shard_map/dot_general | solution.py:20
  79.0 0.2 fusion.2
  79.2 0.0 copy-done.2
  79.2 0.0 copy-done.1
  79.2 0.9 convolution_convert_fusion
  80.1 1.5 %collective-permute-start = (bf16[128,5120]{1,0:T(8,128)(2,1)S(1)}, bf16[128,5120]{1,0:T(8,128)(2,1)S(1)}, u32[]{:S(2)}, u32[]{:S(2)}) collective-permute-start(bf16[128,5120]{1,0:T(8,128)(2,1)S(1)} %convolution_convert_fusion), channel_id=1, source_target_pairs={{0,1},{1,0},{2,3},{3,2},{4,5},{5,4},{6,7},{7,6},{8,9},{9,8},{10,11... | collective-permute-start | bytes 3932168 | tf_op jit(solution)/shard_map/ppermute | solution.py:10
  81.6 0.8 multiply_reduce_fusion
  82.5 0.5 fusion.11
  83.0 27.7 %collective-permute-done = bf16[128,5120]{1,0:T(8,128)(2,1)S(1)} collective-permute-done((bf16[128,5120]{1,0:T(8,128)(2,1)S(1)}, bf16[128,5120]{1,0:T(8,128)(2,1)S(1)}, u32[]{:S(2)}, u32[]{:S(2)}) %collective-permute-start) | collective-permute-done | bytes 1310752 | tf_op jit(solution)/shard_map/ppermute | solution.py:10
  110.7 1.1 copy.10
  (2 shorter events, 0.0 us)
Async XLA Ops:
  7.2 67.2 %copy-start = (bf16[128,5120]{1,0:T(8,128)(2,1)S(1)}, bf16[128,5120]{1,0:T(8,128)(2,1)}, u32[]{:S(2)}) copy-start(bf16[128,5120]{1,0:T(8,128)(2,1)} %param.5) | copy-start | bytes 3932164
  7.2 0.8 copy-start.4
  7.2 0.9 copy-start.3
  7.2 67.2 %all-gather.2.cloned.1.call-start = ((), (), s32[]{:S(2)}) async-start(), calls=%async_computation | async-start | bytes 6553600 | tf_op jit(solution)/shard_map/all_gather | solution.py:19
  52.7 26.5 %copy-start.2 = (s32[128]{0:T(128)S(1)}, s32[128]{0:T(128)}, u32[]{:S(2)}) copy-start(s32[128]{0:T(128)} %param.7) | copy-start | bytes 1540
  74.4 4.8 %copy-start.1 = (bf16[512,5120]{1,0:T(8,128)(2,1)S(1)}, bf16[512,5120]{1,0:T(8,128)(2,1)}, u32[]{:S(2)}) copy-start(bf16[512,5120]{1,0:T(8,128)(2,1)} %all-gather.2.cloned.1.call-done) | copy-start | bytes 15728644
  80.1 30.6 %collective-permute-start = (bf16[128,5120]{1,0:T(8,128)(2,1)S(1)}, bf16[128,5120]{1,0:T(8,128)(2,1)S(1)}, u32[]{:S(2)}, u32[]{:S(2)}) collective-permute-start(bf16[128,5120]{1,0:T(8,128)(2,1)S(1)} %convolution_convert_fusion), channel_id=1, source_target_pairs={{0,1},{1,0},{2,3},{3,2},{4,5},{5,4},{6,7},{7,6},{8,9},{9,8},{10,11... | collective-permute-start | bytes 3932168 | tf_op jit(solution)/shard_map/ppermute | solution.py:10
Sparse Core Ops, SparseCore 0:
  9.9 64.4 all-gather.1
where the time goes:
time: 119 us
  waiting for transfers between devices  50.1 us (42%)
  blocking collectives  44.3 us (37%)
  between operations  14.1 us (12%)
  matrix products  5.91 us (5%)
  other arithmetic  1.65 us (1%)
  starting transfers between devices  1.55 us (1%)
    psum x1, blocking collectives, body(): lax.psum((local_sums, local_counts), ('vocab', 'section'))  44.3 us
    ppermute x1, waiting for transfers between devices, swapped(): return lax.ppermute(value, axis, pairs)  27.7 us
    all_gather x1, waiting for transfers between devices, body(): incoming = lax.all_gather(head_weight, 'vocab', axis=0, tiled=True)  21.7 us
    dot_general x1, matrix products, body(): lax.dot_general(hidden, incoming, (((1,), (1,)), ((), ())), preferred_ele...  4.59 us
  transfers between devices with their start and end apart: 2, of which 2 were waited for; matrix products, arithmetic and copies ran while one was open for 2% of the time, Pallas kernels for 0%

commit v1 on v0

v1 whole, which is shorter than its diff:
```python
import jax
import jax.numpy as jnp
from jax import lax
from jax.sharding import PartitionSpec as P

EDGE = 16


def swapped(value, axis, mask):
    pairs = [(source, source ^ mask) for source in range(lax.axis_size(axis))]
    return lax.ppermute(value, axis, pairs)


def gathered(own, axis):
    count = lax.axis_size(axis)
    cut = own.shape[0] // 2
    pieces = {0: own}
    masks = [1 << bit for bit in range((count - 1).bit_length())]
    for mask in masks:
        pieces[mask] = swapped(own, axis, mask)
    for offset in sorted(range(1, count), key=lambda o: (bin(o).count("1"), o)):
        if offset in pieces:
            continue
        bits = [mask for mask in masks if offset & mask]
        first = swapped(pieces[offset ^ bits[-1]][:cut], axis, bits[-1])
        second = swapped(pieces[offset ^ bits[0]][cut:], axis, bits[0])
        pieces[offset] = jnp.concatenate([first, second], axis=0)
    return [pieces[offset] for offset in range(count)]


def in_order(blocks, axis):
    index = lax.axis_index(axis)
    count = len(blocks)
    bit = 1
    while bit < count:
        odd = (index & bit) != 0
        blocks = [jnp.where(odd, blocks[i ^ bit], blocks[i]) for i in range(count)]
        bit *= 2
    return jnp.concatenate(blocks, axis=1)


def neighbours(rows, axes):
    count = lax.axis_size(axes)
    before = lax.ppermute(rows[:, -EDGE:], axes, [(i, i + 1) for i in range(count - 1)])
    after = lax.ppermute(rows[:, :EDGE], axes, [(i + 1, i) for i in range(count - 1)])
    return jnp.concatenate([before, rows, after], axis=1)


def body(hidden, head_weight, tokens, rewards, group_ids):
    row_count, model_width = hidden.shape
    shard_rows = head_weight.shape[0]
    half = model_width // 2
    odd = lax.axis_index("section") % 2
    shard = lax.axis_index("vocab")

    head_half = lax.dynamic_slice_in_dim(head_weight, odd * half, half, 1)
    own_half = lax.dynamic_slice_in_dim(hidden, odd * half, half, 1)
    other_half = lax.dynamic_slice_in_dim(hidden, (1 - odd) * half, half, 1)

    heads = gathered(head_half, "vocab")
    partner_half = swapped(other_half, "section", 1)

    labelled = jnp.stack([rewards, (group_ids + 1).astype(jnp.float32)])
    wide = neighbours(labelled, ("vocab", "section"))
    member = (labelled[1][:, None] == wide[1][None, :]).astype(jnp.float32)
    sums = jnp.sum(member * wide[0][None, :], axis=1)
    advantage = rewards - sums / jnp.sum(member, axis=1)
    own_facts = jnp.stack([advantage, tokens.astype(jnp.float32)])
    partner_facts = swapped(own_facts, "section", 1)
    facts = jnp.concatenate([own_facts, partner_facts], axis=1)
    all_advantage = facts[0]
    all_tokens = facts[1].astype(jnp.int32)

    both = jnp.concatenate([own_half, partner_half], axis=0)
    scores, chosen = [], []
    for offset, head in enumerate(heads):
        mine = lax.dot_general(
            both, head, (((1,), (1,)), ((), ())), preferred_element_type=jnp.float32
        )
        theirs = swapped(mine, "section", 1)
        theirs = jnp.concatenate([theirs[row_count:], theirs[:row_count]], axis=0)
        scores.append(mine + theirs)
        ids = (shard ^ offset) * shard_rows + jnp.arange(shard_rows, dtype=jnp.int32)
        chosen.append(ids[None, :] == all_tokens[:, None])
    logits = in_order([s[:row_count].astype(jnp.bfloat16) for s in scores], "vocab")
    scores = jnp.concatenate(scores, axis=1)
    chosen = jnp.concatenate(chosen, axis=1)
    heads = jnp.concatenate(heads, axis=0)

    row_max = jnp.max(scores, axis=1, keepdims=True)
    unnormed = jnp.exp(scores - row_max)
    denominator = jnp.sum(unnormed, axis=1, keepdims=True)
    probabilities = unnormed / denominator
    own = slice(0, row_count)
    log_total = (row_max[own] + jnp.log(denominator[own]))[:, 0]
    picked = jnp.sum(jnp.where(chosen[own], scores[own], 0.0), axis=1)
    logprob = picked - log_total
    entropy = log_total - jnp.sum(probabilities[own] * scores[own], axis=1)

    dlogits = (all_advantage[:, None] * (probabilities - chosen.astype(jnp.float32))).astype(
        jnp.bfloat16
    )
    outgoing = jnp.dot(dlogits[:row_count], heads, preferred_element_type=jnp.float32)
    incoming = swapped(outgoing.astype(jnp.bfloat16), "section", 1)
    staying = jnp.dot(dlogits[row_count:], heads, preferred_element_type=jnp.float32)
    staying = staying.astype(jnp.bfloat16)
    previous_grad = jnp.where(
        odd == 1,
        jnp.concatenate([incoming, staying], axis=1),
        jnp.concatenate([staying, incoming], axis=1),
    )
    return (logits, logprob, entropy, previous_grad)


def solution(mesh):
    placed = (
        P(("seq", "vocab", "section"), None),
        P(("seq", "vocab"), None),
        P(("seq", "vocab", "section")),
        P(("seq", "vocab", "section")),
        P(("seq", "vocab", "section")),
    )
    return jax.shard_map(
        body,
        mesh=mesh,
        in_specs=placed,
        out_specs=(
            P(("seq", "vocab", "section"), None),
            P(("seq", "vocab", "section")),
            P(("seq", "vocab", "section")),
            P(("seq", "vocab", "section"), None),
        ),
        check_vma=False,
    )
```

time: 119 us -> 71.5 us (0.60)
  blocking collectives: 44.3 us -> 0 us
  waiting for transfers between devices: 50.1 us -> 30.4 us
  starting transfers between devices: 1.55 us -> 19.9 us
  between operations: 14.1 us -> 0.97 us
  local copies, waits for them, and re-layouts: 1.08 us -> 7.59 us
  other arithmetic: 1.65 us -> 4.04 us
  matrix products: 5.91 us -> 8.19 us
    psum x1 -> x0, blocking collectives: 44.3 us -> none  [body(): lax.psum((local_sums, local_counts), ('vocab', 'section'))]
    all_gather x1 -> x0, waiting for transfers between devices: 21.7 us -> none  [body(): incoming = lax.all_gather(head_weight, 'vocab', axis=0, tiled=True)]
    ppermute x1 -> x11, starting transfers between devices: 1.51 us -> 14.1 us  [swapped(): return lax.ppermute(value, axis, pairs)]
    ppermute x0 -> x2, waiting for transfers between devices: none -> 8.67 us  [the longest x1 8.67 us: neighbours(): lax.ppermute(rows[:, :EDGE], axes, [(i + 1, i) for i in range(count - 1)])]
    ppermute x1 -> x11, waiting for transfers between devices: 27.7 us -> 21.7 us  [swapped(): return lax.ppermute(value, axis, pairs)]
    ppermute x0 -> x2, starting transfers between devices: none -> 5.83 us  [the longest x1 4.55 us: neighbours(): lax.ppermute(rows[:, -EDGE:], axes, [(i, i + 1) for i in range(count - 1)])]
    unnamed x11 -> x13, local copies, waits for them, and re-layouts: 1.08 us -> 4 us
    dynamic_slice x0 -> x1, local copies, waits for them, and re-layouts: none -> 2.43 us  [body(): own_half = lax.dynamic_slice_in_dim(hidden, odd * half, half, 1)]
  transfers between devices with their start and end apart: 2 -> 13, of which waited for: 2 -> 5; matrix products, arithmetic and copies ran while one was open for 2% -> 18% of each run, Pallas kernels for 0% -> 0%
where the time goes in v1:
time: 71.5 us; the launch traced here: 71.1 us
  waiting for transfers between devices  30.4 us (43%)
  starting transfers between devices  19.9 us (28%)
  matrix products  8.19 us (11%)
  local copies, waits for them, and re-layouts  7.59 us (11%)
  other arithmetic  4.04 us (6%)
  between operations  0.97 us (1%)
    ppermute x11, waiting for transfers between devices, swapped(): return lax.ppermute(value, axis, pairs)  21.7 us
    ppermute x11, starting transfers between devices, swapped(): return lax.ppermute(value, axis, pairs)  14.1 us
    ppermute x1, waiting for transfers between devices, neighbours(): lax.ppermute(rows[:, :EDGE], axes, [(i + 1, i) for i in range(count - 1)])  8.67 us
    dot_general x4, matrix products, body(): lax.dot_general(both, head, (((1,), (1,)), ((), ())), preferred_element_t...  7.12 us
    ppermute x1, starting transfers between devices, neighbours(): lax.ppermute(rows[:, -EDGE:], axes, [(i, i + 1) for i in range(count - 1)])  4.55 us
    unnamed x13, local copies, waits for them, and re-layouts  4 us
    dynamic_slice x1, local copies, waits for them, and re-layouts, body(): own_half = lax.dynamic_slice_in_dim(hidden, odd * half, half, 1)  2.43 us
  transfers between devices with their start and end apart: 13, of which 5 were waited for; matrix products, arithmetic and copies ran while one was open for 18% of the time, Pallas kernels for 0%

profile of v1, /device:TPU:0, one launch (start us, length us, event | category | flops | bytes accessed | tf_op | source)
XLA Modules:
  0.0 71.1 jit_solution(3300522574907387010)
XLA Ops:
  0.7 2.0 %constant_dynamic-update-slice_fusion.4 = (bf16[512,2560]{1,0:T(8,128)(2,1)S(1)}, bf16[128,2560]{1,0:T(8,128)(2,1)}) fusion(bf16[128,5120]{1,0:T(8,128)(2,1)} %param.6, s32[]{:T(128)S(6)} %select_n.67), kind=kLoop, calls=%fused_computation.48 | loop fusion | bytes 1966084
  2.7 3.0 %collective-permute-start.3 = (bf16[128,2560]{1,0:T(8,128)(2,1)}, bf16[128,2560]{1,0:T(8,128)(2,1)S(1)}, u32[]{:S(2)}, u32[]{:S(2)}) collective-permute-start(bf16[128,2560]{1,0:T(8,128)(2,1)} %get-tuple-element.19), channel_id=1, source_target_pairs={{0,8},{4,12},{8,0},{12,4},{1,9},{5,13},{9,1},{13,5},{2,10},{6,14},... | collective-permute-start | bytes 1966088 | tf_op jit(solution)/shard_map/ppermute | solution.py:11
  5.7 1.5 %collective-permute-start.1 = (bf16[128,2560]{1,0:T(8,128)(2,1)}, bf16[128,2560]{1,0:T(8,128)(2,1)}, u32[]{:S(2)}, u32[]{:S(2)}) collective-permute-start(bf16[128,2560]{1,0:T(8,128)(2,1)} %get-tuple-element.19), channel_id=1, source_target_pairs={{0,4},{4,0},{8,12},{12,8},{1,5},{5,1},{9,13},{13,9},{2,6},{6,2},{1... | collective-permute-start | bytes 1966088 | tf_op jit(solution)/shard_map/ppermute | solution.py:11
  7.2 2.4 %constant_dynamic-slice_fusion.2 = (bf16[128,2560]{1,0:T(8,128)(2,1)}, bf16[128,2560]{1,0:T(8,128)(2,1)}) fusion(bf16[128,5120]{1,0:T(8,128)(2,1)} %param.5, s32[]{:T(128)S(6)} %select_n.67, s32[]{:T(128)S(6)} %select_n.68), kind=kLoop, calls=%fused_computation.57 | loop fusion | bytes 2621448 | tf_op jit(solution)/shard_map/dynamic_slice | solution.py:57
  9.6 1.6 %collective-permute-start = (bf16[128,2560]{1,0:T(8,128)(2,1)}, bf16[128,2560]{1,0:T(8,128)(2,1)}, u32[]{:S(2)}, u32[]{:S(2)}) collective-permute-start(bf16[128,2560]{1,0:T(8,128)(2,1)} %get-tuple-element.35), channel_id=1, source_target_pairs={{0,1},{1,0},{2,3},{3,2},{4,5},{5,4},{6,7},{7,6},{8,9},{9,8},{10,11... | collective-permute-start | bytes 1966088 | tf_op jit(solution)/shard_map/ppermute | solution.py:11
  11.3 1.3 %collective-permute-start.10 = (f32[2,16]{1,0:T(2,128)S(1)}, f32[2,16]{1,0:T(2,128)S(1)}, u32[]{:S(2)}, u32[]{:S(2)}) collective-permute-start(f32[2,16]{1,0:T(2,128)S(1)} %get-tuple-element.59), channel_id=1, source_target_pairs={{1,0},{2,1},{3,2},{4,3},{5,4},{6,5},{7,6},{8,7},{9,8},{10,9},{11,1... | collective-permute-start | bytes 392 | tf_op jit(solution)/shard_map/ppermute | solution.py:45
  12.5 4.5 %collective-permute-start.9 = (f32[2,16]{1,0:T(2,128)S(1)}, f32[2,16]{1,0:T(2,128)S(1)}, u32[]{:S(2)}, u32[]{:S(2)}) collective-permute-start(f32[2,16]{1,0:T(2,128)S(1)} %get-tuple-element.58), channel_id=1, source_target_pairs={{0,1},{1,2},{2,3},{3,4},{4,5},{5,6},{6,7},{7,8},{8,9},{9,10},{10,1... | collective-permute-start | bytes 392 | tf_op jit(solution)/shard_map/ppermute | solution.py:44
  17.2 8.7 %collective-permute-done.10 = f32[2,16]{1,0:T(2,128)S(1)} collective-permute-done((f32[2,16]{1,0:T(2,128)S(1)}, f32[2,16]{1,0:T(2,128)S(1)}, u32[]{:S(2)}, u32[]{:S(2)}) %collective-permute-start.10) | collective-permute-done | bytes 160 | tf_op jit(solution)/shard_map/ppermute | solution.py:45
  26.1 1.6 %collective-permute-start.11 = (f32[2,128]{1,0:T(2,128)S(1)}, f32[2,128]{1,0:T(2,128)S(1)}, u32[]{:S(2)}, u32[]{:S(2)}) collective-permute-start(f32[2,128]{1,0:T(2,128)S(1)} %pad_maximum_fusion.6), channel_id=1, source_target_pairs={{0,1},{1,0},{2,3},{3,2},{4,5},{5,4},{6,7},{7,6},{8,9},{9,8},{10,11... | collective-permute-start | bytes 3080 | tf_op jit(solution)/shard_map/ppermute | solution.py:11
  27.7 2.0 %collective-permute-done.11 = f32[2,128]{1,0:T(2,128)S(1)} collective-permute-done((f32[2,128]{1,0:T(2,128)S(1)}, f32[2,128]{1,0:T(2,128)S(1)}, u32[]{:S(2)}, u32[]{:S(2)}) %collective-permute-start.11) | collective-permute-done | bytes 1056 | tf_op jit(solution)/shard_map/ppermute | solution.py:11
  30.4 1.8 %fusion.17 = f32[256,128]{0,1:T(8,128)S(1)} fusion(bf16[128,2560]{1,0:T(8,128)(2,1)S(1)} %collective-permute-done.3, bf16[128,2560]{1,0:T(8,128)(2,1)} %collective-permute-done, bf16[128,2560]{1,0:T(8,128)(2,1)} %get-tuple-element.34), kind=kOutput, calls=%fused_computation.72 | convolution fusion | flops 170393600 | bytes 2097152 | tf_op jit(solution)/shard_map/dot_general | solution.py:77
  32.3 1.6 %collective-permute-start.6 = (f32[256,128]{0,1:T(8,128)S(1)}, f32[256,128]{0,1:T(8,128)S(1)}, u32[]{:S(2)}, u32[]{:S(2)}) collective-permute-start(f32[256,128]{0,1:T(8,128)S(1)} %fusion.17), channel_id=1, source_target_pairs={{0,1},{1,0},{2,3},{3,2},{4,5},{5,4},{6,7},{7,6},{8,9},{9,8},{10,11... | collective-permute-start | bytes 393224 | tf_op jit(solution)/shard_map/ppermute | solution.py:11
  33.9 1.9 %collective-permute-start.4 = (bf16[64,2560]{1,0:T(8,128)(2,1)S(1)}, bf16[64,2560]{1,0:T(8,128)(2,1)S(1)}, u32[]{:S(2)}, u32[]{:S(2)}) collective-permute-start(bf16[64,2560]{1,0:T(8,128)(2,1)S(1)} %slice.116), channel_id=1, source_target_pairs={{0,4},{4,0},{8,12},{12,8},{1,5},{5,1},{9,13},{13,9},{2,6},{6,2},{1... | collective-permute-start | bytes 983048 | tf_op jit(solution)/shard_map/ppermute | solution.py:11
  35.9 1.0 %slice.115 = bf16[64,2560]{1,0:T(8,128)(2,1)S(1)} slice(bf16[128,2560]{1,0:T(8,128)(2,1)} %collective-permute-done.1), slice={[0:64], [0:2560]} | slice | bytes 655360 | tf_op jit(solution)/shard_map/slice | solution.py:25
  37.4 1.8 %fusion.15 = f32[256,128]{0,1:T(8,128)S(1)} fusion(bf16[128,2560]{1,0:T(8,128)(2,1)} %get-tuple-element.19, bf16[128,2560]{1,0:T(8,128)(2,1)} %collective-permute-done, bf16[128,2560]{1,0:T(8,128)(2,1)S(1)} %copy-done), kind=kOutput, calls=%fused_computation.70 | convolution fusion | flops 170393600 | bytes 2097152 | tf_op jit(solution)/shard_map/dot_general | solution.py:77
  39.3 2.1 %collective-permute-start.8 = (f32[256,128]{0,1:T(8,128)S(1)}, f32[256,128]{0,1:T(8,128)S(1)}, u32[]{:S(2)}, u32[]{:S(2)}) collective-permute-start(f32[256,128]{0,1:T(8,128)S(1)} %fusion.15), channel_id=1, source_target_pairs={{0,1},{1,0},{2,3},{3,2},{4,5},{5,4},{6,7},{7,6},{8,9},{9,8},{10,11... | collective-permute-start | bytes 393224 | tf_op jit(solution)/shard_map/ppermute | solution.py:11
  41.3 1.8 %fusion.16 = f32[256,128]{0,1:T(8,128)S(1)} fusion(bf16[128,2560]{1,0:T(8,128)(2,1)} %collective-permute-done.1, bf16[128,2560]{1,0:T(8,128)(2,1)} %collective-permute-done, bf16[128,2560]{1,0:T(8,128)(2,1)S(1)} %copy-done), kind=kOutput, calls=%fused_computation.71 | convolution fusion | flops 170393600 | bytes 2097152 | tf_op jit(solution)/shard_map/dot_general | solution.py:77
  43.3 1.1 %constant_dynamic-update-slice_fusion.3 = bf16[512,2560]{1,0:T(8,128)(2,1)S(1)} fusion(bf16[512,2560]{1,0:T(8,128)(2,1)S(1)} %get-tuple-element.18, bf16[128,2560]{1,0:T(8,128)(2,1)} %collective-permute-done.1), kind=kLoop, calls=%fused_computation.47 | loop fusion | bytes 1310720
  44.6 4.3 %collective-permute-done.7 = f32[256,128]{0,1:T(8,128)S(1)} collective-permute-done((f32[256,128]{0,1:T(8,128)S(1)}, f32[256,128]{0,1:T(8,128)S(1)}, u32[]{:S(2)}, u32[]{:S(2)}) %collective-permute-start.7) | collective-permute-done | bytes 131104 | tf_op jit(solution)/shard_map/ppermute | solution.py:11
  48.9 1.6 %fusion = f32[256,128]{0,1:T(8,128)S(1)} fusion(bf16[64,2560]{1,0:T(8,128)(2,1)S(1)} %collective-permute-done.4, bf16[64,2560]{1,0:T(8,128)(2,1)S(1)} %collective-permute-done.2, bf16[128,2560]{1,0:T(8,128)(2,1)} %collective-permute-done, bf16[128,2560]{1,0:T(8,128)(2,1)S(1)} %copy-done), kind=kOutput, calls=%fused_computation.4 | convolution fusion | flops 171704320 | bytes 2097152 | tf_op jit(solution)/shard_map/dot_general | solution.py:77
  50.7 6.0 %collective-permute-done.5 = f32[256,128]{0,1:T(8,128)S(1)} collective-permute-done((f32[256,128]{0,1:T(8,128)S(1)}, f32[256,128]{0,1:T(8,128)S(1)}, u32[]{:S(2)}, u32[]{:S(2)}) %collective-permute-start.5) | collective-permute-done | bytes 131104 | tf_op jit(solution)/shard_map/ppermute | solution.py:11
  57.8 0.8 %multiply_convert_fusion = (bf16[256,512]{0,1:T(8,128)(2,1)S(1)}, f32[256,512]{0,1:T(8,128)S(1)}, f32[256,512]{0,1:T(8,128)S(1)}) fusion(f32[256]{0:T(256)} %bitcast.18, pred[256,128]{0,1:T(8,128)(4,1)S(1)} %get-tuple-element.57, pred[256,128]{0,1:T(8,128)(4,1)S(1)} %get-tuple-element.56, pred[256,128]{0,1:T(8,128)(4,1)S(1)} %get-tuple-element.55, ...), kind=kLoop, calls=%fused_computation.9 | loop fusion | flops 1572864 | bytes 1969152 | tf_op jit(solution)/shard_map/convert_element_type | solution.py:100
  60.3 9.4 %collective-permute-done.12 = bf16[128,2560]{1,0:T(8,128)(2,1)S(1)} collective-permute-done((bf16[128,2560]{1,0:T(8,128)(2,1)S(1)}, bf16[128,2560]{1,0:T(8,128)(2,1)S(1)}, u32[]{:S(2)}, u32[]{:S(2)}) %collective-permute-start.12) | collective-permute-done | bytes 655392 | tf_op jit(solution)/shard_map/ppermute | solution.py:11
  69.8 1.4 %maximum_select_fusion = bf16[128,5120]{1,0:T(8,128)(2,1)} fusion(bf16[128,2560]{1,0:T(8,128)(2,1)S(1)} %convolution_convert_fusion, bf16[128,2560]{1,0:T(8,128)(2,1)S(1)} %collective-permute-done.12, pred[]{:T(512)S(6)} %eq.79), kind=kLoop, calls=%fused_computation.3 | loop fusion | flops 5898240 | bytes 2621441 | tf_op jit(solution)/shard_map/jit(_where)/select_n | solution.py:107
  (57 shorter events, 4.8 us)
Async XLA Ops:
  0.6 10.5 %copy-start.2 = (s32[128]{0:T(128)S(1)}, s32[128]{0:T(128)}, u32[]{:S(2)}) copy-start(s32[128]{0:T(128)} %param.9) | copy-start | bytes 1540
  0.6 10.5 %copy-start.1 = (f32[128]{0:T(128)S(1)}, f32[128]{0:T(128)}, u32[]{:S(2)}) copy-start(f32[128]{0:T(128)} %param.8) | copy-start | bytes 1540
  0.7 16.5 %copy-start.3 = (s32[128]{0:T(128)S(1)}, s32[128]{0:T(128)}, u32[]{:S(2)}) copy-start(s32[128]{0:T(128)} %param.7) | copy-start | bytes 1540
  2.7 27.7 %collective-permute-start.3 = (bf16[128,2560]{1,0:T(8,128)(2,1)}, bf16[128,2560]{1,0:T(8,128)(2,1)S(1)}, u32[]{:S(2)}, u32[]{:S(2)}) collective-permute-start(bf16[128,2560]{1,0:T(8,128)(2,1)} %get-tuple-element.19), channel_id=1, source_target_pairs={{0,8},{4,12},{8,0},{12,4},{1,9},{5,13},{9,1},{13,5},{2,10},{6,14},... | collective-permute-start | bytes 1966088 | tf_op jit(solution)/shard_map/ppermute | solution.py:11
  5.7 30.2 %collective-permute-start.1 = (bf16[128,2560]{1,0:T(8,128)(2,1)}, bf16[128,2560]{1,0:T(8,128)(2,1)}, u32[]{:S(2)}, u32[]{:S(2)}) collective-permute-start(bf16[128,2560]{1,0:T(8,128)(2,1)} %get-tuple-element.19), channel_id=1, source_target_pairs={{0,4},{4,0},{8,12},{12,8},{1,5},{5,1},{9,13},{13,9},{2,6},{6,2},{1... | collective-permute-start | bytes 1966088 | tf_op jit(solution)/shard_map/ppermute | solution.py:11
  9.6 20.8 %collective-permute-start = (bf16[128,2560]{1,0:T(8,128)(2,1)}, bf16[128,2560]{1,0:T(8,128)(2,1)}, u32[]{:S(2)}, u32[]{:S(2)}) collective-permute-start(bf16[128,2560]{1,0:T(8,128)(2,1)} %get-tuple-element.35), channel_id=1, source_target_pairs={{0,1},{1,0},{2,3},{3,2},{4,5},{5,4},{6,7},{7,6},{8,9},{9,8},{10,11... | collective-permute-start | bytes 1966088 | tf_op jit(solution)/shard_map/ppermute | solution.py:11
  11.3 14.6 %collective-permute-start.10 = (f32[2,16]{1,0:T(2,128)S(1)}, f32[2,16]{1,0:T(2,128)S(1)}, u32[]{:S(2)}, u32[]{:S(2)}) collective-permute-start(f32[2,16]{1,0:T(2,128)S(1)} %get-tuple-element.59), channel_id=1, source_target_pairs={{1,0},{2,1},{3,2},{4,3},{5,4},{6,5},{7,6},{8,7},{9,8},{10,9},{11,1... | collective-permute-start | bytes 392 | tf_op jit(solution)/shard_map/ppermute | solution.py:45
  12.5 13.3 %collective-permute-start.9 = (f32[2,16]{1,0:T(2,128)S(1)}, f32[2,16]{1,0:T(2,128)S(1)}, u32[]{:S(2)}, u32[]{:S(2)}) collective-permute-start(f32[2,16]{1,0:T(2,128)S(1)} %get-tuple-element.58), channel_id=1, source_target_pairs={{0,1},{1,2},{2,3},{3,4},{4,5},{5,6},{6,7},{7,8},{8,9},{9,10},{10,1... | collective-permute-start | bytes 392 | tf_op jit(solution)/shard_map/ppermute | solution.py:44
  26.1 3.6 %collective-permute-start.11 = (f32[2,128]{1,0:T(2,128)S(1)}, f32[2,128]{1,0:T(2,128)S(1)}, u32[]{:S(2)}, u32[]{:S(2)}) collective-permute-start(f32[2,128]{1,0:T(2,128)S(1)} %pad_maximum_fusion.6), channel_id=1, source_target_pairs={{0,1},{1,0},{2,3},{3,2},{4,5},{5,4},{6,7},{7,6},{8,9},{9,8},{10,11... | collective-permute-start | bytes 3080 | tf_op jit(solution)/shard_map/ppermute | solution.py:11
  27.7 9.7 %copy-start = (bf16[128,2560]{1,0:T(8,128)(2,1)S(1)}, bf16[128,2560]{1,0:T(8,128)(2,1)}, u32[]{:S(2)}) copy-start(bf16[128,2560]{1,0:T(8,128)(2,1)} %get-tuple-element.34) | copy-start | bytes 1966084
  32.3 12.2 %collective-permute-start.6 = (f32[256,128]{0,1:T(8,128)S(1)}, f32[256,128]{0,1:T(8,128)S(1)}, u32[]{:S(2)}, u32[]{:S(2)}) collective-permute-start(f32[256,128]{0,1:T(8,128)S(1)} %fusion.17), channel_id=1, source_target_pairs={{0,1},{1,0},{2,3},{3,2},{4,5},{5,4},{6,7},{7,6},{8,9},{9,8},{10,11... | collective-permute-start | bytes 393224 | tf_op jit(solution)/shard_map/ppermute | solution.py:11
  33.9 15.0 %collective-permute-start.4 = (bf16[64,2560]{1,0:T(8,128)(2,1)S(1)}, bf16[64,2560]{1,0:T(8,128)(2,1)S(1)}, u32[]{:S(2)}, u32[]{:S(2)}) collective-permute-start(bf16[64,2560]{1,0:T(8,128)(2,1)S(1)} %slice.116), channel_id=1, source_target_pairs={{0,4},{4,0},{8,12},{12,8},{1,5},{5,1},{9,13},{13,9},{2,6},{6,2},{1... | collective-permute-start | bytes 983048 | tf_op jit(solution)/shard_map/ppermute | solution.py:11
  36.9 12.1 %collective-permute-start.2 = (bf16[64,2560]{1,0:T(8,128)(2,1)S(1)}, bf16[64,2560]{1,0:T(8,128)(2,1)S(1)}, u32[]{:S(2)}, u32[]{:S(2)}) collective-permute-start(bf16[64,2560]{1,0:T(8,128)(2,1)S(1)} %slice.115), channel_id=1, source_target_pairs={{0,8},{4,12},{8,0},{12,4},{1,9},{5,13},{9,1},{13,5},{2,10},{6,14},... | collective-permute-start | bytes 983048 | tf_op jit(solution)/shard_map/ppermute | solution.py:11
  39.3 5.3 %collective-permute-start.8 = (f32[256,128]{0,1:T(8,128)S(1)}, f32[256,128]{0,1:T(8,128)S(1)}, u32[]{:S(2)}, u32[]{:S(2)}) collective-permute-start(f32[256,128]{0,1:T(8,128)S(1)} %fusion.15), channel_id=1, source_target_pairs={{0,1},{1,0},{2,3},{3,2},{4,5},{5,4},{6,7},{7,6},{8,9},{9,8},{10,11... | collective-permute-start | bytes 393224 | tf_op jit(solution)/shard_map/ppermute | solution.py:11
  43.2 5.7 %collective-permute-start.7 = (f32[256,128]{0,1:T(8,128)S(1)}, f32[256,128]{0,1:T(8,128)S(1)}, u32[]{:S(2)}, u32[]{:S(2)}) collective-permute-start(f32[256,128]{0,1:T(8,128)S(1)} %fusion.16), channel_id=1, source_target_pairs={{0,1},{1,0},{2,3},{3,2},{4,5},{5,4},{6,7},{7,6},{8,9},{9,8},{10,11... | collective-permute-start | bytes 393224 | tf_op jit(solution)/shard_map/ppermute | solution.py:11
  50.6 6.2 %collective-permute-start.5 = (f32[256,128]{0,1:T(8,128)S(1)}, f32[256,128]{0,1:T(8,128)S(1)}, u32[]{:S(2)}, u32[]{:S(2)}) collective-permute-start(f32[256,128]{0,1:T(8,128)S(1)} %fusion), channel_id=1, source_target_pairs={{0,1},{1,0},{2,3},{3,2},{4,5},{5,4},{6,7},{7,6},{8,9},{9,8},{10,11... | collective-permute-start | bytes 393224 | tf_op jit(solution)/shard_map/ppermute | solution.py:11
  59.1 10.7 %collective-permute-start.12 = (bf16[128,2560]{1,0:T(8,128)(2,1)S(1)}, bf16[128,2560]{1,0:T(8,128)(2,1)S(1)}, u32[]{:S(2)}, u32[]{:S(2)}) collective-permute-start(bf16[128,2560]{1,0:T(8,128)(2,1)S(1)} %convolution_convert_fusion.1), channel_id=1, source_target_pairs={{0,1},{1,0},{2,3},{3,2},{4,5},{5,4},{6,7},{7,6},{8,9},{9,8},{10,11... | collective-permute-start | bytes 1966088 | tf_op jit(solution)/shard_map/ppermute | solution.py:11

commit v2 on v0

v2 whole, which is shorter than its diff:
```python
import functools

import jax
import jax.numpy as jnp
from jax import lax
from jax.experimental import pallas as pl
from jax.experimental.pallas import tpu as pltpu
from jax.sharding import PartitionSpec as P

F32, BF16 = jnp.float32, jnp.bfloat16
ANY = pl.BlockSpec(memory_space=pl.ANY)
SMEM = pl.BlockSpec(memory_space=pltpu.SMEM)
VMEM = pl.BlockSpec(memory_space=pltpu.VMEM)
PARAMS = pltpu.CompilerParams(vmem_limit_bytes=48 * 1024 * 1024)


def swapped(value, axis, mask):
    pairs = [(source, source ^ mask) for source in range(lax.axis_size(axis))]
    return lax.ppermute(value, axis, pairs)


def gathered(upper, lower, axis):
    count = lax.axis_size(axis)
    masks = [1 << bit for bit in range((count - 1).bit_length())]
    uppers, lowers = {0: upper}, {0: lower}
    for mask in masks:
        uppers[mask] = swapped(upper, axis, mask)
    for mask in reversed(masks):
        lowers[mask] = swapped(lower, axis, mask)
    for offset in sorted(range(1, count), key=lambda o: (bin(o).count("1"), o)):
        if offset in uppers:
            continue
        bits = [mask for mask in masks if offset & mask]
        uppers[offset] = swapped(uppers[offset ^ bits[-1]], axis, bits[-1])
        lowers[offset] = swapped(lowers[offset ^ bits[0]], axis, bits[0])
    return [(uppers[offset], lowers[offset]) for offset in range(count)]


def take_kernel(which_ref, value_ref, *refs):
    outs, sem = refs[:-1], refs[-1]
    rows, width = outs[0].shape
    start = pl.multiple_of(which_ref[0] * width, 128)
    copies = [
        pltpu.make_async_copy(
            value_ref.at[pl.ds(i * rows, rows), pl.ds(start, width)], out, sem.at[i]
        )
        for i, out in enumerate(outs)
    ]
    for copy in copies:
        copy.start()
    for copy in copies:
        copy.wait()


def take(which, value, pieces):
    rows, width = value.shape[0] // pieces, value.shape[1] // 2
    return pl.pallas_call(
        take_kernel,
        out_shape=[jax.ShapeDtypeStruct((rows, width), value.dtype)] * pieces,
        in_specs=[SMEM, ANY],
        out_specs=[ANY] * pieces,
        scratch_shapes=[pltpu.SemaphoreType.DMA((pieces,))],
        compiler_params=PARAMS,
        cost_estimate=pl.CostEstimate(
            flops=0, bytes_accessed=value.size * value.dtype.itemsize, transcendentals=0
        ),
        name="take_half",
    )(which, value)


def partial_kernel(which_ref, hidden_ref, partner_ref, *refs):
    heads, (mine_ref, theirs_ref) = refs[:-2], refs[-2:]
    width = partner_ref.shape[1]
    start = pl.multiple_of(which_ref[0] * width, 128)
    head = jnp.concatenate([ref[...] for ref in heads], axis=0)
    dims = (((1,), (1,)), ((), ()))
    theirs_ref[...] = lax.dot_general(partner_ref[...], head, dims, preferred_element_type=F32)
    mine_ref[...] = lax.dot_general(
        hidden_ref[:, pl.ds(start, width)], head, dims, preferred_element_type=F32
    )


def partial_scores(which, hidden, partner_half, heads):
    rows, width = partner_half.shape
    columns = sum(head.shape[0] for head in heads)
    out = jax.ShapeDtypeStruct((rows, columns), F32)
    return pl.pallas_call(
        partial_kernel,
        out_shape=[out, out],
        in_specs=[SMEM] + [VMEM] * (2 + len(heads)),
        out_specs=[VMEM, VMEM],
        compiler_params=PARAMS,
        cost_estimate=pl.CostEstimate(
            flops=4 * rows * columns * width,
            bytes_accessed=2 * width * (2 * rows + columns),
            transcendentals=0,
        ),
        name="partial_scores",
    )(which, hidden, partner_half, *heads)


def loss_kernel(parts, shards, place_ref, tokens_ref, own_ref, before_ref, after_ref, *refs):
    mine, theirs = refs[:parts], refs[parts : 2 * parts]
    heads = refs[2 * parts : -5]
    logits_ref, logprob_ref, entropy_ref, dlogits_ref, outgoing_ref = refs[-5:]
    shard = place_ref[1]
    rows, columns = dlogits_ref.shape
    shard_rows = columns // shards

    eye = lax.broadcasted_iota(jnp.int32, (rows, rows), 0) == lax.broadcasted_iota(
        jnp.int32, (rows, rows), 1
    )

    def upright(row):
        return jnp.sum(jnp.where(eye, row, jnp.zeros_like(row)), axis=1, keepdims=True)

    def flat(column):
        return jnp.sum(jnp.where(eye, column, jnp.zeros_like(column)), axis=0, keepdims=True)

    rewards = upright(own_ref[0:1, :])
    groups = upright(own_ref[1:2, :])
    sums, counts = jnp.zeros((rows, 1), F32), jnp.zeros((rows, 1), F32)
    for ref in (before_ref, own_ref, after_ref):
        member = ref[1:2, :] == groups
        sums += jnp.sum(jnp.where(member, ref[0:1, :], 0.0), axis=1, keepdims=True)
        counts += jnp.sum(jnp.where(member, 1.0, 0.0), axis=1, keepdims=True)
    advantage = rewards - sums / counts
    tokens = upright(tokens_ref[...].astype(F32)).astype(jnp.int32)

    scores = jnp.concatenate([a[...] + b[...] for a, b in zip(mine, theirs)], axis=1)
    for offset in range(shards):
        place = pl.multiple_of((shard ^ offset) * shard_rows, 128)
        block = scores[:, offset * shard_rows : (offset + 1) * shard_rows]
        logits_ref[:, pl.ds(place, shard_rows)] = block.astype(logits_ref.dtype)

    lanes = lax.broadcasted_iota(jnp.int32, (rows, columns), 1)
    relative = ((tokens // shard_rows) ^ shard) * shard_rows + tokens % shard_rows
    chosen = lanes == relative
    row_max = jnp.max(scores, axis=1, keepdims=True)
    unnormed = jnp.exp(scores - row_max)
    denominator = jnp.sum(unnormed, axis=1, keepdims=True)
    probabilities = unnormed / denominator
    log_total = row_max + jnp.log(denominator)
    picked = jnp.sum(jnp.where(chosen, scores, 0.0), axis=1, keepdims=True)
    logprob_ref[...] = flat(picked - log_total)
    entropy_ref[...] = flat(log_total - jnp.sum(probabilities * scores, axis=1, keepdims=True))
    dlogits = (advantage * (probabilities - jnp.where(chosen, 1.0, 0.0))).astype(BF16)
    dlogits_ref[...] = dlogits
    head = jnp.concatenate([ref[...] for ref in heads], axis=0)
    outgoing_ref[...] = jnp.dot(dlogits, head, preferred_element_type=F32).astype(BF16)


def loss(place, tokens, own, before, after, mine, theirs, heads, shards):
    rows = own.shape[1]
    columns = sum(head.shape[0] for head in heads)
    width = heads[0].shape[1]
    flat = jax.ShapeDtypeStruct((1, rows), F32)
    wide = jax.ShapeDtypeStruct((rows, columns), BF16)
    return pl.pallas_call(
        functools.partial(loss_kernel, len(mine), shards),
        out_shape=[wide, flat, flat, wide, jax.ShapeDtypeStruct((rows, width), BF16)],
        in_specs=[SMEM] + [VMEM] * (4 + 2 * len(mine) + len(heads)),
        out_specs=[VMEM] * 5,
        compiler_params=PARAMS,
        cost_estimate=pl.CostEstimate(
            flops=2 * rows * columns * width,
            bytes_accessed=2 * width * (rows + columns),
            transcendentals=rows * columns,
        ),
        name="loss_and_outgoing",
    )(place, tokens, own, before, after, *mine, *theirs, *heads)


def staying_kernel(which_ref, dlogits_ref, *refs):
    heads, (out_ref, held_ref, sem) = refs[:-3], refs[-3:]
    width = held_ref.shape[1]
    start = pl.multiple_of(which_ref[0] * width, 128)
    head = jnp.concatenate([ref[...] for ref in heads], axis=0)
    held_ref[...] = jnp.dot(dlogits_ref[...], head, preferred_element_type=F32).astype(BF16)
    copy = pltpu.make_async_copy(held_ref, out_ref.at[:, pl.ds(start, width)], sem)
    copy.start()
    copy.wait()


def staying_gradient(which, dlogits, heads):
    rows, columns = dlogits.shape
    width = heads[0].shape[1]
    return pl.pallas_call(
        staying_kernel,
        out_shape=jax.ShapeDtypeStruct((rows, 2 * width), BF16),
        in_specs=[SMEM] + [VMEM] * (1 + len(heads)),
        out_specs=ANY,
        scratch_shapes=[pltpu.VMEM((rows, width), BF16), pltpu.SemaphoreType.DMA],
        compiler_params=PARAMS,
        cost_estimate=pl.CostEstimate(
            flops=2 * rows * columns * width,
            bytes_accessed=2 * width * (rows + columns),
            transcendentals=0,
        ),
        name="staying_gradient",
    )(which, dlogits, *heads)


def placed_kernel(which_ref, incoming_ref, _, out_ref, sem):
    width = incoming_ref.shape[1]
    start = pl.multiple_of((1 - which_ref[0]) * width, 128)
    copy = pltpu.make_async_copy(incoming_ref, out_ref.at[:, pl.ds(start, width)], sem)
    copy.start()
    copy.wait()


def placed_beside(which, incoming, gradient):
    return pl.pallas_call(
        placed_kernel,
        out_shape=jax.ShapeDtypeStruct(gradient.shape, gradient.dtype),
        in_specs=[SMEM, ANY, ANY],
        out_specs=ANY,
        scratch_shapes=[pltpu.SemaphoreType.DMA],
        input_output_aliases={2: 0},
        compiler_params=PARAMS,
        name="place_incoming",
    )(which, incoming, gradient)


def body(hidden, head_weight, tokens, rewards, group_ids):
    shards = lax.axis_size("vocab")
    odd = lax.axis_index("section") % 2
    which = odd.reshape(1)
    place = jnp.stack([odd, lax.axis_index("vocab")])

    upper, lower = take(which, head_weight, 2)
    heads = gathered(upper, lower, "vocab")
    (other_half,) = take(1 - which, hidden, 1)
    partner_half = swapped(other_half, "section", 1)

    own = jnp.stack([rewards, (group_ids + 1).astype(F32)])
    count = lax.axis_size(("vocab", "section"))
    after = lax.ppermute(own, ("vocab", "section"), [(i + 1, i) for i in range(count - 1)])
    before = lax.ppermute(own, ("vocab", "section"), [(i, i + 1) for i in range(count - 1)])

    near = [o for o in range(shards) if bin(o).count("1") <= 1]
    far = [o for o in range(shards) if bin(o).count("1") > 1]
    mine, theirs, order = [], [], []
    for offsets in (near, far):
        pieces = [piece for offset in offsets for piece in heads[offset]]
        kept, sent = partial_scores(which, hidden, partner_half, pieces)
        mine.append(kept)
        theirs.append(swapped(sent, "section", 1))
        order += offsets
    pieces = [piece for offset in range(shards) for piece in heads[offset]]
    if order != list(range(shards)):
        mine = reordered(mine, order)
        theirs = reordered(theirs, order)
    logits, logprob, entropy, dlogits, outgoing = loss(
        place, tokens[None, :], own, before, after, mine, theirs, pieces, shards
    )
    partner_dlogits = swapped(dlogits, "section", 1)
    incoming = swapped(outgoing, "section", 1)
    staying = staying_gradient(which, partner_dlogits, pieces)
    previous_grad = placed_beside(which, incoming, staying)
    return (logits, logprob[0], entropy[0], previous_grad)


def reordered(blocks, order):
    whole = jnp.concatenate(blocks, axis=1)
    width = whole.shape[1] // len(order)
    parts = {offset: whole[:, i * width : (i + 1) * width] for i, offset in enumerate(order)}
    return [jnp.concatenate([parts[offset] for offset in sorted(order)], axis=1)]


def solution(mesh):
    placed = (
        P(("seq", "vocab", "section"), None),
        P(("seq", "vocab"), None),
        P(("seq", "vocab", "section")),
        P(("seq", "vocab", "section")),
        P(("seq", "vocab", "section")),
    )
    return jax.shard_map(
        body,
        mesh=mesh,
        in_specs=placed,
        out_specs=(
            P(("seq", "vocab", "section"), None),
            P(("seq", "vocab", "section")),
            P(("seq", "vocab", "section")),
            P(("seq", "vocab", "section"), None),
        ),
        check_vma=False,
    )
```

time: 119 us -> 62.7 us (0.53)
  the two profiles are of different devices: /device:TPU:0 before, /device:TPU:24 now
where the time goes in v2:
time: 62.7 us; the launch traced here: 62.4 us
  waiting for transfers between devices  28.7 us (46%)
  starting transfers between devices  19.9 us (32%)
  Pallas kernels  9.23 us (15%)
  local copies, waits for them, and re-layouts  3.73 us (6%)
  between operations  0.78 us (1%)
    ppermute x11, waiting for transfers between devices, swapped(): return lax.ppermute(value, axis, pairs)  28.7 us
    ppermute x11, starting transfers between devices, swapped(): return lax.ppermute(value, axis, pairs)  11.3 us
    ppermute x1, starting transfers between devices, body(): lax.ppermute(own, ('vocab', 'section'), [(i, i + 1) for i in range(count...  6.18 us
    unnamed x16, local copies, waits for them, and re-layouts  3.73 us
    pallas_call x2, Pallas kernels, partial_scores(): pl.pallas_call(partial_kernel, out_shape=[out, out], in_specs=[SMEM] + [V...  3.36 us
    pallas_call x1, Pallas kernels, staying_gradient(): pl.pallas_call(staying_kernel, out_shape=jax.ShapeDtypeStruct((rows, 2 *...  2.45 us
    pallas_call x1, Pallas kernels, loss(): pl.pallas_call(functools.partial(loss_kernel, len(mine), shards), out_sha...  2.43 us
    ppermute x1, starting transfers between devices, body(): lax.ppermute(own, ('vocab', 'section'), [(i + 1, i) for i in range(count...  2.36 us
  transfers between devices with their start and end apart: 13, of which 4 were waited for; matrix products, arithmetic and copies ran while one was open for 0% of the time, Pallas kernels for 9%

profile of v2, /device:TPU:24, one launch (start us, length us, event | category | flops | bytes accessed | tf_op | source)
XLA Modules:
  0.0 62.4 jit_solution(15960831534605902810)
XLA Ops:
  0.7 1.3 %copy-done = bf16[128,5120]{1,0:T(8,128)(2,1)S(1)} copy-done((bf16[128,5120]{1,0:T(8,128)(2,1)S(1)}, bf16[128,5120]{1,0:T(8,128)(2,1)}, u32[]{:S(2)}) %copy-start) | copy-done | bytes 1310744
  2.0 0.5 collective-permute-start.2
  2.6 1.3 %copy-done.4 = bf16[128,5120]{1,0:T(8,128)(2,1)S(1)} copy-done((bf16[128,5120]{1,0:T(8,128)(2,1)S(1)}, bf16[128,5120]{1,0:T(8,128)(2,1)}, u32[]{:S(2)}) %copy-start.4) | copy-done | bytes 1310744
  4.0 1.6 %collective-permute-start.3 = (bf16[64,2560]{1,0:T(8,128)(2,1)S(1)}, bf16[64,2560]{1,0:T(8,128)(2,1)S(1)}, u32[]{:S(2)}, u32[]{:S(2)}) collective-permute-start(bf16[64,2560]{1,0:T(8,128)(2,1)S(1)} %get-tuple-element.15.refs_0_.refs_4_), channel_id=1, source_target_pairs={{0,4},{4,0},{8,12},{12,8},{1,5},{5,1},{9,13},{13,9},{2,6},{6,2},{1... | collective-permute-start | bytes 983048 | tf_op jit(solution)/shard_map/ppermute | solution.py:19
  5.5 1.5 %collective-permute-start.6 = (bf16[64,2560]{1,0:T(8,128)(2,1)S(1)}, bf16[64,2560]{1,0:T(8,128)(2,1)S(1)}, u32[]{:S(2)}, u32[]{:S(2)}) collective-permute-start(bf16[64,2560]{1,0:T(8,128)(2,1)S(1)} %get-tuple-element.16.refs_1_.refs_5_), channel_id=1, source_target_pairs={{0,8},{4,12},{8,0},{12,4},{1,9},{5,13},{9,1},{13,5},{2,10},{6,14},... | collective-permute-start | bytes 983048 | tf_op jit(solution)/shard_map/ppermute | solution.py:19
  7.0 0.5 collective-permute-start.5
  7.5 0.5 collective-permute-start.4
  8.1 6.6 %collective-permute-done.3.refs_2_.refs_6_ = bf16[64,2560]{1,0:T(8,128)(2,1)S(1)} collective-permute-done((bf16[64,2560]{1,0:T(8,128)(2,1)S(1)}, bf16[64,2560]{1,0:T(8,128)(2,1)S(1)}, u32[]{:S(2)}, u32[]{:S(2)}) %collective-permute-start.3) | collective-permute-done | bytes 327712 | tf_op jit(solution)/shard_map/ppermute | solution.py:19
  14.6 1.5 %collective-permute-start.7 = (bf16[64,2560]{1,0:T(8,128)(2,1)S(1)}, bf16[64,2560]{1,0:T(8,128)(2,1)}, u32[]{:S(2)}, u32[]{:S(2)}) collective-permute-start(bf16[64,2560]{1,0:T(8,128)(2,1)S(1)} %collective-permute-done.3.refs_2_.refs_6_), channel_id=1, source_target_pairs={{0,8},{4,12},{8,0},{12,4},{1,9},{5,13},{9,1},{13,5},{2,10},{6,14},... | collective-permute-start | bytes 983048 | tf_op jit(solution)/shard_map/ppermute | solution.py:19
  16.2 1.5 %collective-permute-start.8 = (bf16[64,2560]{1,0:T(8,128)(2,1)S(1)}, bf16[64,2560]{1,0:T(8,128)(2,1)}, u32[]{:S(2)}, u32[]{:S(2)}) collective-permute-start(bf16[64,2560]{1,0:T(8,128)(2,1)S(1)} %collective-permute-done.6.refs_5_.refs_9_), channel_id=1, source_target_pairs={{0,4},{4,0},{8,12},{12,8},{1,5},{5,1},{9,13},{13,9},{2,6},{6,2},{1... | collective-permute-start | bytes 983048 | tf_op jit(solution)/shard_map/ppermute | solution.py:19
  17.7 5.5 %collective-permute-done.5.refs_4_.refs_8_ = bf16[64,2560]{1,0:T(8,128)(2,1)S(1)} collective-permute-done((bf16[64,2560]{1,0:T(8,128)(2,1)S(1)}, bf16[64,2560]{1,0:T(8,128)(2,1)S(1)}, u32[]{:S(2)}, u32[]{:S(2)}) %collective-permute-start.5) | collective-permute-done | bytes 327712 | tf_op jit(solution)/shard_map/ppermute | solution.py:19
  23.2 1.8 %partial_scores.2 = (f32[128,384]{1,0:T(8,128)S(1)}, f32[128,384]{1,0:T(8,128)}) custom-call(s32[1]{0:T(128)} %bitcast.which_ref, bf16[128,5120]{1,0:T(8,128)(2,1)S(1)} %copy-done.1, bf16[128,2560]{1,0:T(8,128)(2,1)S(1)} %collective-permute-done.2.partner_ref, bf16[64,2560]{1,0:T(8,128)(2,1)S(1)} %get-tuple-element.15.refs_0_.refs_4_, ...), custom_call_target="tpu_custom_call" | custom-call | flops 503316480 | bytes 3276800 | tf_op jit(solution)/shard_map/partial_scores/pallas_call | solution.py:87
  25.0 1.6 %collective-permute-start.9 = (f32[128,384]{1,0:T(8,128)}, f32[128,384]{1,0:T(8,128)}, u32[]{:S(2)}, u32[]{:S(2)}) collective-permute-start(f32[128,384]{1,0:T(8,128)} %get-tuple-element.19), channel_id=1, source_target_pairs={{0,1},{1,0},{2,3},{3,2},{4,5},{5,4},{6,7},{7,6},{8,9},{9,8},{10,11... | collective-permute-start | bytes 589832 | tf_op jit(solution)/shard_map/ppermute | solution.py:19
  26.6 2.4 %collective-permute-start.1 = (f32[2,128]{1,0:T(2,128)S(1)}, f32[2,128]{1,0:T(2,128)S(1)}, u32[]{:S(2)}, u32[]{:S(2)}) collective-permute-start(f32[2,128]{1,0:T(2,128)S(1)} %pad_maximum_fusion.own_ref), channel_id=1, source_target_pairs={{1,0},{2,1},{3,2},{4,3},{5,4},{6,5},{7,6},{8,7},{9,8},{10,9},{11,1... | collective-permute-start | bytes 3080 | tf_op jit(solution)/shard_map/ppermute | solution.py:238
  29.0 6.2 %collective-permute-start = (f32[2,128]{1,0:T(2,128)S(1)}, f32[2,128]{1,0:T(2,128)S(1)}, u32[]{:S(2)}, u32[]{:S(2)}) collective-permute-start(f32[2,128]{1,0:T(2,128)S(1)} %pad_maximum_fusion.own_ref), channel_id=1, source_target_pairs={{0,1},{1,2},{2,3},{3,4},{4,5},{5,6},{6,7},{7,8},{8,9},{9,10},{10,1... | collective-permute-start | bytes 3080 | tf_op jit(solution)/shard_map/ppermute | solution.py:239
  35.2 1.1 %copy-done.3 = bf16[128,2560]{1,0:T(8,128)(2,1)S(1)} copy-done((bf16[128,2560]{1,0:T(8,128)(2,1)S(1)}, bf16[128,2560]{1,0:T(8,128)(2,1)}, u32[]{:S(2)}) %copy-start.3) | copy-done | bytes 655384
  36.3 1.6 %partial_scores.3 = (f32[128,128]{1,0:T(8,128)S(1)}, f32[128,128]{1,0:T(8,128)S(1)}) custom-call(s32[1]{0:T(128)} %bitcast.which_ref, bf16[128,5120]{1,0:T(8,128)(2,1)S(1)} %copy-done.1, bf16[128,2560]{1,0:T(8,128)(2,1)S(1)} %copy-done.3, bf16[64,2560]{1,0:T(8,128)(2,1)} %collective-permute-done.7.refs_0_.refs_10_.refs_6_, ...), custom_call_target="tpu_custom_call" | custom-call | flops 167772160 | bytes 1966080 | tf_op jit(solution)/shard_map/partial_scores/pallas_call | solution.py:87
  37.9 0.1 pad_add_fusion.place_ref
  38.0 4.5 %collective-permute-done.10.refs_3_ = f32[128,128]{1,0:T(8,128)S(1)} collective-permute-done((f32[128,128]{1,0:T(8,128)S(1)}, f32[128,128]{1,0:T(8,128)S(1)}, u32[]{:S(2)}, u32[]{:S(2)}) %collective-permute-start.10) | collective-permute-done | bytes 65568 | tf_op jit(solution)/shard_map/ppermute | solution.py:19
  42.6 2.4 %loss_and_outgoing.1 = (bf16[128,512]{1,0:T(8,128)(2,1)}, f32[1,128]{1,0:T(1,128)}, f32[1,128]{1,0:T(1,128)}, bf16[128,512]{1,0:T(8,128)(2,1)S(1)}, bf16[128,2560]{1,0:T(8,128)(2,1)S(1)}) custom-call(s32[2]{0:T(128)S(1)} %pad_add_fusion.place_ref, s32[1,128]{1,0:T(1,128)S(1)} %bitcast.8, f32[2,128]{1,0:T(2,128)S(1)} %pad_maximum_fusion.own_ref, ...), custom_call_target="tpu_custom_call" | custom-call | flops 335544320 | bytes 3276800 | tf_op jit(solution)/shard_map/loss_and_outgoing/pallas_call | solution.py:159
  45.0 2.0 %collective-permute-start.12 = (bf16[128,512]{1,0:T(8,128)(2,1)S(1)}, bf16[128,512]{1,0:T(8,128)(2,1)S(1)}, u32[]{:S(2)}, u32[]{:S(2)}) collective-permute-start(bf16[128,512]{1,0:T(8,128)(2,1)S(1)} %get-tuple-element.25), channel_id=1, source_target_pairs={{0,1},{1,0},{2,3},{3,2},{4,5},{5,4},{6,7},{7,6},{8,9},{9,8},{10,11... | collective-permute-start | bytes 393224 | tf_op jit(solution)/shard_map/ppermute | solution.py:19
  47.0 12.0 %collective-permute-done.12.dlogits_ref = bf16[128,512]{1,0:T(8,128)(2,1)S(1)} collective-permute-done((bf16[128,512]{1,0:T(8,128)(2,1)S(1)}, bf16[128,512]{1,0:T(8,128)(2,1)S(1)}, u32[]{:S(2)}, u32[]{:S(2)}) %collective-permute-start.12) | collective-permute-done | bytes 131104 | tf_op jit(solution)/shard_map/ppermute | solution.py:19
  59.0 2.5 %staying_gradient.1._ = bf16[128,5120]{1,0:T(8,128)(2,1)} custom-call(s32[1]{0:T(128)} %bitcast.which_ref, bf16[128,512]{1,0:T(8,128)(2,1)S(1)} %collective-permute-done.12.dlogits_ref, bf16[64,2560]{1,0:T(8,128)(2,1)S(1)} %get-tuple-element.15.refs_0_.refs_4_, bf16[64,2560]{1,0:T(8,128)(2,1)S(1)} %get-tuple-element.16.refs_1_.refs_5_, ...), custom_call_target="tpu_custom_call" | custom-call | flops 335544320 | bytes 3276800 | tf_op jit(solution)/shard_map/staying_gradient/pallas_call | solution.py:188
  61.5 0.9 %place_incoming.1 = bf16[128,5120]{1,0:T(8,128)(2,1)} custom-call(s32[1]{0:T(128)} %bitcast.which_ref, bf16[128,2560]{1,0:T(8,128)(2,1)S(1)} %collective-permute-done.11.incoming_ref, bf16[128,5120]{1,0:T(8,128)(2,1)} %staying_gradient.1._), custom_call_target="tpu_custom_call", output_to_operand_aliasing={{}: (2, {})} | custom-call | tf_op jit(solution)/shard_map/place_incoming/pallas_call | solution.py:213
  (28 shorter events, 0.3 us)
Async XLA Ops:
  0.6 1.3 %copy-start = (bf16[128,5120]{1,0:T(8,128)(2,1)S(1)}, bf16[128,5120]{1,0:T(8,128)(2,1)}, u32[]{:S(2)}) copy-start(bf16[128,5120]{1,0:T(8,128)(2,1)} %hidden_ref.3) | copy-start | bytes 3932164
  2.0 15.7 %copy-start.7 = (s32[128]{0:T(128)S(1)}, s32[128]{0:T(128)}, u32[]{:S(2)}) copy-start(s32[128]{0:T(128)} %param.9) | copy-start | bytes 1540
  2.0 21.2 %copy-start.1 = (bf16[128,5120]{1,0:T(8,128)(2,1)S(1)}, bf16[128,5120]{1,0:T(8,128)(2,1)}, u32[]{:S(2)}) copy-start(bf16[128,5120]{1,0:T(8,128)(2,1)} %hidden_ref.3) | copy-start | bytes 3932164
  2.0 21.2 %collective-permute-start.2 = (bf16[128,2560]{1,0:T(8,128)(2,1)S(1)}, bf16[128,2560]{1,0:T(8,128)(2,1)S(1)}, u32[]{:S(2)}, u32[]{:S(2)}) collective-permute-start(bf16[128,2560]{1,0:T(8,128)(2,1)S(1)} %take_half.2), channel_id=1, source_target_pairs={{0,1},{1,0},{2,3},{3,2},{4,5},{5,4},{6,7},{7,6},{8,9},{9,8},{10,11... | collective-permute-start | bytes 1966088 | tf_op jit(solution)/shard_map/ppermute | solution.py:19
  2.6 1.3 %copy-start.4 = (bf16[128,5120]{1,0:T(8,128)(2,1)S(1)}, bf16[128,5120]{1,0:T(8,128)(2,1)}, u32[]{:S(2)}) copy-start(bf16[128,5120]{1,0:T(8,128)(2,1)} %value_ref.3) | copy-start | bytes 3932164
  4.0 10.7 %collective-permute-start.3 = (bf16[64,2560]{1,0:T(8,128)(2,1)S(1)}, bf16[64,2560]{1,0:T(8,128)(2,1)S(1)}, u32[]{:S(2)}, u32[]{:S(2)}) collective-permute-start(bf16[64,2560]{1,0:T(8,128)(2,1)S(1)} %get-tuple-element.15.refs_0_.refs_4_), channel_id=1, source_target_pairs={{0,4},{4,0},{8,12},{12,8},{1,5},{5,1},{9,13},{13,9},{2,6},{6,2},{1... | collective-permute-start | bytes 983048 | tf_op jit(solution)/shard_map/ppermute | solution.py:19
  5.5 10.7 %collective-permute-start.6 = (bf16[64,2560]{1,0:T(8,128)(2,1)S(1)}, bf16[64,2560]{1,0:T(8,128)(2,1)S(1)}, u32[]{:S(2)}, u32[]{:S(2)}) collective-permute-start(bf16[64,2560]{1,0:T(8,128)(2,1)S(1)} %get-tuple-element.16.refs_1_.refs_5_), channel_id=1, source_target_pairs={{0,8},{4,12},{8,0},{12,4},{1,9},{5,13},{9,1},{13,5},{2,10},{6,14},... | collective-permute-start | bytes 983048 | tf_op jit(solution)/shard_map/ppermute | solution.py:19
  7.0 16.2 %collective-permute-start.5 = (bf16[64,2560]{1,0:T(8,128)(2,1)S(1)}, bf16[64,2560]{1,0:T(8,128)(2,1)S(1)}, u32[]{:S(2)}, u32[]{:S(2)}) collective-permute-start(bf16[64,2560]{1,0:T(8,128)(2,1)S(1)} %get-tuple-element.15.refs_0_.refs_4_), channel_id=1, source_target_pairs={{0,8},{4,12},{8,0},{12,4},{1,9},{5,13},{9,1},{13,5},{2,10},{6,14},... | collective-permute-start | bytes 983048 | tf_op jit(solution)/shard_map/ppermute | solution.py:19
  7.5 15.6 %collective-permute-start.4 = (bf16[64,2560]{1,0:T(8,128)(2,1)S(1)}, bf16[64,2560]{1,0:T(8,128)(2,1)S(1)}, u32[]{:S(2)}, u32[]{:S(2)}) collective-permute-start(bf16[64,2560]{1,0:T(8,128)(2,1)S(1)} %get-tuple-element.16.refs_1_.refs_5_), channel_id=1, source_target_pairs={{0,4},{4,0},{8,12},{12,8},{1,5},{5,1},{9,13},{13,9},{2,6},{6,2},{1... | collective-permute-start | bytes 983048 | tf_op jit(solution)/shard_map/ppermute | solution.py:19
  14.6 20.5 %collective-permute-start.7 = (bf16[64,2560]{1,0:T(8,128)(2,1)S(1)}, bf16[64,2560]{1,0:T(8,128)(2,1)}, u32[]{:S(2)}, u32[]{:S(2)}) collective-permute-start(bf16[64,2560]{1,0:T(8,128)(2,1)S(1)} %collective-permute-done.3.refs_2_.refs_6_), channel_id=1, source_target_pairs={{0,8},{4,12},{8,0},{12,4},{1,9},{5,13},{9,1},{13,5},{2,10},{6,14},... | collective-permute-start | bytes 983048 | tf_op jit(solution)/shard_map/ppermute | solution.py:19
  16.2 19.0 %collective-permute-start.8 = (bf16[64,2560]{1,0:T(8,128)(2,1)S(1)}, bf16[64,2560]{1,0:T(8,128)(2,1)}, u32[]{:S(2)}, u32[]{:S(2)}) collective-permute-start(bf16[64,2560]{1,0:T(8,128)(2,1)S(1)} %collective-permute-done.6.refs_5_.refs_9_), channel_id=1, source_target_pairs={{0,4},{4,0},{8,12},{12,8},{1,5},{5,1},{9,13},{13,9},{2,6},{6,2},{1... | collective-permute-start | bytes 983048 | tf_op jit(solution)/shard_map/ppermute | solution.py:19
  17.7 8.9 %copy-start.6 = (f32[128]{0:T(128)S(1)}, f32[128]{0:T(128)}, u32[]{:S(2)}) copy-start(f32[128]{0:T(128)} %param.8) | copy-start | bytes 1540
  23.2 1.8 %copy-start.2 = (bf16[128,2560]{1,0:T(8,128)(2,1)}, bf16[128,2560]{1,0:T(8,128)(2,1)S(1)}, u32[]{:S(2)}) copy-start(bf16[128,2560]{1,0:T(8,128)(2,1)S(1)} %collective-permute-done.2.partner_ref) | copy-start | bytes 1966084
  25.0 17.6 %collective-permute-start.9 = (f32[128,384]{1,0:T(8,128)}, f32[128,384]{1,0:T(8,128)}, u32[]{:S(2)}, u32[]{:S(2)}) collective-permute-start(f32[128,384]{1,0:T(8,128)} %get-tuple-element.19), channel_id=1, source_target_pairs={{0,1},{1,0},{2,3},{3,2},{4,5},{5,4},{6,7},{7,6},{8,9},{9,8},{10,11... | collective-permute-start | bytes 589832 | tf_op jit(solution)/shard_map/ppermute | solution.py:19
  26.6 11.4 %collective-permute-start.1 = (f32[2,128]{1,0:T(2,128)S(1)}, f32[2,128]{1,0:T(2,128)S(1)}, u32[]{:S(2)}, u32[]{:S(2)}) collective-permute-start(f32[2,128]{1,0:T(2,128)S(1)} %pad_maximum_fusion.own_ref), channel_id=1, source_target_pairs={{1,0},{2,1},{3,2},{4,3},{5,4},{6,5},{7,6},{8,7},{9,8},{10,9},{11,1... | collective-permute-start | bytes 3080 | tf_op jit(solution)/shard_map/ppermute | solution.py:238
  29.0 9.1 %collective-permute-start = (f32[2,128]{1,0:T(2,128)S(1)}, f32[2,128]{1,0:T(2,128)S(1)}, u32[]{:S(2)}, u32[]{:S(2)}) collective-permute-start(f32[2,128]{1,0:T(2,128)S(1)} %pad_maximum_fusion.own_ref), channel_id=1, source_target_pairs={{0,1},{1,2},{2,3},{3,4},{4,5},{5,6},{6,7},{7,8},{8,9},{9,10},{10,1... | collective-permute-start | bytes 3080 | tf_op jit(solution)/shard_map/ppermute | solution.py:239
  35.1 7.4 %copy-start.5 = (s32[128]{0:T(128)S(1)}, s32[128]{0:T(128)}, u32[]{:S(2)}) copy-start(s32[128]{0:T(128)} %param.7) | copy-start | bytes 1540
  35.2 1.1 %copy-start.3 = (bf16[128,2560]{1,0:T(8,128)(2,1)S(1)}, bf16[128,2560]{1,0:T(8,128)(2,1)}, u32[]{:S(2)}) copy-start(bf16[128,2560]{1,0:T(8,128)(2,1)} %copy-done.2) | copy-start | bytes 1966084
  37.9 4.7 %collective-permute-start.10 = (f32[128,128]{1,0:T(8,128)S(1)}, f32[128,128]{1,0:T(8,128)S(1)}, u32[]{:S(2)}, u32[]{:S(2)}) collective-permute-start(f32[128,128]{1,0:T(8,128)S(1)} %get-tuple-element.20), channel_id=1, source_target_pairs={{0,1},{1,0},{2,3},{3,2},{4,5},{5,4},{6,7},{7,6},{8,9},{9,8},{10,11... | collective-permute-start | bytes 196616 | tf_op jit(solution)/shard_map/ppermute | solution.py:19
  45.0 16.5 %collective-permute-start.11 = (bf16[128,2560]{1,0:T(8,128)(2,1)S(1)}, bf16[128,2560]{1,0:T(8,128)(2,1)S(1)}, u32[]{:S(2)}, u32[]{:S(2)}) collective-permute-start(bf16[128,2560]{1,0:T(8,128)(2,1)S(1)} %get-tuple-element.24), channel_id=1, source_target_pairs={{0,1},{1,0},{2,3},{3,2},{4,5},{5,4},{6,7},{7,6},{8,9},{9,8},{10,11... | collective-permute-start | bytes 1966088 | tf_op jit(solution)/shard_map/ppermute | solution.py:19
  45.0 14.0 %collective-permute-start.12 = (bf16[128,512]{1,0:T(8,128)(2,1)S(1)}, bf16[128,512]{1,0:T(8,128)(2,1)S(1)}, u32[]{:S(2)}, u32[]{:S(2)}) collective-permute-start(bf16[128,512]{1,0:T(8,128)(2,1)S(1)} %get-tuple-element.25), channel_id=1, source_target_pairs={{0,1},{1,0},{2,3},{3,2},{4,5},{5,4},{6,7},{7,6},{8,9},{9,8},{10,11... | collective-permute-start | bytes 393224 | tf_op jit(solution)/shard_map/ppermute | solution.py:19

commit v3 on v0

v3 whole, which is shorter than its diff:
```python
import functools

import jax
import jax.numpy as jnp
from jax import lax
from jax.experimental import pallas as pl
from jax.experimental.pallas import tpu as pltpu
from jax.sharding import PartitionSpec as P

F32, BF16 = jnp.float32, jnp.bfloat16
HBM = pl.BlockSpec(memory_space=pltpu.HBM)
ANY = pl.BlockSpec(memory_space=pl.ANY)
SMEM = pl.BlockSpec(memory_space=pltpu.SMEM)
VMEM = pl.BlockSpec(memory_space=pltpu.VMEM)
PARAMS = pltpu.CompilerParams(vmem_limit_bytes=48 * 1024 * 1024)


def swapped(value, axis, mask):
    pairs = [(source, source ^ mask) for source in range(lax.axis_size(axis))]
    return lax.ppermute(value, axis, pairs)


def gathered(upper, lower, axis):
    count = lax.axis_size(axis)
    masks = [1 << bit for bit in range((count - 1).bit_length())]
    uppers, lowers = {0: upper}, {0: lower}
    for mask in masks:
        uppers[mask] = swapped(upper, axis, mask)
    for mask in reversed(masks):
        lowers[mask] = swapped(lower, axis, mask)
    for offset in sorted(range(1, count), key=lambda o: (bin(o).count("1"), o)):
        if offset in uppers:
            continue
        bits = [mask for mask in masks if offset & mask]
        uppers[offset] = swapped(uppers[offset ^ bits[-1]], axis, bits[-1])
        lowers[offset] = swapped(lowers[offset ^ bits[0]], axis, bits[0])
    return [(uppers[offset], lowers[offset]) for offset in range(count)]


def halves_kernel(which_ref, hidden_ref, head_ref, other_ref, upper_ref, lower_ref, sem):
    rows, width = other_ref.shape
    other = pl.multiple_of((1 - which_ref[0]) * width, 128)
    mine = pl.multiple_of(which_ref[0] * width, 128)
    copies = []
    for i in range(2):
        part = pl.ds(i * (rows // 2), rows // 2)
        source = hidden_ref.at[part, pl.ds(other, width)]
        copies.append(pltpu.make_async_copy(source, other_ref.at[part, :], sem.at[i]))
    for i, out in enumerate((upper_ref, lower_ref)):
        source = head_ref.at[:, pl.ds(pl.multiple_of(mine + i * (width // 2), 128), width // 2)]
        copies.append(pltpu.make_async_copy(source, out, sem.at[2 + i]))
    for copy in copies:
        copy.start()
    for copy in copies:
        copy.wait()


def halves(which, hidden, head):
    rows, width = hidden.shape[0], hidden.shape[1] // 2
    piece = jax.ShapeDtypeStruct((head.shape[0], width // 2), BF16)
    return pl.pallas_call(
        halves_kernel,
        out_shape=[jax.ShapeDtypeStruct((rows, width), BF16), piece, piece],
        in_specs=[SMEM, HBM, HBM],
        out_specs=[VMEM] * 3,
        scratch_shapes=[pltpu.SemaphoreType.DMA((4,))],
        compiler_params=pltpu.CompilerParams(vmem_limit_bytes=58 * 1024 * 1024),
        name="halves",
    )(which, hidden, head)


def turned_kernel(which_ref, hidden_ref, first_ref, second_ref, *refs):
    out_ref = refs[-1]
    rows, width = first_ref.shape
    block = 256
    for i in range(width // block):
        start = which_ref[0] * width + i * block
        own = hidden_ref[:, pl.ds(pl.multiple_of(start, 128), block)]
        out_ref[i * block : (i + 1) * block, :rows] = own.T
        part = slice(i * block, (i + 1) * block)
        other = first_ref[:, part] + second_ref[:, part]
        out_ref[part, rows:] = other.T


def turned(which, hidden, partner_halves, after):
    rows, width = partner_halves[0].shape
    return pl.pallas_call(
        turned_kernel,
        out_shape=jax.ShapeDtypeStruct((width, 2 * rows), BF16),
        in_specs=[SMEM] + [VMEM] * 3 + [ANY] * len(after),
        out_specs=VMEM,
        compiler_params=PARAMS,
        cost_estimate=pl.CostEstimate(
            flops=0, bytes_accessed=8 * rows * width, transcendentals=0
        ),
        name="turned_rows",
    )(which, hidden, *partner_halves, *after)


def partial_kernel(turned_ref, *refs):
    heads, (mine_ref, theirs_ref) = refs[:-2], refs[-2:]
    shard_rows, depth = heads[0].shape
    rows = mine_ref.shape[1]
    for i in range(len(heads) // 2):
        total = jnp.dot(heads[2 * i][...], turned_ref[:depth, :], preferred_element_type=F32)
        total += jnp.dot(heads[2 * i + 1][...], turned_ref[depth:, :], preferred_element_type=F32)
        mine_ref[i * shard_rows : (i + 1) * shard_rows, :] = total[:, :rows]
        theirs_ref[i * shard_rows : (i + 1) * shard_rows, :] = total[:, rows:]


def partial_scores(turned_rows, heads):
    width, rows = turned_rows.shape
    columns = sum(head.shape[0] for head in heads) // 2
    out = jax.ShapeDtypeStruct((columns, rows // 2), F32)
    return pl.pallas_call(
        partial_kernel,
        out_shape=[out, out],
        in_specs=[VMEM] * (1 + len(heads)),
        out_specs=[VMEM, VMEM],
        compiler_params=PARAMS,
        cost_estimate=pl.CostEstimate(
            flops=2 * rows * columns * width,
            bytes_accessed=2 * width * (rows + columns),
            transcendentals=0,
        ),
        name="partial_scores",
    )(turned_rows, *heads)


def advantage_kernel(own_ref, *refs):
    near, out_ref = refs[:-1], refs[-1]
    rows = own_ref.shape[1]
    eye = lax.broadcasted_iota(jnp.int32, (rows, rows), 0) == lax.broadcasted_iota(
        jnp.int32, (rows, rows), 1
    )
    groups = jnp.sum(jnp.where(eye, own_ref[1:2, :], 0.0), axis=1, keepdims=True)
    sums, counts = jnp.zeros((rows, 1), F32), jnp.zeros((rows, 1), F32)
    for ref in (own_ref, *near):
        member = ref[1:2, :] == groups
        sums += jnp.sum(jnp.where(member, ref[0:1, :], 0.0), axis=1, keepdims=True)
        counts += jnp.sum(jnp.where(member, 1.0, 0.0), axis=1, keepdims=True)
    means = jnp.sum(jnp.where(eye, sums / counts, 0.0), axis=0, keepdims=True)
    out_ref[...] = own_ref[0:1, :] - means


def advantages(own, *near):
    return pl.pallas_call(
        advantage_kernel,
        out_shape=jax.ShapeDtypeStruct((1, own.shape[1]), F32),
        in_specs=[VMEM] * (1 + len(near)),
        out_specs=VMEM,
        compiler_params=PARAMS,
        name="advantage",
    )(own, *near)


def loss_kernel(parts, shards, shard_ref, tokens_ref, advantage_ref, *refs):
    mine, theirs = refs[:parts], refs[parts : 2 * parts]
    logits_ref, logprob_ref, entropy_ref, dlogits_ref = refs[2 * parts :]
    shard = shard_ref[0]
    rows, columns = dlogits_ref.shape
    shard_rows = columns // shards

    scores = jnp.concatenate([a[...] + b[...] for a, b in zip(mine, theirs)], axis=0)
    tokens = tokens_ref[...]
    relative = ((tokens // shard_rows) ^ shard) * shard_rows + tokens % shard_rows
    chosen = lax.broadcasted_iota(jnp.int32, (columns, rows), 0) == relative
    row_max = jnp.max(scores, axis=0, keepdims=True)
    unnormed = jnp.exp(scores - row_max)
    denominator = jnp.sum(unnormed, axis=0, keepdims=True)
    probabilities = unnormed / denominator
    dlogits = advantage_ref[...] * (probabilities - jnp.where(chosen, 1.0, 0.0))
    for i in range(shards):
        block = slice(i * shard_rows, (i + 1) * shard_rows)
        dlogits_ref[:, block] = dlogits[block, :].T.astype(BF16)
        place = pl.multiple_of((shard ^ i) * shard_rows, 128)
        logits_ref[:, pl.ds(place, shard_rows)] = scores[block, :].T.astype(BF16)
    log_total = row_max + jnp.log(denominator)
    picked = jnp.sum(jnp.where(chosen, scores, 0.0), axis=0, keepdims=True)
    logprob_ref[...] = picked - log_total
    entropy_ref[...] = log_total - jnp.sum(probabilities * scores, axis=0, keepdims=True)


def loss(shard, tokens, advantage, mine, theirs, shards):
    rows = tokens.shape[1]
    columns = sum(part.shape[0] for part in mine)
    flat = jax.ShapeDtypeStruct((1, rows), F32)
    wide = jax.ShapeDtypeStruct((rows, columns), BF16)
    return pl.pallas_call(
        functools.partial(loss_kernel, len(mine), shards),
        out_shape=[wide, flat, flat, wide],
        in_specs=[SMEM] + [VMEM] * (2 + 2 * len(mine)),
        out_specs=[VMEM] * 4,
        compiler_params=PARAMS,
        cost_estimate=pl.CostEstimate(
            flops=10 * rows * columns,
            bytes_accessed=12 * rows * columns,
            transcendentals=rows * columns,
        ),
        name="loss",
    )(shard, tokens, advantage, *mine, *theirs)


def multiplied(dlogits, heads, out_ref, start):
    block = 256
    for j in range(heads[0].shape[1] // block):
        part = slice(j * block, (j + 1) * block)
        head = jnp.concatenate([ref[:, part] for ref in heads], axis=0)
        product = jnp.dot(dlogits, head, preferred_element_type=F32)
        out_ref[:, start + j * block : start + (j + 1) * block] = product.astype(BF16)


def gradient_cost(rows, columns, width):
    return pl.CostEstimate(
        flops=2 * rows * columns * width,
        bytes_accessed=2 * width * (rows + columns),
        transcendentals=0,
    )


def first_kernel(dlogits_ref, *refs):
    heads, out_ref = refs[:-1], refs[-1]
    columns = dlogits_ref.shape[1]
    out_ref[:, :columns] = dlogits_ref[...]
    multiplied(dlogits_ref[...], heads, out_ref, columns)


def first_message(dlogits, heads):
    rows, columns = dlogits.shape
    width = heads[0].shape[1]
    return pl.pallas_call(
        first_kernel,
        out_shape=jax.ShapeDtypeStruct((rows, columns + width), BF16),
        in_specs=[VMEM] * (1 + len(heads)),
        out_specs=VMEM,
        compiler_params=PARAMS,
        cost_estimate=gradient_cost(rows, columns, width),
        name="first_message",
    )(dlogits, *heads)


def second_kernel(dlogits_ref, _, *refs):
    multiplied(dlogits_ref[...], refs[:-1], refs[-1], 0)


def second_message(dlogits, first, heads):
    rows, columns = dlogits.shape
    width = heads[0].shape[1]
    return pl.pallas_call(
        second_kernel,
        out_shape=jax.ShapeDtypeStruct((rows, width), BF16),
        in_specs=[VMEM, ANY] + [VMEM] * len(heads),
        out_specs=VMEM,
        compiler_params=PARAMS,
        cost_estimate=gradient_cost(rows, columns, width),
        name="second_message",
    )(dlogits, first, *heads)


def staying_kernel(which_ref, first_ref, *refs):
    heads, (out_ref, held_ref, sem) = refs[:-3], refs[-3:]
    width = held_ref.shape[1]
    depth = width // 2
    columns = first_ref.shape[1] - depth
    mine = pl.multiple_of(which_ref[0] * width, 128)
    other = pl.multiple_of((1 - which_ref[0]) * width, 128)
    copies = [
        pltpu.make_async_copy(
            first_ref.at[:, pl.ds(columns, depth)], out_ref.at[:, pl.ds(other, depth)], sem.at[0]
        )
    ]
    copies[0].start()
    dlogits = first_ref[:, :columns]
    for i in range(2):
        multiplied(dlogits, heads[i::2], held_ref, i * depth)
        copies.append(
            pltpu.make_async_copy(
                held_ref.at[:, pl.ds(i * depth, depth)],
                out_ref.at[:, pl.ds(pl.multiple_of(mine + i * depth, 128), depth)],
                sem.at[i + 1],
            )
        )
        copies[-1].start()
    for copy in copies:
        copy.wait()


def staying_gradient(which, first, heads):
    rows = first.shape[0]
    depth = heads[0].shape[1]
    columns = first.shape[1] - depth
    return pl.pallas_call(
        staying_kernel,
        out_shape=jax.ShapeDtypeStruct((rows, 4 * depth), BF16),
        in_specs=[SMEM] + [VMEM] * (1 + len(heads)),
        out_specs=HBM,
        scratch_shapes=[pltpu.VMEM((rows, 2 * depth), BF16), pltpu.SemaphoreType.DMA((3,))],
        compiler_params=PARAMS,
        cost_estimate=gradient_cost(rows, columns, 2 * depth),
        name="staying_gradient",
    )(which, first, *heads)


def placed_kernel(which_ref, second_ref, _, out_ref, sem):
    rows, depth = second_ref.shape
    start = pl.multiple_of((1 - which_ref[0]) * (2 * depth) + depth, 128)
    copies = []
    for i in range(4):
        part = pl.ds(i * (rows // 4), rows // 4)
        target = out_ref.at[part, pl.ds(start, depth)]
        copies.append(pltpu.make_async_copy(second_ref.at[part, :], target, sem.at[i]))
    for copy in copies:
        copy.start()
    for copy in copies:
        copy.wait()


def placed_beside(which, second, gradient):
    return pl.pallas_call(
        placed_kernel,
        out_shape=jax.ShapeDtypeStruct(gradient.shape, gradient.dtype),
        in_specs=[SMEM, VMEM, HBM],
        out_specs=HBM,
        scratch_shapes=[pltpu.SemaphoreType.DMA((4,))],
        input_output_aliases={2: 0},
        compiler_params=PARAMS,
        name="place_second",
    )(which, second, gradient)


def of_parts(value, axes, parts, pairs):
    count = lax.axis_size(axes)
    moves = [(p * count + a, p * count + b) for p in parts for a, b in pairs]
    return lax.ppermute(value, ("seq",) + axes, moves)


def body(hidden, head_weight, tokens, rewards, group_ids):
    shards = lax.axis_size("vocab")
    which = (lax.axis_index("section") % 2).reshape(1)
    shard = lax.axis_index("vocab").reshape(1)
    parts = lax.axis_size("seq")
    leading, following = range(1, parts), range(1)
    rows_axes = ("vocab", "section")
    count = lax.axis_size(rows_axes)
    sections = lax.axis_size("section")
    pairs = [(i, i ^ 1) for i in range(sections)]
    up = [(i, i + 1) for i in range(count - 1)]
    down = [(i + 1, i) for i in range(count - 1)]
    own = jnp.stack([rewards, (group_ids + 1).astype(F32)])

    other_half, upper, lower = halves(which, hidden, head_weight)
    first_half = of_parts(other_half, ("section",), following, pairs)
    edges = [of_parts(own, rows_axes, following, moves) for moves in (up, down)]

    upper, lower, first_half, edges = lax.optimization_barrier((upper, lower, first_half, edges))
    heads = gathered(upper, lower, "vocab")

    near = [o for o in range(shards) if bin(o).count("1") <= 1]
    far = [o for o in range(shards) if bin(o).count("1") > 1]
    arrived = [piece for o in near[1:] for piece in heads[o]]
    other_half, late, _ = lax.optimization_barrier((other_half, own, arrived))
    second_half = of_parts(other_half, ("section",), leading, pairs)
    edges += [of_parts(late, rows_axes, leading, moves) for moves in (up, down)]
    advantage = advantages(own, *edges)

    rows = turned(which, hidden, (first_half, second_half), (advantage,))
    mine, theirs = [], []
    for offsets in (near, far):
        kept, sent = partial_scores(rows, [piece for o in offsets for piece in heads[o]])
        mine.append(kept)
        theirs.append(swapped(sent, "section", 1))
    mine, theirs = in_order(mine, near + far), in_order(theirs, near + far)
    logits, logprob, entropy, dlogits = loss(
        shard, tokens[None, :], advantage, mine, theirs, shards
    )
    pieces = [piece for pair in heads for piece in pair]
    first = first_message(dlogits, pieces[0::2])
    first_in = swapped(first, "section", 1)
    second_in = swapped(second_message(dlogits, first, pieces[1::2]), "section", 1)
    staying = staying_gradient(which, first_in, pieces)
    previous_grad = placed_beside(which, second_in, staying)
    return (logits, logprob[0], entropy[0], previous_grad)


def in_order(blocks, order):
    if order == sorted(order):
        return blocks
    whole = jnp.concatenate(blocks, axis=0)
    width = whole.shape[0] // len(order)
    parts = {offset: whole[i * width : (i + 1) * width] for i, offset in enumerate(order)}
    return [jnp.concatenate([parts[offset] for offset in sorted(order)], axis=0)]


def solution(mesh):
    placed = (
        P(("seq", "vocab", "section"), None),
        P(("seq", "vocab"), None),
        P(("seq", "vocab", "section")),
        P(("seq", "vocab", "section")),
        P(("seq", "vocab", "section")),
    )
    return jax.shard_map(
        body,
        mesh=mesh,
        in_specs=placed,
        out_specs=(
            P(("seq", "vocab", "section"), None),
            P(("seq", "vocab", "section")),
            P(("seq", "vocab", "section")),
            P(("seq", "vocab", "section"), None),
        ),
        check_vma=False,
    )
```

time: 119 us -> 65 us (0.55)
  blocking collectives: 44.3 us -> 0 us
  starting transfers between devices: 1.55 us -> 23 us
  waiting for transfers between devices: 50.1 us -> 32.3 us
  between operations: 14.1 us -> 0.87 us
  Pallas kernels: 0 us -> 7.88 us
  matrix products: 5.91 us -> 0 us
  other arithmetic: 1.65 us -> 0.01 us
    psum x1 -> x0, blocking collectives: 44.3 us -> none  [body(): lax.psum((local_sums, local_counts), ('vocab', 'section'))]
    all_gather x1 -> x0, waiting for transfers between devices: 21.7 us -> none  [body(): incoming = lax.all_gather(head_weight, 'vocab', axis=0, tiled=True)]
    ppermute x1 -> x10, starting transfers between devices: 1.51 us -> 12.9 us  [swapped(): return lax.ppermute(value, axis, pairs)]
    ppermute x0 -> x6, starting transfers between devices: none -> 10.1 us  [of_parts(): return lax.ppermute(value, ('seq',) + axes, moves)]
    pallas_call x0 -> x10, Pallas kernels: none -> 7.88 us  [the longest x1 2.46 us: halves(): pl.pallas_call(halves_kernel, out_shape=[jax.ShapeDtypeStruct((rows, widt...]
    dot_general x4 -> x0, matrix products: 5.91 us -> none  [the longest x1 4.59 us: body(): lax.dot_general(hidden, incoming, (((1,), (1,)), ((), ())), preferred_ele...]
    ppermute x0 -> x6, waiting for transfers between devices: none -> 5.55 us  [of_parts(): return lax.ppermute(value, ('seq',) + axes, moves)]
    ppermute x1 -> x10, waiting for transfers between devices: 27.7 us -> 26.8 us  [swapped(): return lax.ppermute(value, axis, pairs)]
  transfers between devices with their start and end apart: 2 -> 16, of which waited for: 2 -> 10; matrix products, arithmetic and copies ran while one was open for 2% -> 0% of each run, Pallas kernels for 0% -> 5%
where the time goes in v3:
time: 65 us; the launch traced here: 64.8 us
  waiting for transfers between devices  32.3 us (50%)
  starting transfers between devices  23 us (35%)
  Pallas kernels  7.88 us (12%)
  between operations  0.87 us (1%)
    ppermute x10, waiting for transfers between devices, swapped(): return lax.ppermute(value, axis, pairs)  26.8 us
    ppermute x10, starting transfers between devices, swapped(): return lax.ppermute(value, axis, pairs)  12.9 us
    ppermute x6, starting transfers between devices, of_parts(): return lax.ppermute(value, ('seq',) + axes, moves)  10.1 us
    ppermute x6, waiting for transfers between devices, of_parts(): return lax.ppermute(value, ('seq',) + axes, moves)  5.55 us
    pallas_call x1, Pallas kernels, halves(): pl.pallas_call(halves_kernel, out_shape=[jax.ShapeDtypeStruct((rows, widt...  2.46 us
  transfers between devices with their start and end apart: 16, of which 10 were waited for; matrix products, arithmetic and copies ran while one was open for 0% of the time, Pallas kernels for 5%

profile of v3, /device:TPU:0, one launch (start us, length us, event | category | flops | bytes accessed | tf_op | source)
XLA Modules:
  0.0 64.8 jit_solution(14287924895691633715)
XLA Ops:
  0.7 2.5 %halves.1 = (bf16[128,2560]{1,0:T(8,128)(2,1)}, bf16[128,1280]{1,0:T(8,128)(2,1)}, bf16[128,1280]{1,0:T(8,128)(2,1)}) custom-call(s32[1]{0:T(128)} %bitcast.4.which_ref, bf16[128,5120]{1,0:T(8,128)(2,1)} %hidden_ref.3, bf16[128,5120]{1,0:T(8,128)(2,1)} %head_ref.1), custom_call_target="tpu_custom_call" | custom-call | tf_op jit(solution)/shard_map/halves/pallas_call | solution.py:61
  3.1 4.9 %collective-permute-start = (bf16[128,2560]{1,0:T(8,128)(2,1)}, bf16[128,2560]{1,0:T(8,128)(2,1)S(1)}, u32[]{:S(2)}, u32[]{:S(2)}) collective-permute-start(bf16[128,2560]{1,0:T(8,128)(2,1)} %get-tuple-element.31), channel_id=1, source_target_pairs={{0,1},{1,0},{2,3},{3,2},{4,5},{5,4},{6,7},{7,6},{8,9},{9,8},{10,11... | collective-permute-start | bytes 1966088 | tf_op jit(solution)/shard_map/ppermute | solution.py:334
  8.1 1.9 %collective-permute-start.1 = (f32[2,128]{1,0:T(2,128)S(1)}, f32[2,128]{1,0:T(2,128)S(1)}, u32[]{:S(2)}, u32[]{:S(2)}) collective-permute-start(f32[2,128]{1,0:T(2,128)S(1)} %pad_maximum_fusion.own_ref), channel_id=1, source_target_pairs={{0,1},{1,2},{2,3},{3,4},{4,5},{5,6},{6,7},{7,8},{8,9},{9,10},{10,1... | collective-permute-start | bytes 3080 | tf_op jit(solution)/shard_map/ppermute | solution.py:334
  10.0 1.3 %collective-permute-start.2 = (f32[2,128]{1,0:T(2,128)S(1)}, f32[2,128]{1,0:T(2,128)S(1)}, u32[]{:S(2)}, u32[]{:S(2)}) collective-permute-start(f32[2,128]{1,0:T(2,128)S(1)} %pad_maximum_fusion.own_ref), channel_id=1, source_target_pairs={{1,0},{2,1},{3,2},{4,3},{5,4},{6,5},{7,6},{8,7},{9,8},{10,9},{11,1... | collective-permute-start | bytes 3080 | tf_op jit(solution)/shard_map/ppermute | solution.py:334
  11.3 5.1 %collective-permute-done.1.refs_0_ = f32[2,128]{1,0:T(2,128)S(1)} collective-permute-done((f32[2,128]{1,0:T(2,128)S(1)}, f32[2,128]{1,0:T(2,128)S(1)}, u32[]{:S(2)}, u32[]{:S(2)}) %collective-permute-start.1) | collective-permute-done | bytes 1056 | tf_op jit(solution)/shard_map/ppermute | solution.py:334
  16.9 3.9 %collective-permute-start.3 = (bf16[128,1280]{1,0:T(8,128)(2,1)}, bf16[128,1280]{1,0:T(8,128)(2,1)S(1)}, u32[]{:S(2)}, u32[]{:S(2)}) collective-permute-start(bf16[128,1280]{1,0:T(8,128)(2,1)} %get-tuple-element.27.refs_0_), channel_id=1, source_target_pairs={{0,4},{4,0},{8,12},{12,8},{1,5},{5,1},{9,13},{13,9},{2,6},{6,2},{1... | collective-permute-start | bytes 983048 | tf_op jit(solution)/shard_map/ppermute | solution.py:20
  20.8 2.9 %collective-permute-start.5 = (bf16[128,1280]{1,0:T(8,128)(2,1)}, bf16[128,1280]{1,0:T(8,128)(2,1)S(1)}, u32[]{:S(2)}, u32[]{:S(2)}) collective-permute-start(bf16[128,1280]{1,0:T(8,128)(2,1)} %get-tuple-element.27.refs_0_), channel_id=1, source_target_pairs={{0,8},{4,12},{8,0},{12,4},{1,9},{5,13},{9,1},{13,5},{2,10},{6,14},... | collective-permute-start | bytes 983048 | tf_op jit(solution)/shard_map/ppermute | solution.py:20
  23.8 3.6 %collective-permute-done.3.refs_2_.refs_1_ = bf16[128,1280]{1,0:T(8,128)(2,1)S(1)} collective-permute-done((bf16[128,1280]{1,0:T(8,128)(2,1)}, bf16[128,1280]{1,0:T(8,128)(2,1)S(1)}, u32[]{:S(2)}, u32[]{:S(2)}) %collective-permute-start.3) | collective-permute-done | bytes 327712 | tf_op jit(solution)/shard_map/ppermute | solution.py:20
  27.4 5.7 %collective-permute-done.4.refs_3_.refs_1_ = bf16[128,1280]{1,0:T(8,128)(2,1)S(1)} collective-permute-done((bf16[128,1280]{1,0:T(8,128)(2,1)}, bf16[128,1280]{1,0:T(8,128)(2,1)S(1)}, u32[]{:S(2)}, u32[]{:S(2)}) %collective-permute-start.4) | collective-permute-done | bytes 327712 | tf_op jit(solution)/shard_map/ppermute | solution.py:20
  33.1 1.0 %collective-permute-done.6.refs_5_.refs_2_ = bf16[128,1280]{1,0:T(8,128)(2,1)S(1)} collective-permute-done((bf16[128,1280]{1,0:T(8,128)(2,1)}, bf16[128,1280]{1,0:T(8,128)(2,1)S(1)}, u32[]{:S(2)}, u32[]{:S(2)}) %collective-permute-start.6) | collective-permute-done | bytes 327712 | tf_op jit(solution)/shard_map/ppermute | solution.py:20
  34.1 0.7 %collective-permute-start.9 = (bf16[128,2560]{1,0:T(8,128)(2,1)}, bf16[128,2560]{1,0:T(8,128)(2,1)S(1)}, u32[]{:S(2)}, u32[]{:S(2)}) collective-permute-start(bf16[128,2560]{1,0:T(8,128)(2,1)} %get-tuple-element.31), channel_id=1, source_target_pairs={{16,17},{17,16},{18,19},{19,18},{20,21},{21,20},{22,23},{23,22},{2... | collective-permute-start | bytes 1966088 | tf_op jit(solution)/shard_map/ppermute | solution.py:334
  34.8 1.8 %collective-permute-start.10 = (bf16[128,1280]{1,0:T(8,128)(2,1)S(1)}, bf16[128,1280]{1,0:T(8,128)(2,1)S(1)}, u32[]{:S(2)}, u32[]{:S(2)}) collective-permute-start(bf16[128,1280]{1,0:T(8,128)(2,1)S(1)} %collective-permute-done.3.refs_2_.refs_1_), channel_id=1, source_target_pairs={{0,8},{4,12},{8,0},{12,4},{1,9},{5,13},{9,1},{13,5},{2,10},{6,14},... | collective-permute-start | bytes 983048 | tf_op jit(solution)/shard_map/ppermute | solution.py:20
  36.6 1.3 %collective-permute-start.11 = (bf16[128,1280]{1,0:T(8,128)(2,1)S(1)}, bf16[128,1280]{1,0:T(8,128)(2,1)S(1)}, u32[]{:S(2)}, u32[]{:S(2)}) collective-permute-start(bf16[128,1280]{1,0:T(8,128)(2,1)S(1)} %collective-permute-done.6.refs_5_.refs_2_), channel_id=1, source_target_pairs={{0,4},{4,0},{8,12},{12,8},{1,5},{5,1},{9,13},{13,9},{2,6},{6,2},{1... | collective-permute-start | bytes 983048 | tf_op jit(solution)/shard_map/ppermute | solution.py:20
  37.9 0.6 %collective-permute-start.7 = (f32[2,128]{1,0:T(2,128)S(1)}, f32[2,128]{1,0:T(2,128)S(1)}, u32[]{:S(2)}, u32[]{:S(2)}) collective-permute-start(f32[2,128]{1,0:T(2,128)S(1)} %pad_maximum_fusion.own_ref), channel_id=1, source_target_pairs={{16,17},{17,18},{18,19},{19,20},{20,21},{21,22},{22,23},{23,24},{2... | collective-permute-start | bytes 3080 | tf_op jit(solution)/shard_map/ppermute | solution.py:334
  38.6 0.7 %collective-permute-start.8 = (f32[2,128]{1,0:T(2,128)S(1)}, f32[2,128]{1,0:T(2,128)S(1)}, u32[]{:S(2)}, u32[]{:S(2)}) collective-permute-start(f32[2,128]{1,0:T(2,128)S(1)} %pad_maximum_fusion.own_ref), channel_id=1, source_target_pairs={{17,16},{18,17},{19,18},{20,19},{21,20},{22,21},{23,22},{24,23},{2... | collective-permute-start | bytes 3080 | tf_op jit(solution)/shard_map/ppermute | solution.py:334
  40.7 0.7 %partial_scores.2 = (f32[384,128]{1,0:T(8,128)S(1)}, f32[384,128]{1,0:T(8,128)S(1)}) custom-call(bf16[2560,256]{1,0:T(8,128)(2,1)S(1)} %turned_rows.1.turned_ref, bf16[128,1280]{1,0:T(8,128)(2,1)S(1)} %copy-done.2, bf16[128,1280]{1,0:T(8,128)(2,1)S(1)} %copy-done.1, bf16[128,1280]{1,0:T(8,128)(2,1)S(1)} %collective-permute-done.3.refs_2_.refs_1_, ...), custom_call_target="tpu_custom_call" | custom-call | flops 503316480 | bytes 3276800 | tf_op jit(solution)/shard_map/partial_scores/pallas_call | solution.py:115
  42.0 1.8 %collective-permute-done.11.refs_1_.refs_3_.refs_7_ = bf16[128,1280]{1,0:T(8,128)(2,1)S(1)} collective-permute-done((bf16[128,1280]{1,0:T(8,128)(2,1)S(1)}, bf16[128,1280]{1,0:T(8,128)(2,1)S(1)}, u32[]{:S(2)}, u32[]{:S(2)}) %collective-permute-start.11) | collective-permute-done | bytes 327712 | tf_op jit(solution)/shard_map/ppermute | solution.py:20
  44.3 6.3 %collective-permute-done.13.refs_3_ = f32[128,128]{1,0:T(8,128)S(1)} collective-permute-done((f32[128,128]{1,0:T(8,128)S(1)}, f32[128,128]{1,0:T(8,128)S(1)}, u32[]{:S(2)}, u32[]{:S(2)}) %collective-permute-start.13) | collective-permute-done | bytes 65568 | tf_op jit(solution)/shard_map/ppermute | solution.py:20
  50.7 1.0 %loss.1 = (bf16[128,512]{1,0:T(8,128)(2,1)}, f32[1,128]{1,0:T(1,128)}, f32[1,128]{1,0:T(1,128)}, bf16[128,512]{1,0:T(8,128)(2,1)S(1)}) custom-call(s32[1]{0:T(128)} %bitcast.shard_ref, s32[1,128]{1,0:T(1,128)S(1)} %bitcast.8, f32[1,128]{1,0:T(1,128)S(1)} %advantage.1.refs_0_.advantage_ref, f32[384,128]{1,0:T(8,128)S(1)} %get-tuple-element.32.refs_0_, ...), custom_call_target="tpu_custom_call" | custom-call | flops 655360 | bytes 786432 | tf_op jit(solution)/shard_map/loss/pallas_call | solution.py:189
  52.8 1.7 %collective-permute-start.14 = (bf16[128,1280]{1,0:T(8,128)(2,1)S(1)}, bf16[128,1280]{1,0:T(8,128)(2,1)S(1)}, u32[]{:S(2)}, u32[]{:S(2)}) collective-permute-start(bf16[128,1280]{1,0:T(8,128)(2,1)S(1)} %second_message.1), channel_id=1, source_target_pairs={{0,1},{1,0},{2,3},{3,2},{4,5},{5,4},{6,7},{7,6},{8,9},{9,8},{10,11... | collective-permute-start | bytes 983048 | tf_op jit(solution)/shard_map/ppermute | solution.py:20
  54.5 6.0 %collective-permute-done.15.first_ref = bf16[128,1792]{1,0:T(8,128)(2,1)S(1)} collective-permute-done((bf16[128,1792]{1,0:T(8,128)(2,1)S(1)}, bf16[128,1792]{1,0:T(8,128)(2,1)S(1)}, u32[]{:S(2)}, u32[]{:S(2)}) %collective-permute-start.15) | collective-permute-done | bytes 458784 | tf_op jit(solution)/shard_map/ppermute | solution.py:20
  60.5 1.3 %staying_gradient.1._ = bf16[128,5120]{1,0:T(8,128)(2,1)} custom-call(s32[1]{0:T(128)} %bitcast.4.which_ref, bf16[128,1792]{1,0:T(8,128)(2,1)S(1)} %collective-permute-done.15.first_ref, bf16[128,1280]{1,0:T(8,128)(2,1)S(1)} %copy-done.2, bf16[128,1280]{1,0:T(8,128)(2,1)S(1)} %copy-done.1, bf16[128,1280]{1,0:T(8,128)(2,1)S(1)} %collective-permute-done.3.refs_2_.refs_1_, ...), custom_call_target="tpu_custom_call" | custom-call | flops 335544320 | bytes 3276800 | tf_op jit(solution)/shard_map/staying_gradient/pallas_call | solution.py:292
  61.8 2.2 %collective-permute-done.14.second_ref = bf16[128,1280]{1,0:T(8,128)(2,1)S(1)} collective-permute-done((bf16[128,1280]{1,0:T(8,128)(2,1)S(1)}, bf16[128,1280]{1,0:T(8,128)(2,1)S(1)}, u32[]{:S(2)}, u32[]{:S(2)}) %collective-permute-start.14) | collective-permute-done | bytes 327712 | tf_op jit(solution)/shard_map/ppermute | solution.py:20
  64.0 0.8 %place_second.1 = bf16[128,5120]{1,0:T(8,128)(2,1)} custom-call(s32[1]{0:T(128)} %bitcast.4.which_ref, bf16[128,1280]{1,0:T(8,128)(2,1)S(1)} %collective-permute-done.14.second_ref, bf16[128,5120]{1,0:T(8,128)(2,1)} %staying_gradient.1._), custom_call_target="tpu_custom_call", output_to_operand_aliasing={{}: (2, {})} | custom-call | tf_op jit(solution)/shard_map/place_second/pallas_call | solution.py:319
  (32 shorter events, 4.3 us)
Async XLA Ops:
  0.6 7.4 %copy-start.5 = (s32[128]{0:T(128)S(1)}, s32[128]{0:T(128)}, u32[]{:S(2)}) copy-start(s32[128]{0:T(128)} %param.9) | copy-start | bytes 1540
  0.7 7.4 %copy-start.4 = (f32[128]{0:T(128)S(1)}, f32[128]{0:T(128)}, u32[]{:S(2)}) copy-start(f32[128]{0:T(128)} %param.8) | copy-start | bytes 1540
  0.7 39.0 %copy-start = (bf16[128,5120]{1,0:T(8,128)(2,1)S(1)}, bf16[128,5120]{1,0:T(8,128)(2,1)}, u32[]{:S(2)}) copy-start(bf16[128,5120]{1,0:T(8,128)(2,1)} %hidden_ref.3) | copy-start | bytes 3932164
  3.1 13.8 %collective-permute-start = (bf16[128,2560]{1,0:T(8,128)(2,1)}, bf16[128,2560]{1,0:T(8,128)(2,1)S(1)}, u32[]{:S(2)}, u32[]{:S(2)}) collective-permute-start(bf16[128,2560]{1,0:T(8,128)(2,1)} %get-tuple-element.31), channel_id=1, source_target_pairs={{0,1},{1,0},{2,3},{3,2},{4,5},{5,4},{6,7},{7,6},{8,9},{9,8},{10,11... | collective-permute-start | bytes 1966088 | tf_op jit(solution)/shard_map/ppermute | solution.py:334
  8.1 8.4 %collective-permute-start.1 = (f32[2,128]{1,0:T(2,128)S(1)}, f32[2,128]{1,0:T(2,128)S(1)}, u32[]{:S(2)}, u32[]{:S(2)}) collective-permute-start(f32[2,128]{1,0:T(2,128)S(1)} %pad_maximum_fusion.own_ref), channel_id=1, source_target_pairs={{0,1},{1,2},{2,3},{3,4},{4,5},{5,6},{6,7},{7,8},{8,9},{9,10},{10,1... | collective-permute-start | bytes 3080 | tf_op jit(solution)/shard_map/ppermute | solution.py:334
  10.0 6.8 %collective-permute-start.2 = (f32[2,128]{1,0:T(2,128)S(1)}, f32[2,128]{1,0:T(2,128)S(1)}, u32[]{:S(2)}, u32[]{:S(2)}) collective-permute-start(f32[2,128]{1,0:T(2,128)S(1)} %pad_maximum_fusion.own_ref), channel_id=1, source_target_pairs={{1,0},{2,1},{3,2},{4,3},{5,4},{6,5},{7,6},{8,7},{9,8},{10,9},{11,1... | collective-permute-start | bytes 3080 | tf_op jit(solution)/shard_map/ppermute | solution.py:334
  16.9 10.5 %collective-permute-start.3 = (bf16[128,1280]{1,0:T(8,128)(2,1)}, bf16[128,1280]{1,0:T(8,128)(2,1)S(1)}, u32[]{:S(2)}, u32[]{:S(2)}) collective-permute-start(bf16[128,1280]{1,0:T(8,128)(2,1)} %get-tuple-element.27.refs_0_), channel_id=1, source_target_pairs={{0,4},{4,0},{8,12},{12,8},{1,5},{5,1},{9,13},{13,9},{2,6},{6,2},{1... | collective-permute-start | bytes 983048 | tf_op jit(solution)/shard_map/ppermute | solution.py:20
  20.8 12.3 %collective-permute-start.4 = (bf16[128,1280]{1,0:T(8,128)(2,1)}, bf16[128,1280]{1,0:T(8,128)(2,1)S(1)}, u32[]{:S(2)}, u32[]{:S(2)}) collective-permute-start(bf16[128,1280]{1,0:T(8,128)(2,1)} %get-tuple-element.28.refs_1_.refs_0_), channel_id=1, source_target_pairs={{0,4},{4,0},{8,12},{12,8},{1,5},{5,1},{9,13},{13,9},{2,6},{6,2},{1... | collective-permute-start | bytes 983048 | tf_op jit(solution)/shard_map/ppermute | solution.py:20
  20.8 12.2 %collective-permute-start.5 = (bf16[128,1280]{1,0:T(8,128)(2,1)}, bf16[128,1280]{1,0:T(8,128)(2,1)S(1)}, u32[]{:S(2)}, u32[]{:S(2)}) collective-permute-start(bf16[128,1280]{1,0:T(8,128)(2,1)} %get-tuple-element.27.refs_0_), channel_id=1, source_target_pairs={{0,8},{4,12},{8,0},{12,4},{1,9},{5,13},{9,1},{13,5},{2,10},{6,14},... | collective-permute-start | bytes 983048 | tf_op jit(solution)/shard_map/ppermute | solution.py:20
  23.7 10.4 %collective-permute-start.6 = (bf16[128,1280]{1,0:T(8,128)(2,1)}, bf16[128,1280]{1,0:T(8,128)(2,1)S(1)}, u32[]{:S(2)}, u32[]{:S(2)}) collective-permute-start(bf16[128,1280]{1,0:T(8,128)(2,1)} %get-tuple-element.28.refs_1_.refs_0_), channel_id=1, source_target_pairs={{0,8},{4,12},{8,0},{12,4},{1,9},{5,13},{9,1},{13,5},{2,10},{6,14},... | collective-permute-start | bytes 983048 | tf_op jit(solution)/shard_map/ppermute | solution.py:20
  34.1 5.5 %collective-permute-start.9 = (bf16[128,2560]{1,0:T(8,128)(2,1)}, bf16[128,2560]{1,0:T(8,128)(2,1)S(1)}, u32[]{:S(2)}, u32[]{:S(2)}) collective-permute-start(bf16[128,2560]{1,0:T(8,128)(2,1)} %get-tuple-element.31), channel_id=1, source_target_pairs={{16,17},{17,16},{18,19},{19,18},{20,21},{21,20},{22,23},{23,22},{2... | collective-permute-start | bytes 1966088 | tf_op jit(solution)/shard_map/ppermute | solution.py:334
  34.8 7.1 %collective-permute-start.10 = (bf16[128,1280]{1,0:T(8,128)(2,1)S(1)}, bf16[128,1280]{1,0:T(8,128)(2,1)S(1)}, u32[]{:S(2)}, u32[]{:S(2)}) collective-permute-start(bf16[128,1280]{1,0:T(8,128)(2,1)S(1)} %collective-permute-done.3.refs_2_.refs_1_), channel_id=1, source_target_pairs={{0,8},{4,12},{8,0},{12,4},{1,9},{5,13},{9,1},{13,5},{2,10},{6,14},... | collective-permute-start | bytes 983048 | tf_op jit(solution)/shard_map/ppermute | solution.py:20
  36.6 7.1 %collective-permute-start.11 = (bf16[128,1280]{1,0:T(8,128)(2,1)S(1)}, bf16[128,1280]{1,0:T(8,128)(2,1)S(1)}, u32[]{:S(2)}, u32[]{:S(2)}) collective-permute-start(bf16[128,1280]{1,0:T(8,128)(2,1)S(1)} %collective-permute-done.6.refs_5_.refs_2_), channel_id=1, source_target_pairs={{0,4},{4,0},{8,12},{12,8},{1,5},{5,1},{9,13},{13,9},{2,6},{6,2},{1... | collective-permute-start | bytes 983048 | tf_op jit(solution)/shard_map/ppermute | solution.py:20
  37.9 1.3 %collective-permute-start.7 = (f32[2,128]{1,0:T(2,128)S(1)}, f32[2,128]{1,0:T(2,128)S(1)}, u32[]{:S(2)}, u32[]{:S(2)}) collective-permute-start(f32[2,128]{1,0:T(2,128)S(1)} %pad_maximum_fusion.own_ref), channel_id=1, source_target_pairs={{16,17},{17,18},{18,19},{19,20},{20,21},{21,22},{22,23},{23,24},{2... | collective-permute-start | bytes 3080 | tf_op jit(solution)/shard_map/ppermute | solution.py:334
  38.6 0.7 %collective-permute-start.8 = (f32[2,128]{1,0:T(2,128)S(1)}, f32[2,128]{1,0:T(2,128)S(1)}, u32[]{:S(2)}, u32[]{:S(2)}) collective-permute-start(f32[2,128]{1,0:T(2,128)S(1)} %pad_maximum_fusion.own_ref), channel_id=1, source_target_pairs={{17,16},{18,17},{19,18},{20,19},{21,20},{22,21},{23,22},{24,23},{2... | collective-permute-start | bytes 3080 | tf_op jit(solution)/shard_map/ppermute | solution.py:334
  39.6 1.0 %copy-start.1 = (bf16[128,1280]{1,0:T(8,128)(2,1)S(1)}, bf16[128,1280]{1,0:T(8,128)(2,1)}, u32[]{:S(2)}) copy-start(bf16[128,1280]{1,0:T(8,128)(2,1)} %get-tuple-element.28.refs_1_.refs_0_) | copy-start | bytes 983044
  39.6 1.1 %copy-start.2 = (bf16[128,1280]{1,0:T(8,128)(2,1)S(1)}, bf16[128,1280]{1,0:T(8,128)(2,1)}, u32[]{:S(2)}) copy-start(bf16[128,1280]{1,0:T(8,128)(2,1)} %get-tuple-element.27.refs_0_) | copy-start | bytes 983044
  41.3 9.3 %copy-start.3 = (s32[128]{0:T(128)S(1)}, s32[128]{0:T(128)}, u32[]{:S(2)}) copy-start(s32[128]{0:T(128)} %param.7) | copy-start | bytes 1540
  41.4 9.3 %collective-permute-start.12 = (f32[384,128]{1,0:T(8,128)S(1)}, f32[384,128]{1,0:T(8,128)S(1)}, u32[]{:S(2)}, u32[]{:S(2)}) collective-permute-start(f32[384,128]{1,0:T(8,128)S(1)} %get-tuple-element.34), channel_id=1, source_target_pairs={{0,1},{1,0},{2,3},{3,2},{4,5},{5,4},{6,7},{7,6},{8,9},{9,8},{10,11... | collective-permute-start | bytes 589832 | tf_op jit(solution)/shard_map/ppermute | solution.py:20
  44.1 6.6 %collective-permute-start.13 = (f32[128,128]{1,0:T(8,128)S(1)}, f32[128,128]{1,0:T(8,128)S(1)}, u32[]{:S(2)}, u32[]{:S(2)}) collective-permute-start(f32[128,128]{1,0:T(8,128)S(1)} %get-tuple-element.35), channel_id=1, source_target_pairs={{0,1},{1,0},{2,3},{3,2},{4,5},{5,4},{6,7},{7,6},{8,9},{9,8},{10,11... | collective-permute-start | bytes 196616 | tf_op jit(solution)/shard_map/ppermute | solution.py:20
  52.0 8.5 %collective-permute-start.15 = (bf16[128,1792]{1,0:T(8,128)(2,1)S(1)}, bf16[128,1792]{1,0:T(8,128)(2,1)S(1)}, u32[]{:S(2)}, u32[]{:S(2)}) collective-permute-start(bf16[128,1792]{1,0:T(8,128)(2,1)S(1)} %first_message.1._), channel_id=1, source_target_pairs={{0,1},{1,0},{2,3},{3,2},{4,5},{5,4},{6,7},{7,6},{8,9},{9,8},{10,11... | collective-permute-start | bytes 1376264 | tf_op jit(solution)/shard_map/ppermute | solution.py:20
  52.8 11.3 %collective-permute-start.14 = (bf16[128,1280]{1,0:T(8,128)(2,1)S(1)}, bf16[128,1280]{1,0:T(8,128)(2,1)S(1)}, u32[]{:S(2)}, u32[]{:S(2)}) collective-permute-start(bf16[128,1280]{1,0:T(8,128)(2,1)S(1)} %second_message.1), channel_id=1, source_target_pairs={{0,1},{1,0},{2,3},{3,2},{4,5},{5,4},{6,7},{7,6},{8,9},{9,8},{10,11... | collective-permute-start | bytes 983048 | tf_op jit(solution)/shard_map/ppermute | solution.py:20

commit v4 on v3

--- a/solution.py
+++ b/solution.py
@@ -20,81 +20,83 @@
     return lax.ppermute(value, axis, pairs)
 
 
-def gathered(upper, lower, axis):
+def gathered(first_wave, second_wave, before_passing_on, axis):
     count = lax.axis_size(axis)
     masks = [1 << bit for bit in range((count - 1).bit_length())]
-    uppers, lowers = {0: upper}, {0: lower}
+    uppers, lowers = {0: first_wave[0]}, {0: first_wave[1]}
     for mask in masks:
-        uppers[mask] = swapped(upper, axis, mask)
+        early = mask == masks[0]
+        uppers[mask] = swapped((first_wave if early else second_wave)[0], axis, mask)
     for mask in reversed(masks):
-        lowers[mask] = swapped(lower, axis, mask)
+        early = mask == masks[-1]
+        lowers[mask] = swapped((first_wave if early else second_wave)[1], axis, mask)
     for offset in sorted(range(1, count), key=lambda o: (bin(o).count("1"), o)):
         if offset in uppers:
             continue
         bits = [mask for mask in masks if offset & mask]
-        uppers[offset] = swapped(uppers[offset ^ bits[-1]], axis, bits[-1])
-        lowers[offset] = swapped(lowers[offset ^ bits[0]], axis, bits[0])
+        upper, lower, _ = lax.optimization_barrier(
+            (uppers[offset ^ bits[-1]], lowers[offset ^ bits[0]], before_passing_on)
+        )
+        uppers[offset] = swapped(upper, axis, bits[-1])
+        lowers[offset] = swapped(lower, axis, bits[0])
     return [(uppers[offset], lowers[offset]) for offset in range(count)]
 
 
-def halves_kernel(which_ref, hidden_ref, head_ref, other_ref, upper_ref, lower_ref, sem):
-    rows, width = other_ref.shape
-    other = pl.multiple_of((1 - which_ref[0]) * width, 128)
-    mine = pl.multiple_of(which_ref[0] * width, 128)
+def take_kernel(which_ref, value_ref, *refs):
+    outs, sem = refs[:-1], refs[-1]
+    width = outs[0].shape[1]
+    start = which_ref[0] * width * len(outs)
     copies = []
-    for i in range(2):
-        part = pl.ds(i * (rows // 2), rows // 2)
-        source = hidden_ref.at[part, pl.ds(other, width)]
-        copies.append(pltpu.make_async_copy(source, other_ref.at[part, :], sem.at[i]))
-    for i, out in enumerate((upper_ref, lower_ref)):
-        source = head_ref.at[:, pl.ds(pl.multiple_of(mine + i * (width // 2), 128), width // 2)]
-        copies.append(pltpu.make_async_copy(source, out, sem.at[2 + i]))
+    for i, out in enumerate(outs):
+        source = value_ref.at[:, pl.ds(pl.multiple_of(start + i * width, 128), width)]
+        copies.append(pltpu.make_async_copy(source, out, sem.at[i]))
     for copy in copies:
         copy.start()
     for copy in copies:
         copy.wait()
 
 
-def halves(which, hidden, head):
-    rows, width = hidden.shape[0], hidden.shape[1] // 2
-    piece = jax.ShapeDtypeStruct((head.shape[0], width // 2), BF16)
-    return pl.pallas_call(
-        halves_kernel,
-        out_shape=[jax.ShapeDtypeStruct((rows, width), BF16), piece, piece],
-        in_specs=[SMEM, HBM, HBM],
-        out_specs=[VMEM] * 3,
-        scratch_shapes=[pltpu.SemaphoreType.DMA((4,))],
-        compiler_params=pltpu.CompilerParams(vmem_limit_bytes=58 * 1024 * 1024),
-        name="halves",
-    )(which, hidden, head)
-
-
-def turned_kernel(which_ref, hidden_ref, first_ref, second_ref, *refs):
+def take(which, value, pieces):
+    rows, width = value.shape[0], value.shape[1] // 2 // pieces
+    return pl.pallas_call(
+        take_kernel,
+        out_shape=[jax.ShapeDtypeStruct((rows, width), value.dtype)] * pieces,
+        in_specs=[SMEM, ANY],
+        out_specs=[ANY] * pieces,
+        scratch_shapes=[pltpu.SemaphoreType.DMA((pieces,))],
+        compiler_params=PARAMS,
+        cost_estimate=pl.CostEstimate(
+            flops=0, bytes_accessed=value.size * value.dtype.itemsize, transcendentals=0
+        ),
+        name="take_half",
+    )(which, value)
+
+
+def turned_kernel(which_ref, hidden_ref, partner_ref, *refs):
     out_ref = refs[-1]
-    rows, width = first_ref.shape
+    rows, width = partner_ref.shape
     block = 256
     for i in range(width // block):
         start = which_ref[0] * width + i * block
         own = hidden_ref[:, pl.ds(pl.multiple_of(start, 128), block)]
         out_ref[i * block : (i + 1) * block, :rows] = own.T
         part = slice(i * block, (i + 1) * block)
-        other = first_ref[:, part] + second_ref[:, part]
-        out_ref[part, rows:] = other.T
-
-
-def turned(which, hidden, partner_halves, after):
-    rows, width = partner_halves[0].shape
+        out_ref[part, rows:] = partner_ref[:, part].T
+
+
+def turned(which, hidden, partner_half, after):
+    rows, width = partner_half.shape
     return pl.pallas_call(
         turned_kernel,
         out_shape=jax.ShapeDtypeStruct((width, 2 * rows), BF16),
-        in_specs=[SMEM] + [VMEM] * 3 + [ANY] * len(after),
+        in_specs=[SMEM] + [VMEM] * 2 + [ANY] * len(after),
         out_specs=VMEM,
         compiler_params=PARAMS,
         cost_estimate=pl.CostEstimate(
             flops=0, bytes_accessed=8 * rows * width, transcendentals=0
         ),
         name="turned_rows",
-    )(which, hidden, *partner_halves, *after)
+    )(which, hidden, partner_half, *after)
 
 
 def partial_kernel(turned_ref, *refs):
@@ -328,42 +330,28 @@
     )(which, second, gradient)
 
 
-def of_parts(value, axes, parts, pairs):
-    count = lax.axis_size(axes)
-    moves = [(p * count + a, p * count + b) for p in parts for a, b in pairs]
-    return lax.ppermute(value, ("seq",) + axes, moves)
-
-
 def body(hidden, head_weight, tokens, rewards, group_ids):
     shards = lax.axis_size("vocab")
     which = (lax.axis_index("section") % 2).reshape(1)
     shard = lax.axis_index("vocab").reshape(1)
-    parts = lax.axis_size("seq")
-    leading, following = range(1, parts), range(1)
-    rows_axes = ("vocab", "section")
-    count = lax.axis_size(rows_axes)
-    sections = lax.axis_size("section")
-    pairs = [(i, i ^ 1) for i in range(sections)]
-    up = [(i, i + 1) for i in range(count - 1)]
-    down = [(i + 1, i) for i in range(count - 1)]
-    own = jnp.stack([rewards, (group_ids + 1).astype(F32)])
-
-    other_half, upper, lower = halves(which, hidden, head_weight)
-    first_half = of_parts(other_half, ("section",), following, pairs)
-    edges = [of_parts(own, rows_axes, following, moves) for moves in (up, down)]
-
-    upper, lower, first_half, edges = lax.optimization_barrier((upper, lower, first_half, edges))
-    heads = gathered(upper, lower, "vocab")
-
     near = [o for o in range(shards) if bin(o).count("1") <= 1]
     far = [o for o in range(shards) if bin(o).count("1") > 1]
-    arrived = [piece for o in near[1:] for piece in heads[o]]
-    other_half, late, _ = lax.optimization_barrier((other_half, own, arrived))
-    second_half = of_parts(other_half, ("section",), leading, pairs)
-    edges += [of_parts(late, rows_axes, leading, moves) for moves in (up, down)]
-    advantage = advantages(own, *edges)
-
-    rows = turned(which, hidden, (first_half, second_half), (advantage,))
+
+    pieces = tuple(take(which, head_weight, 2))
+    late_hidden, pieces = lax.optimization_barrier((hidden, pieces))
+    (other_half,) = take(1 - which, late_hidden, 1)
+    other_half, late_pieces = lax.optimization_barrier((other_half, pieces))
+    partner_half = swapped(other_half, "section", 1)
+
+    own = jnp.stack([rewards, (group_ids + 1).astype(F32)])
+    axes = ("vocab", "section")
+    count = lax.axis_size(axes)
+    before = lax.ppermute(own, axes, [(i, i + 1) for i in range(count - 1)])
+    after = lax.ppermute(own, axes, [(i + 1, i) for i in range(count - 1)])
+    advantage = advantages(own, before, after)
+    heads = gathered(pieces, late_pieces, advantage, "vocab")
+
+    rows = turned(which, hidden, partner_half, (advantage,))
     mine, theirs = [], []
     for offsets in (near, far):
         kept, sent = partial_scores(rows, [piece for o in offsets for piece in heads[o]])

time: 65 us -> 64.3 us (0.989)
  starting transfers between devices: 23 us -> 20.1 us
  waiting for transfers between devices: 32.3 us -> 34.8 us
  Pallas kernels: 7.88 us -> 5.48 us
  local copies, waits for them, and re-layouts: 0.63 us -> 2.89 us
    ppermute x6 -> x2, starting transfers between devices: 10.1 us -> 5.84 us  [the longest x1 4.55 us: body(): before = lax.ppermute(own, axes, [(i, i + 1) for i in range(count - 1)])]
    ppermute x6 -> x2, waiting for transfers between devices: 5.55 us -> 8.52 us  [the longest x1 8.51 us: body(): after = lax.ppermute(own, axes, [(i + 1, i) for i in range(count - 1)])]
    pallas_call x1 -> x2, Pallas kernels: 2.46 us -> 0.14 us  [take(): pl.pallas_call(take_kernel, out_shape=[jax.ShapeDtypeStruct((rows, width)...]
    unnamed x12 -> x18, local copies, waits for them, and re-layouts: 0.63 us -> 2.89 us
    ppermute x10 -> x11, starting transfers between devices: 12.9 us -> 14.2 us  [swapped(): return lax.ppermute(value, axis, pairs)]
    ppermute x10 -> x11, waiting for transfers between devices: 26.8 us -> 26.3 us  [swapped(): return lax.ppermute(value, axis, pairs)]
  transfers between devices with their start and end apart: 16 -> 13, of which waited for: 10 -> 7; matrix products, arithmetic and copies ran while one was open for 0% -> 0% of each run, Pallas kernels for 5% -> 5%
where the time goes in v4:
time: 64.3 us; the launch traced here: 64.1 us
  waiting for transfers between devices  34.8 us (54%)
  starting transfers between devices  20.1 us (31%)
  Pallas kernels  5.48 us (9%)
  local copies, waits for them, and re-layouts  2.89 us (4%)
  between operations  0.81 us (1%)
    ppermute x11, waiting for transfers between devices, swapped(): return lax.ppermute(value, axis, pairs)  26.3 us
    ppermute x11, starting transfers between devices, swapped(): return lax.ppermute(value, axis, pairs)  14.2 us
    ppermute x1, waiting for transfers between devices, body(): after = lax.ppermute(own, axes, [(i + 1, i) for i in range(count - 1)])  8.51 us
    ppermute x1, starting transfers between devices, body(): before = lax.ppermute(own, axes, [(i, i + 1) for i in range(count - 1)])  4.55 us
    unnamed x18, local copies, waits for them, and re-layouts  2.89 us
    ppermute x1, starting transfers between devices, body(): after = lax.ppermute(own, axes, [(i + 1, i) for i in range(count - 1)])  1.29 us
  transfers between devices with their start and end apart: 13, of which 7 were waited for; matrix products, arithmetic and copies ran while one was open for 0% of the time, Pallas kernels for 5%

profile of v4, /device:TPU:0, one launch (start us, length us, event | category | flops | bytes accessed | tf_op | source)
XLA Modules:
  0.0 64.1 jit_solution(4526433783498597352)
XLA Ops:
  0.7 1.4 %copy-done.5 = bf16[128,5120]{1,0:T(8,128)(2,1)S(1)} copy-done((bf16[128,5120]{1,0:T(8,128)(2,1)S(1)}, bf16[128,5120]{1,0:T(8,128)(2,1)}, u32[]{:S(2)}) %copy-start.5) | copy-done | bytes 1310744
  2.2 3.0 %collective-permute-start.3 = (bf16[128,1280]{1,0:T(8,128)(2,1)S(1)}, bf16[128,1280]{1,0:T(8,128)(2,1)S(1)}, u32[]{:S(2)}, u32[]{:S(2)}) collective-permute-start(bf16[128,1280]{1,0:T(8,128)(2,1)S(1)} %get-tuple-element.29.refs_0_), channel_id=1, source_target_pairs={{0,4},{4,0},{8,12},{12,8},{1,5},{5,1},{9,13},{13,9},{2,6},{6,2},{1... | collective-permute-start | bytes 983048 | tf_op jit(solution)/shard_map/ppermute | solution.py:20
  5.2 1.5 %collective-permute-start.6 = (bf16[128,1280]{1,0:T(8,128)(2,1)S(1)}, bf16[128,1280]{1,0:T(8,128)(2,1)S(1)}, u32[]{:S(2)}, u32[]{:S(2)}) collective-permute-start(bf16[128,1280]{1,0:T(8,128)(2,1)S(1)} %get-tuple-element.28.refs_1_.refs_0_), channel_id=1, source_target_pairs={{0,8},{4,12},{8,0},{12,4},{1,9},{5,13},{9,1},{13,5},{2,10},{6,14},... | collective-permute-start | bytes 983048 | tf_op jit(solution)/shard_map/ppermute | solution.py:20
  6.8 1.6 %collective-permute-start.2 = (bf16[128,2560]{1,0:T(8,128)(2,1)S(1)}, bf16[128,2560]{1,0:T(8,128)(2,1)S(1)}, u32[]{:S(2)}, u32[]{:S(2)}) collective-permute-start(bf16[128,2560]{1,0:T(8,128)(2,1)S(1)} %take_half.3), channel_id=1, source_target_pairs={{0,1},{1,0},{2,3},{3,2},{4,5},{5,4},{6,7},{7,6},{8,9},{9,8},{10,11... | collective-permute-start | bytes 1966088 | tf_op jit(solution)/shard_map/ppermute | solution.py:20
  8.4 1.3 %collective-permute-start.1 = (f32[2,128]{1,0:T(2,128)S(1)}, f32[2,128]{1,0:T(2,128)S(1)}, u32[]{:S(2)}, u32[]{:S(2)}) collective-permute-start(f32[2,128]{1,0:T(2,128)S(1)} %pad_maximum_fusion.own_ref), channel_id=1, source_target_pairs={{1,0},{2,1},{3,2},{4,3},{5,4},{6,5},{7,6},{8,7},{9,8},{10,9},{11,1... | collective-permute-start | bytes 3080 | tf_op jit(solution)/shard_map/ppermute | solution.py:350
  9.7 4.5 %collective-permute-start = (f32[2,128]{1,0:T(2,128)S(1)}, f32[2,128]{1,0:T(2,128)S(1)}, u32[]{:S(2)}, u32[]{:S(2)}) collective-permute-start(f32[2,128]{1,0:T(2,128)S(1)} %pad_maximum_fusion.own_ref), channel_id=1, source_target_pairs={{0,1},{1,2},{2,3},{3,4},{4,5},{5,6},{6,7},{7,8},{8,9},{9,10},{10,1... | collective-permute-start | bytes 3080 | tf_op jit(solution)/shard_map/ppermute | solution.py:349
  14.3 8.5 %collective-permute-done.1.refs_1_ = f32[2,128]{1,0:T(2,128)S(1)} collective-permute-done((f32[2,128]{1,0:T(2,128)S(1)}, f32[2,128]{1,0:T(2,128)S(1)}, u32[]{:S(2)}, u32[]{:S(2)}) %collective-permute-start.1) | collective-permute-done | bytes 1056 | tf_op jit(solution)/shard_map/ppermute | solution.py:350
  22.8 0.5 collective-permute-start.4
  23.4 2.9 %collective-permute-start.5 = (bf16[128,1280]{1,0:T(8,128)(2,1)S(1)}, bf16[128,1280]{1,0:T(8,128)(2,1)S(1)}, u32[]{:S(2)}, u32[]{:S(2)}) collective-permute-start(bf16[128,1280]{1,0:T(8,128)(2,1)S(1)} %get-tuple-element.29.refs_0_), channel_id=1, source_target_pairs={{0,8},{4,12},{8,0},{12,4},{1,9},{5,13},{9,1},{13,5},{2,10},{6,14},... | collective-permute-start | bytes 983048 | tf_op jit(solution)/shard_map/ppermute | solution.py:20
  26.6 2.0 %collective-permute-start.8 = (bf16[128,1280]{1,0:T(8,128)(2,1)S(1)}, bf16[128,1280]{1,0:T(8,128)(2,1)S(1)}, u32[]{:S(2)}, u32[]{:S(2)}) collective-permute-start(bf16[128,1280]{1,0:T(8,128)(2,1)S(1)} %collective-permute-done.6.refs_5_.refs_2_), channel_id=1, source_target_pairs={{0,4},{4,0},{8,12},{12,8},{1,5},{5,1},{9,13},{13,9},{2,6},{6,2},{1... | collective-permute-start | bytes 983048 | tf_op jit(solution)/shard_map/ppermute | solution.py:20
  28.7 0.4 turned_rows.1.turned_ref
  29.1 4.4 %collective-permute-done.4.refs_3_.refs_1_ = bf16[128,1280]{1,0:T(8,128)(2,1)S(1)} collective-permute-done((bf16[128,1280]{1,0:T(8,128)(2,1)S(1)}, bf16[128,1280]{1,0:T(8,128)(2,1)S(1)}, u32[]{:S(2)}, u32[]{:S(2)}) %collective-permute-start.4) | collective-permute-done | bytes 327712 | tf_op jit(solution)/shard_map/ppermute | solution.py:20
  33.5 1.4 %collective-permute-done.5.refs_4_.refs_2_ = bf16[128,1280]{1,0:T(8,128)(2,1)S(1)} collective-permute-done((bf16[128,1280]{1,0:T(8,128)(2,1)S(1)}, bf16[128,1280]{1,0:T(8,128)(2,1)S(1)}, u32[]{:S(2)}, u32[]{:S(2)}) %collective-permute-start.5) | collective-permute-done | bytes 327712 | tf_op jit(solution)/shard_map/ppermute | solution.py:20
  34.9 0.7 %partial_scores.2 = (f32[384,128]{1,0:T(8,128)S(1)}, f32[384,128]{1,0:T(8,128)S(1)}) custom-call(bf16[2560,256]{1,0:T(8,128)(2,1)S(1)} %turned_rows.1.turned_ref, bf16[128,1280]{1,0:T(8,128)(2,1)S(1)} %get-tuple-element.29.refs_0_, bf16[128,1280]{1,0:T(8,128)(2,1)S(1)} %get-tuple-element.28.refs_1_.refs_0_, ...), custom_call_target="tpu_custom_call" | custom-call | flops 503316480 | bytes 3276800 | tf_op jit(solution)/shard_map/partial_scores/pallas_call | solution.py:117
  35.8 3.4 %collective-permute-done.7.refs_0_.refs_3_.refs_6_ = bf16[128,1280]{1,0:T(8,128)(2,1)S(1)} collective-permute-done((bf16[128,1280]{1,0:T(8,128)(2,1)S(1)}, bf16[128,1280]{1,0:T(8,128)(2,1)S(1)}, u32[]{:S(2)}, u32[]{:S(2)}) %collective-permute-start.7) | collective-permute-done | bytes 327712 | tf_op jit(solution)/shard_map/ppermute | solution.py:20
  39.6 0.4 copy-done.1
  40.2 4.1 %collective-permute-done.10.refs_3_ = f32[128,128]{1,0:T(8,128)S(1)} collective-permute-done((f32[128,128]{1,0:T(8,128)S(1)}, f32[128,128]{1,0:T(8,128)S(1)}, u32[]{:S(2)}, u32[]{:S(2)}) %collective-permute-start.10) | collective-permute-done | bytes 65568 | tf_op jit(solution)/shard_map/ppermute | solution.py:20
  44.3 1.0 %loss.1 = (bf16[128,512]{1,0:T(8,128)(2,1)}, f32[1,128]{1,0:T(1,128)}, f32[1,128]{1,0:T(1,128)}, bf16[128,512]{1,0:T(8,128)(2,1)S(1)}) custom-call(s32[1]{0:T(128)} %bitcast.shard_ref, s32[1,128]{1,0:T(1,128)S(1)} %bitcast.8, f32[1,128]{1,0:T(1,128)S(1)} %advantage.1.refs_0_.advantage_ref, f32[384,128]{1,0:T(8,128)S(1)} %get-tuple-element.30.refs_0_, ...), custom_call_target="tpu_custom_call" | custom-call | flops 655360 | bytes 786432 | tf_op jit(solution)/shard_map/loss/pallas_call | solution.py:191
  45.3 1.0 %copy-done.4 = bf16[128,1280]{1,0:T(8,128)(2,1)S(1)} copy-done((bf16[128,1280]{1,0:T(8,128)(2,1)S(1)}, bf16[128,1280]{1,0:T(8,128)(2,1)}, u32[]{:S(2)}) %copy-start.4) | copy-done | bytes 327704
  47.1 2.0 %collective-permute-start.11 = (bf16[128,1280]{1,0:T(8,128)(2,1)S(1)}, bf16[128,1280]{1,0:T(8,128)(2,1)S(1)}, u32[]{:S(2)}, u32[]{:S(2)}) collective-permute-start(bf16[128,1280]{1,0:T(8,128)(2,1)S(1)} %second_message.1), channel_id=1, source_target_pairs={{0,1},{1,0},{2,3},{3,2},{4,5},{5,4},{6,7},{7,6},{8,9},{9,8},{10,11... | collective-permute-start | bytes 983048 | tf_op jit(solution)/shard_map/ppermute | solution.py:20
  49.1 10.7 %collective-permute-done.12.first_ref = bf16[128,1792]{1,0:T(8,128)(2,1)S(1)} collective-permute-done((bf16[128,1792]{1,0:T(8,128)(2,1)S(1)}, bf16[128,1792]{1,0:T(8,128)(2,1)S(1)}, u32[]{:S(2)}, u32[]{:S(2)}) %collective-permute-start.12) | collective-permute-done | bytes 458784 | tf_op jit(solution)/shard_map/ppermute | solution.py:20
  59.8 1.3 %staying_gradient.1._ = bf16[128,5120]{1,0:T(8,128)(2,1)} custom-call(s32[1]{0:T(128)} %bitcast.4.which_ref, bf16[128,1792]{1,0:T(8,128)(2,1)S(1)} %collective-permute-done.12.first_ref, bf16[128,1280]{1,0:T(8,128)(2,1)S(1)} %get-tuple-element.29.refs_0_, bf16[128,1280]{1,0:T(8,128)(2,1)S(1)} %get-tuple-element.28.refs_1_.refs_0_, ...), custom_call_target="tpu_custom_call" | custom-call | flops 335544320 | bytes 3276800 | tf_op jit(solution)/shard_map/staying_gradient/pallas_call | solution.py:294
  61.1 2.2 %collective-permute-done.11.second_ref = bf16[128,1280]{1,0:T(8,128)(2,1)S(1)} collective-permute-done((bf16[128,1280]{1,0:T(8,128)(2,1)S(1)}, bf16[128,1280]{1,0:T(8,128)(2,1)S(1)}, u32[]{:S(2)}, u32[]{:S(2)}) %collective-permute-start.11) | collective-permute-done | bytes 327712 | tf_op jit(solution)/shard_map/ppermute | solution.py:20
  63.3 0.8 %place_second.1 = bf16[128,5120]{1,0:T(8,128)(2,1)} custom-call(s32[1]{0:T(128)} %bitcast.4.which_ref, bf16[128,1280]{1,0:T(8,128)(2,1)S(1)} %collective-permute-done.11.second_ref, bf16[128,5120]{1,0:T(8,128)(2,1)} %staying_gradient.1._), custom_call_target="tpu_custom_call", output_to_operand_aliasing={{}: (2, {})} | custom-call | tf_op jit(solution)/shard_map/place_second/pallas_call | solution.py:321
  (33 shorter events, 2.2 us)
Async XLA Ops:
  0.6 6.1 %copy-start = (bf16[128,5120]{1,0:T(8,128)(2,1)S(1)}, bf16[128,5120]{1,0:T(8,128)(2,1)}, u32[]{:S(2)}) copy-start(bf16[128,5120]{1,0:T(8,128)(2,1)} %hidden_ref.1) | copy-start | bytes 3932164
  0.7 1.4 %copy-start.5 = (bf16[128,5120]{1,0:T(8,128)(2,1)S(1)}, bf16[128,5120]{1,0:T(8,128)(2,1)}, u32[]{:S(2)}) copy-start(bf16[128,5120]{1,0:T(8,128)(2,1)} %value_ref.1) | copy-start | bytes 3932164
  2.2 6.3 %copy-start.8 = (s32[128]{0:T(128)S(1)}, s32[128]{0:T(128)}, u32[]{:S(2)}) copy-start(s32[128]{0:T(128)} %param.9) | copy-start | bytes 1540
  2.2 6.3 %copy-start.7 = (f32[128]{0:T(128)S(1)}, f32[128]{0:T(128)}, u32[]{:S(2)}) copy-start(f32[128]{0:T(128)} %param.8) | copy-start | bytes 1540
  2.2 24.3 %collective-permute-start.3 = (bf16[128,1280]{1,0:T(8,128)(2,1)S(1)}, bf16[128,1280]{1,0:T(8,128)(2,1)S(1)}, u32[]{:S(2)}, u32[]{:S(2)}) collective-permute-start(bf16[128,1280]{1,0:T(8,128)(2,1)S(1)} %get-tuple-element.29.refs_0_), channel_id=1, source_target_pairs={{0,4},{4,0},{8,12},{12,8},{1,5},{5,1},{9,13},{13,9},{2,6},{6,2},{1... | collective-permute-start | bytes 983048 | tf_op jit(solution)/shard_map/ppermute | solution.py:20
  5.2 21.4 %collective-permute-start.6 = (bf16[128,1280]{1,0:T(8,128)(2,1)S(1)}, bf16[128,1280]{1,0:T(8,128)(2,1)S(1)}, u32[]{:S(2)}, u32[]{:S(2)}) collective-permute-start(bf16[128,1280]{1,0:T(8,128)(2,1)S(1)} %get-tuple-element.28.refs_1_.refs_0_), channel_id=1, source_target_pairs={{0,8},{4,12},{8,0},{12,4},{1,9},{5,13},{9,1},{13,5},{2,10},{6,14},... | collective-permute-start | bytes 983048 | tf_op jit(solution)/shard_map/ppermute | solution.py:20
  6.8 21.9 %collective-permute-start.2 = (bf16[128,2560]{1,0:T(8,128)(2,1)S(1)}, bf16[128,2560]{1,0:T(8,128)(2,1)S(1)}, u32[]{:S(2)}, u32[]{:S(2)}) collective-permute-start(bf16[128,2560]{1,0:T(8,128)(2,1)S(1)} %take_half.3), channel_id=1, source_target_pairs={{0,1},{1,0},{2,3},{3,2},{4,5},{5,4},{6,7},{7,6},{8,9},{9,8},{10,11... | collective-permute-start | bytes 1966088 | tf_op jit(solution)/shard_map/ppermute | solution.py:20
  8.4 14.4 %collective-permute-start.1 = (f32[2,128]{1,0:T(2,128)S(1)}, f32[2,128]{1,0:T(2,128)S(1)}, u32[]{:S(2)}, u32[]{:S(2)}) collective-permute-start(f32[2,128]{1,0:T(2,128)S(1)} %pad_maximum_fusion.own_ref), channel_id=1, source_target_pairs={{1,0},{2,1},{3,2},{4,3},{5,4},{6,5},{7,6},{8,7},{9,8},{10,9},{11,1... | collective-permute-start | bytes 3080 | tf_op jit(solution)/shard_map/ppermute | solution.py:350
  9.7 13.6 %collective-permute-start = (f32[2,128]{1,0:T(2,128)S(1)}, f32[2,128]{1,0:T(2,128)S(1)}, u32[]{:S(2)}, u32[]{:S(2)}) collective-permute-start(f32[2,128]{1,0:T(2,128)S(1)} %pad_maximum_fusion.own_ref), channel_id=1, source_target_pairs={{0,1},{1,2},{2,3},{3,4},{4,5},{5,6},{6,7},{7,8},{8,9},{9,10},{10,1... | collective-permute-start | bytes 3080 | tf_op jit(solution)/shard_map/ppermute | solution.py:349
  22.8 10.6 %collective-permute-start.4 = (bf16[128,1280]{1,0:T(8,128)(2,1)S(1)}, bf16[128,1280]{1,0:T(8,128)(2,1)S(1)}, u32[]{:S(2)}, u32[]{:S(2)}) collective-permute-start(bf16[128,1280]{1,0:T(8,128)(2,1)S(1)} %get-tuple-element.28.refs_1_.refs_0_), channel_id=1, source_target_pairs={{0,4},{4,0},{8,12},{12,8},{1,5},{5,1},{9,13},{13,9},{2,6},{6,2},{1... | collective-permute-start | bytes 983048 | tf_op jit(solution)/shard_map/ppermute | solution.py:20
  23.4 11.5 %collective-permute-start.5 = (bf16[128,1280]{1,0:T(8,128)(2,1)S(1)}, bf16[128,1280]{1,0:T(8,128)(2,1)S(1)}, u32[]{:S(2)}, u32[]{:S(2)}) collective-permute-start(bf16[128,1280]{1,0:T(8,128)(2,1)S(1)} %get-tuple-element.29.refs_0_), channel_id=1, source_target_pairs={{0,8},{4,12},{8,0},{12,4},{1,9},{5,13},{9,1},{13,5},{2,10},{6,14},... | collective-permute-start | bytes 983048 | tf_op jit(solution)/shard_map/ppermute | solution.py:20
  26.5 12.7 %collective-permute-start.7 = (bf16[128,1280]{1,0:T(8,128)(2,1)S(1)}, bf16[128,1280]{1,0:T(8,128)(2,1)S(1)}, u32[]{:S(2)}, u32[]{:S(2)}) collective-permute-start(bf16[128,1280]{1,0:T(8,128)(2,1)S(1)} %collective-permute-done.3.refs_2_.refs_1_), channel_id=1, source_target_pairs={{0,8},{4,12},{8,0},{12,4},{1,9},{5,13},{9,1},{13,5},{2,10},{6,14},... | collective-permute-start | bytes 983048 | tf_op jit(solution)/shard_map/ppermute | solution.py:20
  26.6 12.6 %collective-permute-start.8 = (bf16[128,1280]{1,0:T(8,128)(2,1)S(1)}, bf16[128,1280]{1,0:T(8,128)(2,1)S(1)}, u32[]{:S(2)}, u32[]{:S(2)}) collective-permute-start(bf16[128,1280]{1,0:T(8,128)(2,1)S(1)} %collective-permute-done.6.refs_5_.refs_2_), channel_id=1, source_target_pairs={{0,4},{4,0},{8,12},{12,8},{1,5},{5,1},{9,13},{13,9},{2,6},{6,2},{1... | collective-permute-start | bytes 983048 | tf_op jit(solution)/shard_map/ppermute | solution.py:20
  35.6 8.7 %copy-start.6 = (s32[128]{0:T(128)S(1)}, s32[128]{0:T(128)}, u32[]{:S(2)}) copy-start(s32[128]{0:T(128)} %param.7) | copy-start | bytes 1540
  35.6 8.7 %collective-permute-start.9 = (f32[384,128]{1,0:T(8,128)S(1)}, f32[384,128]{1,0:T(8,128)S(1)}, u32[]{:S(2)}, u32[]{:S(2)}) collective-permute-start(f32[384,128]{1,0:T(8,128)S(1)} %get-tuple-element.34), channel_id=1, source_target_pairs={{0,1},{1,0},{2,3},{3,2},{4,5},{5,4},{6,7},{7,6},{8,9},{9,8},{10,11... | collective-permute-start | bytes 589832 | tf_op jit(solution)/shard_map/ppermute | solution.py:20
  39.2 0.8 %copy-start.3 = (bf16[128,1280]{1,0:T(8,128)(2,1)}, bf16[128,1280]{1,0:T(8,128)(2,1)S(1)}, u32[]{:S(2)}) copy-start(bf16[128,1280]{1,0:T(8,128)(2,1)S(1)} %collective-permute-done.7.refs_0_.refs_3_.refs_6_) | copy-start | bytes 983044
  39.2 0.7 %copy-start.1 = (bf16[128,1280]{1,0:T(8,128)(2,1)}, bf16[128,1280]{1,0:T(8,128)(2,1)S(1)}, u32[]{:S(2)}) copy-start(bf16[128,1280]{1,0:T(8,128)(2,1)S(1)} %collective-permute-done.8.refs_1_.refs_3_.refs_7_) | copy-start | bytes 983044
  40.0 6.8 %copy-start.2 = (bf16[128,1280]{1,0:T(8,128)(2,1)S(1)}, bf16[128,1280]{1,0:T(8,128)(2,1)}, u32[]{:S(2)}) copy-start(bf16[128,1280]{1,0:T(8,128)(2,1)} %copy-done.1) | copy-start | bytes 983044
  40.0 4.3 %collective-permute-start.10 = (f32[128,128]{1,0:T(8,128)S(1)}, f32[128,128]{1,0:T(8,128)S(1)}, u32[]{:S(2)}, u32[]{:S(2)}) collective-permute-start(f32[128,128]{1,0:T(8,128)S(1)} %get-tuple-element.35), channel_id=1, source_target_pairs={{0,1},{1,0},{2,3},{3,2},{4,5},{5,4},{6,7},{7,6},{8,9},{9,8},{10,11... | collective-permute-start | bytes 196616 | tf_op jit(solution)/shard_map/ppermute | solution.py:20
  45.3 1.0 %copy-start.4 = (bf16[128,1280]{1,0:T(8,128)(2,1)S(1)}, bf16[128,1280]{1,0:T(8,128)(2,1)}, u32[]{:S(2)}) copy-start(bf16[128,1280]{1,0:T(8,128)(2,1)} %copy-done.3) | copy-start | bytes 983044
  46.6 13.2 %collective-permute-start.12 = (bf16[128,1792]{1,0:T(8,128)(2,1)S(1)}, bf16[128,1792]{1,0:T(8,128)(2,1)S(1)}, u32[]{:S(2)}, u32[]{:S(2)}) collective-permute-start(bf16[128,1792]{1,0:T(8,128)(2,1)S(1)} %first_message.1._), channel_id=1, source_target_pairs={{0,1},{1,0},{2,3},{3,2},{4,5},{5,4},{6,7},{7,6},{8,9},{9,8},{10,11... | collective-permute-start | bytes 1376264 | tf_op jit(solution)/shard_map/ppermute | solution.py:20
  47.1 16.2 %collective-permute-start.11 = (bf16[128,1280]{1,0:T(8,128)(2,1)S(1)}, bf16[128,1280]{1,0:T(8,128)(2,1)S(1)}, u32[]{:S(2)}, u32[]{:S(2)}) collective-permute-start(bf16[128,1280]{1,0:T(8,128)(2,1)S(1)} %second_message.1), channel_id=1, source_target_pairs={{0,1},{1,0},{2,3},{3,2},{4,5},{5,4},{6,7},{7,6},{8,9},{9,8},{10,11... | collective-permute-start | bytes 983048 | tf_op jit(solution)/shard_map/ppermute | solution.py:20

commit v5 on v4

--- a/solution.py
+++ b/solution.py
@@ -12,7 +12,7 @@
 ANY = pl.BlockSpec(memory_space=pl.ANY)
 SMEM = pl.BlockSpec(memory_space=pltpu.SMEM)
 VMEM = pl.BlockSpec(memory_space=pltpu.VMEM)
-PARAMS = pltpu.CompilerParams(vmem_limit_bytes=48 * 1024 * 1024)
+PARAMS = pltpu.CompilerParams(vmem_limit_bytes=16 * 1024 * 1024)
 
 
 def swapped(value, axis, mask):
@@ -20,7 +20,7 @@
     return lax.ppermute(value, axis, pairs)
 
 
-def gathered(first_wave, second_wave, before_passing_on, axis):
+def gathered(first_wave, second_wave, axis):
     count = lax.axis_size(axis)
     masks = [1 << bit for bit in range((count - 1).bit_length())]
     uppers, lowers = {0: first_wave[0]}, {0: first_wave[1]}
@@ -34,11 +34,8 @@
         if offset in uppers:
             continue
         bits = [mask for mask in masks if offset & mask]
-        upper, lower, _ = lax.optimization_barrier(
-            (uppers[offset ^ bits[-1]], lowers[offset ^ bits[0]], before_passing_on)
-        )
-        uppers[offset] = swapped(upper, axis, bits[-1])
-        lowers[offset] = swapped(lower, axis, bits[0])
+        uppers[offset] = swapped(uppers[offset ^ bits[-1]], axis, bits[-1])
+        lowers[offset] = swapped(lowers[offset ^ bits[0]], axis, bits[0])
     return [(uppers[offset], lowers[offset]) for offset in range(count)]
 
 
@@ -72,8 +69,7 @@
     )(which, value)
 
 
-def turned_kernel(which_ref, hidden_ref, partner_ref, *refs):
-    out_ref = refs[-1]
+def turned_kernel(which_ref, hidden_ref, partner_ref, out_ref):
     rows, width = partner_ref.shape
     block = 256
     for i in range(width // block):
@@ -84,23 +80,23 @@
         out_ref[part, rows:] = partner_ref[:, part].T
 
 
-def turned(which, hidden, partner_half, after):
+def turned(which, hidden, partner_half):
     rows, width = partner_half.shape
     return pl.pallas_call(
         turned_kernel,
         out_shape=jax.ShapeDtypeStruct((width, 2 * rows), BF16),
-        in_specs=[SMEM] + [VMEM] * 2 + [ANY] * len(after),
+        in_specs=[SMEM] + [VMEM] * 2,
         out_specs=VMEM,
         compiler_params=PARAMS,
         cost_estimate=pl.CostEstimate(
             flops=0, bytes_accessed=8 * rows * width, transcendentals=0
         ),
         name="turned_rows",
-    )(which, hidden, partner_half, *after)
-
-
-def partial_kernel(turned_ref, *refs):
-    heads, (mine_ref, theirs_ref) = refs[:-2], refs[-2:]
+    )(which, hidden, partner_half)
+
+
+def partial_kernel(facts, turned_ref, *refs):
+    heads, (mine_ref, theirs_ref) = refs[facts:-2], refs[-2:]
     shard_rows, depth = heads[0].shape
     rows = mine_ref.shape[1]
     for i in range(len(heads) // 2):
@@ -108,16 +104,21 @@
         total += jnp.dot(heads[2 * i + 1][...], turned_ref[depth:, :], preferred_element_type=F32)
         mine_ref[i * shard_rows : (i + 1) * shard_rows, :] = total[:, :rows]
         theirs_ref[i * shard_rows : (i + 1) * shard_rows, :] = total[:, rows:]
-
-
-def partial_scores(turned_rows, heads):
+    if facts:
+        theirs_ref[mine_ref.shape[0] :, :] = refs[0][...]
+
+
+def partial_scores(turned_rows, heads, facts=()):
     width, rows = turned_rows.shape
     columns = sum(head.shape[0] for head in heads) // 2
-    out = jax.ShapeDtypeStruct((columns, rows // 2), F32)
-    return pl.pallas_call(
-        partial_kernel,
-        out_shape=[out, out],
-        in_specs=[VMEM] * (1 + len(heads)),
+    below = sum(fact.shape[0] for fact in facts)
+    return pl.pallas_call(
+        functools.partial(partial_kernel, len(facts)),
+        out_shape=[
+            jax.ShapeDtypeStruct((columns, rows // 2), F32),
+            jax.ShapeDtypeStruct((columns + below, rows // 2), F32),
+        ],
+        in_specs=[VMEM] * (1 + len(facts) + len(heads)),
         out_specs=[VMEM, VMEM],
         compiler_params=PARAMS,
         cost_estimate=pl.CostEstimate(
@@ -126,44 +127,36 @@
             transcendentals=0,
         ),
         name="partial_scores",
-    )(turned_rows, *heads)
-
-
-def advantage_kernel(own_ref, *refs):
-    near, out_ref = refs[:-1], refs[-1]
-    rows = own_ref.shape[1]
+    )(turned_rows, *facts, *heads)
+
+
+def advantage_of(own, outer, partner):
+    rows = own.shape[1]
     eye = lax.broadcasted_iota(jnp.int32, (rows, rows), 0) == lax.broadcasted_iota(
         jnp.int32, (rows, rows), 1
     )
-    groups = jnp.sum(jnp.where(eye, own_ref[1:2, :], 0.0), axis=1, keepdims=True)
+    groups = jnp.sum(jnp.where(eye, own[1:2, :], 0.0), axis=1, keepdims=True)
     sums, counts = jnp.zeros((rows, 1), F32), jnp.zeros((rows, 1), F32)
-    for ref in (own_ref, *near):
-        member = ref[1:2, :] == groups
-        sums += jnp.sum(jnp.where(member, ref[0:1, :], 0.0), axis=1, keepdims=True)
+    for facts in (own, outer, partner):
+        member = facts[1:2, :] == groups
+        sums += jnp.sum(jnp.where(member, facts[0:1, :], 0.0), axis=1, keepdims=True)
         counts += jnp.sum(jnp.where(member, 1.0, 0.0), axis=1, keepdims=True)
-    means = jnp.sum(jnp.where(eye, sums / counts, 0.0), axis=0, keepdims=True)
-    out_ref[...] = own_ref[0:1, :] - means
-
-
-def advantages(own, *near):
-    return pl.pallas_call(
-        advantage_kernel,
-        out_shape=jax.ShapeDtypeStruct((1, own.shape[1]), F32),
-        in_specs=[VMEM] * (1 + len(near)),
-        out_specs=VMEM,
-        compiler_params=PARAMS,
-        name="advantage",
-    )(own, *near)
-
-
-def loss_kernel(parts, shards, shard_ref, tokens_ref, advantage_ref, *refs):
+    return own[0:1, :] - jnp.sum(jnp.where(eye, sums / counts, 0.0), axis=0, keepdims=True)
+
+
+def loss_kernel(parts, shards, shard_ref, tokens_ref, own_ref, outer_ref, *refs):
     mine, theirs = refs[:parts], refs[parts : 2 * parts]
     logits_ref, logprob_ref, entropy_ref, dlogits_ref = refs[2 * parts :]
     shard = shard_ref[0]
     rows, columns = dlogits_ref.shape
     shard_rows = columns // shards
 
-    scores = jnp.concatenate([a[...] + b[...] for a, b in zip(mine, theirs)], axis=0)
+    lengths = [ref.shape[0] for ref in mine]
+    partner = theirs[0][lengths[0] :, :]
+    advantage = advantage_of(own_ref[...], outer_ref[...], partner)
+    scores = jnp.concatenate(
+        [a[...] + b[:n, :] for a, b, n in zip(mine, theirs, lengths)], axis=0
+    )
     tokens = tokens_ref[...]
     relative = ((tokens // shard_rows) ^ shard) * shard_rows + tokens % shard_rows
     chosen = lax.broadcasted_iota(jnp.int32, (columns, rows), 0) == relative
@@ -171,7 +164,7 @@
     unnormed = jnp.exp(scores - row_max)
     denominator = jnp.sum(unnormed, axis=0, keepdims=True)
     probabilities = unnormed / denominator
-    dlogits = advantage_ref[...] * (probabilities - jnp.where(chosen, 1.0, 0.0))
+    dlogits = advantage * (probabilities - jnp.where(chosen, 1.0, 0.0))
     for i in range(shards):
         block = slice(i * shard_rows, (i + 1) * shard_rows)
         dlogits_ref[:, block] = dlogits[block, :].T.astype(BF16)
@@ -183,7 +176,7 @@
     entropy_ref[...] = log_total - jnp.sum(probabilities * scores, axis=0, keepdims=True)
 
 
-def loss(shard, tokens, advantage, mine, theirs, shards):
+def loss(shard, tokens, own, outer, mine, theirs, shards):
     rows = tokens.shape[1]
     columns = sum(part.shape[0] for part in mine)
     flat = jax.ShapeDtypeStruct((1, rows), F32)
@@ -191,7 +184,7 @@
     return pl.pallas_call(
         functools.partial(loss_kernel, len(mine), shards),
         out_shape=[wide, flat, flat, wide],
-        in_specs=[SMEM] + [VMEM] * (2 + 2 * len(mine)),
+        in_specs=[SMEM] + [VMEM] * (3 + 2 * len(mine)),
         out_specs=[VMEM] * 4,
         compiler_params=PARAMS,
         cost_estimate=pl.CostEstimate(
@@ -200,7 +193,7 @@
             transcendentals=rows * columns,
         ),
         name="loss",
-    )(shard, tokens, advantage, *mine, *theirs)
+    )(shard, tokens, own, outer, *mine, *theirs)
 
 
 def multiplied(dlogits, heads, out_ref, start):
@@ -337,29 +330,28 @@
     near = [o for o in range(shards) if bin(o).count("1") <= 1]
     far = [o for o in range(shards) if bin(o).count("1") > 1]
 
+    axes = ("vocab", "section")
+    count = lax.axis_size(axes)
+    own = jnp.stack([rewards, (group_ids + 1).astype(F32)] + [jnp.zeros_like(rewards)] * 6)
+    beside = [(i, i + 1) for i in range(1, count - 1, 2)]
+    outer = lax.ppermute(own, axes, beside + [(b, a) for a, b in beside])
+
     pieces = tuple(take(which, head_weight, 2))
-    late_hidden, pieces = lax.optimization_barrier((hidden, pieces))
+    late_hidden, pieces, outer = lax.optimization_barrier((hidden, pieces, outer))
     (other_half,) = take(1 - which, late_hidden, 1)
     other_half, late_pieces = lax.optimization_barrier((other_half, pieces))
+    heads = gathered(pieces, late_pieces, "vocab")
     partner_half = swapped(other_half, "section", 1)
 
-    own = jnp.stack([rewards, (group_ids + 1).astype(F32)])
-    axes = ("vocab", "section")
-    count = lax.axis_size(axes)
-    before = lax.ppermute(own, axes, [(i, i + 1) for i in range(count - 1)])
-    after = lax.ppermute(own, axes, [(i + 1, i) for i in range(count - 1)])
-    advantage = advantages(own, before, after)
-    heads = gathered(pieces, late_pieces, advantage, "vocab")
-
-    rows = turned(which, hidden, partner_half, (advantage,))
+    rows = turned(which, hidden, partner_half)
     mine, theirs = [], []
-    for offsets in (near, far):
-        kept, sent = partial_scores(rows, [piece for o in offsets for piece in heads[o]])
+    for offsets, facts in ((near, (own,)), (far, ())):
+        kept, sent = partial_scores(rows, [piece for o in offsets for piece in heads[o]], facts)
         mine.append(kept)
         theirs.append(swapped(sent, "section", 1))
-    mine, theirs = in_order(mine, near + far), in_order(theirs, near + far)
+    mine, theirs = in_order(mine, near + far, ()), in_order(theirs, near + far, (own.shape[0],))
     logits, logprob, entropy, dlogits = loss(
-        shard, tokens[None, :], advantage, mine, theirs, shards
+        shard, tokens[None, :], own, outer, mine, theirs, shards
     )
     pieces = [piece for pair in heads for piece in pair]
     first = first_message(dlogits, pieces[0::2])
@@ -370,13 +362,16 @@
     return (logits, logprob[0], entropy[0], previous_grad)
 
 
-def in_order(blocks, order):
+def in_order(blocks, order, below):
     if order == sorted(order):
         return blocks
-    whole = jnp.concatenate(blocks, axis=0)
+    extra = sum(below)
+    first = blocks[0]
+    kept = first.shape[0] - extra
+    whole = jnp.concatenate([first[:kept], *blocks[1:]], axis=0)
     width = whole.shape[0] // len(order)
     parts = {offset: whole[i * width : (i + 1) * width] for i, offset in enumerate(order)}
-    return [jnp.concatenate([parts[offset] for offset in sorted(order)], axis=0)]
+    return [jnp.concatenate([parts[offset] for offset in sorted(order)] + [first[kept:]], axis=0)]
 
 
 def solution(mesh):

time: 64.3 us -> 61.3 us (0.953)
  waiting for transfers between devices: 34.8 us -> 28.1 us
  starting transfers between devices: 20.1 us -> 22.1 us
  other arithmetic: 0.01 us -> 1.49 us
    ppermute x2 -> x1, waiting for transfers between devices: 8.52 us -> 0.01 us  [body(): outer = lax.ppermute(own, axes, beside + [(b, a) for a, b in beside])]
    ppermute x11, starting transfers between devices: 14.2 us -> 21.4 us  [swapped(): return lax.ppermute(value, axis, pairs)]
    ppermute x2 -> x1, starting transfers between devices: 5.84 us -> 0.65 us  [body(): outer = lax.ppermute(own, axes, beside + [(b, a) for a, b in beside])]
    ppermute x11, waiting for transfers between devices: 26.3 us -> 28.1 us  [swapped(): return lax.ppermute(value, axis, pairs)]
    another operation x2, other arithmetic: 0.01 us -> 1.49 us  [body(): jnp.stack([rewards, (group_ids + 1).astype(F32)] + [jnp.zeros_like(reward...]
    unnamed x18 -> x14, local copies, waits for them, and re-layouts: 2.89 us -> 2.77 us
  transfers between devices with their start and end apart: 13 -> 12, of which waited for: 7 -> 7; matrix products, arithmetic and copies ran while one was open for 0% -> 0% of each run, Pallas kernels for 5% -> 5%
where the time goes in v5:
time: 61.3 us; the launch traced here: 60.7 us
  waiting for transfers between devices  28.1 us (46%)
  starting transfers between devices  22.1 us (36%)
  Pallas kernels  5.39 us (9%)
  local copies, waits for them, and re-layouts  2.92 us (5%)
  other arithmetic  1.49 us (2%)
  between operations  0.77 us (1%)
    ppermute x11, waiting for transfers between devices, swapped(): return lax.ppermute(value, axis, pairs)  28.1 us
    ppermute x11, starting transfers between devices, swapped(): return lax.ppermute(value, axis, pairs)  21.4 us
    unnamed x14, local copies, waits for them, and re-layouts  2.77 us
    another operation x2, other arithmetic, body(): jnp.stack([rewards, (group_ids + 1).astype(F32)] + [jnp.zeros_like(reward...  1.49 us
    pallas_call x1, Pallas kernels, staying_gradient(): pl.pallas_call(staying_kernel, out_shape=jax.ShapeDtypeStruct((rows, 4 *...  1.27 us
  transfers between devices with their start and end apart: 12, of which 7 were waited for; matrix products, arithmetic and copies ran while one was open for 0% of the time, Pallas kernels for 5%

profile of v5, /device:TPU:0, one launch (start us, length us, event | category | flops | bytes accessed | tf_op | source)
XLA Modules:
  0.0 60.7 jit_solution(6613931503087435276)
XLA Ops:
  0.6 0.8 %convert_bitcast_fusion = f32[1,128]{1,0:T(1,128)S(1)} fusion(s32[128]{0:T(128)} %param.9), kind=kLoop, calls=%fused_computation.1 | loop fusion | flops 256 | bytes 1024 | tf_op jit(solution)/shard_map/stack | solution.py:335
  1.6 0.7 %maximum_maximum_fusion.refs_0_.own_ref = f32[8,128]{1,0:T(8,128)S(1)} fusion(f32[1,128]{1,0:T(1,128)S(1)} %convert_bitcast_fusion, f32[1,128]{1,0:T(1,128)} %bitcast.9, f32[8]{0:T(128)S(1)} %pad.3.clone, f32[8]{0:T(128)S(1)} %pad.2.clone), kind=kLoop, calls=%fused_computation | loop fusion | flops 3072 | bytes 5184 | tf_op jit(solution)/shard_map/stack | solution.py:335
  2.3 0.6 %collective-permute-start = (f32[8,128]{1,0:T(8,128)S(1)}, f32[8,128]{1,0:T(8,128)S(1)}, u32[]{:S(2)}, u32[]{:S(2)}) collective-permute-start(f32[8,128]{1,0:T(8,128)S(1)} %maximum_maximum_fusion.refs_0_.own_ref), channel_id=1, source_target_pairs={{1,2},{3,4},{5,6},{7,8},{9,10},{11,12},{13,14},{2,1},{4,3},{6,5},{... | collective-permute-start | bytes 12296 | tf_op jit(solution)/shard_map/ppermute | solution.py:337
  3.0 1.3 %copy-done.5 = bf16[128,5120]{1,0:T(8,128)(2,1)S(1)} copy-done((bf16[128,5120]{1,0:T(8,128)(2,1)S(1)}, bf16[128,5120]{1,0:T(8,128)(2,1)}, u32[]{:S(2)}) %copy-start.5) | copy-done | bytes 1310744
  4.5 6.5 %collective-permute-start.1 = (bf16[128,2560]{1,0:T(8,128)(2,1)S(1)}, bf16[128,2560]{1,0:T(8,128)(2,1)S(1)}, u32[]{:S(2)}, u32[]{:S(2)}) collective-permute-start(bf16[128,2560]{1,0:T(8,128)(2,1)S(1)} %take_half.3), channel_id=1, source_target_pairs={{0,1},{1,0},{2,3},{3,2},{4,5},{5,4},{6,7},{7,6},{8,9},{9,8},{10,11... | collective-permute-start | bytes 1966088 | tf_op jit(solution)/shard_map/ppermute | solution.py:20
  10.9 2.8 %collective-permute-start.2 = (bf16[128,1280]{1,0:T(8,128)(2,1)S(1)}, bf16[128,1280]{1,0:T(8,128)(2,1)S(1)}, u32[]{:S(2)}, u32[]{:S(2)}) collective-permute-start(bf16[128,1280]{1,0:T(8,128)(2,1)S(1)} %get-tuple-element.29.refs_1_.refs_0_), channel_id=1, source_target_pairs={{0,4},{4,0},{8,12},{12,8},{1,5},{5,1},{9,13},{13,9},{2,6},{6,2},{1... | collective-permute-start | bytes 983048 | tf_op jit(solution)/shard_map/ppermute | solution.py:20
  13.7 1.4 %collective-permute-start.5 = (bf16[128,1280]{1,0:T(8,128)(2,1)S(1)}, bf16[128,1280]{1,0:T(8,128)(2,1)S(1)}, u32[]{:S(2)}, u32[]{:S(2)}) collective-permute-start(bf16[128,1280]{1,0:T(8,128)(2,1)S(1)} %get-tuple-element.28.refs_2_.refs_0_.refs_1_), channel_id=1, source_target_pairs={{0,8},{4,12},{8,0},{12,4},{1,9},{5,13},{9,1},{13,5},{2,10},{6,14},... | collective-permute-start | bytes 983048 | tf_op jit(solution)/shard_map/ppermute | solution.py:20
  15.2 1.4 %collective-permute-start.3 = (bf16[128,1280]{1,0:T(8,128)(2,1)S(1)}, bf16[128,1280]{1,0:T(8,128)(2,1)S(1)}, u32[]{:S(2)}, u32[]{:S(2)}) collective-permute-start(bf16[128,1280]{1,0:T(8,128)(2,1)S(1)} %get-tuple-element.28.refs_2_.refs_0_.refs_1_), channel_id=1, source_target_pairs={{0,4},{4,0},{8,12},{12,8},{1,5},{5,1},{9,13},{13,9},{2,6},{6,2},{1... | collective-permute-start | bytes 983048 | tf_op jit(solution)/shard_map/ppermute | solution.py:20
  16.6 5.8 %collective-permute-done.2.refs_3_.refs_1_.refs_2_ = bf16[128,1280]{1,0:T(8,128)(2,1)S(1)} collective-permute-done((bf16[128,1280]{1,0:T(8,128)(2,1)S(1)}, bf16[128,1280]{1,0:T(8,128)(2,1)S(1)}, u32[]{:S(2)}, u32[]{:S(2)}) %collective-permute-start.2) | collective-permute-done | bytes 327712 | tf_op jit(solution)/shard_map/ppermute | solution.py:20
  22.4 2.8 %collective-permute-start.6 = (bf16[128,1280]{1,0:T(8,128)(2,1)S(1)}, bf16[128,1280]{1,0:T(8,128)(2,1)S(1)}, u32[]{:S(2)}, u32[]{:S(2)}) collective-permute-start(bf16[128,1280]{1,0:T(8,128)(2,1)S(1)} %collective-permute-done.2.refs_3_.refs_1_.refs_2_), channel_id=1, source_target_pairs={{0,8},{4,12},{8,0},{12,4},{1,9},{5,13},{9,1},{13,5},{2,10},{6,14},... | collective-permute-start | bytes 983048 | tf_op jit(solution)/shard_map/ppermute | solution.py:20
  26.2 3.2 %collective-permute-done.3.refs_4_.refs_1_.refs_3_ = bf16[128,1280]{1,0:T(8,128)(2,1)S(1)} collective-permute-done((bf16[128,1280]{1,0:T(8,128)(2,1)S(1)}, bf16[128,1280]{1,0:T(8,128)(2,1)S(1)}, u32[]{:S(2)}, u32[]{:S(2)}) %collective-permute-start.3) | collective-permute-done | bytes 327712 | tf_op jit(solution)/shard_map/ppermute | solution.py:20
  29.4 2.0 %collective-permute-done.4.refs_5_.refs_2_.refs_4_ = bf16[128,1280]{1,0:T(8,128)(2,1)S(1)} collective-permute-done((bf16[128,1280]{1,0:T(8,128)(2,1)S(1)}, bf16[128,1280]{1,0:T(8,128)(2,1)S(1)}, u32[]{:S(2)}, u32[]{:S(2)}) %collective-permute-start.4) | collective-permute-done | bytes 327712 | tf_op jit(solution)/shard_map/ppermute | solution.py:20
  31.4 0.7 %partial_scores.2 = (f32[384,128]{1,0:T(8,128)S(1)}, f32[392,128]{1,0:T(8,128)S(1)}) custom-call(bf16[2560,256]{1,0:T(8,128)(2,1)S(1)} %turned_rows.1.turned_ref, f32[8,128]{1,0:T(8,128)S(1)} %maximum_maximum_fusion.refs_0_.own_ref, bf16[128,1280]{1,0:T(8,128)(2,1)S(1)} %get-tuple-element.29.refs_1_.refs_0_, ...), custom_call_target="tpu_custom_call" | custom-call | flops 503316480 | bytes 3276800 | tf_op jit(solution)/shard_map/partial_scores/pallas_call | solution.py:115
  32.1 2.0 %collective-permute-start.8 = (f32[392,128]{1,0:T(8,128)S(1)}, f32[392,128]{1,0:T(8,128)S(1)}, u32[]{:S(2)}, u32[]{:S(2)}) collective-permute-start(f32[392,128]{1,0:T(8,128)S(1)} %get-tuple-element.32), channel_id=1, source_target_pairs={{0,1},{1,0},{2,3},{3,2},{4,5},{5,4},{6,7},{7,6},{8,9},{9,8},{10,11... | collective-permute-start | bytes 602120 | tf_op jit(solution)/shard_map/ppermute | solution.py:20
  34.1 1.6 %collective-permute-done.6.refs_0_.refs_3_.refs_6_ = bf16[128,1280]{1,0:T(8,128)(2,1)S(1)} collective-permute-done((bf16[128,1280]{1,0:T(8,128)(2,1)S(1)}, bf16[128,1280]{1,0:T(8,128)(2,1)S(1)}, u32[]{:S(2)}, u32[]{:S(2)}) %collective-permute-start.6) | collective-permute-done | bytes 327712 | tf_op jit(solution)/shard_map/ppermute | solution.py:20
  36.5 1.7 %collective-permute-start.9 = (f32[128,128]{1,0:T(8,128)S(1)}, f32[128,128]{1,0:T(8,128)S(1)}, u32[]{:S(2)}, u32[]{:S(2)}) collective-permute-start(f32[128,128]{1,0:T(8,128)S(1)} %get-tuple-element.33), channel_id=1, source_target_pairs={{0,1},{1,0},{2,3},{3,2},{4,5},{5,4},{6,7},{7,6},{8,9},{9,8},{10,11... | collective-permute-start | bytes 196616 | tf_op jit(solution)/shard_map/ppermute | solution.py:20
  38.2 2.6 %collective-permute-done.9.refs_3_ = f32[128,128]{1,0:T(8,128)S(1)} collective-permute-done((f32[128,128]{1,0:T(8,128)S(1)}, f32[128,128]{1,0:T(8,128)S(1)}, u32[]{:S(2)}, u32[]{:S(2)}) %collective-permute-start.9) | collective-permute-done | bytes 65568 | tf_op jit(solution)/shard_map/ppermute | solution.py:20
  40.8 1.1 %loss.1 = (bf16[128,512]{1,0:T(8,128)(2,1)}, f32[1,128]{1,0:T(1,128)}, f32[1,128]{1,0:T(1,128)}, bf16[128,512]{1,0:T(8,128)(2,1)S(1)}) custom-call(s32[1]{0:T(128)} %bitcast.shard_ref, s32[1,128]{1,0:T(1,128)S(1)} %bitcast.8, f32[8,128]{1,0:T(8,128)S(1)} %maximum_maximum_fusion.refs_0_.own_ref, f32[8,128]{1,0:T(8,128)S(1)} %collective-permute-done.outer_ref, ...), custom_call_target="tpu_custom_call" | custom-call | flops 655360 | bytes 786432 | tf_op jit(solution)/shard_map/loss/pallas_call | solution.py:184
  41.9 1.0 %copy-done.4 = bf16[128,1280]{1,0:T(8,128)(2,1)S(1)} copy-done((bf16[128,1280]{1,0:T(8,128)(2,1)S(1)}, bf16[128,1280]{1,0:T(8,128)(2,1)}, u32[]{:S(2)}) %copy-start.4) | copy-done | bytes 327704
  43.2 1.7 %collective-permute-start.11 = (bf16[128,1792]{1,0:T(8,128)(2,1)S(1)}, bf16[128,1792]{1,0:T(8,128)(2,1)S(1)}, u32[]{:S(2)}, u32[]{:S(2)}) collective-permute-start(bf16[128,1792]{1,0:T(8,128)(2,1)S(1)} %first_message.1._), channel_id=1, source_target_pairs={{0,1},{1,0},{2,3},{3,2},{4,5},{5,4},{6,7},{7,6},{8,9},{9,8},{10,11... | collective-permute-start | bytes 1376264 | tf_op jit(solution)/shard_map/ppermute | solution.py:20
  45.7 10.7 %collective-permute-done.11.first_ref = bf16[128,1792]{1,0:T(8,128)(2,1)S(1)} collective-permute-done((bf16[128,1792]{1,0:T(8,128)(2,1)S(1)}, bf16[128,1792]{1,0:T(8,128)(2,1)S(1)}, u32[]{:S(2)}, u32[]{:S(2)}) %collective-permute-start.11) | collective-permute-done | bytes 458784 | tf_op jit(solution)/shard_map/ppermute | solution.py:20
  56.4 1.3 %staying_gradient.1._ = bf16[128,5120]{1,0:T(8,128)(2,1)} custom-call(s32[1]{0:T(128)} %bitcast.4.which_ref, bf16[128,1792]{1,0:T(8,128)(2,1)S(1)} %collective-permute-done.11.first_ref, bf16[128,1280]{1,0:T(8,128)(2,1)S(1)} %get-tuple-element.29.refs_1_.refs_0_, bf16[128,1280]{1,0:T(8,128)(2,1)S(1)} %get-tuple-element.28.refs_2_.refs_0_.refs_1_, ...), custom_call_target="tpu_custom_call" | custom-call | flops 335544320 | bytes 3276800 | tf_op jit(solution)/shard_map/staying_gradient/pallas_call | solution.py:287
  57.7 2.2 %collective-permute-done.10.second_ref = bf16[128,1280]{1,0:T(8,128)(2,1)S(1)} collective-permute-done((bf16[128,1280]{1,0:T(8,128)(2,1)S(1)}, bf16[128,1280]{1,0:T(8,128)(2,1)S(1)}, u32[]{:S(2)}, u32[]{:S(2)}) %collective-permute-start.10) | collective-permute-done | bytes 327712 | tf_op jit(solution)/shard_map/ppermute | solution.py:20
  59.9 0.8 %place_second.1 = bf16[128,5120]{1,0:T(8,128)(2,1)} custom-call(s32[1]{0:T(128)} %bitcast.4.which_ref, bf16[128,1280]{1,0:T(8,128)(2,1)S(1)} %collective-permute-done.10.second_ref, bf16[128,5120]{1,0:T(8,128)(2,1)} %staying_gradient.1._), custom_call_target="tpu_custom_call", output_to_operand_aliasing={{}: (2, {})} | custom-call | tf_op jit(solution)/shard_map/place_second/pallas_call | solution.py:314
  (30 shorter events, 3.3 us)
Async XLA Ops:
  0.6 3.7 %copy-start = (bf16[128,5120]{1,0:T(8,128)(2,1)S(1)}, bf16[128,5120]{1,0:T(8,128)(2,1)}, u32[]{:S(2)}) copy-start(bf16[128,5120]{1,0:T(8,128)(2,1)} %hidden_ref.1) | copy-start | bytes 3932164
  2.3 2.1 %collective-permute-start = (f32[8,128]{1,0:T(8,128)S(1)}, f32[8,128]{1,0:T(8,128)S(1)}, u32[]{:S(2)}, u32[]{:S(2)}) collective-permute-start(f32[8,128]{1,0:T(8,128)S(1)} %maximum_maximum_fusion.refs_0_.own_ref), channel_id=1, source_target_pairs={{1,2},{3,4},{5,6},{7,8},{9,10},{11,12},{13,14},{2,1},{4,3},{6,5},{... | collective-permute-start | bytes 12296 | tf_op jit(solution)/shard_map/ppermute | solution.py:337
  3.0 1.3 %copy-start.5 = (bf16[128,5120]{1,0:T(8,128)(2,1)S(1)}, bf16[128,5120]{1,0:T(8,128)(2,1)}, u32[]{:S(2)}) copy-start(bf16[128,5120]{1,0:T(8,128)(2,1)} %value_ref.1) | copy-start | bytes 3932164
  4.5 21.3 %collective-permute-start.1 = (bf16[128,2560]{1,0:T(8,128)(2,1)S(1)}, bf16[128,2560]{1,0:T(8,128)(2,1)S(1)}, u32[]{:S(2)}, u32[]{:S(2)}) collective-permute-start(bf16[128,2560]{1,0:T(8,128)(2,1)S(1)} %take_half.3), channel_id=1, source_target_pairs={{0,1},{1,0},{2,3},{3,2},{4,5},{5,4},{6,7},{7,6},{8,9},{9,8},{10,11... | collective-permute-start | bytes 1966088 | tf_op jit(solution)/shard_map/ppermute | solution.py:20
  10.9 11.4 %collective-permute-start.2 = (bf16[128,1280]{1,0:T(8,128)(2,1)S(1)}, bf16[128,1280]{1,0:T(8,128)(2,1)S(1)}, u32[]{:S(2)}, u32[]{:S(2)}) collective-permute-start(bf16[128,1280]{1,0:T(8,128)(2,1)S(1)} %get-tuple-element.29.refs_1_.refs_0_), channel_id=1, source_target_pairs={{0,4},{4,0},{8,12},{12,8},{1,5},{5,1},{9,13},{13,9},{2,6},{6,2},{1... | collective-permute-start | bytes 983048 | tf_op jit(solution)/shard_map/ppermute | solution.py:20
  13.7 11.5 %collective-permute-start.5 = (bf16[128,1280]{1,0:T(8,128)(2,1)S(1)}, bf16[128,1280]{1,0:T(8,128)(2,1)S(1)}, u32[]{:S(2)}, u32[]{:S(2)}) collective-permute-start(bf16[128,1280]{1,0:T(8,128)(2,1)S(1)} %get-tuple-element.28.refs_2_.refs_0_.refs_1_), channel_id=1, source_target_pairs={{0,8},{4,12},{8,0},{12,4},{1,9},{5,13},{9,1},{13,5},{2,10},{6,14},... | collective-permute-start | bytes 983048 | tf_op jit(solution)/shard_map/ppermute | solution.py:20
  15.2 14.2 %collective-permute-start.3 = (bf16[128,1280]{1,0:T(8,128)(2,1)S(1)}, bf16[128,1280]{1,0:T(8,128)(2,1)S(1)}, u32[]{:S(2)}, u32[]{:S(2)}) collective-permute-start(bf16[128,1280]{1,0:T(8,128)(2,1)S(1)} %get-tuple-element.28.refs_2_.refs_0_.refs_1_), channel_id=1, source_target_pairs={{0,4},{4,0},{8,12},{12,8},{1,5},{5,1},{9,13},{13,9},{2,6},{6,2},{1... | collective-permute-start | bytes 983048 | tf_op jit(solution)/shard_map/ppermute | solution.py:20
  16.6 14.8 %collective-permute-start.4 = (bf16[128,1280]{1,0:T(8,128)(2,1)S(1)}, bf16[128,1280]{1,0:T(8,128)(2,1)S(1)}, u32[]{:S(2)}, u32[]{:S(2)}) collective-permute-start(bf16[128,1280]{1,0:T(8,128)(2,1)S(1)} %get-tuple-element.29.refs_1_.refs_0_), channel_id=1, source_target_pairs={{0,8},{4,12},{8,0},{12,4},{1,9},{5,13},{9,1},{13,5},{2,10},{6,14},... | collective-permute-start | bytes 983048 | tf_op jit(solution)/shard_map/ppermute | solution.py:20
  22.4 13.3 %collective-permute-start.6 = (bf16[128,1280]{1,0:T(8,128)(2,1)S(1)}, bf16[128,1280]{1,0:T(8,128)(2,1)S(1)}, u32[]{:S(2)}, u32[]{:S(2)}) collective-permute-start(bf16[128,1280]{1,0:T(8,128)(2,1)S(1)} %collective-permute-done.2.refs_3_.refs_1_.refs_2_), channel_id=1, source_target_pairs={{0,8},{4,12},{8,0},{12,4},{1,9},{5,13},{9,1},{13,5},{2,10},{6,14},... | collective-permute-start | bytes 983048 | tf_op jit(solution)/shard_map/ppermute | solution.py:20
  25.2 10.5 %collective-permute-start.7 = (bf16[128,1280]{1,0:T(8,128)(2,1)S(1)}, bf16[128,1280]{1,0:T(8,128)(2,1)S(1)}, u32[]{:S(2)}, u32[]{:S(2)}) collective-permute-start(bf16[128,1280]{1,0:T(8,128)(2,1)S(1)} %collective-permute-done.5.refs_6_.refs_2_.refs_5_), channel_id=1, source_target_pairs={{0,4},{4,0},{8,12},{12,8},{1,5},{5,1},{9,13},{13,9},{2,6},{6,2},{1... | collective-permute-start | bytes 983048 | tf_op jit(solution)/shard_map/ppermute | solution.py:20
  32.1 8.7 %copy-start.6 = (s32[128]{0:T(128)S(1)}, s32[128]{0:T(128)}, u32[]{:S(2)}) copy-start(s32[128]{0:T(128)} %param.7) | copy-start | bytes 1540
  32.1 8.7 %collective-permute-start.8 = (f32[392,128]{1,0:T(8,128)S(1)}, f32[392,128]{1,0:T(8,128)S(1)}, u32[]{:S(2)}, u32[]{:S(2)}) collective-permute-start(f32[392,128]{1,0:T(8,128)S(1)} %get-tuple-element.32), channel_id=1, source_target_pairs={{0,1},{1,0},{2,3},{3,2},{4,5},{5,4},{6,7},{7,6},{8,9},{9,8},{10,11... | collective-permute-start | bytes 602120 | tf_op jit(solution)/shard_map/ppermute | solution.py:20
  35.7 0.8 %copy-start.3 = (bf16[128,1280]{1,0:T(8,128)(2,1)}, bf16[128,1280]{1,0:T(8,128)(2,1)S(1)}, u32[]{:S(2)}) copy-start(bf16[128,1280]{1,0:T(8,128)(2,1)S(1)} %collective-permute-done.6.refs_0_.refs_3_.refs_6_) | copy-start | bytes 983044
  35.7 0.8 %copy-start.1 = (bf16[128,1280]{1,0:T(8,128)(2,1)}, bf16[128,1280]{1,0:T(8,128)(2,1)S(1)}, u32[]{:S(2)}) copy-start(bf16[128,1280]{1,0:T(8,128)(2,1)S(1)} %collective-permute-done.7.refs_1_.refs_3_.refs_7_) | copy-start | bytes 983044
  36.5 8.4 %copy-start.2 = (bf16[128,1280]{1,0:T(8,128)(2,1)S(1)}, bf16[128,1280]{1,0:T(8,128)(2,1)}, u32[]{:S(2)}) copy-start(bf16[128,1280]{1,0:T(8,128)(2,1)} %copy-done.1) | copy-start | bytes 983044
  36.5 4.3 %collective-permute-start.9 = (f32[128,128]{1,0:T(8,128)S(1)}, f32[128,128]{1,0:T(8,128)S(1)}, u32[]{:S(2)}, u32[]{:S(2)}) collective-permute-start(f32[128,128]{1,0:T(8,128)S(1)} %get-tuple-element.33), channel_id=1, source_target_pairs={{0,1},{1,0},{2,3},{3,2},{4,5},{5,4},{6,7},{7,6},{8,9},{9,8},{10,11... | collective-permute-start | bytes 196616 | tf_op jit(solution)/shard_map/ppermute | solution.py:20
  41.9 1.0 %copy-start.4 = (bf16[128,1280]{1,0:T(8,128)(2,1)S(1)}, bf16[128,1280]{1,0:T(8,128)(2,1)}, u32[]{:S(2)}) copy-start(bf16[128,1280]{1,0:T(8,128)(2,1)} %copy-done.3) | copy-start | bytes 983044
  43.2 13.2 %collective-permute-start.11 = (bf16[128,1792]{1,0:T(8,128)(2,1)S(1)}, bf16[128,1792]{1,0:T(8,128)(2,1)S(1)}, u32[]{:S(2)}, u32[]{:S(2)}) collective-permute-start(bf16[128,1792]{1,0:T(8,128)(2,1)S(1)} %first_message.1._), channel_id=1, source_target_pairs={{0,1},{1,0},{2,3},{3,2},{4,5},{5,4},{6,7},{7,6},{8,9},{9,8},{10,11... | collective-permute-start | bytes 1376264 | tf_op jit(solution)/shard_map/ppermute | solution.py:20
  45.3 14.6 %collective-permute-start.10 = (bf16[128,1280]{1,0:T(8,128)(2,1)S(1)}, bf16[128,1280]{1,0:T(8,128)(2,1)S(1)}, u32[]{:S(2)}, u32[]{:S(2)}) collective-permute-start(bf16[128,1280]{1,0:T(8,128)(2,1)S(1)} %second_message.1), channel_id=1, source_target_pairs={{0,1},{1,0},{2,3},{3,2},{4,5},{5,4},{6,7},{7,6},{8,9},{9,8},{10,11... | collective-permute-start | bytes 983048 | tf_op jit(solution)/shard_map/ppermute | solution.py:20

commit v6 on v5

--- a/solution.py
+++ b/solution.py
@@ -12,7 +12,8 @@
 ANY = pl.BlockSpec(memory_space=pl.ANY)
 SMEM = pl.BlockSpec(memory_space=pltpu.SMEM)
 VMEM = pl.BlockSpec(memory_space=pltpu.VMEM)
-PARAMS = pltpu.CompilerParams(vmem_limit_bytes=16 * 1024 * 1024)
+PARAMS = pltpu.CompilerParams(vmem_limit_bytes=4 * 1024 * 1024)
+BELOW = 8
 
 
 def swapped(value, axis, mask):
@@ -105,13 +106,15 @@
         mine_ref[i * shard_rows : (i + 1) * shard_rows, :] = total[:, :rows]
         theirs_ref[i * shard_rows : (i + 1) * shard_rows, :] = total[:, rows:]
     if facts:
-        theirs_ref[mine_ref.shape[0] :, :] = refs[0][...]
+        below = theirs_ref.shape[0] - mine_ref.shape[0]
+        theirs_ref[mine_ref.shape[0] :, :] = jnp.zeros((below, rows), F32)
+        theirs_ref[pl.ds(mine_ref.shape[0], refs[0].shape[0]), :] = refs[0][...]
 
 
 def partial_scores(turned_rows, heads, facts=()):
     width, rows = turned_rows.shape
     columns = sum(head.shape[0] for head in heads) // 2
-    below = sum(fact.shape[0] for fact in facts)
+    below = BELOW * len(facts)
     return pl.pallas_call(
         functools.partial(partial_kernel, len(facts)),
         out_shape=[
@@ -186,7 +189,7 @@
         out_shape=[wide, flat, flat, wide],
         in_specs=[SMEM] + [VMEM] * (3 + 2 * len(mine)),
         out_specs=[VMEM] * 4,
-        compiler_params=PARAMS,
+        compiler_params=pltpu.CompilerParams(vmem_limit_bytes=2 * 1024**2 + 32 * rows * columns),
         cost_estimate=pl.CostEstimate(
             flops=10 * rows * columns,
             bytes_accessed=12 * rows * columns,
@@ -332,12 +335,12 @@
 
     axes = ("vocab", "section")
     count = lax.axis_size(axes)
-    own = jnp.stack([rewards, (group_ids + 1).astype(F32)] + [jnp.zeros_like(rewards)] * 6)
+    own = jnp.stack([rewards, (group_ids + 1).astype(F32)])
     beside = [(i, i + 1) for i in range(1, count - 1, 2)]
     outer = lax.ppermute(own, axes, beside + [(b, a) for a, b in beside])
 
     pieces = tuple(take(which, head_weight, 2))
-    late_hidden, pieces, outer = lax.optimization_barrier((hidden, pieces, outer))
+    late_hidden, _ = lax.optimization_barrier((hidden, pieces))
     (other_half,) = take(1 - which, late_hidden, 1)
     other_half, late_pieces = lax.optimization_barrier((other_half, pieces))
     heads = gathered(pieces, late_pieces, "vocab")
@@ -346,10 +349,12 @@
     rows = turned(which, hidden, partner_half)
     mine, theirs = [], []
     for offsets, facts in ((near, (own,)), (far, ())):
+        if not facts:
+            rows, outer = lax.optimization_barrier((rows, outer))
         kept, sent = partial_scores(rows, [piece for o in offsets for piece in heads[o]], facts)
         mine.append(kept)
         theirs.append(swapped(sent, "section", 1))
-    mine, theirs = in_order(mine, near + far, ()), in_order(theirs, near + far, (own.shape[0],))
+    mine, theirs = in_order(mine, near + far, 0), in_order(theirs, near + far, BELOW)
     logits, logprob, entropy, dlogits = loss(
         shard, tokens[None, :], own, outer, mine, theirs, shards
     )
@@ -365,9 +370,8 @@
 def in_order(blocks, order, below):
     if order == sorted(order):
         return blocks
-    extra = sum(below)
     first = blocks[0]
-    kept = first.shape[0] - extra
+    kept = first.shape[0] - below
     whole = jnp.concatenate([first[:kept], *blocks[1:]], axis=0)
     width = whole.shape[0] // len(order)
     parts = {offset: whole[i * width : (i + 1) * width] for i, offset in enumerate(order)}

time: 61.3 us -> 55.9 us (0.912)
  the two profiles are of different devices: /device:TPU:0 before, /device:TPU:4 now
where the time goes in v6:
time: 55.9 us; the launch traced here: 55.7 us
  waiting for transfers between devices  31.9 us (57%)
  starting transfers between devices  14.7 us (26%)
  Pallas kernels  5.38 us (10%)
  local copies, waits for them, and re-layouts  2.87 us (5%)
  between operations  0.81 us (1%)
    ppermute x11, waiting for transfers between devices, swapped(): return lax.ppermute(value, axis, pairs)  27.5 us
    ppermute x11, starting transfers between devices, swapped(): return lax.ppermute(value, axis, pairs)  10.1 us
    ppermute x1, starting transfers between devices, body(): outer = lax.ppermute(own, axes, beside + [(b, a) for a, b in beside])  4.63 us
    ppermute x1, waiting for transfers between devices, body(): outer = lax.ppermute(own, axes, beside + [(b, a) for a, b in beside])  4.42 us
    unnamed x18, local copies, waits for them, and re-layouts  2.87 us
    pallas_call x1, Pallas kernels, staying_gradient(): pl.pallas_call(staying_kernel, out_shape=jax.ShapeDtypeStruct((rows, 4 *...  1.27 us
  transfers between devices with their start and end apart: 12, of which 8 were waited for; matrix products, arithmetic and copies ran while one was open for 0% of the time, Pallas kernels for 6%

profile of v6, /device:TPU:4, one launch (start us, length us, event | category | flops | bytes accessed | tf_op | source)
XLA Modules:
  0.0 55.7 jit_solution(1897988530294525992)
XLA Ops:
  0.7 1.4 %copy-done.5 = bf16[128,5120]{1,0:T(8,128)(2,1)S(1)} copy-done((bf16[128,5120]{1,0:T(8,128)(2,1)S(1)}, bf16[128,5120]{1,0:T(8,128)(2,1)}, u32[]{:S(2)}) %copy-start.5) | copy-done | bytes 1310744
  2.2 1.6 %collective-permute-start.2 = (bf16[128,1280]{1,0:T(8,128)(2,1)S(1)}, bf16[128,1280]{1,0:T(8,128)(2,1)S(1)}, u32[]{:S(2)}, u32[]{:S(2)}) collective-permute-start(bf16[128,1280]{1,0:T(8,128)(2,1)S(1)} %get-tuple-element.26.refs_1_.refs_0_), channel_id=1, source_target_pairs={{0,4},{4,0},{8,12},{12,8},{1,5},{5,1},{9,13},{13,9},{2,6},{6,2},{1... | collective-permute-start | bytes 983048 | tf_op jit(solution)/shard_map/ppermute | solution.py:21
  3.7 0.5 collective-permute-start.5
  4.3 1.6 %collective-permute-start = (bf16[128,2560]{1,0:T(8,128)(2,1)S(1)}, bf16[128,2560]{1,0:T(8,128)(2,1)S(1)}, u32[]{:S(2)}, u32[]{:S(2)}) collective-permute-start(bf16[128,2560]{1,0:T(8,128)(2,1)S(1)} %take_half.3), channel_id=1, source_target_pairs={{0,1},{1,0},{2,3},{3,2},{4,5},{5,4},{6,7},{7,6},{8,9},{9,8},{10,11... | collective-permute-start | bytes 1966088 | tf_op jit(solution)/shard_map/ppermute | solution.py:21
  6.0 0.5 collective-permute-start.3
  6.5 1.5 %collective-permute-start.4 = (bf16[128,1280]{1,0:T(8,128)(2,1)S(1)}, bf16[128,1280]{1,0:T(8,128)(2,1)S(1)}, u32[]{:S(2)}, u32[]{:S(2)}) collective-permute-start(bf16[128,1280]{1,0:T(8,128)(2,1)S(1)} %get-tuple-element.26.refs_1_.refs_0_), channel_id=1, source_target_pairs={{0,8},{4,12},{8,0},{12,4},{1,9},{5,13},{9,1},{13,5},{2,10},{6,14},... | collective-permute-start | bytes 983048 | tf_op jit(solution)/shard_map/ppermute | solution.py:21
  8.0 4.8 %collective-permute-done.2.refs_3_.refs_1_.refs_2_ = bf16[128,1280]{1,0:T(8,128)(2,1)S(1)} collective-permute-done((bf16[128,1280]{1,0:T(8,128)(2,1)S(1)}, bf16[128,1280]{1,0:T(8,128)(2,1)S(1)}, u32[]{:S(2)}, u32[]{:S(2)}) %collective-permute-start.2) | collective-permute-done | bytes 327712 | tf_op jit(solution)/shard_map/ppermute | solution.py:21
  12.8 1.5 %collective-permute-done.5.refs_6_.refs_2_.refs_5_ = bf16[128,1280]{1,0:T(8,128)(2,1)S(1)} collective-permute-done((bf16[128,1280]{1,0:T(8,128)(2,1)S(1)}, bf16[128,1280]{1,0:T(8,128)(2,1)S(1)}, u32[]{:S(2)}, u32[]{:S(2)}) %collective-permute-start.5) | collective-permute-done | bytes 327712 | tf_op jit(solution)/shard_map/ppermute | solution.py:21
  14.4 0.5 collective-permute-start.7
  14.9 5.4 %collective-permute-done.partner_ref = bf16[128,2560]{1,0:T(8,128)(2,1)S(1)} collective-permute-done((bf16[128,2560]{1,0:T(8,128)(2,1)S(1)}, bf16[128,2560]{1,0:T(8,128)(2,1)S(1)}, u32[]{:S(2)}, u32[]{:S(2)}) %collective-permute-start) | collective-permute-done | bytes 655392 | tf_op jit(solution)/shard_map/ppermute | solution.py:21
  20.3 0.4 turned_rows.1.turned_ref
  20.7 0.7 %collective-permute-done.4.refs_5_.refs_2_.refs_4_ = bf16[128,1280]{1,0:T(8,128)(2,1)S(1)} collective-permute-done((bf16[128,1280]{1,0:T(8,128)(2,1)S(1)}, bf16[128,1280]{1,0:T(8,128)(2,1)S(1)}, u32[]{:S(2)}, u32[]{:S(2)}) %collective-permute-start.4) | collective-permute-done | bytes 327712 | tf_op jit(solution)/shard_map/ppermute | solution.py:21
  21.4 0.7 %partial_scores.2 = (f32[384,128]{1,0:T(8,128)S(1)}, f32[392,128]{1,0:T(8,128)S(1)}) custom-call(bf16[2560,256]{1,0:T(8,128)(2,1)S(1)} %turned_rows.1.turned_ref, f32[2,128]{1,0:T(2,128)S(1)} %pad_maximum_fusion.refs_0_.own_ref, bf16[128,1280]{1,0:T(8,128)(2,1)S(1)} %get-tuple-element.26.refs_1_.refs_0_, ...), custom_call_target="tpu_custom_call" | custom-call | flops 503316480 | bytes 3276800 | tf_op jit(solution)/shard_map/partial_scores/pallas_call | solution.py:118
  22.1 1.6 %collective-permute-start.8 = (f32[392,128]{1,0:T(8,128)S(1)}, f32[392,128]{1,0:T(8,128)S(1)}, u32[]{:S(2)}, u32[]{:S(2)}) collective-permute-start(f32[392,128]{1,0:T(8,128)S(1)} %get-tuple-element.30), channel_id=1, source_target_pairs={{0,1},{1,0},{2,3},{3,2},{4,5},{5,4},{6,7},{7,6},{8,9},{9,8},{10,11... | collective-permute-start | bytes 602120 | tf_op jit(solution)/shard_map/ppermute | solution.py:21
  23.7 4.6 %collective-permute-start.1 = (f32[2,128]{1,0:T(2,128)S(1)}, f32[2,128]{1,0:T(2,128)S(1)}, u32[]{:S(2)}, u32[]{:S(2)}) collective-permute-start(f32[2,128]{1,0:T(2,128)S(1)} %pad_maximum_fusion.refs_0_.own_ref), channel_id=1, source_target_pairs={{1,2},{3,4},{5,6},{7,8},{9,10},{11,12},{13,14},{2,1},{4,3},{6,5},{... | collective-permute-start | bytes 3080 | tf_op jit(solution)/shard_map/ppermute | solution.py:340
  28.4 4.4 %collective-permute-done.1.outer_ref = f32[2,128]{1,0:T(2,128)S(1)} collective-permute-done((f32[2,128]{1,0:T(2,128)S(1)}, f32[2,128]{1,0:T(2,128)S(1)}, u32[]{:S(2)}, u32[]{:S(2)}) %collective-permute-start.1) | collective-permute-done | bytes 1056 | tf_op jit(solution)/shard_map/ppermute | solution.py:340
  33.6 4.3 %collective-permute-done.9.refs_3_ = f32[128,128]{1,0:T(8,128)S(1)} collective-permute-done((f32[128,128]{1,0:T(8,128)S(1)}, f32[128,128]{1,0:T(8,128)S(1)}, u32[]{:S(2)}, u32[]{:S(2)}) %collective-permute-start.9) | collective-permute-done | bytes 65568 | tf_op jit(solution)/shard_map/ppermute | solution.py:21
  37.9 1.1 %loss.1 = (bf16[128,512]{1,0:T(8,128)(2,1)}, f32[1,128]{1,0:T(1,128)}, f32[1,128]{1,0:T(1,128)}, bf16[128,512]{1,0:T(8,128)(2,1)S(1)}) custom-call(s32[1]{0:T(128)} %bitcast.shard_ref, s32[1,128]{1,0:T(1,128)S(1)} %bitcast.8, f32[2,128]{1,0:T(2,128)S(1)} %pad_maximum_fusion.refs_0_.own_ref, f32[2,128]{1,0:T(2,128)S(1)} %collective-permute-done.1.outer_ref, ...), custom_call_target="tpu_custom_call" | custom-call | flops 655360 | bytes 786432 | tf_op jit(solution)/shard_map/loss/pallas_call | solution.py:187
  39.0 1.0 %copy-done.4 = bf16[128,1280]{1,0:T(8,128)(2,1)S(1)} copy-done((bf16[128,1280]{1,0:T(8,128)(2,1)S(1)}, bf16[128,1280]{1,0:T(8,128)(2,1)}, u32[]{:S(2)}) %copy-start.4) | copy-done | bytes 327704
  40.8 2.1 %collective-permute-start.10 = (bf16[128,1280]{1,0:T(8,128)(2,1)S(1)}, bf16[128,1280]{1,0:T(8,128)(2,1)S(1)}, u32[]{:S(2)}, u32[]{:S(2)}) collective-permute-start(bf16[128,1280]{1,0:T(8,128)(2,1)S(1)} %second_message.1), channel_id=1, source_target_pairs={{0,1},{1,0},{2,3},{3,2},{4,5},{5,4},{6,7},{7,6},{8,9},{9,8},{10,11... | collective-permute-start | bytes 983048 | tf_op jit(solution)/shard_map/ppermute | solution.py:21
  42.8 8.6 %collective-permute-done.11.first_ref = bf16[128,1792]{1,0:T(8,128)(2,1)S(1)} collective-permute-done((bf16[128,1792]{1,0:T(8,128)(2,1)S(1)}, bf16[128,1792]{1,0:T(8,128)(2,1)S(1)}, u32[]{:S(2)}, u32[]{:S(2)}) %collective-permute-start.11) | collective-permute-done | bytes 458784 | tf_op jit(solution)/shard_map/ppermute | solution.py:21
  51.5 1.3 %staying_gradient.1._ = bf16[128,5120]{1,0:T(8,128)(2,1)} custom-call(s32[1]{0:T(128)} %bitcast.4.which_ref, bf16[128,1792]{1,0:T(8,128)(2,1)S(1)} %collective-permute-done.11.first_ref, bf16[128,1280]{1,0:T(8,128)(2,1)S(1)} %get-tuple-element.26.refs_1_.refs_0_, bf16[128,1280]{1,0:T(8,128)(2,1)S(1)} %get-tuple-element.25.refs_2_.refs_0_.refs_1_, ...), custom_call_target="tpu_custom_call" | custom-call | flops 335544320 | bytes 3276800 | tf_op jit(solution)/shard_map/staying_gradient/pallas_call | solution.py:290
  52.7 2.2 %collective-permute-done.10.second_ref = bf16[128,1280]{1,0:T(8,128)(2,1)S(1)} collective-permute-done((bf16[128,1280]{1,0:T(8,128)(2,1)S(1)}, bf16[128,1280]{1,0:T(8,128)(2,1)S(1)}, u32[]{:S(2)}, u32[]{:S(2)}) %collective-permute-start.10) | collective-permute-done | bytes 327712 | tf_op jit(solution)/shard_map/ppermute | solution.py:21
  55.0 0.8 %place_second.1 = bf16[128,5120]{1,0:T(8,128)(2,1)} custom-call(s32[1]{0:T(128)} %bitcast.4.which_ref, bf16[128,1280]{1,0:T(8,128)(2,1)S(1)} %collective-permute-done.10.second_ref, bf16[128,5120]{1,0:T(8,128)(2,1)} %staying_gradient.1._), custom_call_target="tpu_custom_call", output_to_operand_aliasing={{}: (2, {})} | custom-call | tf_op jit(solution)/shard_map/place_second/pallas_call | solution.py:317
  (30 shorter events, 1.8 us)
Async XLA Ops:
  0.6 3.6 %copy-start = (bf16[128,5120]{1,0:T(8,128)(2,1)S(1)}, bf16[128,5120]{1,0:T(8,128)(2,1)}, u32[]{:S(2)}) copy-start(bf16[128,5120]{1,0:T(8,128)(2,1)} %hidden_ref.1) | copy-start | bytes 3932164
  0.7 1.4 %copy-start.5 = (bf16[128,5120]{1,0:T(8,128)(2,1)S(1)}, bf16[128,5120]{1,0:T(8,128)(2,1)}, u32[]{:S(2)}) copy-start(bf16[128,5120]{1,0:T(8,128)(2,1)} %value_ref.1) | copy-start | bytes 3932164
  2.2 12.8 %copy-start.8 = (s32[128]{0:T(128)S(1)}, s32[128]{0:T(128)}, u32[]{:S(2)}) copy-start(s32[128]{0:T(128)} %param.9) | copy-start | bytes 1540
  2.2 12.7 %copy-start.7 = (f32[128]{0:T(128)S(1)}, f32[128]{0:T(128)}, u32[]{:S(2)}) copy-start(f32[128]{0:T(128)} %param.8) | copy-start | bytes 1540
  2.2 10.7 %collective-permute-start.2 = (bf16[128,1280]{1,0:T(8,128)(2,1)S(1)}, bf16[128,1280]{1,0:T(8,128)(2,1)S(1)}, u32[]{:S(2)}, u32[]{:S(2)}) collective-permute-start(bf16[128,1280]{1,0:T(8,128)(2,1)S(1)} %get-tuple-element.26.refs_1_.refs_0_), channel_id=1, source_target_pairs={{0,4},{4,0},{8,12},{12,8},{1,5},{5,1},{9,13},{13,9},{2,6},{6,2},{1... | collective-permute-start | bytes 983048 | tf_op jit(solution)/shard_map/ppermute | solution.py:21
  3.7 10.6 %collective-permute-start.5 = (bf16[128,1280]{1,0:T(8,128)(2,1)S(1)}, bf16[128,1280]{1,0:T(8,128)(2,1)S(1)}, u32[]{:S(2)}, u32[]{:S(2)}) collective-permute-start(bf16[128,1280]{1,0:T(8,128)(2,1)S(1)} %get-tuple-element.25.refs_2_.refs_0_.refs_1_), channel_id=1, source_target_pairs={{0,8},{4,12},{8,0},{12,4},{1,9},{5,13},{9,1},{13,5},{2,10},{6,14},... | collective-permute-start | bytes 983048 | tf_op jit(solution)/shard_map/ppermute | solution.py:21
  4.3 16.0 %collective-permute-start = (bf16[128,2560]{1,0:T(8,128)(2,1)S(1)}, bf16[128,2560]{1,0:T(8,128)(2,1)S(1)}, u32[]{:S(2)}, u32[]{:S(2)}) collective-permute-start(bf16[128,2560]{1,0:T(8,128)(2,1)S(1)} %take_half.3), channel_id=1, source_target_pairs={{0,1},{1,0},{2,3},{3,2},{4,5},{5,4},{6,7},{7,6},{8,9},{9,8},{10,11... | collective-permute-start | bytes 1966088 | tf_op jit(solution)/shard_map/ppermute | solution.py:21
  6.0 14.7 %collective-permute-start.3 = (bf16[128,1280]{1,0:T(8,128)(2,1)S(1)}, bf16[128,1280]{1,0:T(8,128)(2,1)S(1)}, u32[]{:S(2)}, u32[]{:S(2)}) collective-permute-start(bf16[128,1280]{1,0:T(8,128)(2,1)S(1)} %get-tuple-element.25.refs_2_.refs_0_.refs_1_), channel_id=1, source_target_pairs={{0,4},{4,0},{8,12},{12,8},{1,5},{5,1},{9,13},{13,9},{2,6},{6,2},{1... | collective-permute-start | bytes 983048 | tf_op jit(solution)/shard_map/ppermute | solution.py:21
  6.5 14.9 %collective-permute-start.4 = (bf16[128,1280]{1,0:T(8,128)(2,1)S(1)}, bf16[128,1280]{1,0:T(8,128)(2,1)S(1)}, u32[]{:S(2)}, u32[]{:S(2)}) collective-permute-start(bf16[128,1280]{1,0:T(8,128)(2,1)S(1)} %get-tuple-element.26.refs_1_.refs_0_), channel_id=1, source_target_pairs={{0,8},{4,12},{8,0},{12,4},{1,9},{5,13},{9,1},{13,5},{2,10},{6,14},... | collective-permute-start | bytes 983048 | tf_op jit(solution)/shard_map/ppermute | solution.py:21
  12.8 20.0 %collective-permute-start.6 = (bf16[128,1280]{1,0:T(8,128)(2,1)S(1)}, bf16[128,1280]{1,0:T(8,128)(2,1)S(1)}, u32[]{:S(2)}, u32[]{:S(2)}) collective-permute-start(bf16[128,1280]{1,0:T(8,128)(2,1)S(1)} %collective-permute-done.2.refs_3_.refs_1_.refs_2_), channel_id=1, source_target_pairs={{0,8},{4,12},{8,0},{12,4},{1,9},{5,13},{9,1},{13,5},{2,10},{6,14},... | collective-permute-start | bytes 983048 | tf_op jit(solution)/shard_map/ppermute | solution.py:21
  14.4 18.4 %collective-permute-start.7 = (bf16[128,1280]{1,0:T(8,128)(2,1)S(1)}, bf16[128,1280]{1,0:T(8,128)(2,1)S(1)}, u32[]{:S(2)}, u32[]{:S(2)}) collective-permute-start(bf16[128,1280]{1,0:T(8,128)(2,1)S(1)} %collective-permute-done.5.refs_6_.refs_2_.refs_5_), channel_id=1, source_target_pairs={{0,4},{4,0},{8,12},{12,8},{1,5},{5,1},{9,13},{13,9},{2,6},{6,2},{1... | collective-permute-start | bytes 983048 | tf_op jit(solution)/shard_map/ppermute | solution.py:21
  22.1 15.8 %copy-start.6 = (s32[128]{0:T(128)S(1)}, s32[128]{0:T(128)}, u32[]{:S(2)}) copy-start(s32[128]{0:T(128)} %param.7) | copy-start | bytes 1540
  22.1 15.8 %collective-permute-start.8 = (f32[392,128]{1,0:T(8,128)S(1)}, f32[392,128]{1,0:T(8,128)S(1)}, u32[]{:S(2)}, u32[]{:S(2)}) collective-permute-start(f32[392,128]{1,0:T(8,128)S(1)} %get-tuple-element.30), channel_id=1, source_target_pairs={{0,1},{1,0},{2,3},{3,2},{4,5},{5,4},{6,7},{7,6},{8,9},{9,8},{10,11... | collective-permute-start | bytes 602120 | tf_op jit(solution)/shard_map/ppermute | solution.py:21
  23.7 9.0 %collective-permute-start.1 = (f32[2,128]{1,0:T(2,128)S(1)}, f32[2,128]{1,0:T(2,128)S(1)}, u32[]{:S(2)}, u32[]{:S(2)}) collective-permute-start(f32[2,128]{1,0:T(2,128)S(1)} %pad_maximum_fusion.refs_0_.own_ref), channel_id=1, source_target_pairs={{1,2},{3,4},{5,6},{7,8},{9,10},{11,12},{13,14},{2,1},{4,3},{6,5},{... | collective-permute-start | bytes 3080 | tf_op jit(solution)/shard_map/ppermute | solution.py:340
  32.8 0.8 %copy-start.3 = (bf16[128,1280]{1,0:T(8,128)(2,1)}, bf16[128,1280]{1,0:T(8,128)(2,1)S(1)}, u32[]{:S(2)}) copy-start(bf16[128,1280]{1,0:T(8,128)(2,1)S(1)} %collective-permute-done.6.refs_0_.refs_3_.refs_6_) | copy-start | bytes 983044
  32.8 0.8 %copy-start.1 = (bf16[128,1280]{1,0:T(8,128)(2,1)}, bf16[128,1280]{1,0:T(8,128)(2,1)S(1)}, u32[]{:S(2)}) copy-start(bf16[128,1280]{1,0:T(8,128)(2,1)S(1)} %collective-permute-done.7.refs_1_.refs_3_.refs_7_) | copy-start | bytes 983044
  33.6 6.8 %copy-start.2 = (bf16[128,1280]{1,0:T(8,128)(2,1)S(1)}, bf16[128,1280]{1,0:T(8,128)(2,1)}, u32[]{:S(2)}) copy-start(bf16[128,1280]{1,0:T(8,128)(2,1)} %copy-done.1) | copy-start | bytes 983044
  33.6 4.3 %collective-permute-start.9 = (f32[128,128]{1,0:T(8,128)S(1)}, f32[128,128]{1,0:T(8,128)S(1)}, u32[]{:S(2)}, u32[]{:S(2)}) collective-permute-start(f32[128,128]{1,0:T(8,128)S(1)} %get-tuple-element.31), channel_id=1, source_target_pairs={{0,1},{1,0},{2,3},{3,2},{4,5},{5,4},{6,7},{7,6},{8,9},{9,8},{10,11... | collective-permute-start | bytes 196616 | tf_op jit(solution)/shard_map/ppermute | solution.py:21
  39.0 1.0 %copy-start.4 = (bf16[128,1280]{1,0:T(8,128)(2,1)S(1)}, bf16[128,1280]{1,0:T(8,128)(2,1)}, u32[]{:S(2)}) copy-start(bf16[128,1280]{1,0:T(8,128)(2,1)} %copy-done.3) | copy-start | bytes 983044
  40.3 11.1 %collective-permute-start.11 = (bf16[128,1792]{1,0:T(8,128)(2,1)S(1)}, bf16[128,1792]{1,0:T(8,128)(2,1)S(1)}, u32[]{:S(2)}, u32[]{:S(2)}) collective-permute-start(bf16[128,1792]{1,0:T(8,128)(2,1)S(1)} %first_message.1._), channel_id=1, source_target_pairs={{0,1},{1,0},{2,3},{3,2},{4,5},{5,4},{6,7},{7,6},{8,9},{9,8},{10,11... | collective-permute-start | bytes 1376264 | tf_op jit(solution)/shard_map/ppermute | solution.py:21
  40.8 14.2 %collective-permute-start.10 = (bf16[128,1280]{1,0:T(8,128)(2,1)S(1)}, bf16[128,1280]{1,0:T(8,128)(2,1)S(1)}, u32[]{:S(2)}, u32[]{:S(2)}) collective-permute-start(bf16[128,1280]{1,0:T(8,128)(2,1)S(1)} %second_message.1), channel_id=1, source_target_pairs={{0,1},{1,0},{2,3},{3,2},{4,5},{5,4},{6,7},{7,6},{8,9},{9,8},{10,11... | collective-permute-start | bytes 983048 | tf_op jit(solution)/shard_map/ppermute | solution.py:21

commit v7 on v6

--- a/solution.py
+++ b/solution.py
@@ -96,8 +96,10 @@
     )(which, hidden, partner_half)
 
 
-def partial_kernel(facts, turned_ref, *refs):
-    heads, (mine_ref, theirs_ref) = refs[facts:-2], refs[-2:]
+def partial_kernel(facts, count, turned_ref, *refs):
+    heads, (mine_ref, theirs_ref) = refs[facts : facts + count], refs[facts + count :][:2]
+    for held, ref in zip(refs[facts + count + 2 :], heads):
+        held[...] = ref[...]
     shard_rows, depth = heads[0].shape
     rows = mine_ref.shape[1]
     for i in range(len(heads) // 2):
@@ -116,13 +118,14 @@
     columns = sum(head.shape[0] for head in heads) // 2
     below = BELOW * len(facts)
     return pl.pallas_call(
-        functools.partial(partial_kernel, len(facts)),
+        functools.partial(partial_kernel, len(facts), len(heads)),
         out_shape=[
             jax.ShapeDtypeStruct((columns, rows // 2), F32),
             jax.ShapeDtypeStruct((columns + below, rows // 2), F32),
+            *[jax.ShapeDtypeStruct(head.shape, head.dtype) for head in heads if not facts],
         ],
         in_specs=[VMEM] * (1 + len(facts) + len(heads)),
-        out_specs=[VMEM, VMEM],
+        out_specs=[VMEM] * (2 if facts else 2 + len(heads)),
         compiler_params=PARAMS,
         cost_estimate=pl.CostEstimate(
             flops=2 * rows * columns * width,
@@ -337,8 +340,6 @@
     count = lax.axis_size(axes)
     own = jnp.stack([rewards, (group_ids + 1).astype(F32)])
     beside = [(i, i + 1) for i in range(1, count - 1, 2)]
-    outer = lax.ppermute(own, axes, beside + [(b, a) for a, b in beside])
-
     pieces = tuple(take(which, head_weight, 2))
     late_hidden, _ = lax.optimization_barrier((hidden, pieces))
     (other_half,) = take(1 - which, late_hidden, 1)
@@ -346,18 +347,22 @@
     heads = gathered(pieces, late_pieces, "vocab")
     partner_half = swapped(other_half, "section", 1)
 
+    late_own, _ = lax.optimization_barrier((own, (heads[near[1]][1], heads[near[-1]][0])))
+    outer = lax.ppermute(late_own, axes, beside + [(b, a) for a, b in beside])
+    partner_half, outer = lax.optimization_barrier((partner_half, outer))
     rows = turned(which, hidden, partner_half)
     mine, theirs = [], []
     for offsets, facts in ((near, (own,)), (far, ())):
-        if not facts:
-            rows, outer = lax.optimization_barrier((rows, outer))
-        kept, sent = partial_scores(rows, [piece for o in offsets for piece in heads[o]], facts)
+        pieces = [piece for o in offsets for piece in heads[o]]
+        kept, sent, *again = partial_scores(rows, pieces, facts)
         mine.append(kept)
         theirs.append(swapped(sent, "section", 1))
     mine, theirs = in_order(mine, near + far, 0), in_order(theirs, near + far, BELOW)
     logits, logprob, entropy, dlogits = loss(
         shard, tokens[None, :], own, outer, mine, theirs, shards
     )
+    for i, offset in enumerate(far):
+        heads[offset] = again[2 * i : 2 * i + 2]
     pieces = [piece for pair in heads for piece in pair]
     first = first_message(dlogits, pieces[0::2])
     first_in = swapped(first, "section", 1)

time: 55.9 us -> 55.8 us (level)
  local copies, waits for them, and re-layouts: 2.87 us -> 1.43 us
  starting transfers between devices: 14.7 us -> 16 us
    unnamed x18 -> x10, local copies, waits for them, and re-layouts: 2.87 us -> 1.43 us
    ppermute x11, waiting for transfers between devices: 27.5 us -> 28.4 us  [swapped(): return lax.ppermute(value, axis, pairs)]
    ppermute x1, starting transfers between devices: 4.63 us -> 5.41 us  [body(): outer = lax.ppermute(late_own, axes, beside + [(b, a) for a, b in beside])]
    ppermute x1, waiting for transfers between devices: 4.42 us -> 3.63 us  [body(): outer = lax.ppermute(late_own, axes, beside + [(b, a) for a, b in beside])]
where the time goes in v7:
time: 55.8 us; the launch traced here: 55.7 us
  waiting for transfers between devices  32 us (57%)
  starting transfers between devices  16 us (29%)
  Pallas kernels  5.41 us (10%)
  local copies, waits for them, and re-layouts  1.43 us (3%)
  between operations  0.8 us (1%)
    ppermute x11, waiting for transfers between devices, swapped(): return lax.ppermute(value, axis, pairs)  28.4 us
    ppermute x11, starting transfers between devices, swapped(): return lax.ppermute(value, axis, pairs)  10.6 us
    ppermute x1, starting transfers between devices, body(): outer = lax.ppermute(late_own, axes, beside + [(b, a) for a, b in beside])  5.41 us
    ppermute x1, waiting for transfers between devices, body(): outer = lax.ppermute(late_own, axes, beside + [(b, a) for a, b in beside])  3.63 us
    unnamed x10, local copies, waits for them, and re-layouts  1.43 us
    pallas_call x1, Pallas kernels, staying_gradient(): pl.pallas_call(staying_kernel, out_shape=jax.ShapeDtypeStruct((rows, 4 *...  1.26 us
  transfers between devices with their start and end apart: 12, of which 8 were waited for; matrix products, arithmetic and copies ran while one was open for 0% of the time, Pallas kernels for 6%

profile of v7, /device:TPU:4, one launch (start us, length us, event | category | flops | bytes accessed | tf_op | source)
XLA Modules:
  0.0 55.7 jit_solution(207473558580198656)
XLA Ops:
  0.7 1.4 %copy-done.1 = bf16[128,5120]{1,0:T(8,128)(2,1)S(1)} copy-done((bf16[128,5120]{1,0:T(8,128)(2,1)S(1)}, bf16[128,5120]{1,0:T(8,128)(2,1)}, u32[]{:S(2)}) %copy-start.1) | copy-done | bytes 1310744
  2.2 1.6 %collective-permute-start.4 = (bf16[128,1280]{1,0:T(8,128)(2,1)S(1)}, bf16[128,1280]{1,0:T(8,128)(2,1)S(1)}, u32[]{:S(2)}, u32[]{:S(2)}) collective-permute-start(bf16[128,1280]{1,0:T(8,128)(2,1)S(1)} %get-tuple-element.28.refs_1_.refs_0_), channel_id=1, source_target_pairs={{0,4},{4,0},{8,12},{12,8},{1,5},{5,1},{9,13},{13,9},{2,6},{6,2},{1... | collective-permute-start | bytes 983048 | tf_op jit(solution)/shard_map/ppermute | solution.py:21
  3.7 0.5 collective-permute-start.5
  4.3 1.6 %collective-permute-start = (bf16[128,2560]{1,0:T(8,128)(2,1)S(1)}, bf16[128,2560]{1,0:T(8,128)(2,1)S(1)}, u32[]{:S(2)}, u32[]{:S(2)}) collective-permute-start(bf16[128,2560]{1,0:T(8,128)(2,1)S(1)} %take_half.3), channel_id=1, source_target_pairs={{0,1},{1,0},{2,3},{3,2},{4,5},{5,4},{6,7},{7,6},{8,9},{9,8},{10,11... | collective-permute-start | bytes 1966088 | tf_op jit(solution)/shard_map/ppermute | solution.py:21
  6.0 0.5 collective-permute-start.1
  6.5 1.5 %collective-permute-start.2 = (bf16[128,1280]{1,0:T(8,128)(2,1)S(1)}, bf16[128,1280]{1,0:T(8,128)(2,1)S(1)}, u32[]{:S(2)}, u32[]{:S(2)}) collective-permute-start(bf16[128,1280]{1,0:T(8,128)(2,1)S(1)} %get-tuple-element.28.refs_1_.refs_0_), channel_id=1, source_target_pairs={{0,8},{4,12},{8,0},{12,4},{1,9},{5,13},{9,1},{13,5},{2,10},{6,14},... | collective-permute-start | bytes 983048 | tf_op jit(solution)/shard_map/ppermute | solution.py:21
  8.0 4.8 %collective-permute-done.4.refs_3_.refs_1_.refs_2_ = bf16[128,1280]{1,0:T(8,128)(2,1)S(1)} collective-permute-done((bf16[128,1280]{1,0:T(8,128)(2,1)S(1)}, bf16[128,1280]{1,0:T(8,128)(2,1)S(1)}, u32[]{:S(2)}, u32[]{:S(2)}) %collective-permute-start.4) | collective-permute-done | bytes 327712 | tf_op jit(solution)/shard_map/ppermute | solution.py:21
  12.8 1.5 %collective-permute-done.5.refs_6_.refs_2_.refs_5_ = bf16[128,1280]{1,0:T(8,128)(2,1)S(1)} collective-permute-done((bf16[128,1280]{1,0:T(8,128)(2,1)S(1)}, bf16[128,1280]{1,0:T(8,128)(2,1)S(1)}, u32[]{:S(2)}, u32[]{:S(2)}) %collective-permute-start.5) | collective-permute-done | bytes 327712 | tf_op jit(solution)/shard_map/ppermute | solution.py:21
  14.4 0.5 collective-permute-start.7
  14.9 4.9 %collective-permute-done.1.refs_4_.refs_1_.refs_3_ = bf16[128,1280]{1,0:T(8,128)(2,1)S(1)} collective-permute-done((bf16[128,1280]{1,0:T(8,128)(2,1)S(1)}, bf16[128,1280]{1,0:T(8,128)(2,1)S(1)}, u32[]{:S(2)}, u32[]{:S(2)}) %collective-permute-start.1) | collective-permute-done | bytes 327712 | tf_op jit(solution)/shard_map/ppermute | solution.py:21
  19.9 1.5 %collective-permute-done.2.refs_5_.refs_2_.refs_4_ = bf16[128,1280]{1,0:T(8,128)(2,1)S(1)} collective-permute-done((bf16[128,1280]{1,0:T(8,128)(2,1)S(1)}, bf16[128,1280]{1,0:T(8,128)(2,1)S(1)}, u32[]{:S(2)}, u32[]{:S(2)}) %collective-permute-start.2) | collective-permute-done | bytes 327712 | tf_op jit(solution)/shard_map/ppermute | solution.py:21
  21.4 5.4 %collective-permute-start.3 = (f32[2,128]{1,0:T(2,128)S(1)}, f32[2,128]{1,0:T(2,128)S(1)}, u32[]{:S(2)}, u32[]{:S(2)}) collective-permute-start(f32[2,128]{1,0:T(2,128)S(1)} %pad_maximum_fusion.refs_0_.own_ref), channel_id=1, source_target_pairs={{1,2},{3,4},{5,6},{7,8},{9,10},{11,12},{13,14},{2,1},{4,3},{6,5},{... | collective-permute-start | bytes 3080 | tf_op jit(solution)/shard_map/ppermute | solution.py:351
  26.8 3.6 %collective-permute-done.3.outer_ref = f32[2,128]{1,0:T(2,128)S(1)} collective-permute-done((f32[2,128]{1,0:T(2,128)S(1)}, f32[2,128]{1,0:T(2,128)S(1)}, u32[]{:S(2)}, u32[]{:S(2)}) %collective-permute-start.3) | collective-permute-done | bytes 1056 | tf_op jit(solution)/shard_map/ppermute | solution.py:351
  30.4 0.4 turned_rows.1.turned_ref
  30.8 0.7 %partial_scores.2 = (f32[384,128]{1,0:T(8,128)S(1)}, f32[392,128]{1,0:T(8,128)S(1)}) custom-call(bf16[2560,256]{1,0:T(8,128)(2,1)S(1)} %turned_rows.1.turned_ref, f32[2,128]{1,0:T(2,128)S(1)} %pad_maximum_fusion.refs_0_.own_ref, bf16[128,1280]{1,0:T(8,128)(2,1)S(1)} %get-tuple-element.28.refs_1_.refs_0_, ...), custom_call_target="tpu_custom_call" | custom-call | flops 503316480 | bytes 3276800 | tf_op jit(solution)/shard_map/partial_scores/pallas_call | solution.py:120
  31.7 0.4 partial_scores.3
  32.1 2.1 %collective-permute-start.9 = (f32[128,128]{1,0:T(8,128)S(1)}, f32[128,128]{1,0:T(8,128)S(1)}, u32[]{:S(2)}, u32[]{:S(2)}) collective-permute-start(f32[128,128]{1,0:T(8,128)S(1)} %get-tuple-element.35), channel_id=1, source_target_pairs={{0,1},{1,0},{2,3},{3,2},{4,5},{5,4},{6,7},{7,6},{8,9},{9,8},{10,11... | collective-permute-start | bytes 196616 | tf_op jit(solution)/shard_map/ppermute | solution.py:21
  34.1 4.9 %collective-permute-done.9.refs_3_ = f32[128,128]{1,0:T(8,128)S(1)} collective-permute-done((f32[128,128]{1,0:T(8,128)S(1)}, f32[128,128]{1,0:T(8,128)S(1)}, u32[]{:S(2)}, u32[]{:S(2)}) %collective-permute-start.9) | collective-permute-done | bytes 65568 | tf_op jit(solution)/shard_map/ppermute | solution.py:21
  39.0 1.1 %loss.1 = (bf16[128,512]{1,0:T(8,128)(2,1)}, f32[1,128]{1,0:T(1,128)}, f32[1,128]{1,0:T(1,128)}, bf16[128,512]{1,0:T(8,128)(2,1)S(1)}) custom-call(s32[1]{0:T(128)} %bitcast.shard_ref, s32[1,128]{1,0:T(1,128)S(1)} %bitcast.8, f32[2,128]{1,0:T(2,128)S(1)} %pad_maximum_fusion.refs_0_.own_ref, f32[2,128]{1,0:T(2,128)S(1)} %collective-permute-done.3.outer_ref, ...), custom_call_target="tpu_custom_call" | custom-call | flops 655360 | bytes 786432 | tf_op jit(solution)/shard_map/loss/pallas_call | solution.py:190
  40.9 2.0 %collective-permute-start.10 = (bf16[128,1280]{1,0:T(8,128)(2,1)S(1)}, bf16[128,1280]{1,0:T(8,128)(2,1)S(1)}, u32[]{:S(2)}, u32[]{:S(2)}) collective-permute-start(bf16[128,1280]{1,0:T(8,128)(2,1)S(1)} %second_message.1), channel_id=1, source_target_pairs={{0,1},{1,0},{2,3},{3,2},{4,5},{5,4},{6,7},{7,6},{8,9},{9,8},{10,11... | collective-permute-start | bytes 983048 | tf_op jit(solution)/shard_map/ppermute | solution.py:21
  42.9 8.4 %collective-permute-done.11.first_ref = bf16[128,1792]{1,0:T(8,128)(2,1)S(1)} collective-permute-done((bf16[128,1792]{1,0:T(8,128)(2,1)S(1)}, bf16[128,1792]{1,0:T(8,128)(2,1)S(1)}, u32[]{:S(2)}, u32[]{:S(2)}) %collective-permute-start.11) | collective-permute-done | bytes 458784 | tf_op jit(solution)/shard_map/ppermute | solution.py:21
  51.4 1.3 %staying_gradient.1._ = bf16[128,5120]{1,0:T(8,128)(2,1)} custom-call(s32[1]{0:T(128)} %bitcast.4.which_ref, bf16[128,1792]{1,0:T(8,128)(2,1)S(1)} %collective-permute-done.11.first_ref, bf16[128,1280]{1,0:T(8,128)(2,1)S(1)} %get-tuple-element.28.refs_1_.refs_0_, bf16[128,1280]{1,0:T(8,128)(2,1)S(1)} %get-tuple-element.27.refs_2_.refs_0_.refs_1_, ...), custom_call_target="tpu_custom_call" | custom-call | flops 335544320 | bytes 3276800 | tf_op jit(solution)/shard_map/staying_gradient/pallas_call | solution.py:293
  52.7 2.2 %collective-permute-done.10.second_ref = bf16[128,1280]{1,0:T(8,128)(2,1)S(1)} collective-permute-done((bf16[128,1280]{1,0:T(8,128)(2,1)S(1)}, bf16[128,1280]{1,0:T(8,128)(2,1)S(1)}, u32[]{:S(2)}, u32[]{:S(2)}) %collective-permute-start.10) | collective-permute-done | bytes 327712 | tf_op jit(solution)/shard_map/ppermute | solution.py:21
  54.9 0.8 %place_second.1 = bf16[128,5120]{1,0:T(8,128)(2,1)} custom-call(s32[1]{0:T(128)} %bitcast.4.which_ref, bf16[128,1280]{1,0:T(8,128)(2,1)S(1)} %collective-permute-done.10.second_ref, bf16[128,5120]{1,0:T(8,128)(2,1)} %staying_gradient.1._), custom_call_target="tpu_custom_call", output_to_operand_aliasing={{}: (2, {})} | custom-call | tf_op jit(solution)/shard_map/place_second/pallas_call | solution.py:320
  (22 shorter events, 1.1 us)
Async XLA Ops:
  0.6 3.6 %copy-start = (bf16[128,5120]{1,0:T(8,128)(2,1)S(1)}, bf16[128,5120]{1,0:T(8,128)(2,1)}, u32[]{:S(2)}) copy-start(bf16[128,5120]{1,0:T(8,128)(2,1)} %hidden_ref.1) | copy-start | bytes 3932164
  0.7 1.4 %copy-start.1 = (bf16[128,5120]{1,0:T(8,128)(2,1)S(1)}, bf16[128,5120]{1,0:T(8,128)(2,1)}, u32[]{:S(2)}) copy-start(bf16[128,5120]{1,0:T(8,128)(2,1)} %value_ref.1) | copy-start | bytes 3932164
  2.2 12.8 %copy-start.4 = (s32[128]{0:T(128)S(1)}, s32[128]{0:T(128)}, u32[]{:S(2)}) copy-start(s32[128]{0:T(128)} %param.9) | copy-start | bytes 1540
  2.2 12.7 %copy-start.3 = (f32[128]{0:T(128)S(1)}, f32[128]{0:T(128)}, u32[]{:S(2)}) copy-start(f32[128]{0:T(128)} %param.8) | copy-start | bytes 1540
  2.2 10.7 %collective-permute-start.4 = (bf16[128,1280]{1,0:T(8,128)(2,1)S(1)}, bf16[128,1280]{1,0:T(8,128)(2,1)S(1)}, u32[]{:S(2)}, u32[]{:S(2)}) collective-permute-start(bf16[128,1280]{1,0:T(8,128)(2,1)S(1)} %get-tuple-element.28.refs_1_.refs_0_), channel_id=1, source_target_pairs={{0,4},{4,0},{8,12},{12,8},{1,5},{5,1},{9,13},{13,9},{2,6},{6,2},{1... | collective-permute-start | bytes 983048 | tf_op jit(solution)/shard_map/ppermute | solution.py:21
  3.7 10.6 %collective-permute-start.5 = (bf16[128,1280]{1,0:T(8,128)(2,1)S(1)}, bf16[128,1280]{1,0:T(8,128)(2,1)S(1)}, u32[]{:S(2)}, u32[]{:S(2)}) collective-permute-start(bf16[128,1280]{1,0:T(8,128)(2,1)S(1)} %get-tuple-element.27.refs_2_.refs_0_.refs_1_), channel_id=1, source_target_pairs={{0,8},{4,12},{8,0},{12,4},{1,9},{5,13},{9,1},{13,5},{2,10},{6,14},... | collective-permute-start | bytes 983048 | tf_op jit(solution)/shard_map/ppermute | solution.py:21
  4.3 26.1 %collective-permute-start = (bf16[128,2560]{1,0:T(8,128)(2,1)S(1)}, bf16[128,2560]{1,0:T(8,128)(2,1)S(1)}, u32[]{:S(2)}, u32[]{:S(2)}) collective-permute-start(bf16[128,2560]{1,0:T(8,128)(2,1)S(1)} %take_half.3), channel_id=1, source_target_pairs={{0,1},{1,0},{2,3},{3,2},{4,5},{5,4},{6,7},{7,6},{8,9},{9,8},{10,11... | collective-permute-start | bytes 1966088 | tf_op jit(solution)/shard_map/ppermute | solution.py:21
  6.0 13.9 %collective-permute-start.1 = (bf16[128,1280]{1,0:T(8,128)(2,1)S(1)}, bf16[128,1280]{1,0:T(8,128)(2,1)S(1)}, u32[]{:S(2)}, u32[]{:S(2)}) collective-permute-start(bf16[128,1280]{1,0:T(8,128)(2,1)S(1)} %get-tuple-element.27.refs_2_.refs_0_.refs_1_), channel_id=1, source_target_pairs={{0,4},{4,0},{8,12},{12,8},{1,5},{5,1},{9,13},{13,9},{2,6},{6,2},{1... | collective-permute-start | bytes 983048 | tf_op jit(solution)/shard_map/ppermute | solution.py:21
  6.5 14.9 %collective-permute-start.2 = (bf16[128,1280]{1,0:T(8,128)(2,1)S(1)}, bf16[128,1280]{1,0:T(8,128)(2,1)S(1)}, u32[]{:S(2)}, u32[]{:S(2)}) collective-permute-start(bf16[128,1280]{1,0:T(8,128)(2,1)S(1)} %get-tuple-element.28.refs_1_.refs_0_), channel_id=1, source_target_pairs={{0,8},{4,12},{8,0},{12,4},{1,9},{5,13},{9,1},{13,5},{2,10},{6,14},... | collective-permute-start | bytes 983048 | tf_op jit(solution)/shard_map/ppermute | solution.py:21
  12.8 18.8 %collective-permute-start.6 = (bf16[128,1280]{1,0:T(8,128)(2,1)S(1)}, bf16[128,1280]{1,0:T(8,128)(2,1)S(1)}, u32[]{:S(2)}, u32[]{:S(2)}) collective-permute-start(bf16[128,1280]{1,0:T(8,128)(2,1)S(1)} %collective-permute-done.4.refs_3_.refs_1_.refs_2_), channel_id=1, source_target_pairs={{0,8},{4,12},{8,0},{12,4},{1,9},{5,13},{9,1},{13,5},{2,10},{6,14},... | collective-permute-start | bytes 983048 | tf_op jit(solution)/shard_map/ppermute | solution.py:21
  14.4 17.3 %collective-permute-start.7 = (bf16[128,1280]{1,0:T(8,128)(2,1)S(1)}, bf16[128,1280]{1,0:T(8,128)(2,1)S(1)}, u32[]{:S(2)}, u32[]{:S(2)}) collective-permute-start(bf16[128,1280]{1,0:T(8,128)(2,1)S(1)} %collective-permute-done.5.refs_6_.refs_2_.refs_5_), channel_id=1, source_target_pairs={{0,4},{4,0},{8,12},{12,8},{1,5},{5,1},{9,13},{13,9},{2,6},{6,2},{1... | collective-permute-start | bytes 983048 | tf_op jit(solution)/shard_map/ppermute | solution.py:21
  21.4 9.1 %collective-permute-start.3 = (f32[2,128]{1,0:T(2,128)S(1)}, f32[2,128]{1,0:T(2,128)S(1)}, u32[]{:S(2)}, u32[]{:S(2)}) collective-permute-start(f32[2,128]{1,0:T(2,128)S(1)} %pad_maximum_fusion.refs_0_.own_ref), channel_id=1, source_target_pairs={{1,2},{3,4},{5,6},{7,8},{9,10},{11,12},{13,14},{2,1},{4,3},{6,5},{... | collective-permute-start | bytes 3080 | tf_op jit(solution)/shard_map/ppermute | solution.py:351
  31.6 7.4 %copy-start.2 = (s32[128]{0:T(128)S(1)}, s32[128]{0:T(128)}, u32[]{:S(2)}) copy-start(s32[128]{0:T(128)} %param.7) | copy-start | bytes 1540
  31.6 7.4 %collective-permute-start.8 = (f32[392,128]{1,0:T(8,128)S(1)}, f32[392,128]{1,0:T(8,128)S(1)}, u32[]{:S(2)}, u32[]{:S(2)}) collective-permute-start(f32[392,128]{1,0:T(8,128)S(1)} %get-tuple-element.34), channel_id=1, source_target_pairs={{0,1},{1,0},{2,3},{3,2},{4,5},{5,4},{6,7},{7,6},{8,9},{9,8},{10,11... | collective-permute-start | bytes 602120 | tf_op jit(solution)/shard_map/ppermute | solution.py:21
  32.1 6.9 %collective-permute-start.9 = (f32[128,128]{1,0:T(8,128)S(1)}, f32[128,128]{1,0:T(8,128)S(1)}, u32[]{:S(2)}, u32[]{:S(2)}) collective-permute-start(f32[128,128]{1,0:T(8,128)S(1)} %get-tuple-element.35), channel_id=1, source_target_pairs={{0,1},{1,0},{2,3},{3,2},{4,5},{5,4},{6,7},{7,6},{8,9},{9,8},{10,11... | collective-permute-start | bytes 196616 | tf_op jit(solution)/shard_map/ppermute | solution.py:21
  40.4 10.9 %collective-permute-start.11 = (bf16[128,1792]{1,0:T(8,128)(2,1)S(1)}, bf16[128,1792]{1,0:T(8,128)(2,1)S(1)}, u32[]{:S(2)}, u32[]{:S(2)}) collective-permute-start(bf16[128,1792]{1,0:T(8,128)(2,1)S(1)} %first_message.1._), channel_id=1, source_target_pairs={{0,1},{1,0},{2,3},{3,2},{4,5},{5,4},{6,7},{7,6},{8,9},{9,8},{10,11... | collective-permute-start | bytes 1376264 | tf_op jit(solution)/shard_map/ppermute | solution.py:21
  40.9 14.0 %collective-permute-start.10 = (bf16[128,1280]{1,0:T(8,128)(2,1)S(1)}, bf16[128,1280]{1,0:T(8,128)(2,1)S(1)}, u32[]{:S(2)}, u32[]{:S(2)}) collective-permute-start(bf16[128,1280]{1,0:T(8,128)(2,1)S(1)} %second_message.1), channel_id=1, source_target_pairs={{0,1},{1,0},{2,3},{3,2},{4,5},{5,4},{6,7},{7,6},{8,9},{9,8},{10,11... | collective-permute-start | bytes 983048 | tf_op jit(solution)/shard_map/ppermute | solution.py:21

commit v8 on v7

--- a/solution.py
+++ b/solution.py
@@ -136,21 +136,38 @@
     )(turned_rows, *facts, *heads)
 
 
-def advantage_of(own, outer, partner):
-    rows = own.shape[1]
+def advantage_kernel(partner_ref, own_ref, outer_ref, out_ref):
+    rows = own_ref.shape[1]
+    partner = partner_ref[partner_ref.shape[0] - BELOW :, :]
     eye = lax.broadcasted_iota(jnp.int32, (rows, rows), 0) == lax.broadcasted_iota(
         jnp.int32, (rows, rows), 1
     )
-    groups = jnp.sum(jnp.where(eye, own[1:2, :], 0.0), axis=1, keepdims=True)
+
+    def upright(row):
+        return jnp.sum(jnp.where(eye, row, 0.0), axis=1, keepdims=True)
+
+    groups = upright(partner[1:2, :])
     sums, counts = jnp.zeros((rows, 1), F32), jnp.zeros((rows, 1), F32)
-    for facts in (own, outer, partner):
+    for facts in (partner, own_ref[...], outer_ref[...]):
         member = facts[1:2, :] == groups
         sums += jnp.sum(jnp.where(member, facts[0:1, :], 0.0), axis=1, keepdims=True)
         counts += jnp.sum(jnp.where(member, 1.0, 0.0), axis=1, keepdims=True)
-    return own[0:1, :] - jnp.sum(jnp.where(eye, sums / counts, 0.0), axis=0, keepdims=True)
-
-
-def loss_kernel(parts, shards, shard_ref, tokens_ref, own_ref, outer_ref, *refs):
+    out_ref[...] = jnp.broadcast_to(upright(partner[0:1, :]) - sums / counts, (rows, rows))
+
+
+def advantages(partner, own, outer):
+    rows = own.shape[1]
+    return pl.pallas_call(
+        advantage_kernel,
+        out_shape=jax.ShapeDtypeStruct((rows, rows), F32),
+        in_specs=[VMEM] * 3,
+        out_specs=VMEM,
+        compiler_params=PARAMS,
+        name="advantage",
+    )(partner, own, outer)
+
+
+def loss_kernel(parts, shards, shard_ref, tokens_ref, *refs):
     mine, theirs = refs[:parts], refs[parts : 2 * parts]
     logits_ref, logprob_ref, entropy_ref, dlogits_ref = refs[2 * parts :]
     shard = shard_ref[0]
@@ -158,8 +175,6 @@
     shard_rows = columns // shards
 
     lengths = [ref.shape[0] for ref in mine]
-    partner = theirs[0][lengths[0] :, :]
-    advantage = advantage_of(own_ref[...], outer_ref[...], partner)
     scores = jnp.concatenate(
         [a[...] + b[:n, :] for a, b, n in zip(mine, theirs, lengths)], axis=0
     )
@@ -170,7 +185,7 @@
     unnormed = jnp.exp(scores - row_max)
     denominator = jnp.sum(unnormed, axis=0, keepdims=True)
     probabilities = unnormed / denominator
-    dlogits = advantage * (probabilities - jnp.where(chosen, 1.0, 0.0))
+    dlogits = probabilities - jnp.where(chosen, 1.0, 0.0)
     for i in range(shards):
         block = slice(i * shard_rows, (i + 1) * shard_rows)
         dlogits_ref[:, block] = dlogits[block, :].T.astype(BF16)
@@ -182,7 +197,7 @@
     entropy_ref[...] = log_total - jnp.sum(probabilities * scores, axis=0, keepdims=True)
 
 
-def loss(shard, tokens, own, outer, mine, theirs, shards):
+def loss(shard, tokens, mine, theirs, shards):
     rows = tokens.shape[1]
     columns = sum(part.shape[0] for part in mine)
     flat = jax.ShapeDtypeStruct((1, rows), F32)
@@ -190,7 +205,7 @@
     return pl.pallas_call(
         functools.partial(loss_kernel, len(mine), shards),
         out_shape=[wide, flat, flat, wide],
-        in_specs=[SMEM] + [VMEM] * (3 + 2 * len(mine)),
+        in_specs=[SMEM] + [VMEM] * (1 + 2 * len(mine)),
         out_specs=[VMEM] * 4,
         compiler_params=pltpu.CompilerParams(vmem_limit_bytes=2 * 1024**2 + 32 * rows * columns),
         cost_estimate=pl.CostEstimate(
@@ -199,15 +214,21 @@
             transcendentals=rows * columns,
         ),
         name="loss",
-    )(shard, tokens, own, outer, *mine, *theirs)
-
-
-def multiplied(dlogits, heads, out_ref, start):
+    )(shard, tokens, *mine, *theirs)
+
+
+def scaling(advantage, width):
+    return jnp.concatenate([advantage] * (width // advantage.shape[1]), axis=1)
+
+
+def multiplied(dlogits, heads, out_ref, start, scale=None):
     block = 256
+    scale = None if scale is None else scaling(scale, block)
     for j in range(heads[0].shape[1] // block):
         part = slice(j * block, (j + 1) * block)
         head = jnp.concatenate([ref[:, part] for ref in heads], axis=0)
         product = jnp.dot(dlogits, head, preferred_element_type=F32)
+        product = product if scale is None else product * scale
         out_ref[:, start + j * block : start + (j + 1) * block] = product.astype(BF16)
 
 
@@ -258,75 +279,85 @@
     )(dlogits, first, *heads)
 
 
-def staying_kernel(which_ref, first_ref, *refs):
+def scaled(message_ref, advantage, columns, out_ref, start):
+    block = 256
+    scale = scaling(advantage, block)
+    for j in range(0, columns.stop - columns.start, block):
+        value = message_ref[:, columns.start + j : columns.start + j + block].astype(F32)
+        out_ref[:, start + j : start + j + block] = (value * scale).astype(BF16)
+
+
+def staying_kernel(which_ref, first_ref, advantage_ref, *refs):
     heads, (out_ref, held_ref, sem) = refs[:-3], refs[-3:]
-    width = held_ref.shape[1]
-    depth = width // 2
+    depth = held_ref.shape[1] // 3
+    width = 2 * depth
     columns = first_ref.shape[1] - depth
     mine = pl.multiple_of(which_ref[0] * width, 128)
     other = pl.multiple_of((1 - which_ref[0]) * width, 128)
-    copies = [
-        pltpu.make_async_copy(
-            first_ref.at[:, pl.ds(columns, depth)], out_ref.at[:, pl.ds(other, depth)], sem.at[0]
-        )
-    ]
-    copies[0].start()
+    advantage = advantage_ref[...]
+    copies = []
+
+    def put(i, place):
+        source = held_ref.at[:, pl.ds(i * depth, depth)]
+        target = out_ref.at[:, pl.ds(pl.multiple_of(place, 128), depth)]
+        copies.append(pltpu.make_async_copy(source, target, sem.at[i]))
+        copies[-1].start()
+
+    scaled(first_ref, advantage, slice(columns, columns + depth), held_ref, 0)
+    put(0, other)
     dlogits = first_ref[:, :columns]
     for i in range(2):
-        multiplied(dlogits, heads[i::2], held_ref, i * depth)
+        multiplied(dlogits, heads[i::2], held_ref, (i + 1) * depth, advantage)
+        put(i + 1, mine + i * depth)
+    for copy in copies:
+        copy.wait()
+
+
+def staying_gradient(which, first, advantage, heads):
+    rows = first.shape[0]
+    depth = heads[0].shape[1]
+    columns = first.shape[1] - depth
+    return pl.pallas_call(
+        staying_kernel,
+        out_shape=jax.ShapeDtypeStruct((rows, 4 * depth), BF16),
+        in_specs=[SMEM] + [VMEM] * (2 + len(heads)),
+        out_specs=HBM,
+        scratch_shapes=[pltpu.VMEM((rows, 3 * depth), BF16), pltpu.SemaphoreType.DMA((3,))],
+        compiler_params=PARAMS,
+        cost_estimate=gradient_cost(rows, columns, 2 * depth),
+        name="staying_gradient",
+    )(which, first, advantage, *heads)
+
+
+def placed_kernel(which_ref, second_ref, advantage_ref, _, out_ref, held_ref, sem):
+    depth = second_ref.shape[1]
+    parts = 5 if depth % 1280 == 0 else 1
+    width = depth // parts
+    start = (1 - which_ref[0]) * (2 * depth) + depth
+    copies = []
+    for i in range(parts):
+        part = slice(i * width, (i + 1) * width)
+        scaled(second_ref, advantage_ref[...], part, held_ref, i * width)
+        target = out_ref.at[:, pl.ds(pl.multiple_of(start + i * width, 128), width)]
         copies.append(
-            pltpu.make_async_copy(
-                held_ref.at[:, pl.ds(i * depth, depth)],
-                out_ref.at[:, pl.ds(pl.multiple_of(mine + i * depth, 128), depth)],
-                sem.at[i + 1],
-            )
+            pltpu.make_async_copy(held_ref.at[:, pl.ds(i * width, width)], target, sem.at[i])
         )
         copies[-1].start()
     for copy in copies:
         copy.wait()
 
 
-def staying_gradient(which, first, heads):
-    rows = first.shape[0]
-    depth = heads[0].shape[1]
-    columns = first.shape[1] - depth
-    return pl.pallas_call(
-        staying_kernel,
-        out_shape=jax.ShapeDtypeStruct((rows, 4 * depth), BF16),
-        in_specs=[SMEM] + [VMEM] * (1 + len(heads)),
-        out_specs=HBM,
-        scratch_shapes=[pltpu.VMEM((rows, 2 * depth), BF16), pltpu.SemaphoreType.DMA((3,))],
-        compiler_params=PARAMS,
-        cost_estimate=gradient_cost(rows, columns, 2 * depth),
-        name="staying_gradient",
-    )(which, first, *heads)
-
-
-def placed_kernel(which_ref, second_ref, _, out_ref, sem):
-    rows, depth = second_ref.shape
-    start = pl.multiple_of((1 - which_ref[0]) * (2 * depth) + depth, 128)
-    copies = []
-    for i in range(4):
-        part = pl.ds(i * (rows // 4), rows // 4)
-        target = out_ref.at[part, pl.ds(start, depth)]
-        copies.append(pltpu.make_async_copy(second_ref.at[part, :], target, sem.at[i]))
-    for copy in copies:
-        copy.start()
-    for copy in copies:
-        copy.wait()
-
-
-def placed_beside(which, second, gradient):
+def placed_beside(which, second, advantage, gradient):
     return pl.pallas_call(
         placed_kernel,
         out_shape=jax.ShapeDtypeStruct(gradient.shape, gradient.dtype),
-        in_specs=[SMEM, VMEM, HBM],
+        in_specs=[SMEM, VMEM, VMEM, HBM],
         out_specs=HBM,
-        scratch_shapes=[pltpu.SemaphoreType.DMA((4,))],
-        input_output_aliases={2: 0},
+        scratch_shapes=[pltpu.VMEM(second.shape, BF16), pltpu.SemaphoreType.DMA((5,))],
+        input_output_aliases={3: 0},
         compiler_params=PARAMS,
         name="place_second",
-    )(which, second, gradient)
+    )(which, second, advantage, gradient)
 
 
 def body(hidden, head_weight, tokens, rewards, group_ids):
@@ -336,10 +367,7 @@
     near = [o for o in range(shards) if bin(o).count("1") <= 1]
     far = [o for o in range(shards) if bin(o).count("1") > 1]
 
-    axes = ("vocab", "section")
-    count = lax.axis_size(axes)
     own = jnp.stack([rewards, (group_ids + 1).astype(F32)])
-    beside = [(i, i + 1) for i in range(1, count - 1, 2)]
     pieces = tuple(take(which, head_weight, 2))
     late_hidden, _ = lax.optimization_barrier((hidden, pieces))
     (other_half,) = take(1 - which, late_hidden, 1)
@@ -347,9 +375,6 @@
     heads = gathered(pieces, late_pieces, "vocab")
     partner_half = swapped(other_half, "section", 1)
 
-    late_own, _ = lax.optimization_barrier((own, (heads[near[1]][1], heads[near[-1]][0])))
-    outer = lax.ppermute(late_own, axes, beside + [(b, a) for a, b in beside])
-    partner_half, outer = lax.optimization_barrier((partner_half, outer))
     rows = turned(which, hidden, partner_half)
     mine, theirs = [], []
     for offsets, facts in ((near, (own,)), (far, ())):
@@ -357,18 +382,27 @@
         kept, sent, *again = partial_scores(rows, pieces, facts)
         mine.append(kept)
         theirs.append(swapped(sent, "section", 1))
+    partner_facts = theirs[0]
     mine, theirs = in_order(mine, near + far, 0), in_order(theirs, near + far, BELOW)
     logits, logprob, entropy, dlogits = loss(
-        shard, tokens[None, :], own, outer, mine, theirs, shards
+        shard, tokens[None, :], mine, theirs, shards
     )
     for i, offset in enumerate(far):
         heads[offset] = again[2 * i : 2 * i + 2]
     pieces = [piece for pair in heads for piece in pair]
     first = first_message(dlogits, pieces[0::2])
     first_in = swapped(first, "section", 1)
-    second_in = swapped(second_message(dlogits, first, pieces[1::2]), "section", 1)
-    staying = staying_gradient(which, first_in, pieces)
-    previous_grad = placed_beside(which, second_in, staying)
+    second = second_message(dlogits, first, pieces[1::2])
+    second_in = swapped(second, "section", 1)
+
+    late_own, _ = lax.optimization_barrier((own, second))
+    axes = ("vocab", "section")
+    count = lax.axis_size(axes)
+    beyond = [(i + 2, i) for i in range(0, count - 2, 2)] + [(i, i + 2) for i in range(1, count - 2, 2)]
+    outer = lax.ppermute(late_own, axes, beyond)
+    advantage = advantages(partner_facts, own, outer)
+    staying = staying_gradient(which, first_in, advantage, pieces)
+    previous_grad = placed_beside(which, second_in, advantage, staying)
     return (logits, logprob[0], entropy[0], previous_grad)
 
 

time: 55.8 us -> 53.5 us (0.959)
  the two profiles are of different devices: /device:TPU:4 before, /device:TPU:12 now
where the time goes in v8:
time: 53.5 us; the launch traced here: 53.4 us
  waiting for transfers between devices  32.2 us (60%)
  starting transfers between devices  13.4 us (25%)
  Pallas kernels  5.59 us (10%)
  local copies, waits for them, and re-layouts  1.43 us (3%)
  between operations  0.8 us (1%)
    ppermute x11, waiting for transfers between devices, swapped(): return lax.ppermute(value, axis, pairs)  21.2 us
    ppermute x1, waiting for transfers between devices, body(): outer = lax.ppermute(late_own, axes, beyond)  11 us
    ppermute x11, starting transfers between devices, swapped(): return lax.ppermute(value, axis, pairs)  8.86 us
    ppermute x1, starting transfers between devices, body(): outer = lax.ppermute(late_own, axes, beyond)  4.49 us
    unnamed x10, local copies, waits for them, and re-layouts  1.43 us
    pallas_call x1, Pallas kernels, staying_gradient(): pl.pallas_call(staying_kernel, out_shape=jax.ShapeDtypeStruct((rows, 4 *...  1.29 us
    pallas_call x2, Pallas kernels, partial_scores(): pl.pallas_call(functools.partial(partial_kernel, len(facts), len(heads)),...  1.08 us
  transfers between devices with their start and end apart: 12, of which 7 were waited for; matrix products, arithmetic and copies ran while one was open for 0% of the time, Pallas kernels for 6%

profile of v8, /device:TPU:12, one launch (start us, length us, event | category | flops | bytes accessed | tf_op | source)
XLA Modules:
  0.0 53.4 jit_solution(17911664816269676791)
XLA Ops:
  0.7 1.4 %copy-done.1 = bf16[128,5120]{1,0:T(8,128)(2,1)S(1)} copy-done((bf16[128,5120]{1,0:T(8,128)(2,1)S(1)}, bf16[128,5120]{1,0:T(8,128)(2,1)}, u32[]{:S(2)}) %copy-start.1) | copy-done | bytes 1310744
  2.2 1.6 %collective-permute-start.1 = (bf16[128,1280]{1,0:T(8,128)(2,1)S(1)}, bf16[128,1280]{1,0:T(8,128)(2,1)S(1)}, u32[]{:S(2)}, u32[]{:S(2)}) collective-permute-start(bf16[128,1280]{1,0:T(8,128)(2,1)S(1)} %get-tuple-element.26.refs_1_.refs_0_), channel_id=1, source_target_pairs={{0,4},{4,0},{8,12},{12,8},{1,5},{5,1},{9,13},{13,9},{2,6},{6,2},{1... | collective-permute-start | bytes 983048 | tf_op jit(solution)/shard_map/ppermute | solution.py:21
  3.7 0.5 collective-permute-start.4
  4.3 0.5 collective-permute-start
  5.0 1.9 %collective-permute-start.3 = (bf16[128,1280]{1,0:T(8,128)(2,1)S(1)}, bf16[128,1280]{1,0:T(8,128)(2,1)S(1)}, u32[]{:S(2)}, u32[]{:S(2)}) collective-permute-start(bf16[128,1280]{1,0:T(8,128)(2,1)S(1)} %get-tuple-element.26.refs_1_.refs_0_), channel_id=1, source_target_pairs={{0,8},{4,12},{8,0},{12,4},{1,9},{5,13},{9,1},{13,5},{2,10},{6,14},... | collective-permute-start | bytes 983048 | tf_op jit(solution)/shard_map/ppermute | solution.py:21
  6.9 6.0 %collective-permute-done.1.refs_3_.refs_1_.refs_2_ = bf16[128,1280]{1,0:T(8,128)(2,1)S(1)} collective-permute-done((bf16[128,1280]{1,0:T(8,128)(2,1)S(1)}, bf16[128,1280]{1,0:T(8,128)(2,1)S(1)}, u32[]{:S(2)}, u32[]{:S(2)}) %collective-permute-start.1) | collective-permute-done | bytes 327712 | tf_op jit(solution)/shard_map/ppermute | solution.py:21
  12.8 0.5 collective-permute-start.5
  13.3 1.0 %collective-permute-done.4.refs_6_.refs_2_.refs_5_ = bf16[128,1280]{1,0:T(8,128)(2,1)S(1)} collective-permute-done((bf16[128,1280]{1,0:T(8,128)(2,1)S(1)}, bf16[128,1280]{1,0:T(8,128)(2,1)S(1)}, u32[]{:S(2)}, u32[]{:S(2)}) %collective-permute-start.4) | collective-permute-done | bytes 327712 | tf_op jit(solution)/shard_map/ppermute | solution.py:21
  14.4 0.5 %collective-permute-start.6 = (bf16[128,1280]{1,0:T(8,128)(2,1)S(1)}, bf16[128,1280]{1,0:T(8,128)(2,1)S(1)}, u32[]{:S(2)}, u32[]{:S(2)}) collective-permute-start(bf16[128,1280]{1,0:T(8,128)(2,1)S(1)} %collective-permute-done.4.refs_6_.refs_2_.refs_5_), channel_id=1, source_target_pairs={{0,4},{4,0},{8,12},{12,8},{1,5},{5,1},{9,13},{13,9},{2,6},{6,2},{1... | collective-permute-start | bytes 983048 | tf_op jit(solution)/shard_map/ppermute | solution.py:21
  14.9 5.4 %collective-permute-done.partner_ref = bf16[128,2560]{1,0:T(8,128)(2,1)S(1)} collective-permute-done((bf16[128,2560]{1,0:T(8,128)(2,1)S(1)}, bf16[128,2560]{1,0:T(8,128)(2,1)S(1)}, u32[]{:S(2)}, u32[]{:S(2)}) %collective-permute-start) | collective-permute-done | bytes 655392 | tf_op jit(solution)/shard_map/ppermute | solution.py:21
  20.3 0.4 turned_rows.1.turned_ref
  20.7 0.7 %collective-permute-done.3.refs_5_.refs_2_.refs_4_ = bf16[128,1280]{1,0:T(8,128)(2,1)S(1)} collective-permute-done((bf16[128,1280]{1,0:T(8,128)(2,1)S(1)}, bf16[128,1280]{1,0:T(8,128)(2,1)S(1)}, u32[]{:S(2)}, u32[]{:S(2)}) %collective-permute-start.3) | collective-permute-done | bytes 327712 | tf_op jit(solution)/shard_map/ppermute | solution.py:21
  21.4 0.7 %partial_scores.2 = (f32[384,128]{1,0:T(8,128)S(1)}, f32[392,128]{1,0:T(8,128)S(1)}) custom-call(bf16[2560,256]{1,0:T(8,128)(2,1)S(1)} %turned_rows.1.turned_ref, f32[2,128]{1,0:T(2,128)S(1)} %pad_maximum_fusion.refs_0_.own_ref, bf16[128,1280]{1,0:T(8,128)(2,1)S(1)} %get-tuple-element.26.refs_1_.refs_0_, ...), custom_call_target="tpu_custom_call" | custom-call | flops 503316480 | bytes 3276800 | tf_op jit(solution)/shard_map/partial_scores/pallas_call | solution.py:120
  22.1 0.5 collective-permute-start.7
  22.6 4.3 %collective-permute-done.5.refs_0_ = bf16[128,1280]{1,0:T(8,128)(2,1)S(1)} collective-permute-done((bf16[128,1280]{1,0:T(8,128)(2,1)S(1)}, bf16[128,1280]{1,0:T(8,128)(2,1)S(1)}, u32[]{:S(2)}, u32[]{:S(2)}) %collective-permute-start.5) | collective-permute-done | bytes 327712 | tf_op jit(solution)/shard_map/ppermute | solution.py:21
  27.3 0.5 collective-permute-start.8
  27.9 3.8 %collective-permute-done.8.refs_3_ = f32[128,128]{1,0:T(8,128)S(1)} collective-permute-done((f32[128,128]{1,0:T(8,128)S(1)}, f32[128,128]{1,0:T(8,128)S(1)}, u32[]{:S(2)}, u32[]{:S(2)}) %collective-permute-start.8) | collective-permute-done | bytes 65568 | tf_op jit(solution)/shard_map/ppermute | solution.py:21
  31.7 1.0 %loss.1 = (bf16[128,512]{1,0:T(8,128)(2,1)}, f32[1,128]{1,0:T(1,128)}, f32[1,128]{1,0:T(1,128)}, bf16[128,512]{1,0:T(8,128)(2,1)S(1)}) custom-call(s32[1]{0:T(128)} %bitcast.shard_ref, s32[1,128]{1,0:T(1,128)S(1)} %bitcast.8, f32[384,128]{1,0:T(8,128)S(1)} %get-tuple-element.27.refs_0_, f32[128,128]{1,0:T(8,128)S(1)} %get-tuple-element.28.refs_1_, ...), custom_call_target="tpu_custom_call" | custom-call | flops 655360 | bytes 786432 | tf_op jit(solution)/shard_map/loss/pallas_call | solution.py:205
  33.0 0.5 collective-permute-start.11
  33.9 1.6 %collective-permute-start.9 = (bf16[128,1280]{1,0:T(8,128)(2,1)S(1)}, bf16[128,1280]{1,0:T(8,128)(2,1)S(1)}, u32[]{:S(2)}, u32[]{:S(2)}) collective-permute-start(bf16[128,1280]{1,0:T(8,128)(2,1)S(1)} %second_message.1), channel_id=1, source_target_pairs={{0,1},{1,0},{2,3},{3,2},{4,5},{5,4},{6,7},{7,6},{8,9},{9,8},{10,11... | collective-permute-start | bytes 983048 | tf_op jit(solution)/shard_map/ppermute | solution.py:21
  35.5 4.5 %collective-permute-start.10 = (f32[2,128]{1,0:T(2,128)S(1)}, f32[2,128]{1,0:T(2,128)S(1)}, u32[]{:S(2)}, u32[]{:S(2)}) collective-permute-start(f32[2,128]{1,0:T(2,128)S(1)} %pad_maximum_fusion.refs_0_.own_ref), channel_id=1, source_target_pairs={{2,0},{4,2},{6,4},{8,6},{10,8},{12,10},{14,12},{1,3},{3,5},{5,7},{... | collective-permute-start | bytes 3080 | tf_op jit(solution)/shard_map/ppermute | solution.py:402
  40.0 11.0 %collective-permute-done.10.outer_ref = f32[2,128]{1,0:T(2,128)S(1)} collective-permute-done((f32[2,128]{1,0:T(2,128)S(1)}, f32[2,128]{1,0:T(2,128)S(1)}, u32[]{:S(2)}, u32[]{:S(2)}) %collective-permute-start.10) | collective-permute-done | bytes 1056 | tf_op jit(solution)/shard_map/ppermute | solution.py:402
  51.3 1.3 %staying_gradient.1._ = bf16[128,5120]{1,0:T(8,128)(2,1)} custom-call(s32[1]{0:T(128)} %bitcast.2.which_ref, bf16[128,1792]{1,0:T(8,128)(2,1)S(1)} %collective-permute-done.11.first_ref, f32[128,128]{1,0:T(8,128)S(1)} %advantage.1.advantage_ref, bf16[128,1280]{1,0:T(8,128)(2,1)S(1)} %get-tuple-element.26.refs_1_.refs_0_, ...), custom_call_target="tpu_custom_call" | custom-call | flops 335544320 | bytes 3276800 | tf_op jit(solution)/shard_map/staying_gradient/pallas_call | solution.py:320
  52.6 0.8 %place_second.1 = bf16[128,5120]{1,0:T(8,128)(2,1)} custom-call(s32[1]{0:T(128)} %bitcast.2.which_ref, bf16[128,1280]{1,0:T(8,128)(2,1)S(1)} %collective-permute-done.9.second_ref, f32[128,128]{1,0:T(8,128)S(1)} %advantage.1.advantage_ref, bf16[128,5120]{1,0:T(8,128)(2,1)} %staying_gradient.1._), custom_call_target="tpu_custom_call", output_to_operand_aliasing={{}: (3, {})} | custom-call | tf_op jit(solution)/shard_map/place_second/pallas_call | solution.py:351
  (23 shorter events, 1.7 us)
Async XLA Ops:
  0.6 3.6 %copy-start = (bf16[128,5120]{1,0:T(8,128)(2,1)S(1)}, bf16[128,5120]{1,0:T(8,128)(2,1)}, u32[]{:S(2)}) copy-start(bf16[128,5120]{1,0:T(8,128)(2,1)} %hidden_ref.1) | copy-start | bytes 3932164
  0.7 1.4 %copy-start.1 = (bf16[128,5120]{1,0:T(8,128)(2,1)S(1)}, bf16[128,5120]{1,0:T(8,128)(2,1)}, u32[]{:S(2)}) copy-start(bf16[128,5120]{1,0:T(8,128)(2,1)} %value_ref.1) | copy-start | bytes 3932164
  2.2 12.8 %copy-start.4 = (s32[128]{0:T(128)S(1)}, s32[128]{0:T(128)}, u32[]{:S(2)}) copy-start(s32[128]{0:T(128)} %param.9) | copy-start | bytes 1540
  2.2 12.7 %copy-start.3 = (f32[128]{0:T(128)S(1)}, f32[128]{0:T(128)}, u32[]{:S(2)}) copy-start(f32[128]{0:T(128)} %param.8) | copy-start | bytes 1540
  2.2 10.7 %collective-permute-start.1 = (bf16[128,1280]{1,0:T(8,128)(2,1)S(1)}, bf16[128,1280]{1,0:T(8,128)(2,1)S(1)}, u32[]{:S(2)}, u32[]{:S(2)}) collective-permute-start(bf16[128,1280]{1,0:T(8,128)(2,1)S(1)} %get-tuple-element.26.refs_1_.refs_0_), channel_id=1, source_target_pairs={{0,4},{4,0},{8,12},{12,8},{1,5},{5,1},{9,13},{13,9},{2,6},{6,2},{1... | collective-permute-start | bytes 983048 | tf_op jit(solution)/shard_map/ppermute | solution.py:21
  3.7 10.6 %collective-permute-start.4 = (bf16[128,1280]{1,0:T(8,128)(2,1)S(1)}, bf16[128,1280]{1,0:T(8,128)(2,1)S(1)}, u32[]{:S(2)}, u32[]{:S(2)}) collective-permute-start(bf16[128,1280]{1,0:T(8,128)(2,1)S(1)} %get-tuple-element.25.refs_2_.refs_0_.refs_1_), channel_id=1, source_target_pairs={{0,8},{4,12},{8,0},{12,4},{1,9},{5,13},{9,1},{13,5},{2,10},{6,14},... | collective-permute-start | bytes 983048 | tf_op jit(solution)/shard_map/ppermute | solution.py:21
  4.3 16.0 %collective-permute-start = (bf16[128,2560]{1,0:T(8,128)(2,1)S(1)}, bf16[128,2560]{1,0:T(8,128)(2,1)S(1)}, u32[]{:S(2)}, u32[]{:S(2)}) collective-permute-start(bf16[128,2560]{1,0:T(8,128)(2,1)S(1)} %take_half.3), channel_id=1, source_target_pairs={{0,1},{1,0},{2,3},{3,2},{4,5},{5,4},{6,7},{7,6},{8,9},{9,8},{10,11... | collective-permute-start | bytes 1966088 | tf_op jit(solution)/shard_map/ppermute | solution.py:21
  4.8 15.9 %collective-permute-start.2 = (bf16[128,1280]{1,0:T(8,128)(2,1)S(1)}, bf16[128,1280]{1,0:T(8,128)(2,1)S(1)}, u32[]{:S(2)}, u32[]{:S(2)}) collective-permute-start(bf16[128,1280]{1,0:T(8,128)(2,1)S(1)} %get-tuple-element.25.refs_2_.refs_0_.refs_1_), channel_id=1, source_target_pairs={{0,4},{4,0},{8,12},{12,8},{1,5},{5,1},{9,13},{13,9},{2,6},{6,2},{1... | collective-permute-start | bytes 983048 | tf_op jit(solution)/shard_map/ppermute | solution.py:21
  5.0 16.4 %collective-permute-start.3 = (bf16[128,1280]{1,0:T(8,128)(2,1)S(1)}, bf16[128,1280]{1,0:T(8,128)(2,1)S(1)}, u32[]{:S(2)}, u32[]{:S(2)}) collective-permute-start(bf16[128,1280]{1,0:T(8,128)(2,1)S(1)} %get-tuple-element.26.refs_1_.refs_0_), channel_id=1, source_target_pairs={{0,8},{4,12},{8,0},{12,4},{1,9},{5,13},{9,1},{13,5},{2,10},{6,14},... | collective-permute-start | bytes 983048 | tf_op jit(solution)/shard_map/ppermute | solution.py:21
  12.8 14.1 %collective-permute-start.5 = (bf16[128,1280]{1,0:T(8,128)(2,1)S(1)}, bf16[128,1280]{1,0:T(8,128)(2,1)S(1)}, u32[]{:S(2)}, u32[]{:S(2)}) collective-permute-start(bf16[128,1280]{1,0:T(8,128)(2,1)S(1)} %collective-permute-done.1.refs_3_.refs_1_.refs_2_), channel_id=1, source_target_pairs={{0,8},{4,12},{8,0},{12,4},{1,9},{5,13},{9,1},{13,5},{2,10},{6,14},... | collective-permute-start | bytes 983048 | tf_op jit(solution)/shard_map/ppermute | solution.py:21
  14.4 12.6 %collective-permute-start.6 = (bf16[128,1280]{1,0:T(8,128)(2,1)S(1)}, bf16[128,1280]{1,0:T(8,128)(2,1)S(1)}, u32[]{:S(2)}, u32[]{:S(2)}) collective-permute-start(bf16[128,1280]{1,0:T(8,128)(2,1)S(1)} %collective-permute-done.4.refs_6_.refs_2_.refs_5_), channel_id=1, source_target_pairs={{0,4},{4,0},{8,12},{12,8},{1,5},{5,1},{9,13},{13,9},{2,6},{6,2},{1... | collective-permute-start | bytes 983048 | tf_op jit(solution)/shard_map/ppermute | solution.py:21
  22.1 9.6 %copy-start.2 = (s32[128]{0:T(128)S(1)}, s32[128]{0:T(128)}, u32[]{:S(2)}) copy-start(s32[128]{0:T(128)} %param.7) | copy-start | bytes 1540
  22.1 9.6 %collective-permute-start.7 = (f32[392,128]{1,0:T(8,128)S(1)}, f32[392,128]{1,0:T(8,128)S(1)}, u32[]{:S(2)}, u32[]{:S(2)}) collective-permute-start(f32[392,128]{1,0:T(8,128)S(1)} %get-tuple-element.29), channel_id=1, source_target_pairs={{0,1},{1,0},{2,3},{3,2},{4,5},{5,4},{6,7},{7,6},{8,9},{9,8},{10,11... | collective-permute-start | bytes 602120 | tf_op jit(solution)/shard_map/ppermute | solution.py:21
  27.3 4.3 %collective-permute-start.8 = (f32[128,128]{1,0:T(8,128)S(1)}, f32[128,128]{1,0:T(8,128)S(1)}, u32[]{:S(2)}, u32[]{:S(2)}) collective-permute-start(f32[128,128]{1,0:T(8,128)S(1)} %get-tuple-element.30), channel_id=1, source_target_pairs={{0,1},{1,0},{2,3},{3,2},{4,5},{5,4},{6,7},{7,6},{8,9},{9,8},{10,11... | collective-permute-start | bytes 196616 | tf_op jit(solution)/shard_map/ppermute | solution.py:21
  33.0 18.3 %collective-permute-start.11 = (bf16[128,1792]{1,0:T(8,128)(2,1)S(1)}, bf16[128,1792]{1,0:T(8,128)(2,1)S(1)}, u32[]{:S(2)}, u32[]{:S(2)}) collective-permute-start(bf16[128,1792]{1,0:T(8,128)(2,1)S(1)} %first_message.1._), channel_id=1, source_target_pairs={{0,1},{1,0},{2,3},{3,2},{4,5},{5,4},{6,7},{7,6},{8,9},{9,8},{10,11... | collective-permute-start | bytes 1376264 | tf_op jit(solution)/shard_map/ppermute | solution.py:21
  33.9 18.7 %collective-permute-start.9 = (bf16[128,1280]{1,0:T(8,128)(2,1)S(1)}, bf16[128,1280]{1,0:T(8,128)(2,1)S(1)}, u32[]{:S(2)}, u32[]{:S(2)}) collective-permute-start(bf16[128,1280]{1,0:T(8,128)(2,1)S(1)} %second_message.1), channel_id=1, source_target_pairs={{0,1},{1,0},{2,3},{3,2},{4,5},{5,4},{6,7},{7,6},{8,9},{9,8},{10,11... | collective-permute-start | bytes 983048 | tf_op jit(solution)/shard_map/ppermute | solution.py:21
  35.5 15.5 %collective-permute-start.10 = (f32[2,128]{1,0:T(2,128)S(1)}, f32[2,128]{1,0:T(2,128)S(1)}, u32[]{:S(2)}, u32[]{:S(2)}) collective-permute-start(f32[2,128]{1,0:T(2,128)S(1)} %pad_maximum_fusion.refs_0_.own_ref), channel_id=1, source_target_pairs={{2,0},{4,2},{6,4},{8,6},{10,8},{12,10},{14,12},{1,3},{3,5},{5,7},{... | collective-permute-start | bytes 3080 | tf_op jit(solution)/shard_map/ppermute | solution.py:402

commit v9 on v8

--- a/solution.py
+++ b/solution.py
@@ -70,30 +70,52 @@
     )(which, value)
 
 
-def turned_kernel(which_ref, hidden_ref, partner_ref, out_ref):
-    rows, width = partner_ref.shape
+def turned_kernel(which_ref, hidden_ref, out_ref):
+    width = out_ref.shape[0]
     block = 256
     for i in range(width // block):
         start = which_ref[0] * width + i * block
         own = hidden_ref[:, pl.ds(pl.multiple_of(start, 128), block)]
-        out_ref[i * block : (i + 1) * block, :rows] = own.T
+        out_ref[i * block : (i + 1) * block, :] = own.T
+
+
+def turned(which, hidden):
+    rows, width = hidden.shape[0], hidden.shape[1] // 2
+    return pl.pallas_call(
+        turned_kernel,
+        out_shape=jax.ShapeDtypeStruct((width, rows), BF16),
+        in_specs=[SMEM, VMEM],
+        out_specs=VMEM,
+        compiler_params=PARAMS,
+        cost_estimate=pl.CostEstimate(
+            flops=0, bytes_accessed=4 * rows * width, transcendentals=0
+        ),
+        name="turned_rows",
+    )(which, hidden)
+
+
+def beside_kernel(own_ref, first_ref, second_ref, out_ref):
+    rows = own_ref.shape[1]
+    out_ref[:, :rows] = own_ref[...]
+    block = 256
+    for i in range(own_ref.shape[0] // block):
         part = slice(i * block, (i + 1) * block)
-        out_ref[part, rows:] = partner_ref[:, part].T
-
-
-def turned(which, hidden, partner_half):
-    rows, width = partner_half.shape
-    return pl.pallas_call(
-        turned_kernel,
+        out_ref[part, rows:] = (first_ref[:, part] + second_ref[:, part]).T
+
+
+def partner_beside(own, first_half, second_half):
+    width, rows = own.shape
+    return pl.pallas_call(
+        beside_kernel,
         out_shape=jax.ShapeDtypeStruct((width, 2 * rows), BF16),
-        in_specs=[SMEM] + [VMEM] * 2,
+        in_specs=[VMEM] * 3,
         out_specs=VMEM,
         compiler_params=PARAMS,
         cost_estimate=pl.CostEstimate(
             flops=0, bytes_accessed=8 * rows * width, transcendentals=0
         ),
-        name="turned_rows",
-    )(which, hidden, partner_half)
+        name="partner_rows",
+    )(own, first_half, second_half)
 
 
 def partial_kernel(facts, count, turned_ref, *refs):
@@ -360,6 +382,12 @@
     )(which, second, advantage, gradient)
 
 
+def of_parts(value, members):
+    count = lax.axis_size("section")
+    pairs = [(p * count + i, p * count + (i ^ 1)) for p in members for i in range(count)]
+    return lax.ppermute(value, ("seq", "section"), pairs)
+
+
 def body(hidden, head_weight, tokens, rewards, group_ids):
     shards = lax.axis_size("vocab")
     which = (lax.axis_index("section") % 2).reshape(1)
@@ -368,14 +396,22 @@
     far = [o for o in range(shards) if bin(o).count("1") > 1]
 
     own = jnp.stack([rewards, (group_ids + 1).astype(F32)])
+    parts = lax.axis_size("seq")
+    leading, following = range(1, parts), range(1)
+
+    (other_half,) = take(1 - which, hidden, 1)
+    first_half = of_parts(other_half, following)
     pieces = tuple(take(which, head_weight, 2))
+    pieces, first_half = lax.optimization_barrier((pieces, first_half))
     late_hidden, _ = lax.optimization_barrier((hidden, pieces))
-    (other_half,) = take(1 - which, late_hidden, 1)
-    other_half, late_pieces = lax.optimization_barrier((other_half, pieces))
+    own_rows = turned(which, late_hidden)
+    own_rows, late_pieces = lax.optimization_barrier((own_rows, pieces))
     heads = gathered(pieces, late_pieces, "vocab")
-    partner_half = swapped(other_half, "section", 1)
-
-    rows = turned(which, hidden, partner_half)
+    arrived = [piece for o in near[1:] for piece in heads[o]]
+    other_half, _ = lax.optimization_barrier((other_half, arrived))
+    second_half = of_parts(other_half, leading)
+
+    rows = partner_beside(own_rows, first_half, second_half)
     mine, theirs = [], []
     for offsets, facts in ((near, (own,)), (far, ())):
         pieces = [piece for o in offsets for piece in heads[o]]

time: 53.5 us -> 62.3 us (1.16)
  the two profiles are of different devices: /device:TPU:12 before, /device:TPU:10 now
where the time goes in v9:
time: 62.3 us; the launch traced here: 62.1 us
  waiting for transfers between devices  34.9 us (56%)
  starting transfers between devices  18.1 us (29%)
  Pallas kernels  5.7 us (9%)
  local copies, waits for them, and re-layouts  2.64 us (4%)
  between operations  0.83 us (1%)
    ppermute x10, waiting for transfers between devices, swapped(): return lax.ppermute(value, axis, pairs)  19.2 us
    ppermute x10, starting transfers between devices, swapped(): return lax.ppermute(value, axis, pairs)  10.4 us
    ppermute x2, waiting for transfers between devices, of_parts(): return lax.ppermute(value, ('seq', 'section'), pairs)  8.69 us
    ppermute x1, waiting for transfers between devices, body(): outer = lax.ppermute(late_own, axes, beyond)  7 us
    ppermute x1, starting transfers between devices, body(): outer = lax.ppermute(late_own, axes, beyond)  4.48 us
    ppermute x2, starting transfers between devices, of_parts(): return lax.ppermute(value, ('seq', 'section'), pairs)  3.18 us
    unnamed x12, local copies, waits for them, and re-layouts  2.64 us
    pallas_call x1, Pallas kernels, staying_gradient(): pl.pallas_call(staying_kernel, out_shape=jax.ShapeDtypeStruct((rows, 4 *...  1.28 us
  transfers between devices with their start and end apart: 13, of which 9 were waited for; matrix products, arithmetic and copies ran while one was open for 0% of the time, Pallas kernels for 5%

profile of v9, /device:TPU:10, one launch (start us, length us, event | category | flops | bytes accessed | tf_op | source)
XLA Modules:
  0.0 62.1 jit_solution(8934343385789987221)
XLA Ops:
  0.7 1.3 %copy-done = bf16[128,5120]{1,0:T(8,128)(2,1)S(1)} copy-done((bf16[128,5120]{1,0:T(8,128)(2,1)S(1)}, bf16[128,5120]{1,0:T(8,128)(2,1)}, u32[]{:S(2)}) %copy-start) | copy-done | bytes 1310744
  2.0 2.5 %collective-permute-start = (bf16[128,2560]{1,0:T(8,128)(2,1)S(1)}, bf16[128,2560]{1,0:T(8,128)(2,1)S(1)}, u32[]{:S(2)}, u32[]{:S(2)}) collective-permute-start(bf16[128,2560]{1,0:T(8,128)(2,1)S(1)} %take_half.3), channel_id=1, source_target_pairs={{0,1},{1,0},{2,3},{3,2},{4,5},{5,4},{6,7},{7,6},{8,9},{9,8},{10,11... | collective-permute-start | bytes 1966088 | tf_op jit(solution)/shard_map/ppermute | solution.py:388
  4.5 1.3 %copy-done.2 = bf16[128,5120]{1,0:T(8,128)(2,1)S(1)} copy-done((bf16[128,5120]{1,0:T(8,128)(2,1)S(1)}, bf16[128,5120]{1,0:T(8,128)(2,1)}, u32[]{:S(2)}) %copy-start.2) | copy-done | bytes 1310744
  6.0 8.7 %collective-permute-done.first_ref = bf16[128,2560]{1,0:T(8,128)(2,1)S(1)} collective-permute-done((bf16[128,2560]{1,0:T(8,128)(2,1)S(1)}, bf16[128,2560]{1,0:T(8,128)(2,1)S(1)}, u32[]{:S(2)}, u32[]{:S(2)}) %collective-permute-start) | collective-permute-done | bytes 655392 | tf_op jit(solution)/shard_map/ppermute | solution.py:388
  14.9 0.6 collective-permute-start.2
  15.5 1.5 %collective-permute-start.3 = (bf16[128,1280]{1,0:T(8,128)(2,1)S(1)}, bf16[128,1280]{1,0:T(8,128)(2,1)S(1)}, u32[]{:S(2)}, u32[]{:S(2)}) collective-permute-start(bf16[128,1280]{1,0:T(8,128)(2,1)S(1)} %get-tuple-element.33.refs_1_.refs_0_), channel_id=1, source_target_pairs={{0,8},{4,12},{8,0},{12,4},{1,9},{5,13},{9,1},{13,5},{2,10},{6,14},... | collective-permute-start | bytes 983048 | tf_op jit(solution)/shard_map/ppermute | solution.py:21
  17.0 1.5 %collective-permute-start.1 = (bf16[128,1280]{1,0:T(8,128)(2,1)S(1)}, bf16[128,1280]{1,0:T(8,128)(2,1)S(1)}, u32[]{:S(2)}, u32[]{:S(2)}) collective-permute-start(bf16[128,1280]{1,0:T(8,128)(2,1)S(1)} %get-tuple-element.33.refs_1_.refs_0_), channel_id=1, source_target_pairs={{0,4},{4,0},{8,12},{12,8},{1,5},{5,1},{9,13},{13,9},{2,6},{6,2},{1... | collective-permute-start | bytes 983048 | tf_op jit(solution)/shard_map/ppermute | solution.py:21
  19.0 4.6 %collective-permute-done.2.refs_4_.refs_1_.refs_3_ = bf16[128,1280]{1,0:T(8,128)(2,1)S(1)} collective-permute-done((bf16[128,1280]{1,0:T(8,128)(2,1)S(1)}, bf16[128,1280]{1,0:T(8,128)(2,1)S(1)}, u32[]{:S(2)}, u32[]{:S(2)}) %collective-permute-start.2) | collective-permute-done | bytes 327712 | tf_op jit(solution)/shard_map/ppermute | solution.py:21
  23.5 2.5 %collective-permute-done.3.refs_5_.refs_2_.refs_4_ = bf16[128,1280]{1,0:T(8,128)(2,1)S(1)} collective-permute-done((bf16[128,1280]{1,0:T(8,128)(2,1)S(1)}, bf16[128,1280]{1,0:T(8,128)(2,1)S(1)}, u32[]{:S(2)}, u32[]{:S(2)}) %collective-permute-start.3) | collective-permute-done | bytes 327712 | tf_op jit(solution)/shard_map/ppermute | solution.py:21
  26.0 3.0 %collective-permute-done.1.refs_3_.refs_1_.refs_2_ = bf16[128,1280]{1,0:T(8,128)(2,1)S(1)} collective-permute-done((bf16[128,1280]{1,0:T(8,128)(2,1)S(1)}, bf16[128,1280]{1,0:T(8,128)(2,1)S(1)}, u32[]{:S(2)}, u32[]{:S(2)}) %collective-permute-start.1) | collective-permute-done | bytes 327712 | tf_op jit(solution)/shard_map/ppermute | solution.py:21
  29.6 0.7 %collective-permute-start.5 = (bf16[128,2560]{1,0:T(8,128)(2,1)S(1)}, bf16[128,2560]{1,0:T(8,128)(2,1)S(1)}, u32[]{:S(2)}, u32[]{:S(2)}) collective-permute-start(bf16[128,2560]{1,0:T(8,128)(2,1)S(1)} %take_half.3), channel_id=1, source_target_pairs={{16,17},{17,16},{18,19},{19,18},{20,21},{21,20},{22,23},{23,22},{2... | collective-permute-start | bytes 1966088 | tf_op jit(solution)/shard_map/ppermute | solution.py:388
  30.3 1.6 %collective-permute-start.6 = (bf16[128,1280]{1,0:T(8,128)(2,1)S(1)}, bf16[128,1280]{1,0:T(8,128)(2,1)S(1)}, u32[]{:S(2)}, u32[]{:S(2)}) collective-permute-start(bf16[128,1280]{1,0:T(8,128)(2,1)S(1)} %collective-permute-done.1.refs_3_.refs_1_.refs_2_), channel_id=1, source_target_pairs={{0,8},{4,12},{8,0},{12,4},{1,9},{5,13},{9,1},{13,5},{2,10},{6,14},... | collective-permute-start | bytes 983048 | tf_op jit(solution)/shard_map/ppermute | solution.py:21
  31.9 1.3 %collective-permute-start.7 = (bf16[128,1280]{1,0:T(8,128)(2,1)S(1)}, bf16[128,1280]{1,0:T(8,128)(2,1)S(1)}, u32[]{:S(2)}, u32[]{:S(2)}) collective-permute-start(bf16[128,1280]{1,0:T(8,128)(2,1)S(1)} %collective-permute-done.4.refs_6_.refs_2_.refs_5_), channel_id=1, source_target_pairs={{0,4},{4,0},{8,12},{12,8},{1,5},{5,1},{9,13},{13,9},{2,6},{6,2},{1... | collective-permute-start | bytes 983048 | tf_op jit(solution)/shard_map/ppermute | solution.py:21
  33.5 0.7 %partial_scores.2 = (f32[384,128]{1,0:T(8,128)S(1)}, f32[392,128]{1,0:T(8,128)S(1)}) custom-call(bf16[2560,256]{1,0:T(8,128)(2,1)S(1)} %partner_rows.1.turned_ref, f32[2,128]{1,0:T(2,128)S(1)} %pad_maximum_fusion.refs_0_.own_ref, bf16[128,1280]{1,0:T(8,128)(2,1)S(1)} %get-tuple-element.33.refs_1_.refs_0_, ...), custom_call_target="tpu_custom_call" | custom-call | flops 503316480 | bytes 3276800 | tf_op jit(solution)/shard_map/partial_scores/pallas_call | solution.py:142
  34.2 0.7 %collective-permute-start.8 = (f32[392,128]{1,0:T(8,128)S(1)}, f32[392,128]{1,0:T(8,128)S(1)}, u32[]{:S(2)}, u32[]{:S(2)}) collective-permute-start(f32[392,128]{1,0:T(8,128)S(1)} %get-tuple-element.37), channel_id=1, source_target_pairs={{0,1},{1,0},{2,3},{3,2},{4,5},{5,4},{6,7},{7,6},{8,9},{9,8},{10,11... | collective-permute-start | bytes 602120 | tf_op jit(solution)/shard_map/ppermute | solution.py:21
  34.9 2.5 %collective-permute-done.6.refs_0_ = bf16[128,1280]{1,0:T(8,128)(2,1)S(1)} collective-permute-done((bf16[128,1280]{1,0:T(8,128)(2,1)S(1)}, bf16[128,1280]{1,0:T(8,128)(2,1)S(1)}, u32[]{:S(2)}, u32[]{:S(2)}) %collective-permute-start.6) | collective-permute-done | bytes 327712 | tf_op jit(solution)/shard_map/ppermute | solution.py:21
  37.4 1.5 %collective-permute-done.7.refs_1_ = bf16[128,1280]{1,0:T(8,128)(2,1)S(1)} collective-permute-done((bf16[128,1280]{1,0:T(8,128)(2,1)S(1)}, bf16[128,1280]{1,0:T(8,128)(2,1)S(1)}, u32[]{:S(2)}, u32[]{:S(2)}) %collective-permute-start.7) | collective-permute-done | bytes 327712 | tf_op jit(solution)/shard_map/ppermute | solution.py:21
  39.8 4.6 %collective-permute-done.9.refs_3_ = f32[128,128]{1,0:T(8,128)S(1)} collective-permute-done((f32[128,128]{1,0:T(8,128)S(1)}, f32[128,128]{1,0:T(8,128)S(1)}, u32[]{:S(2)}, u32[]{:S(2)}) %collective-permute-start.9) | collective-permute-done | bytes 65568 | tf_op jit(solution)/shard_map/ppermute | solution.py:21
  44.4 1.0 %loss.1 = (bf16[128,512]{1,0:T(8,128)(2,1)}, f32[1,128]{1,0:T(1,128)}, f32[1,128]{1,0:T(1,128)}, bf16[128,512]{1,0:T(8,128)(2,1)S(1)}) custom-call(s32[1]{0:T(128)} %bitcast.shard_ref, s32[1,128]{1,0:T(1,128)S(1)} %bitcast.8, f32[384,128]{1,0:T(8,128)S(1)} %get-tuple-element.35.refs_0_, f32[128,128]{1,0:T(8,128)S(1)} %get-tuple-element.36.refs_1_, ...), custom_call_target="tpu_custom_call" | custom-call | flops 655360 | bytes 786432 | tf_op jit(solution)/shard_map/loss/pallas_call | solution.py:227
  46.6 1.6 %collective-permute-start.10 = (bf16[128,1280]{1,0:T(8,128)(2,1)S(1)}, bf16[128,1280]{1,0:T(8,128)(2,1)S(1)}, u32[]{:S(2)}, u32[]{:S(2)}) collective-permute-start(bf16[128,1280]{1,0:T(8,128)(2,1)S(1)} %second_message.1), channel_id=1, source_target_pairs={{0,1},{1,0},{2,3},{3,2},{4,5},{5,4},{6,7},{7,6},{8,9},{9,8},{10,11... | collective-permute-start | bytes 983048 | tf_op jit(solution)/shard_map/ppermute | solution.py:21
  48.2 4.5 %collective-permute-start.11 = (f32[2,128]{1,0:T(2,128)S(1)}, f32[2,128]{1,0:T(2,128)S(1)}, u32[]{:S(2)}, u32[]{:S(2)}) collective-permute-start(f32[2,128]{1,0:T(2,128)S(1)} %pad_maximum_fusion.refs_0_.own_ref), channel_id=1, source_target_pairs={{2,0},{4,2},{6,4},{8,6},{10,8},{12,10},{14,12},{1,3},{3,5},{5,7},{... | collective-permute-start | bytes 3080 | tf_op jit(solution)/shard_map/ppermute | solution.py:438
  52.7 7.0 %collective-permute-done.11.outer_ref = f32[2,128]{1,0:T(2,128)S(1)} collective-permute-done((f32[2,128]{1,0:T(2,128)S(1)}, f32[2,128]{1,0:T(2,128)S(1)}, u32[]{:S(2)}, u32[]{:S(2)}) %collective-permute-start.11) | collective-permute-done | bytes 1056 | tf_op jit(solution)/shard_map/ppermute | solution.py:438
  60.0 1.3 %staying_gradient.1._ = bf16[128,5120]{1,0:T(8,128)(2,1)} custom-call(s32[1]{0:T(128)} %bitcast.2.which_ref, bf16[128,1792]{1,0:T(8,128)(2,1)S(1)} %collective-permute-done.12.first_ref, f32[128,128]{1,0:T(8,128)S(1)} %advantage.1.advantage_ref, bf16[128,1280]{1,0:T(8,128)(2,1)S(1)} %get-tuple-element.33.refs_1_.refs_0_, ...), custom_call_target="tpu_custom_call" | custom-call | flops 335544320 | bytes 3276800 | tf_op jit(solution)/shard_map/staying_gradient/pallas_call | solution.py:342
  61.3 0.8 %place_second.1 = bf16[128,5120]{1,0:T(8,128)(2,1)} custom-call(s32[1]{0:T(128)} %bitcast.2.which_ref, bf16[128,1280]{1,0:T(8,128)(2,1)S(1)} %collective-permute-done.10.second_ref, f32[128,128]{1,0:T(8,128)S(1)} %advantage.1.advantage_ref, bf16[128,5120]{1,0:T(8,128)(2,1)} %staying_gradient.1._), custom_call_target="tpu_custom_call", output_to_operand_aliasing={{}: (3, {})} | custom-call | tf_op jit(solution)/shard_map/place_second/pallas_call | solution.py:373
  (28 shorter events, 4.1 us)
Async XLA Ops:
  0.6 1.3 %copy-start = (bf16[128,5120]{1,0:T(8,128)(2,1)S(1)}, bf16[128,5120]{1,0:T(8,128)(2,1)}, u32[]{:S(2)}) copy-start(bf16[128,5120]{1,0:T(8,128)(2,1)} %hidden_ref) | copy-start | bytes 3932164
  2.0 12.7 %copy-start.1 = (bf16[128,5120]{1,0:T(8,128)(2,1)S(1)}, bf16[128,5120]{1,0:T(8,128)(2,1)}, u32[]{:S(2)}) copy-start(bf16[128,5120]{1,0:T(8,128)(2,1)} %hidden_ref) | copy-start | bytes 3932164
  2.0 12.6 %collective-permute-start = (bf16[128,2560]{1,0:T(8,128)(2,1)S(1)}, bf16[128,2560]{1,0:T(8,128)(2,1)S(1)}, u32[]{:S(2)}, u32[]{:S(2)}) collective-permute-start(bf16[128,2560]{1,0:T(8,128)(2,1)S(1)} %take_half.3), channel_id=1, source_target_pairs={{0,1},{1,0},{2,3},{3,2},{4,5},{5,4},{6,7},{7,6},{8,9},{9,8},{10,11... | collective-permute-start | bytes 1966088 | tf_op jit(solution)/shard_map/ppermute | solution.py:388
  4.5 1.3 %copy-start.2 = (bf16[128,5120]{1,0:T(8,128)(2,1)S(1)}, bf16[128,5120]{1,0:T(8,128)(2,1)}, u32[]{:S(2)}) copy-start(bf16[128,5120]{1,0:T(8,128)(2,1)} %value_ref.2) | copy-start | bytes 3932164
  5.9 27.3 %copy-start.5 = (s32[128]{0:T(128)S(1)}, s32[128]{0:T(128)}, u32[]{:S(2)}) copy-start(s32[128]{0:T(128)} %param.9) | copy-start | bytes 1540
  5.9 27.3 %copy-start.4 = (f32[128]{0:T(128)S(1)}, f32[128]{0:T(128)}, u32[]{:S(2)}) copy-start(f32[128]{0:T(128)} %param.8) | copy-start | bytes 1540
  14.9 8.7 %collective-permute-start.2 = (bf16[128,1280]{1,0:T(8,128)(2,1)S(1)}, bf16[128,1280]{1,0:T(8,128)(2,1)S(1)}, u32[]{:S(2)}, u32[]{:S(2)}) collective-permute-start(bf16[128,1280]{1,0:T(8,128)(2,1)S(1)} %get-tuple-element.32.refs_2_.refs_0_.refs_1_), channel_id=1, source_target_pairs={{0,4},{4,0},{8,12},{12,8},{1,5},{5,1},{9,13},{13,9},{2,6},{6,2},{1... | collective-permute-start | bytes 983048 | tf_op jit(solution)/shard_map/ppermute | solution.py:21
  15.5 10.6 %collective-permute-start.3 = (bf16[128,1280]{1,0:T(8,128)(2,1)S(1)}, bf16[128,1280]{1,0:T(8,128)(2,1)S(1)}, u32[]{:S(2)}, u32[]{:S(2)}) collective-permute-start(bf16[128,1280]{1,0:T(8,128)(2,1)S(1)} %get-tuple-element.33.refs_1_.refs_0_), channel_id=1, source_target_pairs={{0,8},{4,12},{8,0},{12,4},{1,9},{5,13},{9,1},{13,5},{2,10},{6,14},... | collective-permute-start | bytes 983048 | tf_op jit(solution)/shard_map/ppermute | solution.py:21
  17.0 12.0 %collective-permute-start.1 = (bf16[128,1280]{1,0:T(8,128)(2,1)S(1)}, bf16[128,1280]{1,0:T(8,128)(2,1)S(1)}, u32[]{:S(2)}, u32[]{:S(2)}) collective-permute-start(bf16[128,1280]{1,0:T(8,128)(2,1)S(1)} %get-tuple-element.33.refs_1_.refs_0_), channel_id=1, source_target_pairs={{0,4},{4,0},{8,12},{12,8},{1,5},{5,1},{9,13},{13,9},{2,6},{6,2},{1... | collective-permute-start | bytes 983048 | tf_op jit(solution)/shard_map/ppermute | solution.py:21
  18.5 11.1 %collective-permute-start.4 = (bf16[128,1280]{1,0:T(8,128)(2,1)S(1)}, bf16[128,1280]{1,0:T(8,128)(2,1)S(1)}, u32[]{:S(2)}, u32[]{:S(2)}) collective-permute-start(bf16[128,1280]{1,0:T(8,128)(2,1)S(1)} %get-tuple-element.32.refs_2_.refs_0_.refs_1_), channel_id=1, source_target_pairs={{0,8},{4,12},{8,0},{12,4},{1,9},{5,13},{9,1},{13,5},{2,10},{6,14},... | collective-permute-start | bytes 983048 | tf_op jit(solution)/shard_map/ppermute | solution.py:21
  29.6 3.7 %collective-permute-start.5 = (bf16[128,2560]{1,0:T(8,128)(2,1)S(1)}, bf16[128,2560]{1,0:T(8,128)(2,1)S(1)}, u32[]{:S(2)}, u32[]{:S(2)}) collective-permute-start(bf16[128,2560]{1,0:T(8,128)(2,1)S(1)} %take_half.3), channel_id=1, source_target_pairs={{16,17},{17,16},{18,19},{19,18},{20,21},{21,20},{22,23},{23,22},{2... | collective-permute-start | bytes 1966088 | tf_op jit(solution)/shard_map/ppermute | solution.py:388
  30.3 7.1 %collective-permute-start.6 = (bf16[128,1280]{1,0:T(8,128)(2,1)S(1)}, bf16[128,1280]{1,0:T(8,128)(2,1)S(1)}, u32[]{:S(2)}, u32[]{:S(2)}) collective-permute-start(bf16[128,1280]{1,0:T(8,128)(2,1)S(1)} %collective-permute-done.1.refs_3_.refs_1_.refs_2_), channel_id=1, source_target_pairs={{0,8},{4,12},{8,0},{12,4},{1,9},{5,13},{9,1},{13,5},{2,10},{6,14},... | collective-permute-start | bytes 983048 | tf_op jit(solution)/shard_map/ppermute | solution.py:21
  31.9 7.1 %collective-permute-start.7 = (bf16[128,1280]{1,0:T(8,128)(2,1)S(1)}, bf16[128,1280]{1,0:T(8,128)(2,1)S(1)}, u32[]{:S(2)}, u32[]{:S(2)}) collective-permute-start(bf16[128,1280]{1,0:T(8,128)(2,1)S(1)} %collective-permute-done.4.refs_6_.refs_2_.refs_5_), channel_id=1, source_target_pairs={{0,4},{4,0},{8,12},{12,8},{1,5},{5,1},{9,13},{13,9},{2,6},{6,2},{1... | collective-permute-start | bytes 983048 | tf_op jit(solution)/shard_map/ppermute | solution.py:21
  34.2 10.2 %copy-start.3 = (s32[128]{0:T(128)S(1)}, s32[128]{0:T(128)}, u32[]{:S(2)}) copy-start(s32[128]{0:T(128)} %param.7) | copy-start | bytes 1540
  34.2 10.2 %collective-permute-start.8 = (f32[392,128]{1,0:T(8,128)S(1)}, f32[392,128]{1,0:T(8,128)S(1)}, u32[]{:S(2)}, u32[]{:S(2)}) collective-permute-start(f32[392,128]{1,0:T(8,128)S(1)} %get-tuple-element.37), channel_id=1, source_target_pairs={{0,1},{1,0},{2,3},{3,2},{4,5},{5,4},{6,7},{7,6},{8,9},{9,8},{10,11... | collective-permute-start | bytes 602120 | tf_op jit(solution)/shard_map/ppermute | solution.py:21
  39.3 5.1 %collective-permute-start.9 = (f32[128,128]{1,0:T(8,128)S(1)}, f32[128,128]{1,0:T(8,128)S(1)}, u32[]{:S(2)}, u32[]{:S(2)}) collective-permute-start(f32[128,128]{1,0:T(8,128)S(1)} %get-tuple-element.38), channel_id=1, source_target_pairs={{0,1},{1,0},{2,3},{3,2},{4,5},{5,4},{6,7},{7,6},{8,9},{9,8},{10,11... | collective-permute-start | bytes 196616 | tf_op jit(solution)/shard_map/ppermute | solution.py:21
  45.7 14.3 %collective-permute-start.12 = (bf16[128,1792]{1,0:T(8,128)(2,1)S(1)}, bf16[128,1792]{1,0:T(8,128)(2,1)S(1)}, u32[]{:S(2)}, u32[]{:S(2)}) collective-permute-start(bf16[128,1792]{1,0:T(8,128)(2,1)S(1)} %first_message.1._), channel_id=1, source_target_pairs={{0,1},{1,0},{2,3},{3,2},{4,5},{5,4},{6,7},{7,6},{8,9},{9,8},{10,11... | collective-permute-start | bytes 1376264 | tf_op jit(solution)/shard_map/ppermute | solution.py:21
  46.6 14.7 %collective-permute-start.10 = (bf16[128,1280]{1,0:T(8,128)(2,1)S(1)}, bf16[128,1280]{1,0:T(8,128)(2,1)S(1)}, u32[]{:S(2)}, u32[]{:S(2)}) collective-permute-start(bf16[128,1280]{1,0:T(8,128)(2,1)S(1)} %second_message.1), channel_id=1, source_target_pairs={{0,1},{1,0},{2,3},{3,2},{4,5},{5,4},{6,7},{7,6},{8,9},{9,8},{10,11... | collective-permute-start | bytes 983048 | tf_op jit(solution)/shard_map/ppermute | solution.py:21
  48.2 11.5 %collective-permute-start.11 = (f32[2,128]{1,0:T(2,128)S(1)}, f32[2,128]{1,0:T(2,128)S(1)}, u32[]{:S(2)}, u32[]{:S(2)}) collective-permute-start(f32[2,128]{1,0:T(2,128)S(1)} %pad_maximum_fusion.refs_0_.own_ref), channel_id=1, source_target_pairs={{2,0},{4,2},{6,4},{8,6},{10,8},{12,10},{14,12},{1,3},{3,5},{5,7},{... | collective-permute-start | bytes 3080 | tf_op jit(solution)/shard_map/ppermute | solution.py:438

commit v10 on v7

--- a/solution.py
+++ b/solution.py
@@ -347,9 +347,6 @@
     heads = gathered(pieces, late_pieces, "vocab")
     partner_half = swapped(other_half, "section", 1)
 
-    late_own, _ = lax.optimization_barrier((own, (heads[near[1]][1], heads[near[-1]][0])))
-    outer = lax.ppermute(late_own, axes, beside + [(b, a) for a, b in beside])
-    partner_half, outer = lax.optimization_barrier((partner_half, outer))
     rows = turned(which, hidden, partner_half)
     mine, theirs = [], []
     for offsets, facts in ((near, (own,)), (far, ())):
@@ -357,6 +354,9 @@
         kept, sent, *again = partial_scores(rows, pieces, facts)
         mine.append(kept)
         theirs.append(swapped(sent, "section", 1))
+    late_own, kept = lax.optimization_barrier((own, kept))
+    mine[-1] = kept
+    outer = lax.ppermute(late_own, axes, beside + [(b, a) for a, b in beside])
     mine, theirs = in_order(mine, near + far, 0), in_order(theirs, near + far, BELOW)
     logits, logprob, entropy, dlogits = loss(
         shard, tokens[None, :], own, outer, mine, theirs, shards

time: 55.8 us -> 57.1 us (1.023)
  waiting for transfers between devices: 32 us -> 33.3 us
    ppermute x11, starting transfers between devices: 10.6 us -> 11.7 us  [swapped(): return lax.ppermute(value, axis, pairs)]
    ppermute x1, starting transfers between devices: 5.41 us -> 4.29 us  [body(): outer = lax.ppermute(late_own, axes, beside + [(b, a) for a, b in beside])]
    ppermute x1, waiting for transfers between devices: 3.63 us -> 4.74 us  [body(): outer = lax.ppermute(late_own, axes, beside + [(b, a) for a, b in beside])]
where the time goes in v10:
time: 57.1 us; the launch traced here: 57 us
  waiting for transfers between devices  33.3 us (58%)
  starting transfers between devices  16 us (28%)
  Pallas kernels  5.41 us (9%)
  local copies, waits for them, and re-layouts  1.43 us (3%)
  between operations  0.8 us (1%)
    ppermute x11, waiting for transfers between devices, swapped(): return lax.ppermute(value, axis, pairs)  28.6 us
    ppermute x11, starting transfers between devices, swapped(): return lax.ppermute(value, axis, pairs)  11.7 us
    ppermute x1, waiting for transfers between devices, body(): outer = lax.ppermute(late_own, axes, beside + [(b, a) for a, b in beside])  4.74 us
    ppermute x1, starting transfers between devices, body(): outer = lax.ppermute(late_own, axes, beside + [(b, a) for a, b in beside])  4.29 us
    unnamed x10, local copies, waits for them, and re-layouts  1.43 us
    pallas_call x1, Pallas kernels, staying_gradient(): pl.pallas_call(staying_kernel, out_shape=jax.ShapeDtypeStruct((rows, 4 *...  1.26 us
  transfers between devices with their start and end apart: 12, of which 8 were waited for; matrix products, arithmetic and copies ran while one was open for 0% of the time, Pallas kernels for 6%

profile of v10, /device:TPU:4, one launch (start us, length us, event | category | flops | bytes accessed | tf_op | source)
XLA Modules:
  0.0 57.0 jit_solution(16866363656389722203)
XLA Ops:
  0.7 1.4 %copy-done.1 = bf16[128,5120]{1,0:T(8,128)(2,1)S(1)} copy-done((bf16[128,5120]{1,0:T(8,128)(2,1)S(1)}, bf16[128,5120]{1,0:T(8,128)(2,1)}, u32[]{:S(2)}) %copy-start.1) | copy-done | bytes 1310744
  2.2 1.6 %collective-permute-start.1 = (bf16[128,1280]{1,0:T(8,128)(2,1)S(1)}, bf16[128,1280]{1,0:T(8,128)(2,1)S(1)}, u32[]{:S(2)}, u32[]{:S(2)}) collective-permute-start(bf16[128,1280]{1,0:T(8,128)(2,1)S(1)} %get-tuple-element.29.refs_1_.refs_0_), channel_id=1, source_target_pairs={{0,4},{4,0},{8,12},{12,8},{1,5},{5,1},{9,13},{13,9},{2,6},{6,2},{1... | collective-permute-start | bytes 983048 | tf_op jit(solution)/shard_map/ppermute | solution.py:21
  3.7 0.5 collective-permute-start.3
  4.3 1.6 %collective-permute-start = (bf16[128,2560]{1,0:T(8,128)(2,1)S(1)}, bf16[128,2560]{1,0:T(8,128)(2,1)S(1)}, u32[]{:S(2)}, u32[]{:S(2)}) collective-permute-start(bf16[128,2560]{1,0:T(8,128)(2,1)S(1)} %take_half.3), channel_id=1, source_target_pairs={{0,1},{1,0},{2,3},{3,2},{4,5},{5,4},{6,7},{7,6},{8,9},{9,8},{10,11... | collective-permute-start | bytes 1966088 | tf_op jit(solution)/shard_map/ppermute | solution.py:21
  6.0 0.5 collective-permute-start.6
  6.5 1.5 %collective-permute-start.7 = (bf16[128,1280]{1,0:T(8,128)(2,1)S(1)}, bf16[128,1280]{1,0:T(8,128)(2,1)S(1)}, u32[]{:S(2)}, u32[]{:S(2)}) collective-permute-start(bf16[128,1280]{1,0:T(8,128)(2,1)S(1)} %get-tuple-element.29.refs_1_.refs_0_), channel_id=1, source_target_pairs={{0,8},{4,12},{8,0},{12,4},{1,9},{5,13},{9,1},{13,5},{2,10},{6,14},... | collective-permute-start | bytes 983048 | tf_op jit(solution)/shard_map/ppermute | solution.py:21
  8.0 4.8 %collective-permute-done.1.refs_3_.refs_1_.refs_2_ = bf16[128,1280]{1,0:T(8,128)(2,1)S(1)} collective-permute-done((bf16[128,1280]{1,0:T(8,128)(2,1)S(1)}, bf16[128,1280]{1,0:T(8,128)(2,1)S(1)}, u32[]{:S(2)}, u32[]{:S(2)}) %collective-permute-start.1) | collective-permute-done | bytes 327712 | tf_op jit(solution)/shard_map/ppermute | solution.py:21
  12.8 1.5 %collective-permute-done.3.refs_6_.refs_2_.refs_5_ = bf16[128,1280]{1,0:T(8,128)(2,1)S(1)} collective-permute-done((bf16[128,1280]{1,0:T(8,128)(2,1)S(1)}, bf16[128,1280]{1,0:T(8,128)(2,1)S(1)}, u32[]{:S(2)}, u32[]{:S(2)}) %collective-permute-start.3) | collective-permute-done | bytes 327712 | tf_op jit(solution)/shard_map/ppermute | solution.py:21
  14.4 0.5 collective-permute-start.4
  14.9 5.4 %collective-permute-done.partner_ref = bf16[128,2560]{1,0:T(8,128)(2,1)S(1)} collective-permute-done((bf16[128,2560]{1,0:T(8,128)(2,1)S(1)}, bf16[128,2560]{1,0:T(8,128)(2,1)S(1)}, u32[]{:S(2)}, u32[]{:S(2)}) %collective-permute-start) | collective-permute-done | bytes 655392 | tf_op jit(solution)/shard_map/ppermute | solution.py:21
  20.3 0.4 turned_rows.1.turned_ref
  20.7 0.7 %collective-permute-done.7.refs_5_.refs_2_.refs_4_ = bf16[128,1280]{1,0:T(8,128)(2,1)S(1)} collective-permute-done((bf16[128,1280]{1,0:T(8,128)(2,1)S(1)}, bf16[128,1280]{1,0:T(8,128)(2,1)S(1)}, u32[]{:S(2)}, u32[]{:S(2)}) %collective-permute-start.7) | collective-permute-done | bytes 327712 | tf_op jit(solution)/shard_map/ppermute | solution.py:21
  21.4 0.7 %partial_scores.3 = (f32[384,128]{1,0:T(8,128)S(1)}, f32[392,128]{1,0:T(8,128)S(1)}) custom-call(bf16[2560,256]{1,0:T(8,128)(2,1)S(1)} %turned_rows.1.turned_ref, f32[2,128]{1,0:T(2,128)S(1)} %pad_maximum_fusion.refs_0_.own_ref, bf16[128,1280]{1,0:T(8,128)(2,1)S(1)} %get-tuple-element.29.refs_1_.refs_0_, ...), custom_call_target="tpu_custom_call" | custom-call | flops 503316480 | bytes 3276800 | tf_op jit(solution)/shard_map/partial_scores/pallas_call | solution.py:120
  22.1 1.6 %collective-permute-start.8 = (f32[392,128]{1,0:T(8,128)S(1)}, f32[392,128]{1,0:T(8,128)S(1)}, u32[]{:S(2)}, u32[]{:S(2)}) collective-permute-start(f32[392,128]{1,0:T(8,128)S(1)} %get-tuple-element.32), channel_id=1, source_target_pairs={{0,1},{1,0},{2,3},{3,2},{4,5},{5,4},{6,7},{7,6},{8,9},{9,8},{10,11... | collective-permute-start | bytes 602120 | tf_op jit(solution)/shard_map/ppermute | solution.py:21
  23.7 3.2 %collective-permute-done.2.refs_0_ = bf16[128,1280]{1,0:T(8,128)(2,1)S(1)} collective-permute-done((bf16[128,1280]{1,0:T(8,128)(2,1)S(1)}, bf16[128,1280]{1,0:T(8,128)(2,1)S(1)}, u32[]{:S(2)}, u32[]{:S(2)}) %collective-permute-start.2) | collective-permute-done | bytes 327712 | tf_op jit(solution)/shard_map/ppermute | solution.py:21
  27.3 1.6 %collective-permute-start.9 = (f32[128,128]{1,0:T(8,128)S(1)}, f32[128,128]{1,0:T(8,128)S(1)}, u32[]{:S(2)}, u32[]{:S(2)}) collective-permute-start(f32[128,128]{1,0:T(8,128)S(1)} %get-tuple-element.33), channel_id=1, source_target_pairs={{0,1},{1,0},{2,3},{3,2},{4,5},{5,4},{6,7},{7,6},{8,9},{9,8},{10,11... | collective-permute-start | bytes 196616 | tf_op jit(solution)/shard_map/ppermute | solution.py:21
  29.0 4.3 %collective-permute-start.5 = (f32[2,128]{1,0:T(2,128)S(1)}, f32[2,128]{1,0:T(2,128)S(1)}, u32[]{:S(2)}, u32[]{:S(2)}) collective-permute-start(f32[2,128]{1,0:T(2,128)S(1)} %pad_maximum_fusion.refs_0_.own_ref), channel_id=1, source_target_pairs={{1,2},{3,4},{5,6},{7,8},{9,10},{11,12},{13,14},{2,1},{4,3},{6,5},{... | collective-permute-start | bytes 3080 | tf_op jit(solution)/shard_map/ppermute | solution.py:359
  33.3 4.7 %collective-permute-done.5.outer_ref = f32[2,128]{1,0:T(2,128)S(1)} collective-permute-done((f32[2,128]{1,0:T(2,128)S(1)}, f32[2,128]{1,0:T(2,128)S(1)}, u32[]{:S(2)}, u32[]{:S(2)}) %collective-permute-start.5) | collective-permute-done | bytes 1056 | tf_op jit(solution)/shard_map/ppermute | solution.py:359
  38.0 1.1 %loss.1 = (bf16[128,512]{1,0:T(8,128)(2,1)}, f32[1,128]{1,0:T(1,128)}, f32[1,128]{1,0:T(1,128)}, bf16[128,512]{1,0:T(8,128)(2,1)S(1)}) custom-call(s32[1]{0:T(128)} %bitcast.shard_ref, s32[1,128]{1,0:T(1,128)S(1)} %bitcast.8, f32[2,128]{1,0:T(2,128)S(1)} %pad_maximum_fusion.refs_0_.own_ref, f32[2,128]{1,0:T(2,128)S(1)} %collective-permute-done.5.outer_ref, ...), custom_call_target="tpu_custom_call" | custom-call | flops 655360 | bytes 786432 | tf_op jit(solution)/shard_map/loss/pallas_call | solution.py:190
  39.9 2.1 %collective-permute-start.10 = (bf16[128,1280]{1,0:T(8,128)(2,1)S(1)}, bf16[128,1280]{1,0:T(8,128)(2,1)S(1)}, u32[]{:S(2)}, u32[]{:S(2)}) collective-permute-start(bf16[128,1280]{1,0:T(8,128)(2,1)S(1)} %second_message.1), channel_id=1, source_target_pairs={{0,1},{1,0},{2,3},{3,2},{4,5},{5,4},{6,7},{7,6},{8,9},{9,8},{10,11... | collective-permute-start | bytes 983048 | tf_op jit(solution)/shard_map/ppermute | solution.py:21
  42.0 10.7 %collective-permute-done.11.first_ref = bf16[128,1792]{1,0:T(8,128)(2,1)S(1)} collective-permute-done((bf16[128,1792]{1,0:T(8,128)(2,1)S(1)}, bf16[128,1792]{1,0:T(8,128)(2,1)S(1)}, u32[]{:S(2)}, u32[]{:S(2)}) %collective-permute-start.11) | collective-permute-done | bytes 458784 | tf_op jit(solution)/shard_map/ppermute | solution.py:21
  52.7 1.3 %staying_gradient.1._ = bf16[128,5120]{1,0:T(8,128)(2,1)} custom-call(s32[1]{0:T(128)} %bitcast.4.which_ref, bf16[128,1792]{1,0:T(8,128)(2,1)S(1)} %collective-permute-done.11.first_ref, bf16[128,1280]{1,0:T(8,128)(2,1)S(1)} %get-tuple-element.29.refs_1_.refs_0_, bf16[128,1280]{1,0:T(8,128)(2,1)S(1)} %get-tuple-element.28.refs_2_.refs_0_.refs_1_, ...), custom_call_target="tpu_custom_call" | custom-call | flops 335544320 | bytes 3276800 | tf_op jit(solution)/shard_map/staying_gradient/pallas_call | solution.py:293
  54.0 2.2 %collective-permute-done.10.second_ref = bf16[128,1280]{1,0:T(8,128)(2,1)S(1)} collective-permute-done((bf16[128,1280]{1,0:T(8,128)(2,1)S(1)}, bf16[128,1280]{1,0:T(8,128)(2,1)S(1)}, u32[]{:S(2)}, u32[]{:S(2)}) %collective-permute-start.10) | collective-permute-done | bytes 327712 | tf_op jit(solution)/shard_map/ppermute | solution.py:21
  56.2 0.8 %place_second.1 = bf16[128,5120]{1,0:T(8,128)(2,1)} custom-call(s32[1]{0:T(128)} %bitcast.4.which_ref, bf16[128,1280]{1,0:T(8,128)(2,1)S(1)} %collective-permute-done.10.second_ref, bf16[128,5120]{1,0:T(8,128)(2,1)} %staying_gradient.1._), custom_call_target="tpu_custom_call", output_to_operand_aliasing={{}: (2, {})} | custom-call | tf_op jit(solution)/shard_map/place_second/pallas_call | solution.py:320
  (22 shorter events, 1.3 us)
Async XLA Ops:
  0.6 3.6 %copy-start = (bf16[128,5120]{1,0:T(8,128)(2,1)S(1)}, bf16[128,5120]{1,0:T(8,128)(2,1)}, u32[]{:S(2)}) copy-start(bf16[128,5120]{1,0:T(8,128)(2,1)} %hidden_ref.1) | copy-start | bytes 3932164
  0.7 1.4 %copy-start.1 = (bf16[128,5120]{1,0:T(8,128)(2,1)S(1)}, bf16[128,5120]{1,0:T(8,128)(2,1)}, u32[]{:S(2)}) copy-start(bf16[128,5120]{1,0:T(8,128)(2,1)} %value_ref.1) | copy-start | bytes 3932164
  2.2 12.8 %copy-start.4 = (s32[128]{0:T(128)S(1)}, s32[128]{0:T(128)}, u32[]{:S(2)}) copy-start(s32[128]{0:T(128)} %param.9) | copy-start | bytes 1540
  2.2 12.7 %copy-start.3 = (f32[128]{0:T(128)S(1)}, f32[128]{0:T(128)}, u32[]{:S(2)}) copy-start(f32[128]{0:T(128)} %param.8) | copy-start | bytes 1540
  2.2 10.7 %collective-permute-start.1 = (bf16[128,1280]{1,0:T(8,128)(2,1)S(1)}, bf16[128,1280]{1,0:T(8,128)(2,1)S(1)}, u32[]{:S(2)}, u32[]{:S(2)}) collective-permute-start(bf16[128,1280]{1,0:T(8,128)(2,1)S(1)} %get-tuple-element.29.refs_1_.refs_0_), channel_id=1, source_target_pairs={{0,4},{4,0},{8,12},{12,8},{1,5},{5,1},{9,13},{13,9},{2,6},{6,2},{1... | collective-permute-start | bytes 983048 | tf_op jit(solution)/shard_map/ppermute | solution.py:21
  3.7 10.6 %collective-permute-start.3 = (bf16[128,1280]{1,0:T(8,128)(2,1)S(1)}, bf16[128,1280]{1,0:T(8,128)(2,1)S(1)}, u32[]{:S(2)}, u32[]{:S(2)}) collective-permute-start(bf16[128,1280]{1,0:T(8,128)(2,1)S(1)} %get-tuple-element.28.refs_2_.refs_0_.refs_1_), channel_id=1, source_target_pairs={{0,8},{4,12},{8,0},{12,4},{1,9},{5,13},{9,1},{13,5},{2,10},{6,14},... | collective-permute-start | bytes 983048 | tf_op jit(solution)/shard_map/ppermute | solution.py:21
  4.3 16.0 %collective-permute-start = (bf16[128,2560]{1,0:T(8,128)(2,1)S(1)}, bf16[128,2560]{1,0:T(8,128)(2,1)S(1)}, u32[]{:S(2)}, u32[]{:S(2)}) collective-permute-start(bf16[128,2560]{1,0:T(8,128)(2,1)S(1)} %take_half.3), channel_id=1, source_target_pairs={{0,1},{1,0},{2,3},{3,2},{4,5},{5,4},{6,7},{7,6},{8,9},{9,8},{10,11... | collective-permute-start | bytes 1966088 | tf_op jit(solution)/shard_map/ppermute | solution.py:21
  6.0 14.7 %collective-permute-start.6 = (bf16[128,1280]{1,0:T(8,128)(2,1)S(1)}, bf16[128,1280]{1,0:T(8,128)(2,1)S(1)}, u32[]{:S(2)}, u32[]{:S(2)}) collective-permute-start(bf16[128,1280]{1,0:T(8,128)(2,1)S(1)} %get-tuple-element.28.refs_2_.refs_0_.refs_1_), channel_id=1, source_target_pairs={{0,4},{4,0},{8,12},{12,8},{1,5},{5,1},{9,13},{13,9},{2,6},{6,2},{1... | collective-permute-start | bytes 983048 | tf_op jit(solution)/shard_map/ppermute | solution.py:21
  6.5 14.9 %collective-permute-start.7 = (bf16[128,1280]{1,0:T(8,128)(2,1)S(1)}, bf16[128,1280]{1,0:T(8,128)(2,1)S(1)}, u32[]{:S(2)}, u32[]{:S(2)}) collective-permute-start(bf16[128,1280]{1,0:T(8,128)(2,1)S(1)} %get-tuple-element.29.refs_1_.refs_0_), channel_id=1, source_target_pairs={{0,8},{4,12},{8,0},{12,4},{1,9},{5,13},{9,1},{13,5},{2,10},{6,14},... | collective-permute-start | bytes 983048 | tf_op jit(solution)/shard_map/ppermute | solution.py:21
  12.8 14.1 %collective-permute-start.2 = (bf16[128,1280]{1,0:T(8,128)(2,1)S(1)}, bf16[128,1280]{1,0:T(8,128)(2,1)S(1)}, u32[]{:S(2)}, u32[]{:S(2)}) collective-permute-start(bf16[128,1280]{1,0:T(8,128)(2,1)S(1)} %collective-permute-done.1.refs_3_.refs_1_.refs_2_), channel_id=1, source_target_pairs={{0,8},{4,12},{8,0},{12,4},{1,9},{5,13},{9,1},{13,5},{2,10},{6,14},... | collective-permute-start | bytes 983048 | tf_op jit(solution)/shard_map/ppermute | solution.py:21
  14.4 12.6 %collective-permute-start.4 = (bf16[128,1280]{1,0:T(8,128)(2,1)S(1)}, bf16[128,1280]{1,0:T(8,128)(2,1)S(1)}, u32[]{:S(2)}, u32[]{:S(2)}) collective-permute-start(bf16[128,1280]{1,0:T(8,128)(2,1)S(1)} %collective-permute-done.3.refs_6_.refs_2_.refs_5_), channel_id=1, source_target_pairs={{0,4},{4,0},{8,12},{12,8},{1,5},{5,1},{9,13},{13,9},{2,6},{6,2},{1... | collective-permute-start | bytes 983048 | tf_op jit(solution)/shard_map/ppermute | solution.py:21
  22.1 15.9 %copy-start.2 = (s32[128]{0:T(128)S(1)}, s32[128]{0:T(128)}, u32[]{:S(2)}) copy-start(s32[128]{0:T(128)} %param.7) | copy-start | bytes 1540
  22.1 15.9 %collective-permute-start.8 = (f32[392,128]{1,0:T(8,128)S(1)}, f32[392,128]{1,0:T(8,128)S(1)}, u32[]{:S(2)}, u32[]{:S(2)}) collective-permute-start(f32[392,128]{1,0:T(8,128)S(1)} %get-tuple-element.32), channel_id=1, source_target_pairs={{0,1},{1,0},{2,3},{3,2},{4,5},{5,4},{6,7},{7,6},{8,9},{9,8},{10,11... | collective-permute-start | bytes 602120 | tf_op jit(solution)/shard_map/ppermute | solution.py:21
  27.3 10.7 %collective-permute-start.9 = (f32[128,128]{1,0:T(8,128)S(1)}, f32[128,128]{1,0:T(8,128)S(1)}, u32[]{:S(2)}, u32[]{:S(2)}) collective-permute-start(f32[128,128]{1,0:T(8,128)S(1)} %get-tuple-element.33), channel_id=1, source_target_pairs={{0,1},{1,0},{2,3},{3,2},{4,5},{5,4},{6,7},{7,6},{8,9},{9,8},{10,11... | collective-permute-start | bytes 196616 | tf_op jit(solution)/shard_map/ppermute | solution.py:21
  29.0 9.0 %collective-permute-start.5 = (f32[2,128]{1,0:T(2,128)S(1)}, f32[2,128]{1,0:T(2,128)S(1)}, u32[]{:S(2)}, u32[]{:S(2)}) collective-permute-start(f32[2,128]{1,0:T(2,128)S(1)} %pad_maximum_fusion.refs_0_.own_ref), channel_id=1, source_target_pairs={{1,2},{3,4},{5,6},{7,8},{9,10},{11,12},{13,14},{2,1},{4,3},{6,5},{... | collective-permute-start | bytes 3080 | tf_op jit(solution)/shard_map/ppermute | solution.py:359
  39.5 13.2 %collective-permute-start.11 = (bf16[128,1792]{1,0:T(8,128)(2,1)S(1)}, bf16[128,1792]{1,0:T(8,128)(2,1)S(1)}, u32[]{:S(2)}, u32[]{:S(2)}) collective-permute-start(bf16[128,1792]{1,0:T(8,128)(2,1)S(1)} %first_message.1._), channel_id=1, source_target_pairs={{0,1},{1,0},{2,3},{3,2},{4,5},{5,4},{6,7},{7,6},{8,9},{9,8},{10,11... | collective-permute-start | bytes 1376264 | tf_op jit(solution)/shard_map/ppermute | solution.py:21
  39.9 16.3 %collective-permute-start.10 = (bf16[128,1280]{1,0:T(8,128)(2,1)S(1)}, bf16[128,1280]{1,0:T(8,128)(2,1)S(1)}, u32[]{:S(2)}, u32[]{:S(2)}) collective-permute-start(bf16[128,1280]{1,0:T(8,128)(2,1)S(1)} %second_message.1), channel_id=1, source_target_pairs={{0,1},{1,0},{2,3},{3,2},{4,5},{5,4},{6,7},{7,6},{8,9},{9,8},{10,11... | collective-permute-start | bytes 983048 | tf_op jit(solution)/shard_map/ppermute | solution.py:21

commit v11 on v8

--- a/solution.py
+++ b/solution.py
@@ -163,6 +163,7 @@
         in_specs=[VMEM] * 3,
         out_specs=VMEM,
         compiler_params=PARAMS,
+        cost_estimate=pl.CostEstimate(flops=20 * 10**9, bytes_accessed=0, transcendentals=0),
         name="advantage",
     )(partner, own, outer)
 
@@ -274,7 +275,7 @@
         in_specs=[VMEM, ANY] + [VMEM] * len(heads),
         out_specs=VMEM,
         compiler_params=PARAMS,
-        cost_estimate=gradient_cost(rows, columns, width),
+        cost_estimate=gradient_cost(32 * rows, columns, width),
         name="second_message",
     )(dlogits, first, *heads)
 
@@ -395,7 +396,7 @@
     second = second_message(dlogits, first, pieces[1::2])
     second_in = swapped(second, "section", 1)
 
-    late_own, _ = lax.optimization_barrier((own, second))
+    late_own, _ = lax.optimization_barrier((own, first))
     axes = ("vocab", "section")
     count = lax.axis_size(axes)
     beyond = [(i + 2, i) for i in range(0, count - 2, 2)] + [(i, i + 2) for i in range(1, count - 2, 2)]

time: 53.5 us -> 52.4 us (0.979)
  the two profiles are of different devices: /device:TPU:12 before, /device:TPU:0 now
where the time goes in v11:
time: 52.4 us; the launch traced here: 52.2 us
  waiting for transfers between devices  23.7 us (45%)
  starting transfers between devices  20.7 us (40%)
  Pallas kernels  5.59 us (11%)
  local copies, waits for them, and re-layouts  1.43 us (3%)
  between operations  0.79 us (2%)
    ppermute x11, waiting for transfers between devices, swapped(): return lax.ppermute(value, axis, pairs)  22.7 us
    ppermute x11, starting transfers between devices, swapped(): return lax.ppermute(value, axis, pairs)  19.4 us
    unnamed x10, local copies, waits for them, and re-layouts  1.43 us
    pallas_call x1, Pallas kernels, staying_gradient(): pl.pallas_call(staying_kernel, out_shape=jax.ShapeDtypeStruct((rows, 4 *...  1.29 us
    ppermute x1, starting transfers between devices, body(): outer = lax.ppermute(late_own, axes, beyond)  1.28 us
    pallas_call x2, Pallas kernels, partial_scores(): pl.pallas_call(functools.partial(partial_kernel, len(facts), len(heads)),...  1.08 us
  transfers between devices with their start and end apart: 12, of which 7 were waited for; matrix products, arithmetic and copies ran while one was open for 0% of the time, Pallas kernels for 7%

profile of v11, /device:TPU:0, one launch (start us, length us, event | category | flops | bytes accessed | tf_op | source)
XLA Modules:
  0.0 52.2 jit_solution(3850677801026496972)
XLA Ops:
  0.7 1.4 %copy-done.1 = bf16[128,5120]{1,0:T(8,128)(2,1)S(1)} copy-done((bf16[128,5120]{1,0:T(8,128)(2,1)S(1)}, bf16[128,5120]{1,0:T(8,128)(2,1)}, u32[]{:S(2)}) %copy-start.1) | copy-done | bytes 1310744
  2.2 3.0 %collective-permute-start.1 = (bf16[128,1280]{1,0:T(8,128)(2,1)S(1)}, bf16[128,1280]{1,0:T(8,128)(2,1)S(1)}, u32[]{:S(2)}, u32[]{:S(2)}) collective-permute-start(bf16[128,1280]{1,0:T(8,128)(2,1)S(1)} %get-tuple-element.26.refs_1_.refs_0_), channel_id=1, source_target_pairs={{0,4},{4,0},{8,12},{12,8},{1,5},{5,1},{9,13},{13,9},{2,6},{6,2},{1... | collective-permute-start | bytes 983048 | tf_op jit(solution)/shard_map/ppermute | solution.py:21
  5.2 1.5 %collective-permute-start.4 = (bf16[128,1280]{1,0:T(8,128)(2,1)S(1)}, bf16[128,1280]{1,0:T(8,128)(2,1)S(1)}, u32[]{:S(2)}, u32[]{:S(2)}) collective-permute-start(bf16[128,1280]{1,0:T(8,128)(2,1)S(1)} %get-tuple-element.25.refs_2_.refs_0_.refs_1_), channel_id=1, source_target_pairs={{0,8},{4,12},{8,0},{12,4},{1,9},{5,13},{9,1},{13,5},{2,10},{6,14},... | collective-permute-start | bytes 983048 | tf_op jit(solution)/shard_map/ppermute | solution.py:21
  6.8 1.6 %collective-permute-start = (bf16[128,2560]{1,0:T(8,128)(2,1)S(1)}, bf16[128,2560]{1,0:T(8,128)(2,1)S(1)}, u32[]{:S(2)}, u32[]{:S(2)}) collective-permute-start(bf16[128,2560]{1,0:T(8,128)(2,1)S(1)} %take_half.3), channel_id=1, source_target_pairs={{0,1},{1,0},{2,3},{3,2},{4,5},{5,4},{6,7},{7,6},{8,9},{9,8},{10,11... | collective-permute-start | bytes 1966088 | tf_op jit(solution)/shard_map/ppermute | solution.py:21
  8.4 0.5 %collective-permute-start.2 = (bf16[128,1280]{1,0:T(8,128)(2,1)S(1)}, bf16[128,1280]{1,0:T(8,128)(2,1)S(1)}, u32[]{:S(2)}, u32[]{:S(2)}) collective-permute-start(bf16[128,1280]{1,0:T(8,128)(2,1)S(1)} %get-tuple-element.25.refs_2_.refs_0_.refs_1_), channel_id=1, source_target_pairs={{0,4},{4,0},{8,12},{12,8},{1,5},{5,1},{9,13},{13,9},{2,6},{6,2},{1... | collective-permute-start | bytes 983048 | tf_op jit(solution)/shard_map/ppermute | solution.py:21
  9.0 0.5 collective-permute-start.3
  9.5 4.3 %collective-permute-done.1.refs_3_.refs_1_.refs_2_ = bf16[128,1280]{1,0:T(8,128)(2,1)S(1)} collective-permute-done((bf16[128,1280]{1,0:T(8,128)(2,1)S(1)}, bf16[128,1280]{1,0:T(8,128)(2,1)S(1)}, u32[]{:S(2)}, u32[]{:S(2)}) %collective-permute-start.1) | collective-permute-done | bytes 327712 | tf_op jit(solution)/shard_map/ppermute | solution.py:21
  13.7 2.1 %collective-permute-start.5 = (bf16[128,1280]{1,0:T(8,128)(2,1)S(1)}, bf16[128,1280]{1,0:T(8,128)(2,1)S(1)}, u32[]{:S(2)}, u32[]{:S(2)}) collective-permute-start(bf16[128,1280]{1,0:T(8,128)(2,1)S(1)} %collective-permute-done.1.refs_3_.refs_1_.refs_2_), channel_id=1, source_target_pairs={{0,8},{4,12},{8,0},{12,4},{1,9},{5,13},{9,1},{13,5},{2,10},{6,14},... | collective-permute-start | bytes 983048 | tf_op jit(solution)/shard_map/ppermute | solution.py:21
  15.8 1.5 %collective-permute-start.6 = (bf16[128,1280]{1,0:T(8,128)(2,1)S(1)}, bf16[128,1280]{1,0:T(8,128)(2,1)S(1)}, u32[]{:S(2)}, u32[]{:S(2)}) collective-permute-start(bf16[128,1280]{1,0:T(8,128)(2,1)S(1)} %collective-permute-done.4.refs_6_.refs_2_.refs_5_), channel_id=1, source_target_pairs={{0,4},{4,0},{8,12},{12,8},{1,5},{5,1},{9,13},{13,9},{2,6},{6,2},{1... | collective-permute-start | bytes 983048 | tf_op jit(solution)/shard_map/ppermute | solution.py:21
  17.3 5.4 %collective-permute-done.partner_ref = bf16[128,2560]{1,0:T(8,128)(2,1)S(1)} collective-permute-done((bf16[128,2560]{1,0:T(8,128)(2,1)S(1)}, bf16[128,2560]{1,0:T(8,128)(2,1)S(1)}, u32[]{:S(2)}, u32[]{:S(2)}) %collective-permute-start) | collective-permute-done | bytes 655392 | tf_op jit(solution)/shard_map/ppermute | solution.py:21
  23.2 0.7 %partial_scores.2 = (f32[384,128]{1,0:T(8,128)S(1)}, f32[392,128]{1,0:T(8,128)S(1)}) custom-call(bf16[2560,256]{1,0:T(8,128)(2,1)S(1)} %turned_rows.1.turned_ref, f32[2,128]{1,0:T(2,128)S(1)} %pad_maximum_fusion.refs_0_.own_ref, bf16[128,1280]{1,0:T(8,128)(2,1)S(1)} %get-tuple-element.26.refs_1_.refs_0_, ...), custom_call_target="tpu_custom_call" | custom-call | flops 503316480 | bytes 3276800 | tf_op jit(solution)/shard_map/partial_scores/pallas_call | solution.py:120
  23.9 1.6 %collective-permute-start.7 = (f32[392,128]{1,0:T(8,128)S(1)}, f32[392,128]{1,0:T(8,128)S(1)}, u32[]{:S(2)}, u32[]{:S(2)}) collective-permute-start(f32[392,128]{1,0:T(8,128)S(1)} %get-tuple-element.29), channel_id=1, source_target_pairs={{0,1},{1,0},{2,3},{3,2},{4,5},{5,4},{6,7},{7,6},{8,9},{9,8},{10,11... | collective-permute-start | bytes 602120 | tf_op jit(solution)/shard_map/ppermute | solution.py:21
  25.5 2.9 %collective-permute-done.5.refs_0_ = bf16[128,1280]{1,0:T(8,128)(2,1)S(1)} collective-permute-done((bf16[128,1280]{1,0:T(8,128)(2,1)S(1)}, bf16[128,1280]{1,0:T(8,128)(2,1)S(1)}, u32[]{:S(2)}, u32[]{:S(2)}) %collective-permute-start.5) | collective-permute-done | bytes 327712 | tf_op jit(solution)/shard_map/ppermute | solution.py:21
  28.8 1.6 %collective-permute-start.8 = (f32[128,128]{1,0:T(8,128)S(1)}, f32[128,128]{1,0:T(8,128)S(1)}, u32[]{:S(2)}, u32[]{:S(2)}) collective-permute-start(f32[128,128]{1,0:T(8,128)S(1)} %get-tuple-element.30), channel_id=1, source_target_pairs={{0,1},{1,0},{2,3},{3,2},{4,5},{5,4},{6,7},{7,6},{8,9},{9,8},{10,11... | collective-permute-start | bytes 196616 | tf_op jit(solution)/shard_map/ppermute | solution.py:21
  30.4 2.7 %collective-permute-done.8.refs_3_ = f32[128,128]{1,0:T(8,128)S(1)} collective-permute-done((f32[128,128]{1,0:T(8,128)S(1)}, f32[128,128]{1,0:T(8,128)S(1)}, u32[]{:S(2)}, u32[]{:S(2)}) %collective-permute-start.8) | collective-permute-done | bytes 65568 | tf_op jit(solution)/shard_map/ppermute | solution.py:21
  33.1 1.0 %loss.1 = (bf16[128,512]{1,0:T(8,128)(2,1)}, f32[1,128]{1,0:T(1,128)}, f32[1,128]{1,0:T(1,128)}, bf16[128,512]{1,0:T(8,128)(2,1)S(1)}) custom-call(s32[1]{0:T(128)} %bitcast.shard_ref, s32[1,128]{1,0:T(1,128)S(1)} %bitcast.8, f32[384,128]{1,0:T(8,128)S(1)} %get-tuple-element.27.refs_0_, f32[128,128]{1,0:T(8,128)S(1)} %get-tuple-element.28.refs_1_, ...), custom_call_target="tpu_custom_call" | custom-call | flops 655360 | bytes 786432 | tf_op jit(solution)/shard_map/loss/pallas_call | solution.py:206
  34.4 1.6 %collective-permute-start.11 = (bf16[128,1792]{1,0:T(8,128)(2,1)S(1)}, bf16[128,1792]{1,0:T(8,128)(2,1)S(1)}, u32[]{:S(2)}, u32[]{:S(2)}) collective-permute-start(bf16[128,1792]{1,0:T(8,128)(2,1)S(1)} %first_message.1._), channel_id=1, source_target_pairs={{0,1},{1,0},{2,3},{3,2},{4,5},{5,4},{6,7},{7,6},{8,9},{9,8},{10,11... | collective-permute-start | bytes 1376264 | tf_op jit(solution)/shard_map/ppermute | solution.py:21
  36.1 1.3 %collective-permute-start.10 = (f32[2,128]{1,0:T(2,128)S(1)}, f32[2,128]{1,0:T(2,128)S(1)}, u32[]{:S(2)}, u32[]{:S(2)}) collective-permute-start(f32[2,128]{1,0:T(2,128)S(1)} %pad_maximum_fusion.refs_0_.own_ref), channel_id=1, source_target_pairs={{2,0},{4,2},{6,4},{8,6},{10,8},{12,10},{14,12},{1,3},{3,5},{5,7},{... | collective-permute-start | bytes 3080 | tf_op jit(solution)/shard_map/ppermute | solution.py:403
  37.7 3.7 %collective-permute-start.9 = (bf16[128,1280]{1,0:T(8,128)(2,1)S(1)}, bf16[128,1280]{1,0:T(8,128)(2,1)S(1)}, u32[]{:S(2)}, u32[]{:S(2)}) collective-permute-start(bf16[128,1280]{1,0:T(8,128)(2,1)S(1)} %second_message.1), channel_id=1, source_target_pairs={{0,1},{1,0},{2,3},{3,2},{4,5},{5,4},{6,7},{7,6},{8,9},{9,8},{10,11... | collective-permute-start | bytes 983048 | tf_op jit(solution)/shard_map/ppermute | solution.py:21
  41.4 1.0 %collective-permute-done.10.outer_ref = f32[2,128]{1,0:T(2,128)S(1)} collective-permute-done((f32[2,128]{1,0:T(2,128)S(1)}, f32[2,128]{1,0:T(2,128)S(1)}, u32[]{:S(2)}, u32[]{:S(2)}) %collective-permute-start.10) | collective-permute-done | bytes 1056 | tf_op jit(solution)/shard_map/ppermute | solution.py:403
  42.7 5.2 %collective-permute-done.11.first_ref = bf16[128,1792]{1,0:T(8,128)(2,1)S(1)} collective-permute-done((bf16[128,1792]{1,0:T(8,128)(2,1)S(1)}, bf16[128,1792]{1,0:T(8,128)(2,1)S(1)}, u32[]{:S(2)}, u32[]{:S(2)}) %collective-permute-start.11) | collective-permute-done | bytes 458784 | tf_op jit(solution)/shard_map/ppermute | solution.py:21
  48.0 1.3 %staying_gradient.1._ = bf16[128,5120]{1,0:T(8,128)(2,1)} custom-call(s32[1]{0:T(128)} %bitcast.2.which_ref, bf16[128,1792]{1,0:T(8,128)(2,1)S(1)} %collective-permute-done.11.first_ref, f32[128,128]{1,0:T(8,128)S(1)} %advantage.1.advantage_ref, bf16[128,1280]{1,0:T(8,128)(2,1)S(1)} %get-tuple-element.26.refs_1_.refs_0_, ...), custom_call_target="tpu_custom_call" | custom-call | flops 335544320 | bytes 3276800 | tf_op jit(solution)/shard_map/staying_gradient/pallas_call | solution.py:321
  49.3 2.2 %collective-permute-done.9.second_ref = bf16[128,1280]{1,0:T(8,128)(2,1)S(1)} collective-permute-done((bf16[128,1280]{1,0:T(8,128)(2,1)S(1)}, bf16[128,1280]{1,0:T(8,128)(2,1)S(1)}, u32[]{:S(2)}, u32[]{:S(2)}) %collective-permute-start.9) | collective-permute-done | bytes 327712 | tf_op jit(solution)/shard_map/ppermute | solution.py:21
  51.5 0.8 %place_second.1 = bf16[128,5120]{1,0:T(8,128)(2,1)} custom-call(s32[1]{0:T(128)} %bitcast.2.which_ref, bf16[128,1280]{1,0:T(8,128)(2,1)S(1)} %collective-permute-done.9.second_ref, f32[128,128]{1,0:T(8,128)S(1)} %advantage.1.advantage_ref, bf16[128,5120]{1,0:T(8,128)(2,1)} %staying_gradient.1._), custom_call_target="tpu_custom_call", output_to_operand_aliasing={{}: (3, {})} | custom-call | tf_op jit(solution)/shard_map/place_second/pallas_call | solution.py:352
  (23 shorter events, 1.9 us)
Async XLA Ops:
  0.6 6.1 %copy-start = (bf16[128,5120]{1,0:T(8,128)(2,1)S(1)}, bf16[128,5120]{1,0:T(8,128)(2,1)}, u32[]{:S(2)}) copy-start(bf16[128,5120]{1,0:T(8,128)(2,1)} %hidden_ref.1) | copy-start | bytes 3932164
  0.7 1.4 %copy-start.1 = (bf16[128,5120]{1,0:T(8,128)(2,1)S(1)}, bf16[128,5120]{1,0:T(8,128)(2,1)}, u32[]{:S(2)}) copy-start(bf16[128,5120]{1,0:T(8,128)(2,1)} %value_ref.1) | copy-start | bytes 3932164
  2.2 15.2 %copy-start.4 = (s32[128]{0:T(128)S(1)}, s32[128]{0:T(128)}, u32[]{:S(2)}) copy-start(s32[128]{0:T(128)} %param.9) | copy-start | bytes 1540
  2.2 15.1 %copy-start.3 = (f32[128]{0:T(128)S(1)}, f32[128]{0:T(128)}, u32[]{:S(2)}) copy-start(f32[128]{0:T(128)} %param.8) | copy-start | bytes 1540
  2.2 11.5 %collective-permute-start.1 = (bf16[128,1280]{1,0:T(8,128)(2,1)S(1)}, bf16[128,1280]{1,0:T(8,128)(2,1)S(1)}, u32[]{:S(2)}, u32[]{:S(2)}) collective-permute-start(bf16[128,1280]{1,0:T(8,128)(2,1)S(1)} %get-tuple-element.26.refs_1_.refs_0_), channel_id=1, source_target_pairs={{0,4},{4,0},{8,12},{12,8},{1,5},{5,1},{9,13},{13,9},{2,6},{6,2},{1... | collective-permute-start | bytes 983048 | tf_op jit(solution)/shard_map/ppermute | solution.py:21
  5.2 10.6 %collective-permute-start.4 = (bf16[128,1280]{1,0:T(8,128)(2,1)S(1)}, bf16[128,1280]{1,0:T(8,128)(2,1)S(1)}, u32[]{:S(2)}, u32[]{:S(2)}) collective-permute-start(bf16[128,1280]{1,0:T(8,128)(2,1)S(1)} %get-tuple-element.25.refs_2_.refs_0_.refs_1_), channel_id=1, source_target_pairs={{0,8},{4,12},{8,0},{12,4},{1,9},{5,13},{9,1},{13,5},{2,10},{6,14},... | collective-permute-start | bytes 983048 | tf_op jit(solution)/shard_map/ppermute | solution.py:21
  6.8 16.0 %collective-permute-start = (bf16[128,2560]{1,0:T(8,128)(2,1)S(1)}, bf16[128,2560]{1,0:T(8,128)(2,1)S(1)}, u32[]{:S(2)}, u32[]{:S(2)}) collective-permute-start(bf16[128,2560]{1,0:T(8,128)(2,1)S(1)} %take_half.3), channel_id=1, source_target_pairs={{0,1},{1,0},{2,3},{3,2},{4,5},{5,4},{6,7},{7,6},{8,9},{9,8},{10,11... | collective-permute-start | bytes 1966088 | tf_op jit(solution)/shard_map/ppermute | solution.py:21
  8.4 14.7 %collective-permute-start.2 = (bf16[128,1280]{1,0:T(8,128)(2,1)S(1)}, bf16[128,1280]{1,0:T(8,128)(2,1)S(1)}, u32[]{:S(2)}, u32[]{:S(2)}) collective-permute-start(bf16[128,1280]{1,0:T(8,128)(2,1)S(1)} %get-tuple-element.25.refs_2_.refs_0_.refs_1_), channel_id=1, source_target_pairs={{0,4},{4,0},{8,12},{12,8},{1,5},{5,1},{9,13},{13,9},{2,6},{6,2},{1... | collective-permute-start | bytes 983048 | tf_op jit(solution)/shard_map/ppermute | solution.py:21
  9.0 14.2 %collective-permute-start.3 = (bf16[128,1280]{1,0:T(8,128)(2,1)S(1)}, bf16[128,1280]{1,0:T(8,128)(2,1)S(1)}, u32[]{:S(2)}, u32[]{:S(2)}) collective-permute-start(bf16[128,1280]{1,0:T(8,128)(2,1)S(1)} %get-tuple-element.26.refs_1_.refs_0_), channel_id=1, source_target_pairs={{0,8},{4,12},{8,0},{12,4},{1,9},{5,13},{9,1},{13,5},{2,10},{6,14},... | collective-permute-start | bytes 983048 | tf_op jit(solution)/shard_map/ppermute | solution.py:21
  13.7 14.7 %collective-permute-start.5 = (bf16[128,1280]{1,0:T(8,128)(2,1)S(1)}, bf16[128,1280]{1,0:T(8,128)(2,1)S(1)}, u32[]{:S(2)}, u32[]{:S(2)}) collective-permute-start(bf16[128,1280]{1,0:T(8,128)(2,1)S(1)} %collective-permute-done.1.refs_3_.refs_1_.refs_2_), channel_id=1, source_target_pairs={{0,8},{4,12},{8,0},{12,4},{1,9},{5,13},{9,1},{13,5},{2,10},{6,14},... | collective-permute-start | bytes 983048 | tf_op jit(solution)/shard_map/ppermute | solution.py:21
  15.8 12.6 %collective-permute-start.6 = (bf16[128,1280]{1,0:T(8,128)(2,1)S(1)}, bf16[128,1280]{1,0:T(8,128)(2,1)S(1)}, u32[]{:S(2)}, u32[]{:S(2)}) collective-permute-start(bf16[128,1280]{1,0:T(8,128)(2,1)S(1)} %collective-permute-done.4.refs_6_.refs_2_.refs_5_), channel_id=1, source_target_pairs={{0,4},{4,0},{8,12},{12,8},{1,5},{5,1},{9,13},{13,9},{2,6},{6,2},{1... | collective-permute-start | bytes 983048 | tf_op jit(solution)/shard_map/ppermute | solution.py:21
  23.9 9.2 %copy-start.2 = (s32[128]{0:T(128)S(1)}, s32[128]{0:T(128)}, u32[]{:S(2)}) copy-start(s32[128]{0:T(128)} %param.7) | copy-start | bytes 1540
  23.9 9.2 %collective-permute-start.7 = (f32[392,128]{1,0:T(8,128)S(1)}, f32[392,128]{1,0:T(8,128)S(1)}, u32[]{:S(2)}, u32[]{:S(2)}) collective-permute-start(f32[392,128]{1,0:T(8,128)S(1)} %get-tuple-element.29), channel_id=1, source_target_pairs={{0,1},{1,0},{2,3},{3,2},{4,5},{5,4},{6,7},{7,6},{8,9},{9,8},{10,11... | collective-permute-start | bytes 602120 | tf_op jit(solution)/shard_map/ppermute | solution.py:21
  28.8 4.3 %collective-permute-start.8 = (f32[128,128]{1,0:T(8,128)S(1)}, f32[128,128]{1,0:T(8,128)S(1)}, u32[]{:S(2)}, u32[]{:S(2)}) collective-permute-start(f32[128,128]{1,0:T(8,128)S(1)} %get-tuple-element.30), channel_id=1, source_target_pairs={{0,1},{1,0},{2,3},{3,2},{4,5},{5,4},{6,7},{7,6},{8,9},{9,8},{10,11... | collective-permute-start | bytes 196616 | tf_op jit(solution)/shard_map/ppermute | solution.py:21
  34.4 13.5 %collective-permute-start.11 = (bf16[128,1792]{1,0:T(8,128)(2,1)S(1)}, bf16[128,1792]{1,0:T(8,128)(2,1)S(1)}, u32[]{:S(2)}, u32[]{:S(2)}) collective-permute-start(bf16[128,1792]{1,0:T(8,128)(2,1)S(1)} %first_message.1._), channel_id=1, source_target_pairs={{0,1},{1,0},{2,3},{3,2},{4,5},{5,4},{6,7},{7,6},{8,9},{9,8},{10,11... | collective-permute-start | bytes 1376264 | tf_op jit(solution)/shard_map/ppermute | solution.py:21
  36.1 6.4 %collective-permute-start.10 = (f32[2,128]{1,0:T(2,128)S(1)}, f32[2,128]{1,0:T(2,128)S(1)}, u32[]{:S(2)}, u32[]{:S(2)}) collective-permute-start(f32[2,128]{1,0:T(2,128)S(1)} %pad_maximum_fusion.refs_0_.own_ref), channel_id=1, source_target_pairs={{2,0},{4,2},{6,4},{8,6},{10,8},{12,10},{14,12},{1,3},{3,5},{5,7},{... | collective-permute-start | bytes 3080 | tf_op jit(solution)/shard_map/ppermute | solution.py:403
  37.7 13.7 %collective-permute-start.9 = (bf16[128,1280]{1,0:T(8,128)(2,1)S(1)}, bf16[128,1280]{1,0:T(8,128)(2,1)S(1)}, u32[]{:S(2)}, u32[]{:S(2)}) collective-permute-start(bf16[128,1280]{1,0:T(8,128)(2,1)S(1)} %second_message.1), channel_id=1, source_target_pairs={{0,1},{1,0},{2,3},{3,2},{4,5},{5,4},{6,7},{7,6},{8,9},{9,8},{10,11... | collective-permute-start | bytes 983048 | tf_op jit(solution)/shard_map/ppermute | solution.py:21

commit v12 on v11

--- a/solution.py
+++ b/solution.py
@@ -168,53 +168,57 @@
     )(partner, own, outer)
 
 
-def loss_kernel(parts, shards, shard_ref, tokens_ref, *refs):
-    mine, theirs = refs[:parts], refs[parts : 2 * parts]
-    logits_ref, logprob_ref, entropy_ref, dlogits_ref = refs[2 * parts :]
-    shard = shard_ref[0]
-    rows, columns = dlogits_ref.shape
+def softmax_of(shard, tokens, mine, theirs, shards):
+    scores = jnp.concatenate(
+        [a[...] + b[: a.shape[0], :] for a, b in zip(mine, theirs)], axis=0
+    )
+    columns, rows = scores.shape
     shard_rows = columns // shards
-
-    lengths = [ref.shape[0] for ref in mine]
-    scores = jnp.concatenate(
-        [a[...] + b[:n, :] for a, b, n in zip(mine, theirs, lengths)], axis=0
-    )
-    tokens = tokens_ref[...]
     relative = ((tokens // shard_rows) ^ shard) * shard_rows + tokens % shard_rows
     chosen = lax.broadcasted_iota(jnp.int32, (columns, rows), 0) == relative
     row_max = jnp.max(scores, axis=0, keepdims=True)
     unnormed = jnp.exp(scores - row_max)
-    denominator = jnp.sum(unnormed, axis=0, keepdims=True)
-    probabilities = unnormed / denominator
-    dlogits = probabilities - jnp.where(chosen, 1.0, 0.0)
+    return scores, chosen, row_max, unnormed, jnp.sum(unnormed, axis=0, keepdims=True)
+
+
+def outputs_kernel(parts, shards, shard_ref, tokens_ref, *refs):
+    mine, theirs = refs[:parts], refs[parts : 2 * parts]
+    logits_ref, logprob_ref, entropy_ref = refs[2 * parts :]
+    scores, chosen, row_max, unnormed, denominator = softmax_of(
+        shard_ref[0], tokens_ref[...], mine, theirs, shards
+    )
+    shard_rows = scores.shape[0] // shards
     for i in range(shards):
         block = slice(i * shard_rows, (i + 1) * shard_rows)
-        dlogits_ref[:, block] = dlogits[block, :].T.astype(BF16)
-        place = pl.multiple_of((shard ^ i) * shard_rows, 128)
+        place = pl.multiple_of((shard_ref[0] ^ i) * shard_rows, 128)
         logits_ref[:, pl.ds(place, shard_rows)] = scores[block, :].T.astype(BF16)
     log_total = row_max + jnp.log(denominator)
     picked = jnp.sum(jnp.where(chosen, scores, 0.0), axis=0, keepdims=True)
     logprob_ref[...] = picked - log_total
+    probabilities = unnormed / denominator
     entropy_ref[...] = log_total - jnp.sum(probabilities * scores, axis=0, keepdims=True)
 
 
-def loss(shard, tokens, mine, theirs, shards):
+def softmax_params(rows, columns):
+    return pltpu.CompilerParams(vmem_limit_bytes=2 * 1024**2 + 32 * rows * columns)
+
+
+def outputs(shard, tokens, mine, theirs, shards):
     rows = tokens.shape[1]
     columns = sum(part.shape[0] for part in mine)
     flat = jax.ShapeDtypeStruct((1, rows), F32)
-    wide = jax.ShapeDtypeStruct((rows, columns), BF16)
-    return pl.pallas_call(
-        functools.partial(loss_kernel, len(mine), shards),
-        out_shape=[wide, flat, flat, wide],
+    return pl.pallas_call(
+        functools.partial(outputs_kernel, len(mine), shards),
+        out_shape=[jax.ShapeDtypeStruct((rows, columns), BF16), flat, flat],
         in_specs=[SMEM] + [VMEM] * (1 + 2 * len(mine)),
-        out_specs=[VMEM] * 4,
-        compiler_params=pltpu.CompilerParams(vmem_limit_bytes=2 * 1024**2 + 32 * rows * columns),
+        out_specs=[VMEM] * 3,
+        compiler_params=softmax_params(rows, columns),
         cost_estimate=pl.CostEstimate(
             flops=10 * rows * columns,
             bytes_accessed=12 * rows * columns,
             transcendentals=rows * columns,
         ),
-        name="loss",
+        name="outputs",
     )(shard, tokens, *mine, *theirs)
 
 
@@ -241,43 +245,54 @@
     )
 
 
-def first_kernel(dlogits_ref, *refs):
+def first_kernel(parts, shards, shard_ref, tokens_ref, *refs):
+    mine, theirs = refs[:parts], refs[parts : 2 * parts]
+    heads, out_ref = refs[2 * parts : -1], refs[-1]
+    _, chosen, _, unnormed, denominator = softmax_of(
+        shard_ref[0], tokens_ref[...], mine, theirs, shards
+    )
+    columns = unnormed.shape[0]
+    shard_rows = columns // shards
+    dlogits = unnormed / denominator - jnp.where(chosen, 1.0, 0.0)
+    for i in range(shards):
+        block = slice(i * shard_rows, (i + 1) * shard_rows)
+        out_ref[:, block] = dlogits[block, :].T.astype(BF16)
+    multiplied(out_ref[:, :columns], heads, out_ref, columns)
+
+
+def first_message(shard, tokens, mine, theirs, heads, shards):
+    rows = tokens.shape[1]
+    columns = sum(part.shape[0] for part in mine)
+    width = heads[0].shape[1]
+    return pl.pallas_call(
+        functools.partial(first_kernel, len(mine), shards),
+        out_shape=jax.ShapeDtypeStruct((rows, columns + width), BF16),
+        in_specs=[SMEM] + [VMEM] * (1 + 2 * len(mine) + len(heads)),
+        out_specs=VMEM,
+        compiler_params=softmax_params(rows, columns),
+        cost_estimate=gradient_cost(rows, columns, width),
+        name="first_message",
+    )(shard, tokens, *mine, *theirs, *heads)
+
+
+def second_kernel(first_ref, *refs):
     heads, out_ref = refs[:-1], refs[-1]
-    columns = dlogits_ref.shape[1]
-    out_ref[:, :columns] = dlogits_ref[...]
-    multiplied(dlogits_ref[...], heads, out_ref, columns)
-
-
-def first_message(dlogits, heads):
-    rows, columns = dlogits.shape
-    width = heads[0].shape[1]
-    return pl.pallas_call(
-        first_kernel,
-        out_shape=jax.ShapeDtypeStruct((rows, columns + width), BF16),
+    columns = first_ref.shape[1] - heads[0].shape[1]
+    multiplied(first_ref[:, :columns], heads, out_ref, 0)
+
+
+def second_message(first, heads):
+    rows, width = first.shape[0], heads[0].shape[1]
+    columns = first.shape[1] - width
+    return pl.pallas_call(
+        second_kernel,
+        out_shape=jax.ShapeDtypeStruct((rows, width), BF16),
         in_specs=[VMEM] * (1 + len(heads)),
         out_specs=VMEM,
         compiler_params=PARAMS,
-        cost_estimate=gradient_cost(rows, columns, width),
-        name="first_message",
-    )(dlogits, *heads)
-
-
-def second_kernel(dlogits_ref, _, *refs):
-    multiplied(dlogits_ref[...], refs[:-1], refs[-1], 0)
-
-
-def second_message(dlogits, first, heads):
-    rows, columns = dlogits.shape
-    width = heads[0].shape[1]
-    return pl.pallas_call(
-        second_kernel,
-        out_shape=jax.ShapeDtypeStruct((rows, width), BF16),
-        in_specs=[VMEM, ANY] + [VMEM] * len(heads),
-        out_specs=VMEM,
-        compiler_params=PARAMS,
         cost_estimate=gradient_cost(32 * rows, columns, width),
         name="second_message",
-    )(dlogits, first, *heads)
+    )(first, *heads)
 
 
 def scaled(message_ref, advantage, columns, out_ref, start):
@@ -385,18 +400,20 @@
         theirs.append(swapped(sent, "section", 1))
     partner_facts = theirs[0]
     mine, theirs = in_order(mine, near + far, 0), in_order(theirs, near + far, BELOW)
-    logits, logprob, entropy, dlogits = loss(
-        shard, tokens[None, :], mine, theirs, shards
-    )
     for i, offset in enumerate(far):
         heads[offset] = again[2 * i : 2 * i + 2]
     pieces = [piece for pair in heads for piece in pair]
-    first = first_message(dlogits, pieces[0::2])
+    flat_tokens = tokens[None, :]
+    first = first_message(shard, flat_tokens, mine, theirs, pieces[0::2], shards)
     first_in = swapped(first, "section", 1)
-    second = second_message(dlogits, first, pieces[1::2])
+    second = second_message(first, pieces[1::2])
     second_in = swapped(second, "section", 1)
 
-    late_own, _ = lax.optimization_barrier((own, first))
+    late_own, late_tokens, _ = lax.optimization_barrier((own, flat_tokens, first))
+    logits, logprob, entropy = outputs(shard, late_tokens, mine, theirs, shards)
+    partner_facts, logits, logprob, entropy = lax.optimization_barrier(
+        (partner_facts, logits, logprob, entropy)
+    )
     axes = ("vocab", "section")
     count = lax.axis_size(axes)
     beyond = [(i + 2, i) for i in range(0, count - 2, 2)] + [(i, i + 2) for i in range(1, count - 2, 2)]

time: 52.4 us -> 52.3 us (level)
  waiting for transfers between devices: 23.7 us -> 22.9 us
  local copies, waits for them, and re-layouts: 1.43 us -> 2.16 us
    ppermute x1, waiting for transfers between devices: 1 us -> 0.2 us  [body(): outer = lax.ppermute(late_own, axes, beyond)]
    unnamed x10 -> x14, local copies, waits for them, and re-layouts: 1.43 us -> 2.16 us
  transfers between devices with their start and end apart: 12 -> 12, of which waited for: 7 -> 7; matrix products, arithmetic and copies ran while one was open for 0% -> 0% of each run, Pallas kernels for 7% -> 8%
where the time goes in v12:
time: 52.3 us; the launch traced here: 52.2 us
  waiting for transfers between devices  22.9 us (44%)
  starting transfers between devices  20.6 us (39%)
  Pallas kernels  5.71 us (11%)
  local copies, waits for them, and re-layouts  2.16 us (4%)
  between operations  0.81 us (2%)
    ppermute x11, waiting for transfers between devices, swapped(): return lax.ppermute(value, axis, pairs)  22.7 us
    ppermute x11, starting transfers between devices, swapped(): return lax.ppermute(value, axis, pairs)  19.3 us
    unnamed x14, local copies, waits for them, and re-layouts  2.16 us
    pallas_call x1, Pallas kernels, staying_gradient(): pl.pallas_call(staying_kernel, out_shape=jax.ShapeDtypeStruct((rows, 4 *...  1.3 us
    ppermute x1, starting transfers between devices, body(): outer = lax.ppermute(late_own, axes, beyond)  1.28 us
    pallas_call x2, Pallas kernels, partial_scores(): pl.pallas_call(functools.partial(partial_kernel, len(facts), len(heads)),...  1.08 us
  transfers between devices with their start and end apart: 12, of which 7 were waited for; matrix products, arithmetic and copies ran while one was open for 0% of the time, Pallas kernels for 8%

profile of v12, /device:TPU:0, one launch (start us, length us, event | category | flops | bytes accessed | tf_op | source)
XLA Modules:
  0.0 52.2 jit_solution(11683714869368673378)
XLA Ops:
  0.7 1.4 %copy-done.1 = bf16[128,5120]{1,0:T(8,128)(2,1)S(1)} copy-done((bf16[128,5120]{1,0:T(8,128)(2,1)S(1)}, bf16[128,5120]{1,0:T(8,128)(2,1)}, u32[]{:S(2)}) %copy-start.1) | copy-done | bytes 1310744
  2.2 3.0 %collective-permute-start.1 = (bf16[128,1280]{1,0:T(8,128)(2,1)S(1)}, bf16[128,1280]{1,0:T(8,128)(2,1)S(1)}, u32[]{:S(2)}, u32[]{:S(2)}) collective-permute-start(bf16[128,1280]{1,0:T(8,128)(2,1)S(1)} %get-tuple-element.30.refs_1_.refs_4_.refs_0_), channel_id=1, source_target_pairs={{0,4},{4,0},{8,12},{12,8},{1,5},{5,1},{9,13},{13,9},{2,6},{6,2},{1... | collective-permute-start | bytes 983048 | tf_op jit(solution)/shard_map/ppermute | solution.py:21
  5.2 1.5 %collective-permute-start.4 = (bf16[128,1280]{1,0:T(8,128)(2,1)S(1)}, bf16[128,1280]{1,0:T(8,128)(2,1)S(1)}, u32[]{:S(2)}, u32[]{:S(2)}) collective-permute-start(bf16[128,1280]{1,0:T(8,128)(2,1)S(1)} %get-tuple-element.29.refs_2_.refs_0_.refs_1_), channel_id=1, source_target_pairs={{0,8},{4,12},{8,0},{12,4},{1,9},{5,13},{9,1},{13,5},{2,10},{6,14},... | collective-permute-start | bytes 983048 | tf_op jit(solution)/shard_map/ppermute | solution.py:21
  6.8 1.6 %collective-permute-start = (bf16[128,2560]{1,0:T(8,128)(2,1)S(1)}, bf16[128,2560]{1,0:T(8,128)(2,1)S(1)}, u32[]{:S(2)}, u32[]{:S(2)}) collective-permute-start(bf16[128,2560]{1,0:T(8,128)(2,1)S(1)} %take_half.3), channel_id=1, source_target_pairs={{0,1},{1,0},{2,3},{3,2},{4,5},{5,4},{6,7},{7,6},{8,9},{9,8},{10,11... | collective-permute-start | bytes 1966088 | tf_op jit(solution)/shard_map/ppermute | solution.py:21
  8.4 0.5 %collective-permute-start.2 = (bf16[128,1280]{1,0:T(8,128)(2,1)S(1)}, bf16[128,1280]{1,0:T(8,128)(2,1)S(1)}, u32[]{:S(2)}, u32[]{:S(2)}) collective-permute-start(bf16[128,1280]{1,0:T(8,128)(2,1)S(1)} %get-tuple-element.29.refs_2_.refs_0_.refs_1_), channel_id=1, source_target_pairs={{0,4},{4,0},{8,12},{12,8},{1,5},{5,1},{9,13},{13,9},{2,6},{6,2},{1... | collective-permute-start | bytes 983048 | tf_op jit(solution)/shard_map/ppermute | solution.py:21
  9.5 4.3 %collective-permute-done.1.refs_3_.refs_5_.refs_2_ = bf16[128,1280]{1,0:T(8,128)(2,1)S(1)} collective-permute-done((bf16[128,1280]{1,0:T(8,128)(2,1)S(1)}, bf16[128,1280]{1,0:T(8,128)(2,1)S(1)}, u32[]{:S(2)}, u32[]{:S(2)}) %collective-permute-start.1) | collective-permute-done | bytes 327712 | tf_op jit(solution)/shard_map/ppermute | solution.py:21
  13.7 2.1 %collective-permute-start.6 = (bf16[128,1280]{1,0:T(8,128)(2,1)S(1)}, bf16[128,1280]{1,0:T(8,128)(2,1)S(1)}, u32[]{:S(2)}, u32[]{:S(2)}) collective-permute-start(bf16[128,1280]{1,0:T(8,128)(2,1)S(1)} %collective-permute-done.1.refs_3_.refs_5_.refs_2_), channel_id=1, source_target_pairs={{0,8},{4,12},{8,0},{12,4},{1,9},{5,13},{9,1},{13,5},{2,10},{6,14},... | collective-permute-start | bytes 983048 | tf_op jit(solution)/shard_map/ppermute | solution.py:21
  15.8 1.5 %collective-permute-start.7 = (bf16[128,1280]{1,0:T(8,128)(2,1)S(1)}, bf16[128,1280]{1,0:T(8,128)(2,1)S(1)}, u32[]{:S(2)}, u32[]{:S(2)}) collective-permute-start(bf16[128,1280]{1,0:T(8,128)(2,1)S(1)} %collective-permute-done.4.refs_6_.refs_2_.refs_5_), channel_id=1, source_target_pairs={{0,4},{4,0},{8,12},{12,8},{1,5},{5,1},{9,13},{13,9},{2,6},{6,2},{1... | collective-permute-start | bytes 983048 | tf_op jit(solution)/shard_map/ppermute | solution.py:21
  17.3 5.4 %collective-permute-done.partner_ref = bf16[128,2560]{1,0:T(8,128)(2,1)S(1)} collective-permute-done((bf16[128,2560]{1,0:T(8,128)(2,1)S(1)}, bf16[128,2560]{1,0:T(8,128)(2,1)S(1)}, u32[]{:S(2)}, u32[]{:S(2)}) %collective-permute-start) | collective-permute-done | bytes 655392 | tf_op jit(solution)/shard_map/ppermute | solution.py:21
  23.2 0.7 %partial_scores.2 = (f32[384,128]{1,0:T(8,128)S(1)}, f32[392,128]{1,0:T(8,128)S(1)}) custom-call(bf16[2560,256]{1,0:T(8,128)(2,1)S(1)} %turned_rows.1.turned_ref, f32[2,128]{1,0:T(2,128)S(1)} %pad_maximum_fusion.refs_0_.own_ref, bf16[128,1280]{1,0:T(8,128)(2,1)S(1)} %get-tuple-element.30.refs_1_.refs_4_.refs_0_, ...), custom_call_target="tpu_custom_call" | custom-call | flops 503316480 | bytes 3276800 | tf_op jit(solution)/shard_map/partial_scores/pallas_call | solution.py:120
  23.9 1.6 %collective-permute-start.5 = (f32[392,128]{1,0:T(8,128)S(1)}, f32[392,128]{1,0:T(8,128)S(1)}, u32[]{:S(2)}, u32[]{:S(2)}) collective-permute-start(f32[392,128]{1,0:T(8,128)S(1)} %get-tuple-element.31), channel_id=1, source_target_pairs={{0,1},{1,0},{2,3},{3,2},{4,5},{5,4},{6,7},{7,6},{8,9},{9,8},{10,11... | collective-permute-start | bytes 602120 | tf_op jit(solution)/shard_map/ppermute | solution.py:21
  25.5 2.9 %collective-permute-done.6.refs_0_ = bf16[128,1280]{1,0:T(8,128)(2,1)S(1)} collective-permute-done((bf16[128,1280]{1,0:T(8,128)(2,1)S(1)}, bf16[128,1280]{1,0:T(8,128)(2,1)S(1)}, u32[]{:S(2)}, u32[]{:S(2)}) %collective-permute-start.6) | collective-permute-done | bytes 327712 | tf_op jit(solution)/shard_map/ppermute | solution.py:21
  28.8 0.7 %copy-done.2 = bf16[128,1280]{1,0:T(8,128)(2,1)} copy-done((bf16[128,1280]{1,0:T(8,128)(2,1)}, bf16[128,1280]{1,0:T(8,128)(2,1)S(1)}, u32[]{:S(2)}) %copy-start.2) | copy-done | bytes 327704
  29.5 1.6 %collective-permute-start.8 = (f32[128,128]{1,0:T(8,128)S(1)}, f32[128,128]{1,0:T(8,128)S(1)}, u32[]{:S(2)}, u32[]{:S(2)}) collective-permute-start(f32[128,128]{1,0:T(8,128)S(1)} %get-tuple-element.34), channel_id=1, source_target_pairs={{0,1},{1,0},{2,3},{3,2},{4,5},{5,4},{6,7},{7,6},{8,9},{9,8},{10,11... | collective-permute-start | bytes 196616 | tf_op jit(solution)/shard_map/ppermute | solution.py:21
  31.1 2.7 %collective-permute-done.8.refs_3_ = f32[128,128]{1,0:T(8,128)S(1)} collective-permute-done((f32[128,128]{1,0:T(8,128)S(1)}, f32[128,128]{1,0:T(8,128)S(1)}, u32[]{:S(2)}, u32[]{:S(2)}) %collective-permute-start.8) | collective-permute-done | bytes 65568 | tf_op jit(solution)/shard_map/ppermute | solution.py:21
  33.8 0.6 %first_message.1.first_ref = bf16[128,1792]{1,0:T(8,128)(2,1)S(1)} custom-call(s32[1]{0:T(128)} %bitcast.3.shard_ref, s32[1,128]{1,0:T(1,128)S(1)} %bitcast.8, f32[384,128]{1,0:T(8,128)S(1)} %get-tuple-element.32.refs_0_, f32[128,128]{1,0:T(8,128)S(1)} %get-tuple-element.33.refs_1_, f32[392,128]{1,0:T(8,128)S(1)} %collective-permute-done.5.refs_2_.partner_ref, ...), custom_call_target="tpu_custom_call" | custom-call | flops 167772160 | bytes 1638400 | tf_op jit(solution)/shard_map/first_message/pallas_call | solution.py:267
  34.4 1.6 %collective-permute-start.11 = (bf16[128,1792]{1,0:T(8,128)(2,1)S(1)}, bf16[128,1792]{1,0:T(8,128)(2,1)S(1)}, u32[]{:S(2)}, u32[]{:S(2)}) collective-permute-start(bf16[128,1792]{1,0:T(8,128)(2,1)S(1)} %first_message.1.first_ref), channel_id=1, source_target_pairs={{0,1},{1,0},{2,3},{3,2},{4,5},{5,4},{6,7},{7,6},{8,9},{9,8},{10,11... | collective-permute-start | bytes 1376264 | tf_op jit(solution)/shard_map/ppermute | solution.py:21
  36.0 1.3 %collective-permute-start.10 = (f32[2,128]{1,0:T(2,128)S(1)}, f32[2,128]{1,0:T(2,128)S(1)}, u32[]{:S(2)}, u32[]{:S(2)}) collective-permute-start(f32[2,128]{1,0:T(2,128)S(1)} %pad_maximum_fusion.refs_0_.own_ref), channel_id=1, source_target_pairs={{2,0},{4,2},{6,4},{8,6},{10,8},{12,10},{14,12},{1,3},{3,5},{5,7},{... | collective-permute-start | bytes 3080 | tf_op jit(solution)/shard_map/ppermute | solution.py:420
  37.6 0.9 %outputs.1 = (bf16[128,512]{1,0:T(8,128)(2,1)}, f32[1,128]{1,0:T(1,128)}, f32[1,128]{1,0:T(1,128)}) custom-call(s32[1]{0:T(128)} %bitcast.3.shard_ref, s32[1,128]{1,0:T(1,128)S(1)} %bitcast.9, f32[384,128]{1,0:T(8,128)S(1)} %get-tuple-element.32.refs_0_, f32[128,128]{1,0:T(8,128)S(1)} %get-tuple-element.33.refs_1_, ...), custom_call_target="tpu_custom_call" | custom-call | flops 655360 | bytes 786432 | tf_op jit(solution)/shard_map/outputs/pallas_call | solution.py:210
  38.5 3.7 %collective-permute-start.9 = (bf16[128,1280]{1,0:T(8,128)(2,1)S(1)}, bf16[128,1280]{1,0:T(8,128)(2,1)S(1)}, u32[]{:S(2)}, u32[]{:S(2)}) collective-permute-start(bf16[128,1280]{1,0:T(8,128)(2,1)S(1)} %second_message.1), channel_id=1, source_target_pairs={{0,1},{1,0},{2,3},{3,2},{4,5},{5,4},{6,7},{7,6},{8,9},{9,8},{10,11... | collective-permute-start | bytes 983048 | tf_op jit(solution)/shard_map/ppermute | solution.py:21
  42.6 5.2 %collective-permute-done.11.first_ref = bf16[128,1792]{1,0:T(8,128)(2,1)S(1)} collective-permute-done((bf16[128,1792]{1,0:T(8,128)(2,1)S(1)}, bf16[128,1792]{1,0:T(8,128)(2,1)S(1)}, u32[]{:S(2)}, u32[]{:S(2)}) %collective-permute-start.11) | collective-permute-done | bytes 458784 | tf_op jit(solution)/shard_map/ppermute | solution.py:21
  47.9 1.3 %staying_gradient.1._ = bf16[128,5120]{1,0:T(8,128)(2,1)} custom-call(s32[1]{0:T(128)} %bitcast.which_ref, bf16[128,1792]{1,0:T(8,128)(2,1)S(1)} %collective-permute-done.11.first_ref, f32[128,128]{1,0:T(8,128)S(1)} %advantage.1.advantage_ref, bf16[128,1280]{1,0:T(8,128)(2,1)S(1)} %get-tuple-element.30.refs_1_.refs_4_.refs_0_, ...), custom_call_target="tpu_custom_call" | custom-call | flops 335544320 | bytes 3276800 | tf_op jit(solution)/shard_map/staying_gradient/pallas_call | solution.py:336
  49.2 2.2 %collective-permute-done.9.second_ref = bf16[128,1280]{1,0:T(8,128)(2,1)S(1)} collective-permute-done((bf16[128,1280]{1,0:T(8,128)(2,1)S(1)}, bf16[128,1280]{1,0:T(8,128)(2,1)S(1)}, u32[]{:S(2)}, u32[]{:S(2)}) %collective-permute-start.9) | collective-permute-done | bytes 327712 | tf_op jit(solution)/shard_map/ppermute | solution.py:21
  51.4 0.8 %place_second.1 = bf16[128,5120]{1,0:T(8,128)(2,1)} custom-call(s32[1]{0:T(128)} %bitcast.which_ref, bf16[128,1280]{1,0:T(8,128)(2,1)S(1)} %collective-permute-done.9.second_ref, f32[128,128]{1,0:T(8,128)S(1)} %advantage.1.advantage_ref, bf16[128,5120]{1,0:T(8,128)(2,1)} %staying_gradient.1._), custom_call_target="tpu_custom_call", output_to_operand_aliasing={{}: (3, {})} | custom-call | tf_op jit(solution)/shard_map/place_second/pallas_call | solution.py:367
  (27 shorter events, 2.3 us)
Async XLA Ops:
  0.6 6.1 %copy-start = (bf16[128,5120]{1,0:T(8,128)(2,1)S(1)}, bf16[128,5120]{1,0:T(8,128)(2,1)}, u32[]{:S(2)}) copy-start(bf16[128,5120]{1,0:T(8,128)(2,1)} %hidden_ref.1) | copy-start | bytes 3932164
  0.7 1.4 %copy-start.1 = (bf16[128,5120]{1,0:T(8,128)(2,1)S(1)}, bf16[128,5120]{1,0:T(8,128)(2,1)}, u32[]{:S(2)}) copy-start(bf16[128,5120]{1,0:T(8,128)(2,1)} %value_ref.1) | copy-start | bytes 3932164
  2.2 15.2 %copy-start.6 = (s32[128]{0:T(128)S(1)}, s32[128]{0:T(128)}, u32[]{:S(2)}) copy-start(s32[128]{0:T(128)} %param.9) | copy-start | bytes 1540
  2.2 15.1 %copy-start.5 = (f32[128]{0:T(128)S(1)}, f32[128]{0:T(128)}, u32[]{:S(2)}) copy-start(f32[128]{0:T(128)} %param.8) | copy-start | bytes 1540
  2.2 11.5 %collective-permute-start.1 = (bf16[128,1280]{1,0:T(8,128)(2,1)S(1)}, bf16[128,1280]{1,0:T(8,128)(2,1)S(1)}, u32[]{:S(2)}, u32[]{:S(2)}) collective-permute-start(bf16[128,1280]{1,0:T(8,128)(2,1)S(1)} %get-tuple-element.30.refs_1_.refs_4_.refs_0_), channel_id=1, source_target_pairs={{0,4},{4,0},{8,12},{12,8},{1,5},{5,1},{9,13},{13,9},{2,6},{6,2},{1... | collective-permute-start | bytes 983048 | tf_op jit(solution)/shard_map/ppermute | solution.py:21
  5.2 10.6 %collective-permute-start.4 = (bf16[128,1280]{1,0:T(8,128)(2,1)S(1)}, bf16[128,1280]{1,0:T(8,128)(2,1)S(1)}, u32[]{:S(2)}, u32[]{:S(2)}) collective-permute-start(bf16[128,1280]{1,0:T(8,128)(2,1)S(1)} %get-tuple-element.29.refs_2_.refs_0_.refs_1_), channel_id=1, source_target_pairs={{0,8},{4,12},{8,0},{12,4},{1,9},{5,13},{9,1},{13,5},{2,10},{6,14},... | collective-permute-start | bytes 983048 | tf_op jit(solution)/shard_map/ppermute | solution.py:21
  6.8 16.0 %collective-permute-start = (bf16[128,2560]{1,0:T(8,128)(2,1)S(1)}, bf16[128,2560]{1,0:T(8,128)(2,1)S(1)}, u32[]{:S(2)}, u32[]{:S(2)}) collective-permute-start(bf16[128,2560]{1,0:T(8,128)(2,1)S(1)} %take_half.3), channel_id=1, source_target_pairs={{0,1},{1,0},{2,3},{3,2},{4,5},{5,4},{6,7},{7,6},{8,9},{9,8},{10,11... | collective-permute-start | bytes 1966088 | tf_op jit(solution)/shard_map/ppermute | solution.py:21
  8.4 14.7 %collective-permute-start.2 = (bf16[128,1280]{1,0:T(8,128)(2,1)S(1)}, bf16[128,1280]{1,0:T(8,128)(2,1)S(1)}, u32[]{:S(2)}, u32[]{:S(2)}) collective-permute-start(bf16[128,1280]{1,0:T(8,128)(2,1)S(1)} %get-tuple-element.29.refs_2_.refs_0_.refs_1_), channel_id=1, source_target_pairs={{0,4},{4,0},{8,12},{12,8},{1,5},{5,1},{9,13},{13,9},{2,6},{6,2},{1... | collective-permute-start | bytes 983048 | tf_op jit(solution)/shard_map/ppermute | solution.py:21
  9.0 14.2 %collective-permute-start.3 = (bf16[128,1280]{1,0:T(8,128)(2,1)S(1)}, bf16[128,1280]{1,0:T(8,128)(2,1)S(1)}, u32[]{:S(2)}, u32[]{:S(2)}) collective-permute-start(bf16[128,1280]{1,0:T(8,128)(2,1)S(1)} %get-tuple-element.30.refs_1_.refs_4_.refs_0_), channel_id=1, source_target_pairs={{0,8},{4,12},{8,0},{12,4},{1,9},{5,13},{9,1},{13,5},{2,10},{6,14},... | collective-permute-start | bytes 983048 | tf_op jit(solution)/shard_map/ppermute | solution.py:21
  13.7 14.7 %collective-permute-start.6 = (bf16[128,1280]{1,0:T(8,128)(2,1)S(1)}, bf16[128,1280]{1,0:T(8,128)(2,1)S(1)}, u32[]{:S(2)}, u32[]{:S(2)}) collective-permute-start(bf16[128,1280]{1,0:T(8,128)(2,1)S(1)} %collective-permute-done.1.refs_3_.refs_5_.refs_2_), channel_id=1, source_target_pairs={{0,8},{4,12},{8,0},{12,4},{1,9},{5,13},{9,1},{13,5},{2,10},{6,14},... | collective-permute-start | bytes 983048 | tf_op jit(solution)/shard_map/ppermute | solution.py:21
  15.8 12.6 %collective-permute-start.7 = (bf16[128,1280]{1,0:T(8,128)(2,1)S(1)}, bf16[128,1280]{1,0:T(8,128)(2,1)S(1)}, u32[]{:S(2)}, u32[]{:S(2)}) collective-permute-start(bf16[128,1280]{1,0:T(8,128)(2,1)S(1)} %collective-permute-done.4.refs_6_.refs_2_.refs_5_), channel_id=1, source_target_pairs={{0,4},{4,0},{8,12},{12,8},{1,5},{5,1},{9,13},{13,9},{2,6},{6,2},{1... | collective-permute-start | bytes 983048 | tf_op jit(solution)/shard_map/ppermute | solution.py:21
  23.9 9.9 %copy-start.4 = (s32[128]{0:T(128)S(1)}, s32[128]{0:T(128)}, u32[]{:S(2)}) copy-start(s32[128]{0:T(128)} %param.7) | copy-start | bytes 1540
  23.9 9.9 %collective-permute-start.5 = (f32[392,128]{1,0:T(8,128)S(1)}, f32[392,128]{1,0:T(8,128)S(1)}, u32[]{:S(2)}, u32[]{:S(2)}) collective-permute-start(f32[392,128]{1,0:T(8,128)S(1)} %get-tuple-element.31), channel_id=1, source_target_pairs={{0,1},{1,0},{2,3},{3,2},{4,5},{5,4},{6,7},{7,6},{8,9},{9,8},{10,11... | collective-permute-start | bytes 602120 | tf_op jit(solution)/shard_map/ppermute | solution.py:21
  28.8 0.7 %copy-start.2 = (bf16[128,1280]{1,0:T(8,128)(2,1)}, bf16[128,1280]{1,0:T(8,128)(2,1)S(1)}, u32[]{:S(2)}) copy-start(bf16[128,1280]{1,0:T(8,128)(2,1)S(1)} %get-tuple-element.43.refs_3_.refs_7_) | copy-start | bytes 983044
  29.5 4.3 %collective-permute-start.8 = (f32[128,128]{1,0:T(8,128)S(1)}, f32[128,128]{1,0:T(8,128)S(1)}, u32[]{:S(2)}, u32[]{:S(2)}) collective-permute-start(f32[128,128]{1,0:T(8,128)S(1)} %get-tuple-element.34), channel_id=1, source_target_pairs={{0,1},{1,0},{2,3},{3,2},{4,5},{5,4},{6,7},{7,6},{8,9},{9,8},{10,11... | collective-permute-start | bytes 196616 | tf_op jit(solution)/shard_map/ppermute | solution.py:21
  31.1 6.2 %copy-start.3 = (bf16[128,1280]{1,0:T(8,128)(2,1)S(1)}, bf16[128,1280]{1,0:T(8,128)(2,1)}, u32[]{:S(2)}) copy-start(bf16[128,1280]{1,0:T(8,128)(2,1)} %copy-done.2) | copy-start | bytes 983044
  34.4 13.5 %collective-permute-start.11 = (bf16[128,1792]{1,0:T(8,128)(2,1)S(1)}, bf16[128,1792]{1,0:T(8,128)(2,1)S(1)}, u32[]{:S(2)}, u32[]{:S(2)}) collective-permute-start(bf16[128,1792]{1,0:T(8,128)(2,1)S(1)} %first_message.1.first_ref), channel_id=1, source_target_pairs={{0,1},{1,0},{2,3},{3,2},{4,5},{5,4},{6,7},{7,6},{8,9},{9,8},{10,11... | collective-permute-start | bytes 1376264 | tf_op jit(solution)/shard_map/ppermute | solution.py:21
  36.0 6.4 %collective-permute-start.10 = (f32[2,128]{1,0:T(2,128)S(1)}, f32[2,128]{1,0:T(2,128)S(1)}, u32[]{:S(2)}, u32[]{:S(2)}) collective-permute-start(f32[2,128]{1,0:T(2,128)S(1)} %pad_maximum_fusion.refs_0_.own_ref), channel_id=1, source_target_pairs={{2,0},{4,2},{6,4},{8,6},{10,8},{12,10},{14,12},{1,3},{3,5},{5,7},{... | collective-permute-start | bytes 3080 | tf_op jit(solution)/shard_map/ppermute | solution.py:420
  38.5 12.9 %collective-permute-start.9 = (bf16[128,1280]{1,0:T(8,128)(2,1)S(1)}, bf16[128,1280]{1,0:T(8,128)(2,1)S(1)}, u32[]{:S(2)}, u32[]{:S(2)}) collective-permute-start(bf16[128,1280]{1,0:T(8,128)(2,1)S(1)} %second_message.1), channel_id=1, source_target_pairs={{0,1},{1,0},{2,3},{3,2},{4,5},{5,4},{6,7},{7,6},{8,9},{9,8},{10,11... | collective-permute-start | bytes 983048 | tf_op jit(solution)/shard_map/ppermute | solution.py:21

commit v13 on v12

--- a/solution.py
+++ b/solution.py
@@ -200,7 +200,7 @@
 
 
 def softmax_params(rows, columns):
-    return pltpu.CompilerParams(vmem_limit_bytes=2 * 1024**2 + 32 * rows * columns)
+    return pltpu.CompilerParams(vmem_limit_bytes=1024**2 + 16 * rows * columns)
 
 
 def outputs(shard, tokens, mine, theirs, shards):
@@ -247,7 +247,7 @@
 
 def first_kernel(parts, shards, shard_ref, tokens_ref, *refs):
     mine, theirs = refs[:parts], refs[parts : 2 * parts]
-    heads, out_ref = refs[2 * parts : -1], refs[-1]
+    heads, out_ref = refs[2 * parts : 2 * parts + shards], refs[-1]
     _, chosen, _, unnormed, denominator = softmax_of(
         shard_ref[0], tokens_ref[...], mine, theirs, shards
     )
@@ -404,7 +404,7 @@
         heads[offset] = again[2 * i : 2 * i + 2]
     pieces = [piece for pair in heads for piece in pair]
     flat_tokens = tokens[None, :]
-    first = first_message(shard, flat_tokens, mine, theirs, pieces[0::2], shards)
+    first = first_message(shard, flat_tokens, mine, theirs, pieces[0::2] + pieces[1::2], shards)
     first_in = swapped(first, "section", 1)
     second = second_message(first, pieces[1::2])
     second_in = swapped(second, "section", 1)

time: 52.3 us -> 51.7 us (0.989)
  local copies, waits for them, and re-layouts: 2.16 us -> 1.43 us
    unnamed x14 -> x10, local copies, waits for them, and re-layouts: 2.16 us -> 1.43 us
where the time goes in v13:
time: 51.7 us; the launch traced here: 51.5 us
  waiting for transfers between devices  22.9 us (44%)
  starting transfers between devices  20.6 us (40%)
  Pallas kernels  5.71 us (11%)
  local copies, waits for them, and re-layouts  1.43 us (3%)
  between operations  0.79 us (2%)
    ppermute x11, waiting for transfers between devices, swapped(): return lax.ppermute(value, axis, pairs)  22.7 us
    ppermute x11, starting transfers between devices, swapped(): return lax.ppermute(value, axis, pairs)  19.4 us
    unnamed x10, local copies, waits for them, and re-layouts  1.43 us
    ppermute x1, starting transfers between devices, body(): outer = lax.ppermute(late_own, axes, beyond)  1.28 us
    pallas_call x1, Pallas kernels, staying_gradient(): pl.pallas_call(staying_kernel, out_shape=jax.ShapeDtypeStruct((rows, 4 *...  1.28 us
    pallas_call x2, Pallas kernels, partial_scores(): pl.pallas_call(functools.partial(partial_kernel, len(facts), len(heads)),...  1.08 us
  transfers between devices with their start and end apart: 12, of which 7 were waited for; matrix products, arithmetic and copies ran while one was open for 0% of the time, Pallas kernels for 8%

profile of v13, /device:TPU:0, one launch (start us, length us, event | category | flops | bytes accessed | tf_op | source)
XLA Modules:
  0.0 51.5 jit_solution(13655134311127471676)
XLA Ops:
  0.7 1.4 %copy-done.1 = bf16[128,5120]{1,0:T(8,128)(2,1)S(1)} copy-done((bf16[128,5120]{1,0:T(8,128)(2,1)S(1)}, bf16[128,5120]{1,0:T(8,128)(2,1)}, u32[]{:S(2)}) %copy-start.1) | copy-done | bytes 1310744
  2.2 3.0 %collective-permute-start.1 = (bf16[128,1280]{1,0:T(8,128)(2,1)S(1)}, bf16[128,1280]{1,0:T(8,128)(2,1)S(1)}, u32[]{:S(2)}, u32[]{:S(2)}) collective-permute-start(bf16[128,1280]{1,0:T(8,128)(2,1)S(1)} %get-tuple-element.30.refs_1_.refs_4_.refs_0_), channel_id=1, source_target_pairs={{0,4},{4,0},{8,12},{12,8},{1,5},{5,1},{9,13},{13,9},{2,6},{6,2},{1... | collective-permute-start | bytes 983048 | tf_op jit(solution)/shard_map/ppermute | solution.py:21
  5.2 1.5 %collective-permute-start.4 = (bf16[128,1280]{1,0:T(8,128)(2,1)S(1)}, bf16[128,1280]{1,0:T(8,128)(2,1)S(1)}, u32[]{:S(2)}, u32[]{:S(2)}) collective-permute-start(bf16[128,1280]{1,0:T(8,128)(2,1)S(1)} %get-tuple-element.29.refs_2_.refs_8_.refs_0_.refs_1_), channel_id=1, source_target_pairs={{0,8},{4,12},{8,0},{12,4},{1,9},{5,13},{9,1},{13,5},{2,10},{6,14},... | collective-permute-start | bytes 983048 | tf_op jit(solution)/shard_map/ppermute | solution.py:21
  6.8 1.6 %collective-permute-start = (bf16[128,2560]{1,0:T(8,128)(2,1)S(1)}, bf16[128,2560]{1,0:T(8,128)(2,1)S(1)}, u32[]{:S(2)}, u32[]{:S(2)}) collective-permute-start(bf16[128,2560]{1,0:T(8,128)(2,1)S(1)} %take_half.3), channel_id=1, source_target_pairs={{0,1},{1,0},{2,3},{3,2},{4,5},{5,4},{6,7},{7,6},{8,9},{9,8},{10,11... | collective-permute-start | bytes 1966088 | tf_op jit(solution)/shard_map/ppermute | solution.py:21
  8.4 0.5 %collective-permute-start.2 = (bf16[128,1280]{1,0:T(8,128)(2,1)S(1)}, bf16[128,1280]{1,0:T(8,128)(2,1)S(1)}, u32[]{:S(2)}, u32[]{:S(2)}) collective-permute-start(bf16[128,1280]{1,0:T(8,128)(2,1)S(1)} %get-tuple-element.29.refs_2_.refs_8_.refs_0_.refs_1_), channel_id=1, source_target_pairs={{0,4},{4,0},{8,12},{12,8},{1,5},{5,1},{9,13},{13,9},{2,6},{6,2},{1... | collective-permute-start | bytes 983048 | tf_op jit(solution)/shard_map/ppermute | solution.py:21
  9.0 0.5 collective-permute-start.3
  9.5 4.3 %collective-permute-done.1.refs_3_.refs_5_.refs_2_ = bf16[128,1280]{1,0:T(8,128)(2,1)S(1)} collective-permute-done((bf16[128,1280]{1,0:T(8,128)(2,1)S(1)}, bf16[128,1280]{1,0:T(8,128)(2,1)S(1)}, u32[]{:S(2)}, u32[]{:S(2)}) %collective-permute-start.1) | collective-permute-done | bytes 327712 | tf_op jit(solution)/shard_map/ppermute | solution.py:21
  13.7 2.1 %collective-permute-start.6 = (bf16[128,1280]{1,0:T(8,128)(2,1)S(1)}, bf16[128,1280]{1,0:T(8,128)(2,1)S(1)}, u32[]{:S(2)}, u32[]{:S(2)}) collective-permute-start(bf16[128,1280]{1,0:T(8,128)(2,1)S(1)} %collective-permute-done.1.refs_3_.refs_5_.refs_2_), channel_id=1, source_target_pairs={{0,8},{4,12},{8,0},{12,4},{1,9},{5,13},{9,1},{13,5},{2,10},{6,14},... | collective-permute-start | bytes 983048 | tf_op jit(solution)/shard_map/ppermute | solution.py:21
  15.8 1.5 %collective-permute-start.7 = (bf16[128,1280]{1,0:T(8,128)(2,1)S(1)}, bf16[128,1280]{1,0:T(8,128)(2,1)S(1)}, u32[]{:S(2)}, u32[]{:S(2)}) collective-permute-start(bf16[128,1280]{1,0:T(8,128)(2,1)S(1)} %collective-permute-done.4.refs_6_.refs_10_.refs_2_.refs_5_), channel_id=1, source_target_pairs={{0,4},{4,0},{8,12},{12,8},{1,5},{5,1},{9,13},{13,9},{2,6},{6,2},{1... | collective-permute-start | bytes 983048 | tf_op jit(solution)/shard_map/ppermute | solution.py:21
  17.3 5.4 %collective-permute-done.partner_ref = bf16[128,2560]{1,0:T(8,128)(2,1)S(1)} collective-permute-done((bf16[128,2560]{1,0:T(8,128)(2,1)S(1)}, bf16[128,2560]{1,0:T(8,128)(2,1)S(1)}, u32[]{:S(2)}, u32[]{:S(2)}) %collective-permute-start) | collective-permute-done | bytes 655392 | tf_op jit(solution)/shard_map/ppermute | solution.py:21
  23.2 0.7 %partial_scores.2 = (f32[384,128]{1,0:T(8,128)S(1)}, f32[392,128]{1,0:T(8,128)S(1)}) custom-call(bf16[2560,256]{1,0:T(8,128)(2,1)S(1)} %turned_rows.1.turned_ref, f32[2,128]{1,0:T(2,128)S(1)} %pad_maximum_fusion.refs_0_.own_ref, bf16[128,1280]{1,0:T(8,128)(2,1)S(1)} %get-tuple-element.30.refs_1_.refs_4_.refs_0_, ...), custom_call_target="tpu_custom_call" | custom-call | flops 503316480 | bytes 3276800 | tf_op jit(solution)/shard_map/partial_scores/pallas_call | solution.py:120
  23.9 1.6 %collective-permute-start.5 = (f32[392,128]{1,0:T(8,128)S(1)}, f32[392,128]{1,0:T(8,128)S(1)}, u32[]{:S(2)}, u32[]{:S(2)}) collective-permute-start(f32[392,128]{1,0:T(8,128)S(1)} %get-tuple-element.31), channel_id=1, source_target_pairs={{0,1},{1,0},{2,3},{3,2},{4,5},{5,4},{6,7},{7,6},{8,9},{9,8},{10,11... | collective-permute-start | bytes 602120 | tf_op jit(solution)/shard_map/ppermute | solution.py:21
  25.5 2.9 %collective-permute-done.6.refs_0_ = bf16[128,1280]{1,0:T(8,128)(2,1)S(1)} collective-permute-done((bf16[128,1280]{1,0:T(8,128)(2,1)S(1)}, bf16[128,1280]{1,0:T(8,128)(2,1)S(1)}, u32[]{:S(2)}, u32[]{:S(2)}) %collective-permute-start.6) | collective-permute-done | bytes 327712 | tf_op jit(solution)/shard_map/ppermute | solution.py:21
  28.8 1.6 %collective-permute-start.8 = (f32[128,128]{1,0:T(8,128)S(1)}, f32[128,128]{1,0:T(8,128)S(1)}, u32[]{:S(2)}, u32[]{:S(2)}) collective-permute-start(f32[128,128]{1,0:T(8,128)S(1)} %get-tuple-element.34), channel_id=1, source_target_pairs={{0,1},{1,0},{2,3},{3,2},{4,5},{5,4},{6,7},{7,6},{8,9},{9,8},{10,11... | collective-permute-start | bytes 196616 | tf_op jit(solution)/shard_map/ppermute | solution.py:21
  30.4 2.7 %collective-permute-done.8.refs_3_ = f32[128,128]{1,0:T(8,128)S(1)} collective-permute-done((f32[128,128]{1,0:T(8,128)S(1)}, f32[128,128]{1,0:T(8,128)S(1)}, u32[]{:S(2)}, u32[]{:S(2)}) %collective-permute-start.8) | collective-permute-done | bytes 65568 | tf_op jit(solution)/shard_map/ppermute | solution.py:21
  33.1 0.6 %first_message.1.first_ref = bf16[128,1792]{1,0:T(8,128)(2,1)S(1)} custom-call(s32[1]{0:T(128)} %bitcast.3.shard_ref, s32[1,128]{1,0:T(1,128)S(1)} %bitcast.8, f32[384,128]{1,0:T(8,128)S(1)} %get-tuple-element.32.refs_0_, f32[128,128]{1,0:T(8,128)S(1)} %get-tuple-element.33.refs_1_, f32[392,128]{1,0:T(8,128)S(1)} %collective-permute-done.5.refs_2_.partner_ref, ...), custom_call_target="tpu_custom_call" | custom-call | flops 167772160 | bytes 1638400 | tf_op jit(solution)/shard_map/first_message/pallas_call | solution.py:267
  33.7 1.6 %collective-permute-start.11 = (bf16[128,1792]{1,0:T(8,128)(2,1)S(1)}, bf16[128,1792]{1,0:T(8,128)(2,1)S(1)}, u32[]{:S(2)}, u32[]{:S(2)}) collective-permute-start(bf16[128,1792]{1,0:T(8,128)(2,1)S(1)} %first_message.1.first_ref), channel_id=1, source_target_pairs={{0,1},{1,0},{2,3},{3,2},{4,5},{5,4},{6,7},{7,6},{8,9},{9,8},{10,11... | collective-permute-start | bytes 1376264 | tf_op jit(solution)/shard_map/ppermute | solution.py:21
  35.3 1.3 %collective-permute-start.10 = (f32[2,128]{1,0:T(2,128)S(1)}, f32[2,128]{1,0:T(2,128)S(1)}, u32[]{:S(2)}, u32[]{:S(2)}) collective-permute-start(f32[2,128]{1,0:T(2,128)S(1)} %pad_maximum_fusion.refs_0_.own_ref), channel_id=1, source_target_pairs={{2,0},{4,2},{6,4},{8,6},{10,8},{12,10},{14,12},{1,3},{3,5},{5,7},{... | collective-permute-start | bytes 3080 | tf_op jit(solution)/shard_map/ppermute | solution.py:420
  37.0 0.9 %outputs.1 = (bf16[128,512]{1,0:T(8,128)(2,1)}, f32[1,128]{1,0:T(1,128)}, f32[1,128]{1,0:T(1,128)}) custom-call(s32[1]{0:T(128)} %bitcast.3.shard_ref, s32[1,128]{1,0:T(1,128)S(1)} %bitcast.9, f32[384,128]{1,0:T(8,128)S(1)} %get-tuple-element.32.refs_0_, f32[128,128]{1,0:T(8,128)S(1)} %get-tuple-element.33.refs_1_, ...), custom_call_target="tpu_custom_call" | custom-call | flops 655360 | bytes 786432 | tf_op jit(solution)/shard_map/outputs/pallas_call | solution.py:210
  37.8 3.7 %collective-permute-start.9 = (bf16[128,1280]{1,0:T(8,128)(2,1)S(1)}, bf16[128,1280]{1,0:T(8,128)(2,1)S(1)}, u32[]{:S(2)}, u32[]{:S(2)}) collective-permute-start(bf16[128,1280]{1,0:T(8,128)(2,1)S(1)} %second_message.1), channel_id=1, source_target_pairs={{0,1},{1,0},{2,3},{3,2},{4,5},{5,4},{6,7},{7,6},{8,9},{9,8},{10,11... | collective-permute-start | bytes 983048 | tf_op jit(solution)/shard_map/ppermute | solution.py:21
  42.0 5.3 %collective-permute-done.11.first_ref = bf16[128,1792]{1,0:T(8,128)(2,1)S(1)} collective-permute-done((bf16[128,1792]{1,0:T(8,128)(2,1)S(1)}, bf16[128,1792]{1,0:T(8,128)(2,1)S(1)}, u32[]{:S(2)}, u32[]{:S(2)}) %collective-permute-start.11) | collective-permute-done | bytes 458784 | tf_op jit(solution)/shard_map/ppermute | solution.py:21
  47.2 1.3 %staying_gradient.1._ = bf16[128,5120]{1,0:T(8,128)(2,1)} custom-call(s32[1]{0:T(128)} %bitcast.which_ref, bf16[128,1792]{1,0:T(8,128)(2,1)S(1)} %collective-permute-done.11.first_ref, f32[128,128]{1,0:T(8,128)S(1)} %advantage.1.advantage_ref, bf16[128,1280]{1,0:T(8,128)(2,1)S(1)} %get-tuple-element.30.refs_1_.refs_4_.refs_0_, ...), custom_call_target="tpu_custom_call" | custom-call | flops 335544320 | bytes 3276800 | tf_op jit(solution)/shard_map/staying_gradient/pallas_call | solution.py:336
  48.5 2.2 %collective-permute-done.9.second_ref = bf16[128,1280]{1,0:T(8,128)(2,1)S(1)} collective-permute-done((bf16[128,1280]{1,0:T(8,128)(2,1)S(1)}, bf16[128,1280]{1,0:T(8,128)(2,1)S(1)}, u32[]{:S(2)}, u32[]{:S(2)}) %collective-permute-start.9) | collective-permute-done | bytes 327712 | tf_op jit(solution)/shard_map/ppermute | solution.py:21
  50.7 0.8 %place_second.1 = bf16[128,5120]{1,0:T(8,128)(2,1)} custom-call(s32[1]{0:T(128)} %bitcast.which_ref, bf16[128,1280]{1,0:T(8,128)(2,1)S(1)} %collective-permute-done.9.second_ref, f32[128,128]{1,0:T(8,128)S(1)} %advantage.1.advantage_ref, bf16[128,5120]{1,0:T(8,128)(2,1)} %staying_gradient.1._), custom_call_target="tpu_custom_call", output_to_operand_aliasing={{}: (3, {})} | custom-call | tf_op jit(solution)/shard_map/place_second/pallas_call | solution.py:367
  (23 shorter events, 1.8 us)
Async XLA Ops:
  0.6 6.1 %copy-start = (bf16[128,5120]{1,0:T(8,128)(2,1)S(1)}, bf16[128,5120]{1,0:T(8,128)(2,1)}, u32[]{:S(2)}) copy-start(bf16[128,5120]{1,0:T(8,128)(2,1)} %hidden_ref.1) | copy-start | bytes 3932164
  0.7 1.4 %copy-start.1 = (bf16[128,5120]{1,0:T(8,128)(2,1)S(1)}, bf16[128,5120]{1,0:T(8,128)(2,1)}, u32[]{:S(2)}) copy-start(bf16[128,5120]{1,0:T(8,128)(2,1)} %value_ref.1) | copy-start | bytes 3932164
  2.2 15.2 %copy-start.4 = (s32[128]{0:T(128)S(1)}, s32[128]{0:T(128)}, u32[]{:S(2)}) copy-start(s32[128]{0:T(128)} %param.9) | copy-start | bytes 1540
  2.2 15.1 %copy-start.3 = (f32[128]{0:T(128)S(1)}, f32[128]{0:T(128)}, u32[]{:S(2)}) copy-start(f32[128]{0:T(128)} %param.8) | copy-start | bytes 1540
  2.2 11.5 %collective-permute-start.1 = (bf16[128,1280]{1,0:T(8,128)(2,1)S(1)}, bf16[128,1280]{1,0:T(8,128)(2,1)S(1)}, u32[]{:S(2)}, u32[]{:S(2)}) collective-permute-start(bf16[128,1280]{1,0:T(8,128)(2,1)S(1)} %get-tuple-element.30.refs_1_.refs_4_.refs_0_), channel_id=1, source_target_pairs={{0,4},{4,0},{8,12},{12,8},{1,5},{5,1},{9,13},{13,9},{2,6},{6,2},{1... | collective-permute-start | bytes 983048 | tf_op jit(solution)/shard_map/ppermute | solution.py:21
  5.2 10.6 %collective-permute-start.4 = (bf16[128,1280]{1,0:T(8,128)(2,1)S(1)}, bf16[128,1280]{1,0:T(8,128)(2,1)S(1)}, u32[]{:S(2)}, u32[]{:S(2)}) collective-permute-start(bf16[128,1280]{1,0:T(8,128)(2,1)S(1)} %get-tuple-element.29.refs_2_.refs_8_.refs_0_.refs_1_), channel_id=1, source_target_pairs={{0,8},{4,12},{8,0},{12,4},{1,9},{5,13},{9,1},{13,5},{2,10},{6,14},... | collective-permute-start | bytes 983048 | tf_op jit(solution)/shard_map/ppermute | solution.py:21
  6.8 16.0 %collective-permute-start = (bf16[128,2560]{1,0:T(8,128)(2,1)S(1)}, bf16[128,2560]{1,0:T(8,128)(2,1)S(1)}, u32[]{:S(2)}, u32[]{:S(2)}) collective-permute-start(bf16[128,2560]{1,0:T(8,128)(2,1)S(1)} %take_half.3), channel_id=1, source_target_pairs={{0,1},{1,0},{2,3},{3,2},{4,5},{5,4},{6,7},{7,6},{8,9},{9,8},{10,11... | collective-permute-start | bytes 1966088 | tf_op jit(solution)/shard_map/ppermute | solution.py:21
  8.4 14.7 %collective-permute-start.2 = (bf16[128,1280]{1,0:T(8,128)(2,1)S(1)}, bf16[128,1280]{1,0:T(8,128)(2,1)S(1)}, u32[]{:S(2)}, u32[]{:S(2)}) collective-permute-start(bf16[128,1280]{1,0:T(8,128)(2,1)S(1)} %get-tuple-element.29.refs_2_.refs_8_.refs_0_.refs_1_), channel_id=1, source_target_pairs={{0,4},{4,0},{8,12},{12,8},{1,5},{5,1},{9,13},{13,9},{2,6},{6,2},{1... | collective-permute-start | bytes 983048 | tf_op jit(solution)/shard_map/ppermute | solution.py:21
  9.0 14.2 %collective-permute-start.3 = (bf16[128,1280]{1,0:T(8,128)(2,1)S(1)}, bf16[128,1280]{1,0:T(8,128)(2,1)S(1)}, u32[]{:S(2)}, u32[]{:S(2)}) collective-permute-start(bf16[128,1280]{1,0:T(8,128)(2,1)S(1)} %get-tuple-element.30.refs_1_.refs_4_.refs_0_), channel_id=1, source_target_pairs={{0,8},{4,12},{8,0},{12,4},{1,9},{5,13},{9,1},{13,5},{2,10},{6,14},... | collective-permute-start | bytes 983048 | tf_op jit(solution)/shard_map/ppermute | solution.py:21
  13.7 14.7 %collective-permute-start.6 = (bf16[128,1280]{1,0:T(8,128)(2,1)S(1)}, bf16[128,1280]{1,0:T(8,128)(2,1)S(1)}, u32[]{:S(2)}, u32[]{:S(2)}) collective-permute-start(bf16[128,1280]{1,0:T(8,128)(2,1)S(1)} %collective-permute-done.1.refs_3_.refs_5_.refs_2_), channel_id=1, source_target_pairs={{0,8},{4,12},{8,0},{12,4},{1,9},{5,13},{9,1},{13,5},{2,10},{6,14},... | collective-permute-start | bytes 983048 | tf_op jit(solution)/shard_map/ppermute | solution.py:21
  15.8 12.6 %collective-permute-start.7 = (bf16[128,1280]{1,0:T(8,128)(2,1)S(1)}, bf16[128,1280]{1,0:T(8,128)(2,1)S(1)}, u32[]{:S(2)}, u32[]{:S(2)}) collective-permute-start(bf16[128,1280]{1,0:T(8,128)(2,1)S(1)} %collective-permute-done.4.refs_6_.refs_10_.refs_2_.refs_5_), channel_id=1, source_target_pairs={{0,4},{4,0},{8,12},{12,8},{1,5},{5,1},{9,13},{13,9},{2,6},{6,2},{1... | collective-permute-start | bytes 983048 | tf_op jit(solution)/shard_map/ppermute | solution.py:21
  23.9 9.2 %copy-start.2 = (s32[128]{0:T(128)S(1)}, s32[128]{0:T(128)}, u32[]{:S(2)}) copy-start(s32[128]{0:T(128)} %param.7) | copy-start | bytes 1540
  23.9 9.2 %collective-permute-start.5 = (f32[392,128]{1,0:T(8,128)S(1)}, f32[392,128]{1,0:T(8,128)S(1)}, u32[]{:S(2)}, u32[]{:S(2)}) collective-permute-start(f32[392,128]{1,0:T(8,128)S(1)} %get-tuple-element.31), channel_id=1, source_target_pairs={{0,1},{1,0},{2,3},{3,2},{4,5},{5,4},{6,7},{7,6},{8,9},{9,8},{10,11... | collective-permute-start | bytes 602120 | tf_op jit(solution)/shard_map/ppermute | solution.py:21
  28.8 4.3 %collective-permute-start.8 = (f32[128,128]{1,0:T(8,128)S(1)}, f32[128,128]{1,0:T(8,128)S(1)}, u32[]{:S(2)}, u32[]{:S(2)}) collective-permute-start(f32[128,128]{1,0:T(8,128)S(1)} %get-tuple-element.34), channel_id=1, source_target_pairs={{0,1},{1,0},{2,3},{3,2},{4,5},{5,4},{6,7},{7,6},{8,9},{9,8},{10,11... | collective-permute-start | bytes 196616 | tf_op jit(solution)/shard_map/ppermute | solution.py:21
  33.7 13.5 %collective-permute-start.11 = (bf16[128,1792]{1,0:T(8,128)(2,1)S(1)}, bf16[128,1792]{1,0:T(8,128)(2,1)S(1)}, u32[]{:S(2)}, u32[]{:S(2)}) collective-permute-start(bf16[128,1792]{1,0:T(8,128)(2,1)S(1)} %first_message.1.first_ref), channel_id=1, source_target_pairs={{0,1},{1,0},{2,3},{3,2},{4,5},{5,4},{6,7},{7,6},{8,9},{9,8},{10,11... | collective-permute-start | bytes 1376264 | tf_op jit(solution)/shard_map/ppermute | solution.py:21
  35.3 6.4 %collective-permute-start.10 = (f32[2,128]{1,0:T(2,128)S(1)}, f32[2,128]{1,0:T(2,128)S(1)}, u32[]{:S(2)}, u32[]{:S(2)}) collective-permute-start(f32[2,128]{1,0:T(2,128)S(1)} %pad_maximum_fusion.refs_0_.own_ref), channel_id=1, source_target_pairs={{2,0},{4,2},{6,4},{8,6},{10,8},{12,10},{14,12},{1,3},{3,5},{5,7},{... | collective-permute-start | bytes 3080 | tf_op jit(solution)/shard_map/ppermute | solution.py:420
  37.8 12.9 %collective-permute-start.9 = (bf16[128,1280]{1,0:T(8,128)(2,1)S(1)}, bf16[128,1280]{1,0:T(8,128)(2,1)S(1)}, u32[]{:S(2)}, u32[]{:S(2)}) collective-permute-start(bf16[128,1280]{1,0:T(8,128)(2,1)S(1)} %second_message.1), channel_id=1, source_target_pairs={{0,1},{1,0},{2,3},{3,2},{4,5},{5,4},{6,7},{7,6},{8,9},{9,8},{10,11... | collective-permute-start | bytes 983048 | tf_op jit(solution)/shard_map/ppermute | solution.py:21

commit v14 on v13

--- a/solution.py
+++ b/solution.py
@@ -40,34 +40,36 @@
     return [(uppers[offset], lowers[offset]) for offset in range(count)]
 
 
-def take_kernel(which_ref, value_ref, *refs):
-    outs, sem = refs[:-1], refs[-1]
-    width = outs[0].shape[1]
+def take_kernel(count, which_ref, *refs):
+    values, outs, sem = refs[:count], refs[count:-1], refs[-1]
+    rows, width = values[0].shape[0], outs[0].shape[1]
     start = which_ref[0] * width * len(outs)
     copies = []
     for i, out in enumerate(outs):
-        source = value_ref.at[:, pl.ds(pl.multiple_of(start + i * width, 128), width)]
-        copies.append(pltpu.make_async_copy(source, out, sem.at[i]))
+        for j, value in enumerate(values):
+            source = value.at[:, pl.ds(pl.multiple_of(start + i * width, 128), width)]
+            target = out.at[pl.ds(j * rows, rows), :]
+            copies.append(pltpu.make_async_copy(source, target, sem.at[i, j]))
     for copy in copies:
         copy.start()
     for copy in copies:
         copy.wait()
 
 
-def take(which, value, pieces):
-    rows, width = value.shape[0], value.shape[1] // 2 // pieces
-    return pl.pallas_call(
-        take_kernel,
-        out_shape=[jax.ShapeDtypeStruct((rows, width), value.dtype)] * pieces,
-        in_specs=[SMEM, ANY],
+def take(which, values, pieces):
+    rows, width = len(values) * values[0].shape[0], values[0].shape[1] // 2 // pieces
+    return pl.pallas_call(
+        functools.partial(take_kernel, len(values)),
+        out_shape=[jax.ShapeDtypeStruct((rows, width), BF16)] * pieces,
+        in_specs=[SMEM] + [ANY] * len(values),
         out_specs=[ANY] * pieces,
-        scratch_shapes=[pltpu.SemaphoreType.DMA((pieces,))],
+        scratch_shapes=[pltpu.SemaphoreType.DMA((pieces, len(values)))],
         compiler_params=PARAMS,
         cost_estimate=pl.CostEstimate(
-            flops=0, bytes_accessed=value.size * value.dtype.itemsize, transcendentals=0
+            flops=0, bytes_accessed=4 * rows * width * pieces, transcendentals=0
         ),
         name="take_half",
-    )(which, value)
+    )(which, *values)
 
 
 def turned_kernel(which_ref, hidden_ref, partner_ref, out_ref):
@@ -384,9 +386,10 @@
     far = [o for o in range(shards) if bin(o).count("1") > 1]
 
     own = jnp.stack([rewards, (group_ids + 1).astype(F32)])
-    pieces = tuple(take(which, head_weight, 2))
+    middle = head_weight.shape[0] // 2
+    pieces = tuple(take(which, (head_weight[:middle], head_weight[middle:]), 2))
     late_hidden, _ = lax.optimization_barrier((hidden, pieces))
-    (other_half,) = take(1 - which, late_hidden, 1)
+    (other_half,) = take(1 - which, (late_hidden,), 1)
     other_half, late_pieces = lax.optimization_barrier((other_half, pieces))
     heads = gathered(pieces, late_pieces, "vocab")
     partner_half = swapped(other_half, "section", 1)

time: 51.7 us -> 51.7 us (level)
    unnamed x10 -> x8, local copies, waits for them, and re-layouts: 1.43 us -> 0.03 us
    slice x0 -> x1, local copies, waits for them, and re-layouts: none -> 1.37 us  [body(): pieces = tuple(take(which, (head_weight[:middle], head_weight[middle:]), 2))]
where the time goes in v14:
time: 51.7 us; the launch traced here: 51.5 us
  waiting for transfers between devices  22.9 us (44%)
  starting transfers between devices  20.6 us (40%)
  Pallas kernels  5.78 us (11%)
  local copies, waits for them, and re-layouts  1.4 us (3%)
  between operations  0.79 us (2%)
    ppermute x11, waiting for transfers between devices, swapped(): return lax.ppermute(value, axis, pairs)  22.7 us
    ppermute x11, starting transfers between devices, swapped(): return lax.ppermute(value, axis, pairs)  19.4 us
    slice x1, local copies, waits for them, and re-layouts, body(): pieces = tuple(take(which, (head_weight[:middle], head_weight[middle:]), 2))  1.37 us
    ppermute x1, starting transfers between devices, body(): outer = lax.ppermute(late_own, axes, beyond)  1.28 us
    pallas_call x1, Pallas kernels, staying_gradient(): pl.pallas_call(staying_kernel, out_shape=jax.ShapeDtypeStruct((rows, 4 *...  1.28 us
    pallas_call x2, Pallas kernels, partial_scores(): pl.pallas_call(functools.partial(partial_kernel, len(facts), len(heads)),...  1.09 us
  transfers between devices with their start and end apart: 12, of which 7 were waited for; matrix products, arithmetic and copies ran while one was open for 0% of the time, Pallas kernels for 8%

profile of v14, /device:TPU:0, one launch (start us, length us, event | category | flops | bytes accessed | tf_op | source)
XLA Modules:
  0.0 51.5 jit_solution(5339689046580629198)
XLA Ops:
  0.6 1.4 %fusion = (bf16[64,5120]{1,0:T(8,128)(2,1)S(1)}, bf16[64,5120]{1,0:T(8,128)(2,1)S(1)}) fusion(bf16[128,5120]{1,0:T(8,128)(2,1)} %param.6), kind=kLoop, calls=%fused_computation.2 | loop fusion | bytes 2621440 | tf_op jit(solution)/shard_map/slice | solution.py:390
  2.2 3.0 %collective-permute-start.1 = (bf16[128,1280]{1,0:T(8,128)(2,1)S(1)}, bf16[128,1280]{1,0:T(8,128)(2,1)S(1)}, u32[]{:S(2)}, u32[]{:S(2)}) collective-permute-start(bf16[128,1280]{1,0:T(8,128)(2,1)S(1)} %get-tuple-element.30.refs_1_.refs_4_.refs_0_), channel_id=1, source_target_pairs={{0,4},{4,0},{8,12},{12,8},{1,5},{5,1},{9,13},{13,9},{2,6},{6,2},{1... | collective-permute-start | bytes 983048 | tf_op jit(solution)/shard_map/ppermute | solution.py:21
  5.2 1.5 %collective-permute-start.4 = (bf16[128,1280]{1,0:T(8,128)(2,1)S(1)}, bf16[128,1280]{1,0:T(8,128)(2,1)S(1)}, u32[]{:S(2)}, u32[]{:S(2)}) collective-permute-start(bf16[128,1280]{1,0:T(8,128)(2,1)S(1)} %get-tuple-element.29.refs_2_.refs_8_.refs_0_.refs_1_), channel_id=1, source_target_pairs={{0,8},{4,12},{8,0},{12,4},{1,9},{5,13},{9,1},{13,5},{2,10},{6,14},... | collective-permute-start | bytes 983048 | tf_op jit(solution)/shard_map/ppermute | solution.py:21
  6.8 1.6 %collective-permute-start = (bf16[128,2560]{1,0:T(8,128)(2,1)S(1)}, bf16[128,2560]{1,0:T(8,128)(2,1)S(1)}, u32[]{:S(2)}, u32[]{:S(2)}) collective-permute-start(bf16[128,2560]{1,0:T(8,128)(2,1)S(1)} %take_half.3), channel_id=1, source_target_pairs={{0,1},{1,0},{2,3},{3,2},{4,5},{5,4},{6,7},{7,6},{8,9},{9,8},{10,11... | collective-permute-start | bytes 1966088 | tf_op jit(solution)/shard_map/ppermute | solution.py:21
  8.5 0.5 %collective-permute-start.2 = (bf16[128,1280]{1,0:T(8,128)(2,1)S(1)}, bf16[128,1280]{1,0:T(8,128)(2,1)S(1)}, u32[]{:S(2)}, u32[]{:S(2)}) collective-permute-start(bf16[128,1280]{1,0:T(8,128)(2,1)S(1)} %get-tuple-element.29.refs_2_.refs_8_.refs_0_.refs_1_), channel_id=1, source_target_pairs={{0,4},{4,0},{8,12},{12,8},{1,5},{5,1},{9,13},{13,9},{2,6},{6,2},{1... | collective-permute-start | bytes 983048 | tf_op jit(solution)/shard_map/ppermute | solution.py:21
  9.0 0.5 collective-permute-start.3
  9.5 4.3 %collective-permute-done.1.refs_3_.refs_5_.refs_2_ = bf16[128,1280]{1,0:T(8,128)(2,1)S(1)} collective-permute-done((bf16[128,1280]{1,0:T(8,128)(2,1)S(1)}, bf16[128,1280]{1,0:T(8,128)(2,1)S(1)}, u32[]{:S(2)}, u32[]{:S(2)}) %collective-permute-start.1) | collective-permute-done | bytes 327712 | tf_op jit(solution)/shard_map/ppermute | solution.py:21
  13.8 2.1 %collective-permute-start.6 = (bf16[128,1280]{1,0:T(8,128)(2,1)S(1)}, bf16[128,1280]{1,0:T(8,128)(2,1)S(1)}, u32[]{:S(2)}, u32[]{:S(2)}) collective-permute-start(bf16[128,1280]{1,0:T(8,128)(2,1)S(1)} %collective-permute-done.1.refs_3_.refs_5_.refs_2_), channel_id=1, source_target_pairs={{0,8},{4,12},{8,0},{12,4},{1,9},{5,13},{9,1},{13,5},{2,10},{6,14},... | collective-permute-start | bytes 983048 | tf_op jit(solution)/shard_map/ppermute | solution.py:21
  15.9 1.5 %collective-permute-start.7 = (bf16[128,1280]{1,0:T(8,128)(2,1)S(1)}, bf16[128,1280]{1,0:T(8,128)(2,1)S(1)}, u32[]{:S(2)}, u32[]{:S(2)}) collective-permute-start(bf16[128,1280]{1,0:T(8,128)(2,1)S(1)} %collective-permute-done.4.refs_6_.refs_10_.refs_2_.refs_5_), channel_id=1, source_target_pairs={{0,4},{4,0},{8,12},{12,8},{1,5},{5,1},{9,13},{13,9},{2,6},{6,2},{1... | collective-permute-start | bytes 983048 | tf_op jit(solution)/shard_map/ppermute | solution.py:21
  17.4 5.4 %collective-permute-done.partner_ref = bf16[128,2560]{1,0:T(8,128)(2,1)S(1)} collective-permute-done((bf16[128,2560]{1,0:T(8,128)(2,1)S(1)}, bf16[128,2560]{1,0:T(8,128)(2,1)S(1)}, u32[]{:S(2)}, u32[]{:S(2)}) %collective-permute-start) | collective-permute-done | bytes 655392 | tf_op jit(solution)/shard_map/ppermute | solution.py:21
  23.2 0.7 %partial_scores.2 = (f32[384,128]{1,0:T(8,128)S(1)}, f32[392,128]{1,0:T(8,128)S(1)}) custom-call(bf16[2560,256]{1,0:T(8,128)(2,1)S(1)} %turned_rows.1.turned_ref, f32[2,128]{1,0:T(2,128)S(1)} %pad_maximum_fusion.refs_0_.own_ref, bf16[128,1280]{1,0:T(8,128)(2,1)S(1)} %get-tuple-element.30.refs_1_.refs_4_.refs_0_, ...), custom_call_target="tpu_custom_call" | custom-call | flops 503316480 | bytes 3276800 | tf_op jit(solution)/shard_map/partial_scores/pallas_call | solution.py:122
  23.9 1.6 %collective-permute-start.5 = (f32[392,128]{1,0:T(8,128)S(1)}, f32[392,128]{1,0:T(8,128)S(1)}, u32[]{:S(2)}, u32[]{:S(2)}) collective-permute-start(f32[392,128]{1,0:T(8,128)S(1)} %get-tuple-element.31), channel_id=1, source_target_pairs={{0,1},{1,0},{2,3},{3,2},{4,5},{5,4},{6,7},{7,6},{8,9},{9,8},{10,11... | collective-permute-start | bytes 602120 | tf_op jit(solution)/shard_map/ppermute | solution.py:21
  25.6 2.9 %collective-permute-done.6.refs_0_ = bf16[128,1280]{1,0:T(8,128)(2,1)S(1)} collective-permute-done((bf16[128,1280]{1,0:T(8,128)(2,1)S(1)}, bf16[128,1280]{1,0:T(8,128)(2,1)S(1)}, u32[]{:S(2)}, u32[]{:S(2)}) %collective-permute-start.6) | collective-permute-done | bytes 327712 | tf_op jit(solution)/shard_map/ppermute | solution.py:21
  28.8 1.6 %collective-permute-start.8 = (f32[128,128]{1,0:T(8,128)S(1)}, f32[128,128]{1,0:T(8,128)S(1)}, u32[]{:S(2)}, u32[]{:S(2)}) collective-permute-start(f32[128,128]{1,0:T(8,128)S(1)} %get-tuple-element.34), channel_id=1, source_target_pairs={{0,1},{1,0},{2,3},{3,2},{4,5},{5,4},{6,7},{7,6},{8,9},{9,8},{10,11... | collective-permute-start | bytes 196616 | tf_op jit(solution)/shard_map/ppermute | solution.py:21
  30.5 2.7 %collective-permute-done.8.refs_3_ = f32[128,128]{1,0:T(8,128)S(1)} collective-permute-done((f32[128,128]{1,0:T(8,128)S(1)}, f32[128,128]{1,0:T(8,128)S(1)}, u32[]{:S(2)}, u32[]{:S(2)}) %collective-permute-start.8) | collective-permute-done | bytes 65568 | tf_op jit(solution)/shard_map/ppermute | solution.py:21
  33.2 0.6 %first_message.1.first_ref = bf16[128,1792]{1,0:T(8,128)(2,1)S(1)} custom-call(s32[1]{0:T(128)} %bitcast.3.shard_ref, s32[1,128]{1,0:T(1,128)S(1)} %bitcast.8, f32[384,128]{1,0:T(8,128)S(1)} %get-tuple-element.32.refs_0_, f32[128,128]{1,0:T(8,128)S(1)} %get-tuple-element.33.refs_1_, f32[392,128]{1,0:T(8,128)S(1)} %collective-permute-done.5.refs_2_.partner_ref, ...), custom_call_target="tpu_custom_call" | custom-call | flops 167772160 | bytes 1638400 | tf_op jit(solution)/shard_map/first_message/pallas_call | solution.py:269
  33.7 1.6 %collective-permute-start.11 = (bf16[128,1792]{1,0:T(8,128)(2,1)S(1)}, bf16[128,1792]{1,0:T(8,128)(2,1)S(1)}, u32[]{:S(2)}, u32[]{:S(2)}) collective-permute-start(bf16[128,1792]{1,0:T(8,128)(2,1)S(1)} %first_message.1.first_ref), channel_id=1, source_target_pairs={{0,1},{1,0},{2,3},{3,2},{4,5},{5,4},{6,7},{7,6},{8,9},{9,8},{10,11... | collective-permute-start | bytes 1376264 | tf_op jit(solution)/shard_map/ppermute | solution.py:21
  35.4 1.3 %collective-permute-start.10 = (f32[2,128]{1,0:T(2,128)S(1)}, f32[2,128]{1,0:T(2,128)S(1)}, u32[]{:S(2)}, u32[]{:S(2)}) collective-permute-start(f32[2,128]{1,0:T(2,128)S(1)} %pad_maximum_fusion.refs_0_.own_ref), channel_id=1, source_target_pairs={{2,0},{4,2},{6,4},{8,6},{10,8},{12,10},{14,12},{1,3},{3,5},{5,7},{... | collective-permute-start | bytes 3080 | tf_op jit(solution)/shard_map/ppermute | solution.py:423
  37.0 0.9 %outputs.1 = (bf16[128,512]{1,0:T(8,128)(2,1)}, f32[1,128]{1,0:T(1,128)}, f32[1,128]{1,0:T(1,128)}) custom-call(s32[1]{0:T(128)} %bitcast.3.shard_ref, s32[1,128]{1,0:T(1,128)S(1)} %bitcast.9, f32[384,128]{1,0:T(8,128)S(1)} %get-tuple-element.32.refs_0_, f32[128,128]{1,0:T(8,128)S(1)} %get-tuple-element.33.refs_1_, ...), custom_call_target="tpu_custom_call" | custom-call | flops 655360 | bytes 786432 | tf_op jit(solution)/shard_map/outputs/pallas_call | solution.py:212
  37.9 3.6 %collective-permute-start.9 = (bf16[128,1280]{1,0:T(8,128)(2,1)S(1)}, bf16[128,1280]{1,0:T(8,128)(2,1)S(1)}, u32[]{:S(2)}, u32[]{:S(2)}) collective-permute-start(bf16[128,1280]{1,0:T(8,128)(2,1)S(1)} %second_message.1), channel_id=1, source_target_pairs={{0,1},{1,0},{2,3},{3,2},{4,5},{5,4},{6,7},{7,6},{8,9},{9,8},{10,11... | collective-permute-start | bytes 983048 | tf_op jit(solution)/shard_map/ppermute | solution.py:21
  42.0 5.2 %collective-permute-done.11.first_ref = bf16[128,1792]{1,0:T(8,128)(2,1)S(1)} collective-permute-done((bf16[128,1792]{1,0:T(8,128)(2,1)S(1)}, bf16[128,1792]{1,0:T(8,128)(2,1)S(1)}, u32[]{:S(2)}, u32[]{:S(2)}) %collective-permute-start.11) | collective-permute-done | bytes 458784 | tf_op jit(solution)/shard_map/ppermute | solution.py:21
  47.3 1.3 %staying_gradient.1._ = bf16[128,5120]{1,0:T(8,128)(2,1)} custom-call(s32[1]{0:T(128)} %bitcast.which_ref, bf16[128,1792]{1,0:T(8,128)(2,1)S(1)} %collective-permute-done.11.first_ref, f32[128,128]{1,0:T(8,128)S(1)} %advantage.1.advantage_ref, bf16[128,1280]{1,0:T(8,128)(2,1)S(1)} %get-tuple-element.30.refs_1_.refs_4_.refs_0_, ...), custom_call_target="tpu_custom_call" | custom-call | flops 335544320 | bytes 3276800 | tf_op jit(solution)/shard_map/staying_gradient/pallas_call | solution.py:338
  48.5 2.2 %collective-permute-done.9.second_ref = bf16[128,1280]{1,0:T(8,128)(2,1)S(1)} collective-permute-done((bf16[128,1280]{1,0:T(8,128)(2,1)S(1)}, bf16[128,1280]{1,0:T(8,128)(2,1)S(1)}, u32[]{:S(2)}, u32[]{:S(2)}) %collective-permute-start.9) | collective-permute-done | bytes 327712 | tf_op jit(solution)/shard_map/ppermute | solution.py:21
  50.8 0.8 %place_second.1 = bf16[128,5120]{1,0:T(8,128)(2,1)} custom-call(s32[1]{0:T(128)} %bitcast.which_ref, bf16[128,1280]{1,0:T(8,128)(2,1)S(1)} %collective-permute-done.9.second_ref, f32[128,128]{1,0:T(8,128)S(1)} %advantage.1.advantage_ref, bf16[128,5120]{1,0:T(8,128)(2,1)} %staying_gradient.1._), custom_call_target="tpu_custom_call", output_to_operand_aliasing={{}: (3, {})} | custom-call | tf_op jit(solution)/shard_map/place_second/pallas_call | solution.py:369
  (22 shorter events, 1.9 us)
Async XLA Ops:
  2.0 4.7 %copy-start = (bf16[128,5120]{1,0:T(8,128)(2,1)S(1)}, bf16[128,5120]{1,0:T(8,128)(2,1)}, u32[]{:S(2)}) copy-start(bf16[128,5120]{1,0:T(8,128)(2,1)} %hidden_ref.1) | copy-start | bytes 3932164
  2.2 15.2 %copy-start.3 = (s32[128]{0:T(128)S(1)}, s32[128]{0:T(128)}, u32[]{:S(2)}) copy-start(s32[128]{0:T(128)} %param.9) | copy-start | bytes 1540
  2.2 15.1 %copy-start.2 = (f32[128]{0:T(128)S(1)}, f32[128]{0:T(128)}, u32[]{:S(2)}) copy-start(f32[128]{0:T(128)} %param.8) | copy-start | bytes 1540
  2.2 11.5 %collective-permute-start.1 = (bf16[128,1280]{1,0:T(8,128)(2,1)S(1)}, bf16[128,1280]{1,0:T(8,128)(2,1)S(1)}, u32[]{:S(2)}, u32[]{:S(2)}) collective-permute-start(bf16[128,1280]{1,0:T(8,128)(2,1)S(1)} %get-tuple-element.30.refs_1_.refs_4_.refs_0_), channel_id=1, source_target_pairs={{0,4},{4,0},{8,12},{12,8},{1,5},{5,1},{9,13},{13,9},{2,6},{6,2},{1... | collective-permute-start | bytes 983048 | tf_op jit(solution)/shard_map/ppermute | solution.py:21
  5.2 10.6 %collective-permute-start.4 = (bf16[128,1280]{1,0:T(8,128)(2,1)S(1)}, bf16[128,1280]{1,0:T(8,128)(2,1)S(1)}, u32[]{:S(2)}, u32[]{:S(2)}) collective-permute-start(bf16[128,1280]{1,0:T(8,128)(2,1)S(1)} %get-tuple-element.29.refs_2_.refs_8_.refs_0_.refs_1_), channel_id=1, source_target_pairs={{0,8},{4,12},{8,0},{12,4},{1,9},{5,13},{9,1},{13,5},{2,10},{6,14},... | collective-permute-start | bytes 983048 | tf_op jit(solution)/shard_map/ppermute | solution.py:21
  6.8 16.0 %collective-permute-start = (bf16[128,2560]{1,0:T(8,128)(2,1)S(1)}, bf16[128,2560]{1,0:T(8,128)(2,1)S(1)}, u32[]{:S(2)}, u32[]{:S(2)}) collective-permute-start(bf16[128,2560]{1,0:T(8,128)(2,1)S(1)} %take_half.3), channel_id=1, source_target_pairs={{0,1},{1,0},{2,3},{3,2},{4,5},{5,4},{6,7},{7,6},{8,9},{9,8},{10,11... | collective-permute-start | bytes 1966088 | tf_op jit(solution)/shard_map/ppermute | solution.py:21
  8.5 14.7 %collective-permute-start.2 = (bf16[128,1280]{1,0:T(8,128)(2,1)S(1)}, bf16[128,1280]{1,0:T(8,128)(2,1)S(1)}, u32[]{:S(2)}, u32[]{:S(2)}) collective-permute-start(bf16[128,1280]{1,0:T(8,128)(2,1)S(1)} %get-tuple-element.29.refs_2_.refs_8_.refs_0_.refs_1_), channel_id=1, source_target_pairs={{0,4},{4,0},{8,12},{12,8},{1,5},{5,1},{9,13},{13,9},{2,6},{6,2},{1... | collective-permute-start | bytes 983048 | tf_op jit(solution)/shard_map/ppermute | solution.py:21
  9.0 14.2 %collective-permute-start.3 = (bf16[128,1280]{1,0:T(8,128)(2,1)S(1)}, bf16[128,1280]{1,0:T(8,128)(2,1)S(1)}, u32[]{:S(2)}, u32[]{:S(2)}) collective-permute-start(bf16[128,1280]{1,0:T(8,128)(2,1)S(1)} %get-tuple-element.30.refs_1_.refs_4_.refs_0_), channel_id=1, source_target_pairs={{0,8},{4,12},{8,0},{12,4},{1,9},{5,13},{9,1},{13,5},{2,10},{6,14},... | collective-permute-start | bytes 983048 | tf_op jit(solution)/shard_map/ppermute | solution.py:21
  13.8 14.7 %collective-permute-start.6 = (bf16[128,1280]{1,0:T(8,128)(2,1)S(1)}, bf16[128,1280]{1,0:T(8,128)(2,1)S(1)}, u32[]{:S(2)}, u32[]{:S(2)}) collective-permute-start(bf16[128,1280]{1,0:T(8,128)(2,1)S(1)} %collective-permute-done.1.refs_3_.refs_5_.refs_2_), channel_id=1, source_target_pairs={{0,8},{4,12},{8,0},{12,4},{1,9},{5,13},{9,1},{13,5},{2,10},{6,14},... | collective-permute-start | bytes 983048 | tf_op jit(solution)/shard_map/ppermute | solution.py:21
  15.9 12.6 %collective-permute-start.7 = (bf16[128,1280]{1,0:T(8,128)(2,1)S(1)}, bf16[128,1280]{1,0:T(8,128)(2,1)S(1)}, u32[]{:S(2)}, u32[]{:S(2)}) collective-permute-start(bf16[128,1280]{1,0:T(8,128)(2,1)S(1)} %collective-permute-done.4.refs_6_.refs_10_.refs_2_.refs_5_), channel_id=1, source_target_pairs={{0,4},{4,0},{8,12},{12,8},{1,5},{5,1},{9,13},{13,9},{2,6},{6,2},{1... | collective-permute-start | bytes 983048 | tf_op jit(solution)/shard_map/ppermute | solution.py:21
  23.9 9.3 %copy-start.1 = (s32[128]{0:T(128)S(1)}, s32[128]{0:T(128)}, u32[]{:S(2)}) copy-start(s32[128]{0:T(128)} %param.7) | copy-start | bytes 1540
  23.9 9.2 %collective-permute-start.5 = (f32[392,128]{1,0:T(8,128)S(1)}, f32[392,128]{1,0:T(8,128)S(1)}, u32[]{:S(2)}, u32[]{:S(2)}) collective-permute-start(f32[392,128]{1,0:T(8,128)S(1)} %get-tuple-element.31), channel_id=1, source_target_pairs={{0,1},{1,0},{2,3},{3,2},{4,5},{5,4},{6,7},{7,6},{8,9},{9,8},{10,11... | collective-permute-start | bytes 602120 | tf_op jit(solution)/shard_map/ppermute | solution.py:21
  28.8 4.3 %collective-permute-start.8 = (f32[128,128]{1,0:T(8,128)S(1)}, f32[128,128]{1,0:T(8,128)S(1)}, u32[]{:S(2)}, u32[]{:S(2)}) collective-permute-start(f32[128,128]{1,0:T(8,128)S(1)} %get-tuple-element.34), channel_id=1, source_target_pairs={{0,1},{1,0},{2,3},{3,2},{4,5},{5,4},{6,7},{7,6},{8,9},{9,8},{10,11... | collective-permute-start | bytes 196616 | tf_op jit(solution)/shard_map/ppermute | solution.py:21
  33.7 13.5 %collective-permute-start.11 = (bf16[128,1792]{1,0:T(8,128)(2,1)S(1)}, bf16[128,1792]{1,0:T(8,128)(2,1)S(1)}, u32[]{:S(2)}, u32[]{:S(2)}) collective-permute-start(bf16[128,1792]{1,0:T(8,128)(2,1)S(1)} %first_message.1.first_ref), channel_id=1, source_target_pairs={{0,1},{1,0},{2,3},{3,2},{4,5},{5,4},{6,7},{7,6},{8,9},{9,8},{10,11... | collective-permute-start | bytes 1376264 | tf_op jit(solution)/shard_map/ppermute | solution.py:21
  35.4 6.4 %collective-permute-start.10 = (f32[2,128]{1,0:T(2,128)S(1)}, f32[2,128]{1,0:T(2,128)S(1)}, u32[]{:S(2)}, u32[]{:S(2)}) collective-permute-start(f32[2,128]{1,0:T(2,128)S(1)} %pad_maximum_fusion.refs_0_.own_ref), channel_id=1, source_target_pairs={{2,0},{4,2},{6,4},{8,6},{10,8},{12,10},{14,12},{1,3},{3,5},{5,7},{... | collective-permute-start | bytes 3080 | tf_op jit(solution)/shard_map/ppermute | solution.py:423
  37.9 12.9 %collective-permute-start.9 = (bf16[128,1280]{1,0:T(8,128)(2,1)S(1)}, bf16[128,1280]{1,0:T(8,128)(2,1)S(1)}, u32[]{:S(2)}, u32[]{:S(2)}) collective-permute-start(bf16[128,1280]{1,0:T(8,128)(2,1)S(1)} %second_message.1), channel_id=1, source_target_pairs={{0,1},{1,0},{2,3},{3,2},{4,5},{5,4},{6,7},{7,6},{8,9},{9,8},{10,11... | collective-permute-start | bytes 983048 | tf_op jit(solution)/shard_map/ppermute | solution.py:21

commit v15 on v13

--- a/solution.py
+++ b/solution.py
@@ -409,7 +409,8 @@
     second = second_message(first, pieces[1::2])
     second_in = swapped(second, "section", 1)
 
-    late_own, late_tokens, _ = lax.optimization_barrier((own, flat_tokens, first))
+    late_own, _ = lax.optimization_barrier((own, first))
+    late_tokens, _ = lax.optimization_barrier((flat_tokens, second))
     logits, logprob, entropy = outputs(shard, late_tokens, mine, theirs, shards)
     partner_facts, logits, logprob, entropy = lax.optimization_barrier(
         (partner_facts, logits, logprob, entropy)

time: 51.7 us -> 57.4 us (1.11)
  waiting for transfers between devices: 22.9 us -> 29 us
    ppermute x11, waiting for transfers between devices: 22.7 us -> 29 us  [swapped(): return lax.ppermute(value, axis, pairs)]
  transfers between devices with their start and end apart: 12 -> 12, of which waited for: 7 -> 5; matrix products, arithmetic and copies ran while one was open for 0% -> 0% of each run, Pallas kernels for 8% -> 8%
where the time goes in v15:
time: 57.4 us; the launch traced here: 57.2 us
  waiting for transfers between devices  29 us (51%)
  starting transfers between devices  20.3 us (35%)
  Pallas kernels  5.72 us (10%)
  local copies, waits for them, and re-layouts  1.43 us (2%)
  between operations  0.8 us (1%)
    ppermute x11, waiting for transfers between devices, swapped(): return lax.ppermute(value, axis, pairs)  29 us
    ppermute x11, starting transfers between devices, swapped(): return lax.ppermute(value, axis, pairs)  19 us
    unnamed x10, local copies, waits for them, and re-layouts  1.43 us
    ppermute x1, starting transfers between devices, body(): outer = lax.ppermute(late_own, axes, beyond)  1.29 us
    pallas_call x1, Pallas kernels, staying_gradient(): pl.pallas_call(staying_kernel, out_shape=jax.ShapeDtypeStruct((rows, 4 *...  1.29 us
  transfers between devices with their start and end apart: 12, of which 5 were waited for; matrix products, arithmetic and copies ran while one was open for 0% of the time, Pallas kernels for 8%

profile of v15, /device:TPU:0, one launch (start us, length us, event | category | flops | bytes accessed | tf_op | source)
XLA Modules:
  0.0 57.2 jit_solution(342539786626035607)
XLA Ops:
  0.7 1.4 %copy-done.1 = bf16[128,5120]{1,0:T(8,128)(2,1)S(1)} copy-done((bf16[128,5120]{1,0:T(8,128)(2,1)S(1)}, bf16[128,5120]{1,0:T(8,128)(2,1)}, u32[]{:S(2)}) %copy-start.1) | copy-done | bytes 1310744
  2.2 3.0 %collective-permute-start.1 = (bf16[128,1280]{1,0:T(8,128)(2,1)S(1)}, bf16[128,1280]{1,0:T(8,128)(2,1)S(1)}, u32[]{:S(2)}, u32[]{:S(2)}) collective-permute-start(bf16[128,1280]{1,0:T(8,128)(2,1)S(1)} %get-tuple-element.30.refs_1_.refs_4_.refs_0_), channel_id=1, source_target_pairs={{0,4},{4,0},{8,12},{12,8},{1,5},{5,1},{9,13},{13,9},{2,6},{6,2},{1... | collective-permute-start | bytes 983048 | tf_op jit(solution)/shard_map/ppermute | solution.py:21
  5.2 1.5 %collective-permute-start.4 = (bf16[128,1280]{1,0:T(8,128)(2,1)S(1)}, bf16[128,1280]{1,0:T(8,128)(2,1)S(1)}, u32[]{:S(2)}, u32[]{:S(2)}) collective-permute-start(bf16[128,1280]{1,0:T(8,128)(2,1)S(1)} %get-tuple-element.29.refs_2_.refs_8_.refs_0_.refs_1_), channel_id=1, source_target_pairs={{0,8},{4,12},{8,0},{12,4},{1,9},{5,13},{9,1},{13,5},{2,10},{6,14},... | collective-permute-start | bytes 983048 | tf_op jit(solution)/shard_map/ppermute | solution.py:21
  6.8 1.6 %collective-permute-start = (bf16[128,2560]{1,0:T(8,128)(2,1)S(1)}, bf16[128,2560]{1,0:T(8,128)(2,1)S(1)}, u32[]{:S(2)}, u32[]{:S(2)}) collective-permute-start(bf16[128,2560]{1,0:T(8,128)(2,1)S(1)} %take_half.3), channel_id=1, source_target_pairs={{0,1},{1,0},{2,3},{3,2},{4,5},{5,4},{6,7},{7,6},{8,9},{9,8},{10,11... | collective-permute-start | bytes 1966088 | tf_op jit(solution)/shard_map/ppermute | solution.py:21
  8.4 0.5 collective-permute-start.2
  9.0 0.5 collective-permute-start.3
  9.5 4.3 %collective-permute-done.1.refs_3_.refs_5_.refs_2_ = bf16[128,1280]{1,0:T(8,128)(2,1)S(1)} collective-permute-done((bf16[128,1280]{1,0:T(8,128)(2,1)S(1)}, bf16[128,1280]{1,0:T(8,128)(2,1)S(1)}, u32[]{:S(2)}, u32[]{:S(2)}) %collective-permute-start.1) | collective-permute-done | bytes 327712 | tf_op jit(solution)/shard_map/ppermute | solution.py:21
  13.7 2.1 %collective-permute-start.6 = (bf16[128,1280]{1,0:T(8,128)(2,1)S(1)}, bf16[128,1280]{1,0:T(8,128)(2,1)S(1)}, u32[]{:S(2)}, u32[]{:S(2)}) collective-permute-start(bf16[128,1280]{1,0:T(8,128)(2,1)S(1)} %collective-permute-done.1.refs_3_.refs_5_.refs_2_), channel_id=1, source_target_pairs={{0,8},{4,12},{8,0},{12,4},{1,9},{5,13},{9,1},{13,5},{2,10},{6,14},... | collective-permute-start | bytes 983048 | tf_op jit(solution)/shard_map/ppermute | solution.py:21
  15.8 1.5 %collective-permute-start.7 = (bf16[128,1280]{1,0:T(8,128)(2,1)S(1)}, bf16[128,1280]{1,0:T(8,128)(2,1)S(1)}, u32[]{:S(2)}, u32[]{:S(2)}) collective-permute-start(bf16[128,1280]{1,0:T(8,128)(2,1)S(1)} %collective-permute-done.4.refs_6_.refs_10_.refs_2_.refs_5_), channel_id=1, source_target_pairs={{0,4},{4,0},{8,12},{12,8},{1,5},{5,1},{9,13},{13,9},{2,6},{6,2},{1... | collective-permute-start | bytes 983048 | tf_op jit(solution)/shard_map/ppermute | solution.py:21
  17.3 5.4 %collective-permute-done.partner_ref = bf16[128,2560]{1,0:T(8,128)(2,1)S(1)} collective-permute-done((bf16[128,2560]{1,0:T(8,128)(2,1)S(1)}, bf16[128,2560]{1,0:T(8,128)(2,1)S(1)}, u32[]{:S(2)}, u32[]{:S(2)}) %collective-permute-start) | collective-permute-done | bytes 655392 | tf_op jit(solution)/shard_map/ppermute | solution.py:21
  22.8 0.4 turned_rows.1.turned_ref
  23.2 0.7 %partial_scores.2 = (f32[384,128]{1,0:T(8,128)S(1)}, f32[392,128]{1,0:T(8,128)S(1)}) custom-call(bf16[2560,256]{1,0:T(8,128)(2,1)S(1)} %turned_rows.1.turned_ref, f32[2,128]{1,0:T(2,128)S(1)} %pad_maximum_fusion.refs_0_.own_ref, bf16[128,1280]{1,0:T(8,128)(2,1)S(1)} %get-tuple-element.30.refs_1_.refs_4_.refs_0_, ...), custom_call_target="tpu_custom_call" | custom-call | flops 503316480 | bytes 3276800 | tf_op jit(solution)/shard_map/partial_scores/pallas_call | solution.py:120
  23.9 1.6 %collective-permute-start.5 = (f32[392,128]{1,0:T(8,128)S(1)}, f32[392,128]{1,0:T(8,128)S(1)}, u32[]{:S(2)}, u32[]{:S(2)}) collective-permute-start(f32[392,128]{1,0:T(8,128)S(1)} %get-tuple-element.31), channel_id=1, source_target_pairs={{0,1},{1,0},{2,3},{3,2},{4,5},{5,4},{6,7},{7,6},{8,9},{9,8},{10,11... | collective-permute-start | bytes 602120 | tf_op jit(solution)/shard_map/ppermute | solution.py:21
  25.5 2.9 %collective-permute-done.6.refs_0_ = bf16[128,1280]{1,0:T(8,128)(2,1)S(1)} collective-permute-done((bf16[128,1280]{1,0:T(8,128)(2,1)S(1)}, bf16[128,1280]{1,0:T(8,128)(2,1)S(1)}, u32[]{:S(2)}, u32[]{:S(2)}) %collective-permute-start.6) | collective-permute-done | bytes 327712 | tf_op jit(solution)/shard_map/ppermute | solution.py:21
  28.4 0.4 partial_scores.3
  28.8 1.6 %collective-permute-start.8 = (f32[128,128]{1,0:T(8,128)S(1)}, f32[128,128]{1,0:T(8,128)S(1)}, u32[]{:S(2)}, u32[]{:S(2)}) collective-permute-start(f32[128,128]{1,0:T(8,128)S(1)} %get-tuple-element.34), channel_id=1, source_target_pairs={{0,1},{1,0},{2,3},{3,2},{4,5},{5,4},{6,7},{7,6},{8,9},{9,8},{10,11... | collective-permute-start | bytes 196616 | tf_op jit(solution)/shard_map/ppermute | solution.py:21
  30.4 2.7 %collective-permute-done.8.refs_3_ = f32[128,128]{1,0:T(8,128)S(1)} collective-permute-done((f32[128,128]{1,0:T(8,128)S(1)}, f32[128,128]{1,0:T(8,128)S(1)}, u32[]{:S(2)}, u32[]{:S(2)}) %collective-permute-start.8) | collective-permute-done | bytes 65568 | tf_op jit(solution)/shard_map/ppermute | solution.py:21
  33.1 0.6 first_message.1.first_ref
  33.7 1.3 %collective-permute-start.10 = (f32[2,128]{1,0:T(2,128)S(1)}, f32[2,128]{1,0:T(2,128)S(1)}, u32[]{:S(2)}, u32[]{:S(2)}) collective-permute-start(f32[2,128]{1,0:T(2,128)S(1)} %pad_maximum_fusion.refs_0_.own_ref), channel_id=1, source_target_pairs={{2,0},{4,2},{6,4},{8,6},{10,8},{12,10},{14,12},{1,3},{3,5},{5,7},{... | collective-permute-start | bytes 3080 | tf_op jit(solution)/shard_map/ppermute | solution.py:421
  35.4 4.8 %collective-permute-start.9 = (bf16[128,1280]{1,0:T(8,128)(2,1)S(1)}, bf16[128,1280]{1,0:T(8,128)(2,1)S(1)}, u32[]{:S(2)}, u32[]{:S(2)}) collective-permute-start(bf16[128,1280]{1,0:T(8,128)(2,1)S(1)} %second_message.1), channel_id=1, source_target_pairs={{0,1},{1,0},{2,3},{3,2},{4,5},{5,4},{6,7},{7,6},{8,9},{9,8},{10,11... | collective-permute-start | bytes 983048 | tf_op jit(solution)/shard_map/ppermute | solution.py:21
  40.3 0.8 %outputs.1 = (bf16[128,512]{1,0:T(8,128)(2,1)}, f32[1,128]{1,0:T(1,128)}, f32[1,128]{1,0:T(1,128)}) custom-call(s32[1]{0:T(128)} %bitcast.3.shard_ref, s32[1,128]{1,0:T(1,128)S(1)} %bitcast.9, f32[384,128]{1,0:T(8,128)S(1)} %get-tuple-element.32.refs_0_, f32[128,128]{1,0:T(8,128)S(1)} %get-tuple-element.33.refs_1_, ...), custom_call_target="tpu_custom_call" | custom-call | flops 655360 | bytes 786432 | tf_op jit(solution)/shard_map/outputs/pallas_call | solution.py:210
  41.4 13.7 %collective-permute-done.11.first_ref = bf16[128,1792]{1,0:T(8,128)(2,1)S(1)} collective-permute-done((bf16[128,1792]{1,0:T(8,128)(2,1)S(1)}, bf16[128,1792]{1,0:T(8,128)(2,1)S(1)}, u32[]{:S(2)}, u32[]{:S(2)}) %collective-permute-start.11) | collective-permute-done | bytes 458784 | tf_op jit(solution)/shard_map/ppermute | solution.py:21
  55.1 1.3 %staying_gradient.1._ = bf16[128,5120]{1,0:T(8,128)(2,1)} custom-call(s32[1]{0:T(128)} %bitcast.which_ref, bf16[128,1792]{1,0:T(8,128)(2,1)S(1)} %collective-permute-done.11.first_ref, f32[128,128]{1,0:T(8,128)S(1)} %advantage.1.advantage_ref, bf16[128,1280]{1,0:T(8,128)(2,1)S(1)} %get-tuple-element.30.refs_1_.refs_4_.refs_0_, ...), custom_call_target="tpu_custom_call" | custom-call | flops 335544320 | bytes 3276800 | tf_op jit(solution)/shard_map/staying_gradient/pallas_call | solution.py:336
  56.4 0.8 %place_second.1 = bf16[128,5120]{1,0:T(8,128)(2,1)} custom-call(s32[1]{0:T(128)} %bitcast.which_ref, bf16[128,1280]{1,0:T(8,128)(2,1)S(1)} %collective-permute-done.9.second_ref, f32[128,128]{1,0:T(8,128)S(1)} %advantage.1.advantage_ref, bf16[128,5120]{1,0:T(8,128)(2,1)} %staying_gradient.1._), custom_call_target="tpu_custom_call", output_to_operand_aliasing={{}: (3, {})} | custom-call | tf_op jit(solution)/shard_map/place_second/pallas_call | solution.py:367
  (23 shorter events, 0.9 us)
Async XLA Ops:
  0.6 6.1 %copy-start = (bf16[128,5120]{1,0:T(8,128)(2,1)S(1)}, bf16[128,5120]{1,0:T(8,128)(2,1)}, u32[]{:S(2)}) copy-start(bf16[128,5120]{1,0:T(8,128)(2,1)} %hidden_ref.1) | copy-start | bytes 3932164
  0.7 1.4 %copy-start.1 = (bf16[128,5120]{1,0:T(8,128)(2,1)S(1)}, bf16[128,5120]{1,0:T(8,128)(2,1)}, u32[]{:S(2)}) copy-start(bf16[128,5120]{1,0:T(8,128)(2,1)} %value_ref.1) | copy-start | bytes 3932164
  2.2 15.2 %copy-start.4 = (s32[128]{0:T(128)S(1)}, s32[128]{0:T(128)}, u32[]{:S(2)}) copy-start(s32[128]{0:T(128)} %param.9) | copy-start | bytes 1540
  2.2 15.1 %copy-start.3 = (f32[128]{0:T(128)S(1)}, f32[128]{0:T(128)}, u32[]{:S(2)}) copy-start(f32[128]{0:T(128)} %param.8) | copy-start | bytes 1540
  2.2 11.5 %collective-permute-start.1 = (bf16[128,1280]{1,0:T(8,128)(2,1)S(1)}, bf16[128,1280]{1,0:T(8,128)(2,1)S(1)}, u32[]{:S(2)}, u32[]{:S(2)}) collective-permute-start(bf16[128,1280]{1,0:T(8,128)(2,1)S(1)} %get-tuple-element.30.refs_1_.refs_4_.refs_0_), channel_id=1, source_target_pairs={{0,4},{4,0},{8,12},{12,8},{1,5},{5,1},{9,13},{13,9},{2,6},{6,2},{1... | collective-permute-start | bytes 983048 | tf_op jit(solution)/shard_map/ppermute | solution.py:21
  5.2 10.6 %collective-permute-start.4 = (bf16[128,1280]{1,0:T(8,128)(2,1)S(1)}, bf16[128,1280]{1,0:T(8,128)(2,1)S(1)}, u32[]{:S(2)}, u32[]{:S(2)}) collective-permute-start(bf16[128,1280]{1,0:T(8,128)(2,1)S(1)} %get-tuple-element.29.refs_2_.refs_8_.refs_0_.refs_1_), channel_id=1, source_target_pairs={{0,8},{4,12},{8,0},{12,4},{1,9},{5,13},{9,1},{13,5},{2,10},{6,14},... | collective-permute-start | bytes 983048 | tf_op jit(solution)/shard_map/ppermute | solution.py:21
  6.8 16.0 %collective-permute-start = (bf16[128,2560]{1,0:T(8,128)(2,1)S(1)}, bf16[128,2560]{1,0:T(8,128)(2,1)S(1)}, u32[]{:S(2)}, u32[]{:S(2)}) collective-permute-start(bf16[128,2560]{1,0:T(8,128)(2,1)S(1)} %take_half.3), channel_id=1, source_target_pairs={{0,1},{1,0},{2,3},{3,2},{4,5},{5,4},{6,7},{7,6},{8,9},{9,8},{10,11... | collective-permute-start | bytes 1966088 | tf_op jit(solution)/shard_map/ppermute | solution.py:21
  8.4 14.7 %collective-permute-start.2 = (bf16[128,1280]{1,0:T(8,128)(2,1)S(1)}, bf16[128,1280]{1,0:T(8,128)(2,1)S(1)}, u32[]{:S(2)}, u32[]{:S(2)}) collective-permute-start(bf16[128,1280]{1,0:T(8,128)(2,1)S(1)} %get-tuple-element.29.refs_2_.refs_8_.refs_0_.refs_1_), channel_id=1, source_target_pairs={{0,4},{4,0},{8,12},{12,8},{1,5},{5,1},{9,13},{13,9},{2,6},{6,2},{1... | collective-permute-start | bytes 983048 | tf_op jit(solution)/shard_map/ppermute | solution.py:21
  9.0 14.2 %collective-permute-start.3 = (bf16[128,1280]{1,0:T(8,128)(2,1)S(1)}, bf16[128,1280]{1,0:T(8,128)(2,1)S(1)}, u32[]{:S(2)}, u32[]{:S(2)}) collective-permute-start(bf16[128,1280]{1,0:T(8,128)(2,1)S(1)} %get-tuple-element.30.refs_1_.refs_4_.refs_0_), channel_id=1, source_target_pairs={{0,8},{4,12},{8,0},{12,4},{1,9},{5,13},{9,1},{13,5},{2,10},{6,14},... | collective-permute-start | bytes 983048 | tf_op jit(solution)/shard_map/ppermute | solution.py:21
  13.7 14.7 %collective-permute-start.6 = (bf16[128,1280]{1,0:T(8,128)(2,1)S(1)}, bf16[128,1280]{1,0:T(8,128)(2,1)S(1)}, u32[]{:S(2)}, u32[]{:S(2)}) collective-permute-start(bf16[128,1280]{1,0:T(8,128)(2,1)S(1)} %collective-permute-done.1.refs_3_.refs_5_.refs_2_), channel_id=1, source_target_pairs={{0,8},{4,12},{8,0},{12,4},{1,9},{5,13},{9,1},{13,5},{2,10},{6,14},... | collective-permute-start | bytes 983048 | tf_op jit(solution)/shard_map/ppermute | solution.py:21
  15.8 12.6 %collective-permute-start.7 = (bf16[128,1280]{1,0:T(8,128)(2,1)S(1)}, bf16[128,1280]{1,0:T(8,128)(2,1)S(1)}, u32[]{:S(2)}, u32[]{:S(2)}) collective-permute-start(bf16[128,1280]{1,0:T(8,128)(2,1)S(1)} %collective-permute-done.4.refs_6_.refs_10_.refs_2_.refs_5_), channel_id=1, source_target_pairs={{0,4},{4,0},{8,12},{12,8},{1,5},{5,1},{9,13},{13,9},{2,6},{6,2},{1... | collective-permute-start | bytes 983048 | tf_op jit(solution)/shard_map/ppermute | solution.py:21
  23.9 9.2 %copy-start.2 = (s32[128]{0:T(128)S(1)}, s32[128]{0:T(128)}, u32[]{:S(2)}) copy-start(s32[128]{0:T(128)} %param.7) | copy-start | bytes 1540
  23.9 9.2 %collective-permute-start.5 = (f32[392,128]{1,0:T(8,128)S(1)}, f32[392,128]{1,0:T(8,128)S(1)}, u32[]{:S(2)}, u32[]{:S(2)}) collective-permute-start(f32[392,128]{1,0:T(8,128)S(1)} %get-tuple-element.31), channel_id=1, source_target_pairs={{0,1},{1,0},{2,3},{3,2},{4,5},{5,4},{6,7},{7,6},{8,9},{9,8},{10,11... | collective-permute-start | bytes 602120 | tf_op jit(solution)/shard_map/ppermute | solution.py:21
  28.8 4.3 %collective-permute-start.8 = (f32[128,128]{1,0:T(8,128)S(1)}, f32[128,128]{1,0:T(8,128)S(1)}, u32[]{:S(2)}, u32[]{:S(2)}) collective-permute-start(f32[128,128]{1,0:T(8,128)S(1)} %get-tuple-element.34), channel_id=1, source_target_pairs={{0,1},{1,0},{2,3},{3,2},{4,5},{5,4},{6,7},{7,6},{8,9},{9,8},{10,11... | collective-permute-start | bytes 196616 | tf_op jit(solution)/shard_map/ppermute | solution.py:21
  33.7 7.4 %collective-permute-start.10 = (f32[2,128]{1,0:T(2,128)S(1)}, f32[2,128]{1,0:T(2,128)S(1)}, u32[]{:S(2)}, u32[]{:S(2)}) collective-permute-start(f32[2,128]{1,0:T(2,128)S(1)} %pad_maximum_fusion.refs_0_.own_ref), channel_id=1, source_target_pairs={{2,0},{4,2},{6,4},{8,6},{10,8},{12,10},{14,12},{1,3},{3,5},{5,7},{... | collective-permute-start | bytes 3080 | tf_op jit(solution)/shard_map/ppermute | solution.py:421
  35.4 21.1 %collective-permute-start.9 = (bf16[128,1280]{1,0:T(8,128)(2,1)S(1)}, bf16[128,1280]{1,0:T(8,128)(2,1)S(1)}, u32[]{:S(2)}, u32[]{:S(2)}) collective-permute-start(bf16[128,1280]{1,0:T(8,128)(2,1)S(1)} %second_message.1), channel_id=1, source_target_pairs={{0,1},{1,0},{2,3},{3,2},{4,5},{5,4},{6,7},{7,6},{8,9},{9,8},{10,11... | collective-permute-start | bytes 983048 | tf_op jit(solution)/shard_map/ppermute | solution.py:21
  40.2 14.9 %collective-permute-start.11 = (bf16[128,1792]{1,0:T(8,128)(2,1)S(1)}, bf16[128,1792]{1,0:T(8,128)(2,1)S(1)}, u32[]{:S(2)}, u32[]{:S(2)}) collective-permute-start(bf16[128,1792]{1,0:T(8,128)(2,1)S(1)} %first_message.1.first_ref), channel_id=1, source_target_pairs={{0,1},{1,0},{2,3},{3,2},{4,5},{5,4},{6,7},{7,6},{8,9},{9,8},{10,11... | collective-permute-start | bytes 1376264 | tf_op jit(solution)/shard_map/ppermute | solution.py:21

commit v16 on v13

--- a/solution.py
+++ b/solution.py
@@ -347,7 +347,7 @@
 
 def placed_kernel(which_ref, second_ref, advantage_ref, _, out_ref, held_ref, sem):
     depth = second_ref.shape[1]
-    parts = 5 if depth % 1280 == 0 else 1
+    parts = 1
     width = depth // parts
     start = (1 - which_ref[0]) * (2 * depth) + depth
     copies = []
@@ -369,7 +369,7 @@
         out_shape=jax.ShapeDtypeStruct(gradient.shape, gradient.dtype),
         in_specs=[SMEM, VMEM, VMEM, HBM],
         out_specs=HBM,
-        scratch_shapes=[pltpu.VMEM(second.shape, BF16), pltpu.SemaphoreType.DMA((5,))],
+        scratch_shapes=[pltpu.VMEM(second.shape, BF16), pltpu.SemaphoreType.DMA((1,))],
         input_output_aliases={3: 0},
         compiler_params=PARAMS,
         name="place_second",

time: 51.7 us -> 51.7 us (level)
  no operation moved by 1% of the time
where the time goes in v16:
time: 51.7 us; the launch traced here: 51.5 us
  waiting for transfers between devices  22.9 us (44%)
  starting transfers between devices  20.6 us (40%)
  Pallas kernels  5.72 us (11%)
  local copies, waits for them, and re-layouts  1.43 us (3%)
  between operations  0.79 us (2%)
    ppermute x11, waiting for transfers between devices, swapped(): return lax.ppermute(value, axis, pairs)  22.7 us
    ppermute x11, starting transfers between devices, swapped(): return lax.ppermute(value, axis, pairs)  19.4 us
    unnamed x10, local copies, waits for them, and re-layouts  1.43 us
    ppermute x1, starting transfers between devices, body(): outer = lax.ppermute(late_own, axes, beyond)  1.28 us
    pallas_call x1, Pallas kernels, staying_gradient(): pl.pallas_call(staying_kernel, out_shape=jax.ShapeDtypeStruct((rows, 4 *...  1.28 us
    pallas_call x2, Pallas kernels, partial_scores(): pl.pallas_call(functools.partial(partial_kernel, len(facts), len(heads)),...  1.08 us
  transfers between devices with their start and end apart: 12, of which 7 were waited for; matrix products, arithmetic and copies ran while one was open for 0% of the time, Pallas kernels for 8%

profile of v16, /device:TPU:0, one launch (start us, length us, event | category | flops | bytes accessed | tf_op | source)
XLA Modules:
  0.0 51.5 jit_solution(4833498060513431042)
XLA Ops:
  0.7 1.4 %copy-done.1 = bf16[128,5120]{1,0:T(8,128)(2,1)S(1)} copy-done((bf16[128,5120]{1,0:T(8,128)(2,1)S(1)}, bf16[128,5120]{1,0:T(8,128)(2,1)}, u32[]{:S(2)}) %copy-start.1) | copy-done | bytes 1310744
  2.2 3.0 %collective-permute-start.1 = (bf16[128,1280]{1,0:T(8,128)(2,1)S(1)}, bf16[128,1280]{1,0:T(8,128)(2,1)S(1)}, u32[]{:S(2)}, u32[]{:S(2)}) collective-permute-start(bf16[128,1280]{1,0:T(8,128)(2,1)S(1)} %get-tuple-element.30.refs_1_.refs_4_.refs_0_), channel_id=1, source_target_pairs={{0,4},{4,0},{8,12},{12,8},{1,5},{5,1},{9,13},{13,9},{2,6},{6,2},{1... | collective-permute-start | bytes 983048 | tf_op jit(solution)/shard_map/ppermute | solution.py:21
  5.2 1.5 %collective-permute-start.4 = (bf16[128,1280]{1,0:T(8,128)(2,1)S(1)}, bf16[128,1280]{1,0:T(8,128)(2,1)S(1)}, u32[]{:S(2)}, u32[]{:S(2)}) collective-permute-start(bf16[128,1280]{1,0:T(8,128)(2,1)S(1)} %get-tuple-element.29.refs_2_.refs_8_.refs_0_.refs_1_), channel_id=1, source_target_pairs={{0,8},{4,12},{8,0},{12,4},{1,9},{5,13},{9,1},{13,5},{2,10},{6,14},... | collective-permute-start | bytes 983048 | tf_op jit(solution)/shard_map/ppermute | solution.py:21
  6.8 1.6 %collective-permute-start = (bf16[128,2560]{1,0:T(8,128)(2,1)S(1)}, bf16[128,2560]{1,0:T(8,128)(2,1)S(1)}, u32[]{:S(2)}, u32[]{:S(2)}) collective-permute-start(bf16[128,2560]{1,0:T(8,128)(2,1)S(1)} %take_half.3), channel_id=1, source_target_pairs={{0,1},{1,0},{2,3},{3,2},{4,5},{5,4},{6,7},{7,6},{8,9},{9,8},{10,11... | collective-permute-start | bytes 1966088 | tf_op jit(solution)/shard_map/ppermute | solution.py:21
  8.4 0.5 %collective-permute-start.2 = (bf16[128,1280]{1,0:T(8,128)(2,1)S(1)}, bf16[128,1280]{1,0:T(8,128)(2,1)S(1)}, u32[]{:S(2)}, u32[]{:S(2)}) collective-permute-start(bf16[128,1280]{1,0:T(8,128)(2,1)S(1)} %get-tuple-element.29.refs_2_.refs_8_.refs_0_.refs_1_), channel_id=1, source_target_pairs={{0,4},{4,0},{8,12},{12,8},{1,5},{5,1},{9,13},{13,9},{2,6},{6,2},{1... | collective-permute-start | bytes 983048 | tf_op jit(solution)/shard_map/ppermute | solution.py:21
  9.0 0.5 collective-permute-start.3
  9.5 4.3 %collective-permute-done.1.refs_3_.refs_5_.refs_2_ = bf16[128,1280]{1,0:T(8,128)(2,1)S(1)} collective-permute-done((bf16[128,1280]{1,0:T(8,128)(2,1)S(1)}, bf16[128,1280]{1,0:T(8,128)(2,1)S(1)}, u32[]{:S(2)}, u32[]{:S(2)}) %collective-permute-start.1) | collective-permute-done | bytes 327712 | tf_op jit(solution)/shard_map/ppermute | solution.py:21
  13.7 2.1 %collective-permute-start.6 = (bf16[128,1280]{1,0:T(8,128)(2,1)S(1)}, bf16[128,1280]{1,0:T(8,128)(2,1)S(1)}, u32[]{:S(2)}, u32[]{:S(2)}) collective-permute-start(bf16[128,1280]{1,0:T(8,128)(2,1)S(1)} %collective-permute-done.1.refs_3_.refs_5_.refs_2_), channel_id=1, source_target_pairs={{0,8},{4,12},{8,0},{12,4},{1,9},{5,13},{9,1},{13,5},{2,10},{6,14},... | collective-permute-start | bytes 983048 | tf_op jit(solution)/shard_map/ppermute | solution.py:21
  15.8 1.5 %collective-permute-start.7 = (bf16[128,1280]{1,0:T(8,128)(2,1)S(1)}, bf16[128,1280]{1,0:T(8,128)(2,1)S(1)}, u32[]{:S(2)}, u32[]{:S(2)}) collective-permute-start(bf16[128,1280]{1,0:T(8,128)(2,1)S(1)} %collective-permute-done.4.refs_6_.refs_10_.refs_2_.refs_5_), channel_id=1, source_target_pairs={{0,4},{4,0},{8,12},{12,8},{1,5},{5,1},{9,13},{13,9},{2,6},{6,2},{1... | collective-permute-start | bytes 983048 | tf_op jit(solution)/shard_map/ppermute | solution.py:21
  17.3 5.4 %collective-permute-done.partner_ref = bf16[128,2560]{1,0:T(8,128)(2,1)S(1)} collective-permute-done((bf16[128,2560]{1,0:T(8,128)(2,1)S(1)}, bf16[128,2560]{1,0:T(8,128)(2,1)S(1)}, u32[]{:S(2)}, u32[]{:S(2)}) %collective-permute-start) | collective-permute-done | bytes 655392 | tf_op jit(solution)/shard_map/ppermute | solution.py:21
  23.2 0.7 %partial_scores.2 = (f32[384,128]{1,0:T(8,128)S(1)}, f32[392,128]{1,0:T(8,128)S(1)}) custom-call(bf16[2560,256]{1,0:T(8,128)(2,1)S(1)} %turned_rows.1.turned_ref, f32[2,128]{1,0:T(2,128)S(1)} %pad_maximum_fusion.refs_0_.own_ref, bf16[128,1280]{1,0:T(8,128)(2,1)S(1)} %get-tuple-element.30.refs_1_.refs_4_.refs_0_, ...), custom_call_target="tpu_custom_call" | custom-call | flops 503316480 | bytes 3276800 | tf_op jit(solution)/shard_map/partial_scores/pallas_call | solution.py:120
  23.9 1.6 %collective-permute-start.5 = (f32[392,128]{1,0:T(8,128)S(1)}, f32[392,128]{1,0:T(8,128)S(1)}, u32[]{:S(2)}, u32[]{:S(2)}) collective-permute-start(f32[392,128]{1,0:T(8,128)S(1)} %get-tuple-element.31), channel_id=1, source_target_pairs={{0,1},{1,0},{2,3},{3,2},{4,5},{5,4},{6,7},{7,6},{8,9},{9,8},{10,11... | collective-permute-start | bytes 602120 | tf_op jit(solution)/shard_map/ppermute | solution.py:21
  25.5 2.9 %collective-permute-done.6.refs_0_ = bf16[128,1280]{1,0:T(8,128)(2,1)S(1)} collective-permute-done((bf16[128,1280]{1,0:T(8,128)(2,1)S(1)}, bf16[128,1280]{1,0:T(8,128)(2,1)S(1)}, u32[]{:S(2)}, u32[]{:S(2)}) %collective-permute-start.6) | collective-permute-done | bytes 327712 | tf_op jit(solution)/shard_map/ppermute | solution.py:21
  28.8 1.6 %collective-permute-start.8 = (f32[128,128]{1,0:T(8,128)S(1)}, f32[128,128]{1,0:T(8,128)S(1)}, u32[]{:S(2)}, u32[]{:S(2)}) collective-permute-start(f32[128,128]{1,0:T(8,128)S(1)} %get-tuple-element.34), channel_id=1, source_target_pairs={{0,1},{1,0},{2,3},{3,2},{4,5},{5,4},{6,7},{7,6},{8,9},{9,8},{10,11... | collective-permute-start | bytes 196616 | tf_op jit(solution)/shard_map/ppermute | solution.py:21
  30.4 2.7 %collective-permute-done.8.refs_3_ = f32[128,128]{1,0:T(8,128)S(1)} collective-permute-done((f32[128,128]{1,0:T(8,128)S(1)}, f32[128,128]{1,0:T(8,128)S(1)}, u32[]{:S(2)}, u32[]{:S(2)}) %collective-permute-start.8) | collective-permute-done | bytes 65568 | tf_op jit(solution)/shard_map/ppermute | solution.py:21
  33.1 0.6 %first_message.1.first_ref = bf16[128,1792]{1,0:T(8,128)(2,1)S(1)} custom-call(s32[1]{0:T(128)} %bitcast.3.shard_ref, s32[1,128]{1,0:T(1,128)S(1)} %bitcast.8, f32[384,128]{1,0:T(8,128)S(1)} %get-tuple-element.32.refs_0_, f32[128,128]{1,0:T(8,128)S(1)} %get-tuple-element.33.refs_1_, f32[392,128]{1,0:T(8,128)S(1)} %collective-permute-done.5.refs_2_.partner_ref, ...), custom_call_target="tpu_custom_call" | custom-call | flops 167772160 | bytes 1638400 | tf_op jit(solution)/shard_map/first_message/pallas_call | solution.py:267
  33.7 1.6 %collective-permute-start.11 = (bf16[128,1792]{1,0:T(8,128)(2,1)S(1)}, bf16[128,1792]{1,0:T(8,128)(2,1)S(1)}, u32[]{:S(2)}, u32[]{:S(2)}) collective-permute-start(bf16[128,1792]{1,0:T(8,128)(2,1)S(1)} %first_message.1.first_ref), channel_id=1, source_target_pairs={{0,1},{1,0},{2,3},{3,2},{4,5},{5,4},{6,7},{7,6},{8,9},{9,8},{10,11... | collective-permute-start | bytes 1376264 | tf_op jit(solution)/shard_map/ppermute | solution.py:21
  35.3 1.3 %collective-permute-start.10 = (f32[2,128]{1,0:T(2,128)S(1)}, f32[2,128]{1,0:T(2,128)S(1)}, u32[]{:S(2)}, u32[]{:S(2)}) collective-permute-start(f32[2,128]{1,0:T(2,128)S(1)} %pad_maximum_fusion.refs_0_.own_ref), channel_id=1, source_target_pairs={{2,0},{4,2},{6,4},{8,6},{10,8},{12,10},{14,12},{1,3},{3,5},{5,7},{... | collective-permute-start | bytes 3080 | tf_op jit(solution)/shard_map/ppermute | solution.py:420
  37.0 0.9 %outputs.1 = (bf16[128,512]{1,0:T(8,128)(2,1)}, f32[1,128]{1,0:T(1,128)}, f32[1,128]{1,0:T(1,128)}) custom-call(s32[1]{0:T(128)} %bitcast.3.shard_ref, s32[1,128]{1,0:T(1,128)S(1)} %bitcast.9, f32[384,128]{1,0:T(8,128)S(1)} %get-tuple-element.32.refs_0_, f32[128,128]{1,0:T(8,128)S(1)} %get-tuple-element.33.refs_1_, ...), custom_call_target="tpu_custom_call" | custom-call | flops 655360 | bytes 786432 | tf_op jit(solution)/shard_map/outputs/pallas_call | solution.py:210
  37.8 3.7 %collective-permute-start.9 = (bf16[128,1280]{1,0:T(8,128)(2,1)S(1)}, bf16[128,1280]{1,0:T(8,128)(2,1)S(1)}, u32[]{:S(2)}, u32[]{:S(2)}) collective-permute-start(bf16[128,1280]{1,0:T(8,128)(2,1)S(1)} %second_message.1), channel_id=1, source_target_pairs={{0,1},{1,0},{2,3},{3,2},{4,5},{5,4},{6,7},{7,6},{8,9},{9,8},{10,11... | collective-permute-start | bytes 983048 | tf_op jit(solution)/shard_map/ppermute | solution.py:21
  42.0 5.3 %collective-permute-done.11.first_ref = bf16[128,1792]{1,0:T(8,128)(2,1)S(1)} collective-permute-done((bf16[128,1792]{1,0:T(8,128)(2,1)S(1)}, bf16[128,1792]{1,0:T(8,128)(2,1)S(1)}, u32[]{:S(2)}, u32[]{:S(2)}) %collective-permute-start.11) | collective-permute-done | bytes 458784 | tf_op jit(solution)/shard_map/ppermute | solution.py:21
  47.2 1.3 %staying_gradient.1._ = bf16[128,5120]{1,0:T(8,128)(2,1)} custom-call(s32[1]{0:T(128)} %bitcast.which_ref, bf16[128,1792]{1,0:T(8,128)(2,1)S(1)} %collective-permute-done.11.first_ref, f32[128,128]{1,0:T(8,128)S(1)} %advantage.1.advantage_ref, bf16[128,1280]{1,0:T(8,128)(2,1)S(1)} %get-tuple-element.30.refs_1_.refs_4_.refs_0_, ...), custom_call_target="tpu_custom_call" | custom-call | flops 335544320 | bytes 3276800 | tf_op jit(solution)/shard_map/staying_gradient/pallas_call | solution.py:336
  48.5 2.2 %collective-permute-done.9.second_ref = bf16[128,1280]{1,0:T(8,128)(2,1)S(1)} collective-permute-done((bf16[128,1280]{1,0:T(8,128)(2,1)S(1)}, bf16[128,1280]{1,0:T(8,128)(2,1)S(1)}, u32[]{:S(2)}, u32[]{:S(2)}) %collective-permute-start.9) | collective-permute-done | bytes 327712 | tf_op jit(solution)/shard_map/ppermute | solution.py:21
  50.7 0.8 %place_second.1 = bf16[128,5120]{1,0:T(8,128)(2,1)} custom-call(s32[1]{0:T(128)} %bitcast.which_ref, bf16[128,1280]{1,0:T(8,128)(2,1)S(1)} %collective-permute-done.9.second_ref, f32[128,128]{1,0:T(8,128)S(1)} %advantage.1.advantage_ref, bf16[128,5120]{1,0:T(8,128)(2,1)} %staying_gradient.1._), custom_call_target="tpu_custom_call", output_to_operand_aliasing={{}: (3, {})} | custom-call | tf_op jit(solution)/shard_map/place_second/pallas_call | solution.py:367
  (23 shorter events, 1.8 us)
Async XLA Ops:
  0.6 6.1 %copy-start = (bf16[128,5120]{1,0:T(8,128)(2,1)S(1)}, bf16[128,5120]{1,0:T(8,128)(2,1)}, u32[]{:S(2)}) copy-start(bf16[128,5120]{1,0:T(8,128)(2,1)} %hidden_ref.1) | copy-start | bytes 3932164
  0.7 1.4 %copy-start.1 = (bf16[128,5120]{1,0:T(8,128)(2,1)S(1)}, bf16[128,5120]{1,0:T(8,128)(2,1)}, u32[]{:S(2)}) copy-start(bf16[128,5120]{1,0:T(8,128)(2,1)} %value_ref.1) | copy-start | bytes 3932164
  2.2 15.2 %copy-start.4 = (s32[128]{0:T(128)S(1)}, s32[128]{0:T(128)}, u32[]{:S(2)}) copy-start(s32[128]{0:T(128)} %param.9) | copy-start | bytes 1540
  2.2 15.1 %copy-start.3 = (f32[128]{0:T(128)S(1)}, f32[128]{0:T(128)}, u32[]{:S(2)}) copy-start(f32[128]{0:T(128)} %param.8) | copy-start | bytes 1540
  2.2 11.5 %collective-permute-start.1 = (bf16[128,1280]{1,0:T(8,128)(2,1)S(1)}, bf16[128,1280]{1,0:T(8,128)(2,1)S(1)}, u32[]{:S(2)}, u32[]{:S(2)}) collective-permute-start(bf16[128,1280]{1,0:T(8,128)(2,1)S(1)} %get-tuple-element.30.refs_1_.refs_4_.refs_0_), channel_id=1, source_target_pairs={{0,4},{4,0},{8,12},{12,8},{1,5},{5,1},{9,13},{13,9},{2,6},{6,2},{1... | collective-permute-start | bytes 983048 | tf_op jit(solution)/shard_map/ppermute | solution.py:21
  5.2 10.6 %collective-permute-start.4 = (bf16[128,1280]{1,0:T(8,128)(2,1)S(1)}, bf16[128,1280]{1,0:T(8,128)(2,1)S(1)}, u32[]{:S(2)}, u32[]{:S(2)}) collective-permute-start(bf16[128,1280]{1,0:T(8,128)(2,1)S(1)} %get-tuple-element.29.refs_2_.refs_8_.refs_0_.refs_1_), channel_id=1, source_target_pairs={{0,8},{4,12},{8,0},{12,4},{1,9},{5,13},{9,1},{13,5},{2,10},{6,14},... | collective-permute-start | bytes 983048 | tf_op jit(solution)/shard_map/ppermute | solution.py:21
  6.8 16.0 %collective-permute-start = (bf16[128,2560]{1,0:T(8,128)(2,1)S(1)}, bf16[128,2560]{1,0:T(8,128)(2,1)S(1)}, u32[]{:S(2)}, u32[]{:S(2)}) collective-permute-start(bf16[128,2560]{1,0:T(8,128)(2,1)S(1)} %take_half.3), channel_id=1, source_target_pairs={{0,1},{1,0},{2,3},{3,2},{4,5},{5,4},{6,7},{7,6},{8,9},{9,8},{10,11... | collective-permute-start | bytes 1966088 | tf_op jit(solution)/shard_map/ppermute | solution.py:21
  8.4 14.7 %collective-permute-start.2 = (bf16[128,1280]{1,0:T(8,128)(2,1)S(1)}, bf16[128,1280]{1,0:T(8,128)(2,1)S(1)}, u32[]{:S(2)}, u32[]{:S(2)}) collective-permute-start(bf16[128,1280]{1,0:T(8,128)(2,1)S(1)} %get-tuple-element.29.refs_2_.refs_8_.refs_0_.refs_1_), channel_id=1, source_target_pairs={{0,4},{4,0},{8,12},{12,8},{1,5},{5,1},{9,13},{13,9},{2,6},{6,2},{1... | collective-permute-start | bytes 983048 | tf_op jit(solution)/shard_map/ppermute | solution.py:21
  9.0 14.2 %collective-permute-start.3 = (bf16[128,1280]{1,0:T(8,128)(2,1)S(1)}, bf16[128,1280]{1,0:T(8,128)(2,1)S(1)}, u32[]{:S(2)}, u32[]{:S(2)}) collective-permute-start(bf16[128,1280]{1,0:T(8,128)(2,1)S(1)} %get-tuple-element.30.refs_1_.refs_4_.refs_0_), channel_id=1, source_target_pairs={{0,8},{4,12},{8,0},{12,4},{1,9},{5,13},{9,1},{13,5},{2,10},{6,14},... | collective-permute-start | bytes 983048 | tf_op jit(solution)/shard_map/ppermute | solution.py:21
  13.7 14.7 %collective-permute-start.6 = (bf16[128,1280]{1,0:T(8,128)(2,1)S(1)}, bf16[128,1280]{1,0:T(8,128)(2,1)S(1)}, u32[]{:S(2)}, u32[]{:S(2)}) collective-permute-start(bf16[128,1280]{1,0:T(8,128)(2,1)S(1)} %collective-permute-done.1.refs_3_.refs_5_.refs_2_), channel_id=1, source_target_pairs={{0,8},{4,12},{8,0},{12,4},{1,9},{5,13},{9,1},{13,5},{2,10},{6,14},... | collective-permute-start | bytes 983048 | tf_op jit(solution)/shard_map/ppermute | solution.py:21
  15.8 12.6 %collective-permute-start.7 = (bf16[128,1280]{1,0:T(8,128)(2,1)S(1)}, bf16[128,1280]{1,0:T(8,128)(2,1)S(1)}, u32[]{:S(2)}, u32[]{:S(2)}) collective-permute-start(bf16[128,1280]{1,0:T(8,128)(2,1)S(1)} %collective-permute-done.4.refs_6_.refs_10_.refs_2_.refs_5_), channel_id=1, source_target_pairs={{0,4},{4,0},{8,12},{12,8},{1,5},{5,1},{9,13},{13,9},{2,6},{6,2},{1... | collective-permute-start | bytes 983048 | tf_op jit(solution)/shard_map/ppermute | solution.py:21
  23.9 9.2 %copy-start.2 = (s32[128]{0:T(128)S(1)}, s32[128]{0:T(128)}, u32[]{:S(2)}) copy-start(s32[128]{0:T(128)} %param.7) | copy-start | bytes 1540
  23.9 9.2 %collective-permute-start.5 = (f32[392,128]{1,0:T(8,128)S(1)}, f32[392,128]{1,0:T(8,128)S(1)}, u32[]{:S(2)}, u32[]{:S(2)}) collective-permute-start(f32[392,128]{1,0:T(8,128)S(1)} %get-tuple-element.31), channel_id=1, source_target_pairs={{0,1},{1,0},{2,3},{3,2},{4,5},{5,4},{6,7},{7,6},{8,9},{9,8},{10,11... | collective-permute-start | bytes 602120 | tf_op jit(solution)/shard_map/ppermute | solution.py:21
  28.8 4.3 %collective-permute-start.8 = (f32[128,128]{1,0:T(8,128)S(1)}, f32[128,128]{1,0:T(8,128)S(1)}, u32[]{:S(2)}, u32[]{:S(2)}) collective-permute-start(f32[128,128]{1,0:T(8,128)S(1)} %get-tuple-element.34), channel_id=1, source_target_pairs={{0,1},{1,0},{2,3},{3,2},{4,5},{5,4},{6,7},{7,6},{8,9},{9,8},{10,11... | collective-permute-start | bytes 196616 | tf_op jit(solution)/shard_map/ppermute | solution.py:21
  33.7 13.5 %collective-permute-start.11 = (bf16[128,1792]{1,0:T(8,128)(2,1)S(1)}, bf16[128,1792]{1,0:T(8,128)(2,1)S(1)}, u32[]{:S(2)}, u32[]{:S(2)}) collective-permute-start(bf16[128,1792]{1,0:T(8,128)(2,1)S(1)} %first_message.1.first_ref), channel_id=1, source_target_pairs={{0,1},{1,0},{2,3},{3,2},{4,5},{5,4},{6,7},{7,6},{8,9},{9,8},{10,11... | collective-permute-start | bytes 1376264 | tf_op jit(solution)/shard_map/ppermute | solution.py:21
  35.3 6.4 %collective-permute-start.10 = (f32[2,128]{1,0:T(2,128)S(1)}, f32[2,128]{1,0:T(2,128)S(1)}, u32[]{:S(2)}, u32[]{:S(2)}) collective-permute-start(f32[2,128]{1,0:T(2,128)S(1)} %pad_maximum_fusion.refs_0_.own_ref), channel_id=1, source_target_pairs={{2,0},{4,2},{6,4},{8,6},{10,8},{12,10},{14,12},{1,3},{3,5},{5,7},{... | collective-permute-start | bytes 3080 | tf_op jit(solution)/shard_map/ppermute | solution.py:420
  37.8 12.9 %collective-permute-start.9 = (bf16[128,1280]{1,0:T(8,128)(2,1)S(1)}, bf16[128,1280]{1,0:T(8,128)(2,1)S(1)}, u32[]{:S(2)}, u32[]{:S(2)}) collective-permute-start(bf16[128,1280]{1,0:T(8,128)(2,1)S(1)} %second_message.1), channel_id=1, source_target_pairs={{0,1},{1,0},{2,3},{3,2},{4,5},{5,4},{6,7},{7,6},{8,9},{9,8},{10,11... | collective-permute-start | bytes 983048 | tf_op jit(solution)/shard_map/ppermute | solution.py:21
